TPU v7x, 256 devices: a whole 4x4x8 slice. The times are simulated.
256 devices in a mesh: seq: 32 (over z, x), head: 8 (over y, core).
Axes of the slice: x: 4, y: 4, z: 8, core: 2. Of those that a mesh axis runs over, the one named last changes fastest.
Arguments:
- mixer_input: bfloat16 [32768, 8192], P('seq', 'head'), may hold values from -6 to 6
- state_input: bfloat16 [32768, 256], P('seq'), may hold values from -6 to 6
- gate_input: bfloat16 [32768, 8192], P('seq', 'head'), may hold values from -6 to 6
- step_raw: float32 [32768, 64], P('seq', 'head'), may hold values from -2 to 1
- decay_rate: float32 [64], P('head'), may hold values from 2e-05 to 0.05
- conv_inner: bfloat16 [4, 8192], P(None, 'head'), may hold values from -3 to 3
- conv_state: bfloat16 [4, 256], replicated, may hold values from -3 to 3
- level_table: float32 [8, 13, 64], P(None, None, 'head'), may hold values from 0.25 to 2
- stretch_kind: int32 [512], P('seq'), may hold values from 0 to 7
- norm_gain: float32 [8192], P('head'), may hold values from 0.1 to 1.9
Outputs:
- mixed_out: bfloat16 [32768, 8192], P('seq', 'head')
Inputs may be any that keep to these rules, and one draw needn't show every extreme that they name: `stretch_kind`: each stretch of 64 tokens names one row of level_table.
All inputs are finite; a program needn't handle non-finite values.
Results may differ from a plain program's by a relative error of at most 0.0036.
Values may be sent and summed in bfloat16 or wider, within the bound.
No kernel may reach another device: no remote copies, remote signals or barrier semaphores. Data moves between devices by JAX's collectives and lax.ppermute only.
A program may use at most 128 MiB of HBM per device.

v0:
```python
import jax
import jax.numpy as jnp
from jax import lax
from jax.sharding import PartitionSpec as P

HIGHEST = lax.Precision.HIGHEST


def passed_along(value, axis, steps):
    count = lax.axis_size(axis)
    first, last = (max(0, -steps), min(count, count - steps))
    return lax.ppermute(value, axis, [(source, source + steps) for source in range(first, last)])


def bit_length(values, limit):
    result = jnp.zeros_like(values)
    for power in range(limit):
        result = result + (values >= 2**power).astype(jnp.int32)
    return result


def causal_conv(padded, kernel, length):
    width = kernel.shape[0]
    summed = jnp.zeros((length, padded.shape[1]), jnp.float32)
    for offset in range(width):
        summed = summed + padded[offset : offset + length].astype(jnp.float32) * kernel[
            offset
        ].astype(jnp.float32)
    return jax.nn.silu(summed).astype(jnp.bfloat16)


def token_table(kinds, level_table, stretch_len):
    kind_count, level_count, heads = level_table.shape
    stretches = kinds.shape[0]
    onehot = (kinds[:, None] == jnp.arange(kind_count, dtype=jnp.int32)[None, :]).astype(
        jnp.float32
    )
    rows = jnp.dot(onehot, level_table.reshape(kind_count, level_count * heads), precision=HIGHEST)
    rows = rows.reshape(stretches, 1, level_count, heads)
    return jnp.broadcast_to(rows, (stretches, stretch_len, level_count, heads)).reshape(
        stretches * stretch_len, level_count, heads
    )


def local_states(inner, keys_b, step_size, running):
    length = inner.shape[0]
    heads = running.shape[1]
    head_dim = inner.shape[1] // heads
    keys_f = keys_b.astype(jnp.float32)
    final = running[length - 1]

    def local_one_head(head):
        values = lax.dynamic_slice_in_dim(inner, head * head_dim, head_dim, 1)
        run_here = lax.dynamic_index_in_dim(running, head, 1, keepdims=False)
        step_here = lax.dynamic_index_in_dim(step_size, head, 1, keepdims=False)
        scale = (
            jnp.exp(lax.dynamic_index_in_dim(final, head, 0, keepdims=False) - run_here) * step_here
        )
        scaled_keys = (keys_f * scale[:, None]).astype(jnp.bfloat16)
        return jnp.dot(scaled_keys.T, values, preferred_element_type=jnp.float32)

    return lax.map(local_one_head, jnp.arange(heads, dtype=jnp.int32))


def fold_levels(sources, target, decays, states, seq_bits):
    device_ids = jnp.arange(decays.shape[0], dtype=jnp.int32)
    between = ((device_ids[None, :] > sources[:, None]) & (device_ids[None, :] < target)).astype(
        jnp.float32
    )
    span = jnp.dot(between, decays, precision=HIGHEST)
    level = bit_length(jnp.bitwise_xor(sources, target), seq_bits) - 1
    chosen = (
        (level[:, None] == jnp.arange(seq_bits, dtype=jnp.int32)[None, :])
        & (sources < target)[:, None]
    ).astype(jnp.float32)
    factor = chosen[:, :, None] * jnp.exp(span)[:, None, :]
    return jnp.einsum("jbh,jhnp->bhnp", factor, states, precision=HIGHEST)


def block_output(
    inner, keys_b, queries_c, step_size, running, token_weights, level_states, local_bits, seq_bits
):
    length = inner.shape[0]
    heads = running.shape[1]
    head_dim = inner.shape[1] // heads
    state_dim = keys_b.shape[1]
    stretch_len = length // 2**local_bits
    position = jnp.arange(length, dtype=jnp.int32)
    stretch_local = position // stretch_len
    pair_level = bit_length(
        jnp.bitwise_xor(stretch_local[:, None], stretch_local[None, :]), local_bits + 1
    )
    causal = position[:, None] >= position[None, :]
    scores = jnp.dot(queries_c, keys_b.T, preferred_element_type=jnp.float32)
    far_weights = (
        token_weights[:, local_bits + 1 : local_bits + 1 + seq_bits, :]
        * jnp.exp(running)[:, None, :]
    )
    queries_f = queries_c.astype(jnp.float32)
    far_rounded = level_states.astype(jnp.bfloat16)

    def block_one_head(head):
        values = lax.dynamic_slice_in_dim(inner, head * head_dim, head_dim, 1)
        weights_here = lax.dynamic_index_in_dim(token_weights, head, 2, keepdims=False)
        pair_weight = jnp.zeros((length, length), jnp.float32)
        for level in range(local_bits + 1):
            pair_weight = jnp.where(
                pair_level == level, weights_here[:, level][:, None], pair_weight
            )
        run_here = lax.dynamic_index_in_dim(running, head, 1, keepdims=False)
        step_here = lax.dynamic_index_in_dim(step_size, head, 1, keepdims=False)
        decay = jnp.exp(jnp.where(causal, run_here[:, None] - run_here[None, :], -jnp.inf))
        mixing = (scores * decay * step_here[None, :] * pair_weight).astype(jnp.bfloat16)
        local_out = jnp.dot(mixing, values, preferred_element_type=jnp.float32)
        far_here = lax.dynamic_index_in_dim(far_weights, head, 2, keepdims=False)
        lifted = (
            (far_here[:, :, None] * queries_f[:, None, :])
            .reshape(length, seq_bits * state_dim)
            .astype(jnp.bfloat16)
        )
        states_here = lax.dynamic_index_in_dim(far_rounded, head, 1, keepdims=False).reshape(
            seq_bits * state_dim, head_dim
        )
        return local_out + jnp.dot(lifted, states_here, preferred_element_type=jnp.float32)

    outputs = lax.map(block_one_head, jnp.arange(heads, dtype=jnp.int32))
    return jnp.transpose(outputs, (1, 0, 2)).reshape(length, heads * head_dim)


def local(
    mixer_input,
    state_input,
    gate_input,
    step_raw,
    decay_rate,
    conv_inner,
    conv_state,
    level_table,
    stretch_kind,
    norm_gain,
):
    length, local_width = mixer_input.shape
    state_dim = state_input.shape[1] // 2
    stretches_here = stretch_kind.shape[0]
    stretch_len = length // stretches_here
    local_bits = stretches_here.bit_length() - 1
    seq_bits = lax.axis_size("seq").bit_length() - 1
    width = conv_inner.shape[0]
    tails = jnp.concatenate(
        [mixer_input[length - width + 1 :], state_input[length - width + 1 :]], axis=1
    )
    previous = passed_along(tails, "seq", 1)
    inner = causal_conv(
        jnp.concatenate([previous[:, :local_width], mixer_input], axis=0), conv_inner, length
    )
    state_rows = causal_conv(
        jnp.concatenate([previous[:, local_width:], state_input], axis=0), conv_state, length
    )
    keys_b = state_rows[:, :state_dim]
    queries_c = state_rows[:, state_dim:]
    step_size = jax.nn.softplus(step_raw)
    log_decay = -decay_rate[None, :] * step_size
    running = jnp.cumsum(log_decay, axis=0)
    block_decay = running[length - 1]
    token_weights = token_table(stretch_kind, level_table, stretch_len)
    own_state = local_states(inner, keys_b, step_size, running)
    target = lax.axis_index("seq")
    decays = lax.all_gather(block_decay[None, :], "seq", axis=0, tiled=True)
    piece = lax.all_gather(own_state[None], "seq", axis=0, tiled=True)
    sources = jnp.arange(piece.shape[0], dtype=jnp.int32)
    level_states = fold_levels(sources, target, decays, piece, seq_bits)
    mixed = block_output(
        inner,
        keys_b,
        queries_c,
        step_size,
        running,
        token_weights,
        level_states,
        local_bits,
        seq_bits,
    )
    gated = mixed * jax.nn.silu(gate_input.astype(jnp.float32))
    squares = lax.psum(jnp.sum(gated * gated, axis=1), "head")
    total_width = local_width * lax.axis_size("head")
    scale = lax.rsqrt(squares / total_width + 1e-05)
    return (gated * scale[:, None] * norm_gain[None, :]).astype(jnp.bfloat16)


def solution(mesh):
    return jax.shard_map(
        local,
        mesh=mesh,
        in_specs=(
            P("seq", "head"),
            P("seq", None),
            P("seq", "head"),
            P("seq", "head"),
            P("head"),
            P(None, "head"),
            P(),
            P(None, None, "head"),
            P("seq"),
            P("head"),
        ),
        out_specs=P("seq", "head"),
        check_vma=False,
    )
```

profile of v0, /device:TPU:32, one launch (start us, length us, event | category | flops | bytes accessed | tf_op | source)
XLA Modules:
  0.0 383.2 jit_solution(11300511833036215478)
XLA Ops:
  8.0 3.4 collective-permute-start
  14.6 2.3 reduce-window.6
  21.0 6.1 %multiply_convert_fusion.6 = bf16[1024,1024]{1,0:T(8,128)(2,1)S(1)} fusion(bf16[1024,1024]{1,0:T(8,128)(2,1)} %param.14, bf16[3,1024]{1,0:T(4,128)(2,1)S(1)} %slice.135, f32[1024]{0:T(1024)S(1)} %bitcast.145, f32[1024]{0:T(1024)S(1)} %bitcast.146, f32[1024]{0:T(1024)S(1)} %bitcast.144, f32[1024]{0:T(1024)S(1)} %bitcast.143), kind=kLoop, calls=%fused_computation.49 | loop fusion | flops 26214400 | bytes 4216832 | tf_op jit(solution)/shard_map/convert_element_type | solution.py:29
  27.1 44.5 %while.22 = (s32[]{:T(128)}, f32[8,128,128]{2,1,0:T(8,128)}, s32[8]{0:T(128)S(1)}, f32[8]{0:T(128)S(1)}, f32[1024,8]{0,1:T(8,128)S(1)}, /*index=5*/f32[1024,8]{0...) while((s32[]{:T(128)}, f32[8,128,128]{2,1,0:T(8,128)}, ...), condition=%wide.region_3.4_spmd, body=%wide.region_2.3_spmd.sunk | while | flops 33818632 | bytes 869105 | solution.py:62
  73.7 40.8 %all-gather.1 = f32[32,1,8]{2,1,0:T(1,128)S(1)} all-gather(f32[1,1,8]{2,1,0:T(1,128)S(1)} %bitcast.151), channel_id=1, replica_groups=mesh['seq'=32,'head'=8] {'seq'}, dimensions={0}, use_global_device_ids=true | all-gather | bytes 1056 | tf_op jit(solution)/shard_map/all_gather | solution.py:168
  115.7 3.7 fusion.33
  119.4 93.4 %all-gather.4.cloned.1.call-done = f32[256,128,128]{2,1,0:T(8,128)} async-done(((f32[8,128,128]{2,1,0:T(8,128)}), f32[256,128,128]{2,1,0:T(8,128)}) %all-gather.4.cloned.1.call-update) | async-done | bytes 16777232 | tf_op jit(solution)/shard_map/all_gather | solution.py:169
  212.8 22.3 %convert_bitcast_fusion = bf16[5,8,128,128]{3,0,2,1:T(8,128)(2,1)S(1)} fusion(f32[32,8,128,128]{3,2,1,0:T(8,128)} %bitcast.126, f32[32,8]{0,1:T(8,128)S(1)} %convolution_exponential_fusion, f32[32,5]{0,1:T(8,128)S(1)} %fusion.50), kind=kOutput, calls=%fused_computation.55 | convolution fusion | flops 252314880 | bytes 18089600 | tf_op jit(solution)/shard_map/jbh,jhnp->bhnp/dot_general | solution.py:77
  235.1 1.4 copy.50
  236.5 117.7 %while.23 = (s32[]{:T(128)}, f32[8,1024,128]{2,1,0:T(8,128)}, s32[8]{0:T(128)S(1)}, f32[1024,8]{0,1:T(8,128)S(1)}, f32[1024,1024]{1,0:T(8,128)}, /*index=5*/f32[...) while((s32[]{:T(128)}, f32[8,1024,128]{2,1,0:T(8,128)}, ...), condition=%wide.region_5.6_spmd.clone.clone, body=%wide.region_4.5_spmd.clone.clone.sunk | while | flops 471203840 | bytes 10081037 | solution.py:126
  241.5 7.0 %fusion.79 = f32[1024,128]{1,0:T(8,128)S(1)} fusion(f32[1024,1024]{1,0:T(8,128)} %get-tuple-element.533, s32[1024]{0:T(1024)S(1)} %get-tuple-element.540, f32[1024]{0:T(1024)S(1)} %bitcast.134, f32[1024]{0:T(1024)S(1)} %bitcast.135, f32[1024]{0:T(1024)S(1)} %bitcast.136, f32[1024]{0:T(1024)S(1)} %bitcast.137, f32[1024]{0:T(1024)S(1)} %bitcast.133, ...), kind=kOutput, calls=%fused_computation.18.clone.1 | convolution fusion | flops 301989888 | bytes 5021700 | tf_op jit(solution)/shard_map/while/body/eval_jaxpr/dot_general | solution.py:114
  256.2 7.0 %fusion.79 = f32[1024,128]{1,0:T(8,128)S(1)} fusion(f32[1024,1024]{1,0:T(8,128)} %get-tuple-element.533, s32[1024]{0:T(1024)S(1)} %get-tuple-element.540, f32[1024]{0:T(1024)S(1)} %bitcast.134, f32[1024]{0:T(1024)S(1)} %bitcast.135, f32[1024]{0:T(1024)S(1)} %bitcast.136, f32[1024]{0:T(1024)S(1)} %bitcast.137, f32[1024]{0:T(1024)S(1)} %bitcast.133, ...), kind=kOutput, calls=%fused_computation.18.clone.1 | convolution fusion | flops 301989888 | bytes 5021700 | tf_op jit(solution)/shard_map/while/body/eval_jaxpr/dot_general | solution.py:114
  264.5 1.4 fusion.80
  270.9 7.0 %fusion.79 = f32[1024,128]{1,0:T(8,128)S(1)} fusion(f32[1024,1024]{1,0:T(8,128)} %get-tuple-element.533, s32[1024]{0:T(1024)S(1)} %get-tuple-element.540, f32[1024]{0:T(1024)S(1)} %bitcast.134, f32[1024]{0:T(1024)S(1)} %bitcast.135, f32[1024]{0:T(1024)S(1)} %bitcast.136, f32[1024]{0:T(1024)S(1)} %bitcast.137, f32[1024]{0:T(1024)S(1)} %bitcast.133, ...), kind=kOutput, calls=%fused_computation.18.clone.1 | convolution fusion | flops 301989888 | bytes 5021700 | tf_op jit(solution)/shard_map/while/body/eval_jaxpr/dot_general | solution.py:114
  279.2 1.4 fusion.80
  285.7 7.0 %fusion.79 = f32[1024,128]{1,0:T(8,128)S(1)} fusion(f32[1024,1024]{1,0:T(8,128)} %get-tuple-element.533, s32[1024]{0:T(1024)S(1)} %get-tuple-element.540, f32[1024]{0:T(1024)S(1)} %bitcast.134, f32[1024]{0:T(1024)S(1)} %bitcast.135, f32[1024]{0:T(1024)S(1)} %bitcast.136, f32[1024]{0:T(1024)S(1)} %bitcast.137, f32[1024]{0:T(1024)S(1)} %bitcast.133, ...), kind=kOutput, calls=%fused_computation.18.clone.1 | convolution fusion | flops 301989888 | bytes 5021700 | tf_op jit(solution)/shard_map/while/body/eval_jaxpr/dot_general | solution.py:114
  300.4 7.0 %fusion.79 = f32[1024,128]{1,0:T(8,128)S(1)} fusion(f32[1024,1024]{1,0:T(8,128)} %get-tuple-element.533, s32[1024]{0:T(1024)S(1)} %get-tuple-element.540, f32[1024]{0:T(1024)S(1)} %bitcast.134, f32[1024]{0:T(1024)S(1)} %bitcast.135, f32[1024]{0:T(1024)S(1)} %bitcast.136, f32[1024]{0:T(1024)S(1)} %bitcast.137, f32[1024]{0:T(1024)S(1)} %bitcast.133, ...), kind=kOutput, calls=%fused_computation.18.clone.1 | convolution fusion | flops 301989888 | bytes 5021700 | tf_op jit(solution)/shard_map/while/body/eval_jaxpr/dot_general | solution.py:114
  315.1 7.0 %fusion.79 = f32[1024,128]{1,0:T(8,128)S(1)} fusion(f32[1024,1024]{1,0:T(8,128)} %get-tuple-element.533, s32[1024]{0:T(1024)S(1)} %get-tuple-element.540, f32[1024]{0:T(1024)S(1)} %bitcast.134, f32[1024]{0:T(1024)S(1)} %bitcast.135, f32[1024]{0:T(1024)S(1)} %bitcast.136, f32[1024]{0:T(1024)S(1)} %bitcast.137, f32[1024]{0:T(1024)S(1)} %bitcast.133, ...), kind=kOutput, calls=%fused_computation.18.clone.1 | convolution fusion | flops 301989888 | bytes 5021700 | tf_op jit(solution)/shard_map/while/body/eval_jaxpr/dot_general | solution.py:114
  329.8 7.0 %fusion.79 = f32[1024,128]{1,0:T(8,128)S(1)} fusion(f32[1024,1024]{1,0:T(8,128)} %get-tuple-element.533, s32[1024]{0:T(1024)S(1)} %get-tuple-element.540, f32[1024]{0:T(1024)S(1)} %bitcast.134, f32[1024]{0:T(1024)S(1)} %bitcast.135, f32[1024]{0:T(1024)S(1)} %bitcast.136, f32[1024]{0:T(1024)S(1)} %bitcast.137, f32[1024]{0:T(1024)S(1)} %bitcast.133, ...), kind=kOutput, calls=%fused_computation.18.clone.1 | convolution fusion | flops 301989888 | bytes 5021700 | tf_op jit(solution)/shard_map/while/body/eval_jaxpr/dot_general | solution.py:114
  344.5 7.0 %fusion.79 = f32[1024,128]{1,0:T(8,128)S(1)} fusion(f32[1024,1024]{1,0:T(8,128)} %get-tuple-element.533, s32[1024]{0:T(1024)S(1)} %get-tuple-element.540, f32[1024]{0:T(1024)S(1)} %bitcast.134, f32[1024]{0:T(1024)S(1)} %bitcast.135, f32[1024]{0:T(1024)S(1)} %bitcast.136, f32[1024]{0:T(1024)S(1)} %bitcast.137, f32[1024]{0:T(1024)S(1)} %bitcast.133, ...), kind=kOutput, calls=%fused_computation.18.clone.1 | convolution fusion | flops 301989888 | bytes 5021700 | tf_op jit(solution)/shard_map/while/body/eval_jaxpr/dot_general | solution.py:114
  352.8 1.4 fusion.80
  354.2 3.5 multiply_reduce_fusion
  357.7 14.2 %psum.7 = f32[1024]{0:T(1024)S(1)} all-reduce(f32[1024]{0:T(1024)S(1)} %multiply_reduce_fusion), channel_id=1, replica_groups=mesh['seq'=32,'head'=8] {'head'}, use_global_device_ids=true, to_apply=%region_7.8 | all-reduce | flops 1024 | bytes 8192 | tf_op jit(solution)/shard_map/psum | solution.py:184
  371.9 4.4 %multiply_convert_fusion.5 = bf16[1024,1024]{1,0:T(8,128)(2,1)} fusion(f32[1024]{0:T(1024)S(1)} %copy-done.5, f32[1024]{0:T(1024)S(1)} %add_rsqrt_fusion, bf16[1024,1024]{1,0:T(8,128)(2,1)S(1)} %copy-done, f32[8,1024,128]{2,1,0:T(8,128)} %get-tuple-element.127), kind=kLoop, calls=%fused_computation.47 | loop fusion | flops 9437184 | bytes 8396800 | tf_op jit(solution)/shard_map/convert_element_type | solution.py:187
  (164 shorter events, 72.3 us)
Async XLA Ops:
  6.5 206.3 %all-gather.4.cloned.1.call-start = ((), (), s32[]{:S(2)}) async-start(), calls=%async_computation | async-start | bytes 17301504 | tf_op jit(solution)/shard_map/all_gather | solution.py:169
  8.0 10.7 %collective-permute-start = (bf16[3,1280]{1,0:T(4,128)(2,1)S(1)}, bf16[3,1280]{1,0:T(4,128)(2,1)S(1)}, u32[]{:S(2)}, u32[]{:S(2)}) collective-permute-start(bf16[3,1280]{1,0:T(4,128)(2,1)S(1)} %pad_maximum_fusion.2), channel_id=1, source_target_pairs={{0,8},{8,16},{16,24},{24,32},{32,40},{40,48},{48,56},{56,64},{64,7... | collective-permute-start | bytes 23048 | tf_op jit(solution)/shard_map/ppermute | solution.py:12
  19.9 0.9 copy-start.2
  20.9 50.7 %copy-start.4 = (f32[8,13,8]{1,2,0:T(8,128)S(1)}, f32[8,13,8]{1,2,0:T(8,128)}, u32[]{:S(2)}) copy-start(f32[8,13,8]{1,2,0:T(8,128)} %param.21) | copy-start | bytes 9988
  20.9 51.2 %copy-start.6 = (s32[16]{0:T(128)S(1)}, s32[16]{0:T(128)}, u32[]{:S(2)}) copy-start(s32[16]{0:T(128)} %param.22) | copy-start | bytes 196
  71.6 0.6 copy-start.3
  71.6 163.5 %copy-start.1 = (bf16[1024,1024]{1,0:T(8,128)(2,1)}, bf16[1024,1024]{1,0:T(8,128)(2,1)S(1)}, u32[]{:S(2)}) copy-start(bf16[1024,1024]{1,0:T(8,128)(2,1)S(1)} %get-tuple-element.548) | copy-start | bytes 6291460
  236.5 117.7 %copy-start = (bf16[1024,1024]{1,0:T(8,128)(2,1)S(1)}, bf16[1024,1024]{1,0:T(8,128)(2,1)}, u32[]{:S(2)}) copy-start(bf16[1024,1024]{1,0:T(8,128)(2,1)} %param.16) | copy-start | bytes 6291460
  354.1 17.8 %copy-start.5 = (f32[1024]{0:T(1024)S(1)}, f32[1024]{0:T(1024)}, u32[]{:S(2)}) copy-start(f32[1024]{0:T(1024)} %param.23) | copy-start | bytes 12292
Sparse Core Ops, SparseCore 0:
  71.7 141.0 all-gather.3
where the time goes:
time: 387 us; the launch traced here: 383 us
  matrix products  102 us (26%)
  waiting for transfers between devices  93.4 us (24%)
  blocking collectives  55 us (14%)
  local copies, waits for them, and re-layouts  44.9 us (12%)
  loops' own time  41.3 us (11%)
  other arithmetic  29.1 us (8%)
  between operations  13.6 us (4%)
    all_gather x1, waiting for transfers between devices, local(): piece = lax.all_gather(own_state[None], 'seq', axis=0, tiled=True)  93.4 us
    dot_general x8, matrix products, block_one_head(): local_out = jnp.dot(mixing, values, preferred_element_type=jnp.float32)  56.4 us
    all_gather x1, blocking collectives, local(): decays = lax.all_gather(block_decay[None, :], 'seq', axis=0, tiled=True)  40.8 us
    dot_general x1, matrix products, fold_levels(): return jnp.einsum('jbh,jhnp->bhnp', factor, states, precision=HIGHEST)  22.3 us
    another operation x1, loops' own time, block_output(): outputs = lax.map(block_one_head, jnp.arange(heads, dtype=jnp.int32))  20.8 us
    another operation x1, loops' own time, local_states(): return lax.map(local_one_head, jnp.arange(heads, dtype=jnp.int32))  20.5 us
    psum x1, blocking collectives, local(): squares = lax.psum(jnp.sum(gated * gated, axis=1), 'head')  14.2 us
    dot_general x8, matrix products, block_one_head(): jnp.dot(lifted, states_here, preferred_element_type=jnp.float32)  10.9 us
  transfers between devices with their start and end apart: 2, of which 1 were waited for; matrix products, arithmetic and copies ran while one was open for 4% of the time, Pallas kernels for 0%

commit v1 on v0

v1 whole, which is shorter than its diff:
```python
import functools
import jax
import jax.numpy as jnp
from jax import lax
from jax.experimental import pallas as pl
from jax.experimental.pallas import tpu as pltpu
from jax.sharding import PartitionSpec as P

F32 = jnp.float32
BF16 = jnp.bfloat16
HIGHEST = lax.Precision.HIGHEST

XS = 4
ZS = 8
YS = 4
CORES = 2
PAIR = 2
DIM = 128
HALO = 16
TILE = 128
MESSAGE = PAIR * DIM + 8


def seq_perm(move):
    pairs = []
    for z in range(ZS):
        for x in range(XS):
            target = move(z, x)
            if target is not None:
                pairs.append((z * XS + x, target[0] * XS + target[1]))
    return pairs


def head_perm(move):
    pairs = []
    for y in range(YS):
        for core in range(CORES):
            target = move(y, core)
            pairs.append((y * CORES + core, target[0] * CORES + target[1]))
    return pairs


def along_x(value, step):
    return lax.ppermute(value, "seq", seq_perm(lambda z, x: (z, (x + step) % XS)))


def silu(value):
    return value / (1.0 + jnp.exp(-value))


def whole(*dims):
    return pl.BlockSpec(dims, lambda *_: (0,) * len(dims))


def conv(block, halo, taps):
    length = block.shape[0]
    width = taps.shape[0]
    joined = jnp.concatenate([halo[HALO - 8 :].astype(F32), block.astype(F32)], axis=0)
    taps = taps.astype(F32)
    total = jnp.zeros((length, block.shape[1]), F32)
    for offset in range(width):
        shift = width - 1 - offset
        moved = joined if shift == 0 else pltpu.roll(joined, shift, axis=0)
        total = total + moved[8:] * taps[offset : offset + 1]
    return silu(total).astype(BF16)


def prepare_kernel(
    place,
    mixer,
    mixer_halo,
    state,
    state_halo,
    taps,
    state_taps,
    step_raw,
    rate,
    inner,
    rows,
    running_out,
    step_out,
    part0,
    part1,
    part2,
    part3,
    keys_t,
    scale,
    last,
):
    turn = pl.program_id(0)
    parts = (part0, part1, part2, part3)
    heads, length = step_raw.shape

    @pl.when(turn == 0)
    def _():
        raw = step_raw[...]
        step = jnp.maximum(raw, 0.0) + jnp.log1p(jnp.exp(-jnp.abs(raw)))
        running = -rate[...] * step
        lane = lax.broadcasted_iota(jnp.int32, (heads, length), 1)
        shift = 1
        while shift < length:
            moved = pltpu.roll(running, shift, axis=1)
            running = running + jnp.where(lane >= shift, moved, 0.0)
            shift *= 2
        final = running[:, length - 1 :]
        running_out[...] = running
        step_out[...] = step
        scale[...] = jnp.exp(final - running) * step
        last[...] = jnp.broadcast_to(final, last.shape)
        state_rows = conv(state[...], state_halo[...], state_taps[...])
        rows[...] = state_rows
        keys_t[...] = state_rows[:, :DIM].astype(F32).T

    values = conv(mixer[...], mixer_halo[...], taps[...])
    inner[...] = values
    pair = lax.rem(place[0] + turn, XS)
    states = []
    for head in range(PAIR):
        row = scale[pl.ds(pair * PAIR + head, 1), :]
        scaled_t = (keys_t[...] * row).astype(BF16)
        states.append(
            jnp.dot(
                scaled_t, values[:, head * DIM : (head + 1) * DIM], preferred_element_type=F32
            )
        )
    first = last[pl.ds(pair * PAIR, 1), :]
    second = last[pl.ds(pair * PAIR + 1, 1), :]
    spot = lax.broadcasted_iota(jnp.int32, (8, DIM), 0)
    decay_rows = jnp.where(spot == 0, first, jnp.where(spot == 1, second, 0.0))
    for index, part in enumerate(parts):

        @pl.when(turn == index)
        def _(part=part):
            part[:DIM] = states[0]
            part[DIM : 2 * DIM] = states[1]
            part[2 * DIM :] = decay_rows


def prepare(place, mixer, halo, state, taps, state_taps, step_raw_t, rate):
    length, width = mixer.shape
    heads = step_raw_t.shape[0]
    wide = PAIR * DIM

    def column(turn, place):
        return (0, lax.rem(place[0] + turn, XS))

    part = jax.ShapeDtypeStruct((MESSAGE, DIM), F32)
    return pl.pallas_call(
        prepare_kernel,
        grid_spec=pltpu.PrefetchScalarGridSpec(
            num_scalar_prefetch=1,
            grid=(XS,),
            in_specs=[
                pl.BlockSpec((length, wide), column),
                pl.BlockSpec((HALO, wide), column),
                whole(length, 2 * DIM),
                pl.BlockSpec((HALO, 2 * DIM), lambda *_: (0, width // (2 * DIM))),
                pl.BlockSpec((taps.shape[0], wide), column),
                whole(*state_taps.shape),
                whole(heads, length),
                whole(heads, 1),
            ],
            out_specs=[
                pl.BlockSpec((length, wide), column),
                whole(length, 2 * DIM),
                whole(heads, length),
                whole(heads, length),
            ]
            + [whole(MESSAGE, DIM)] * XS,
            scratch_shapes=[
                pltpu.VMEM((DIM, length), F32),
                pltpu.VMEM((heads, length), F32),
                pltpu.VMEM((heads, DIM), F32),
            ],
        ),
        out_shape=[
            jax.ShapeDtypeStruct((length, width), BF16),
            jax.ShapeDtypeStruct((length, 2 * DIM), BF16),
            jax.ShapeDtypeStruct((heads, length), F32),
            jax.ShapeDtypeStruct((heads, length), F32),
        ]
        + [part] * XS,
        compiler_params=pltpu.CompilerParams(vmem_limit_bytes=24 * 2**20),
        cost_estimate=pl.CostEstimate(
            flops=2 * length * width * DIM, bytes_accessed=8 * 2**20, transcendentals=2 * length * width
        ),
        name="prepare",
    )(place, mixer, halo, state, halo, taps, state_taps, step_raw_t, rate)


def local_kernel(inner, rows, running_in, step_in, table, kinds, out, far_rows, scores, weights):
    head = pl.program_id(0)
    length = inner.shape[0]
    tiles = length // TILE
    local_bits = 4

    @pl.when(head == 0)
    def _():
        for i in range(tiles):
            wide = (i + 1) * TILE
            scores[i * TILE : wide, :wide] = lax.dot_general(
                rows[i * TILE : wide, DIM:],
                rows[:wide, :DIM],
                (((1,), (1,)), ((), ())),
                preferred_element_type=F32,
            )
        spot = lax.broadcasted_iota(jnp.int32, (8, length), 0)
        onehot = (spot == kinds[...]).astype(F32)
        weights[...] = jnp.dot(table[...], onehot, precision=HIGHEST, preferred_element_type=F32)

    running = running_in[pl.ds(head, 1), :]
    step = step_in[pl.ds(head, 1), :]
    starts = [running[:, i * TILE : i * TILE + 1] for i in range(tiles)]
    ahead = jnp.concatenate(
        [jnp.exp(running[:, i * TILE : (i + 1) * TILE] - starts[i]) for i in range(tiles)], axis=1
    )
    near = weights[pl.ds(pl.multiple_of(head * 16, 16), 8), :] * ahead
    far = weights[pl.ds(pl.multiple_of(head * 16 + 8, 8), 8), :] * jnp.exp(running)
    far_rows[0] = far
    near_columns = near.T
    row = lax.broadcasted_iota(jnp.int32, (TILE, TILE), 0)
    lane = lax.broadcasted_iota(jnp.int32, (TILE, TILE), 1)
    causal = row >= lane
    crossed = (row >= TILE // 2) & (lane < TILE // 2)
    for i in range(tiles):
        wide = (i + 1) * TILE
        behind = jnp.exp(starts[i] - running[:, :wide]) * step[:, :wide]
        here = near_columns[i * TILE : wide]
        level_columns = [
            jnp.broadcast_to(here[:, level : level + 1], (TILE, TILE))
            for level in range(local_bits + 1)
        ]
        pieces = []
        for j in range(i + 1):
            piece = scores[i * TILE : wide, j * TILE : (j + 1) * TILE]
            piece = piece * behind[:, j * TILE : (j + 1) * TILE]
            if j < i:
                piece = piece * level_columns[(i ^ j).bit_length() + 1]
            else:
                piece = piece * jnp.where(crossed, level_columns[1], level_columns[0])
                piece = jnp.where(causal, piece, 0.0)
            pieces.append(piece.astype(BF16))
        mixing = jnp.concatenate(pieces, axis=1)
        out[i * TILE : wide] = jnp.dot(mixing, inner[:wide], preferred_element_type=F32)


def local_part(inner, rows, running, step, table, kinds):
    length, width = inner.shape
    heads = width // DIM
    return pl.pallas_call(
        local_kernel,
        grid=(heads,),
        in_specs=[
            pl.BlockSpec((length, DIM), lambda head: (0, head)),
            whole(length, 2 * DIM),
            whole(heads, length),
            whole(heads, length),
            whole(*table.shape),
            whole(1, length),
        ],
        out_specs=[
            pl.BlockSpec((length, DIM), lambda head: (0, head)),
            pl.BlockSpec((1, 8, length), lambda head: (head, 0, 0)),
        ],
        out_shape=[
            jax.ShapeDtypeStruct((length, width), F32),
            jax.ShapeDtypeStruct((heads, 8, length), F32),
        ],
        scratch_shapes=[pltpu.VMEM((length, length), F32), pltpu.VMEM((heads * 16, length), F32)],
        compiler_params=pltpu.CompilerParams(vmem_limit_bytes=24 * 2**20),
        cost_estimate=pl.CostEstimate(
            flops=8 * length * length * DIM, bytes_accessed=8 * 2**20, transcendentals=2**18
        ),
        name="local_part",
    )(inner, rows, running, step, table, kinds)


def flag(condition):
    return jnp.where(condition, 1.0, 0.0).astype(F32)


def fold_row_kernel(place, p0, p1, p2, p3, row_out, m0, m1, m2, m3):
    x = place[0]
    parts = (p0, p1, p2, p3)
    owner = [lax.rem(x + XS - k, XS) for k in range(XS)]
    decays = [part[2 * DIM :] for part in parts]

    def from_block(block):
        return [flag(owner[k] == block) for k in range(XS)]

    def pick(values, chosen):
        return sum(value * mark for value, mark in zip(values, chosen))

    block_marks = [from_block(block) for block in range(XS)]
    later = [
        jnp.exp(sum(decays[m] * flag(owner[m] > owner[k]) for m in range(XS))) for k in range(XS)
    ]
    decay_one = jnp.exp(pick(decays, block_marks[1]))
    decay_two = jnp.exp(pick(decays, block_marks[2]))
    for head in range(PAIR):
        span = slice(head * DIM, (head + 1) * DIM)
        blocks = [part[span] for part in parts]
        row_out[span] = sum(blocks[k] * later[k][head : head + 1] for k in range(XS))
        first = pick(blocks, block_marks[0])
        third = pick(blocks, block_marks[2])
        joined = first * decay_one[head : head + 1] + pick(blocks, block_marks[1])
        for k, message in enumerate((m0, m1, m2, m3)):
            target = lax.rem(x + k, XS)
            message[span] = (
                first * flag(target == 1) + third * flag(target == 3)
            ).astype(BF16)
            message[PAIR * DIM + head * DIM : PAIR * DIM + (head + 1) * DIM] = (
                joined
                * (flag(target == 2) + flag(target == 3) * decay_two[head : head + 1])
            ).astype(BF16)
    row_out[2 * DIM :] = sum(decays)


SMEM = pl.BlockSpec(memory_space=pltpu.SMEM)


def fold_row(place, parts):
    return pl.pallas_call(
        fold_row_kernel,
        in_specs=[SMEM] + [whole(MESSAGE, DIM)] * XS,
        out_specs=[whole(MESSAGE, DIM)] + [whole(4 * DIM, DIM)] * XS,
        out_shape=[jax.ShapeDtypeStruct((MESSAGE, DIM), F32)]
        + [jax.ShapeDtypeStruct((4 * DIM, DIM), BF16)] * XS,
        grid=(1,),
        cost_estimate=pl.CostEstimate(flops=2**20, bytes_accessed=2**20, transcendentals=2**10),
        name="fold_row",
    )(place, *parts)


def fold_pair_kernel(place, own, other, pair_out):
    upper = flag(lax.rem(place[1], 2) == 1)
    own_decay = own[2 * DIM :]
    other_decay = other[2 * DIM :]
    own_scale = jnp.exp(other_decay * (1.0 - upper))
    other_scale = jnp.exp(own_decay * upper)
    for head in range(PAIR):
        span = slice(head * DIM, (head + 1) * DIM)
        pair_out[span] = (
            own[span] * own_scale[head : head + 1] + other[span] * other_scale[head : head + 1]
        )
    pair_out[2 * DIM :] = own_decay + other_decay


def fold_pair(place, own, other):
    return pl.pallas_call(
        fold_pair_kernel,
        in_specs=[SMEM] + [whole(MESSAGE, DIM)] * 2,
        out_specs=whole(MESSAGE, DIM),
        out_shape=jax.ShapeDtypeStruct((MESSAGE, DIM), F32),
        grid=(1,),
        cost_estimate=pl.CostEstimate(flops=2**18, bytes_accessed=2**19, transcendentals=2**10),
        name="fold_pair",
    )(place, own, other)


def fold_far_kernel(place, d0, d1, d2, d3, other, g1, g2, g3, m0, m1, m2, m3):
    x = place[0]
    z = place[1]
    upper = flag(lax.rem(z, 2) == 1)
    pair = lax.div(z, 2)
    odd_pair = flag(lax.rem(pair, 2) == 1)
    third_pair = flag(pair == 2)
    last_pair = flag(pair == 3)
    decays = [d0[...], d1[...], d2[...], d3[...]]
    owner = [lax.rem(x + XS - k, XS) for k in range(XS)]
    in_pair = other[2 * DIM :] * upper
    after = in_pair + g1[2 * DIM :] * last_pair
    inside_first = jnp.exp(g1[2 * DIM :])
    inside_last = jnp.exp(g2[2 * DIM :])
    for head in range(PAIR):
        span = slice(head * DIM, (head + 1) * DIM)
        row = slice(head, head + 1)
        two = other[span]
        three = g1[span]
        four = (g2[span] * inside_first[row] + three) * third_pair + (
            g3[span] * inside_last[row] + g2[span]
        ) * last_pair
        for k, message in enumerate((m0, m1, m2, m3)):
            target = lax.rem(x + k, XS)
            before = sum(decays[m][row] * flag(owner[m] < target) for m in range(XS))
            factors = (
                jnp.exp(before) * upper,
                jnp.exp(before + in_pair[row]) * odd_pair,
                jnp.exp(before + after[row]),
            )
            for level, (state, factor) in enumerate(zip((two, three, four), factors)):
                base = level * PAIR * DIM + head * DIM
                message[base : base + DIM] = (state * factor).astype(BF16)


def fold_far(place, parts, other, gathered):
    decay_rows = pl.BlockSpec((8, DIM), lambda *_: (2 * DIM // 8, 0))
    return pl.pallas_call(
        fold_far_kernel,
        in_specs=[SMEM] + [decay_rows] * XS + [whole(MESSAGE, DIM)] * 4,
        out_specs=[whole(6 * DIM, DIM)] * XS,
        out_shape=[jax.ShapeDtypeStruct((6 * DIM, DIM), BF16)] * XS,
        grid=(1,),
        cost_estimate=pl.CostEstimate(flops=2**20, bytes_accessed=2**20, transcendentals=2**12),
        name="fold_far",
    )(place, *parts, other, *gathered)


def far_kernel(
    place, local, gate, rows, far_rows, n0, n1, n2, n3, f0, f1, f2, f3, gated, squares, held, total
):
    turn = pl.program_id(0)
    length = local.shape[0]
    for k, (near, far) in enumerate(((n0, f0), (n1, f1), (n2, f2), (n3, f3))):

        @pl.when(turn == k)
        def _(near=near, far=far):
            for head in range(PAIR):
                for level in range(2):
                    base = (level * PAIR + head) * DIM
                    held[head, level * DIM : (level + 1) * DIM] = near[base : base + DIM]
                for level in range(3):
                    base = (level * PAIR + head) * DIM
                    held[head, (level + 2) * DIM : (level + 3) * DIM] = far[base : base + DIM]

    @pl.when(turn == 0)
    def _():
        total[...] = jnp.zeros_like(total)

    step = 256
    columns = [far_rows[head].T for head in range(PAIR)]
    for start in range(0, length, step):
        span = slice(start, start + step)
        queries = rows[span, DIM:].astype(F32)
        gates = silu(gate[span].astype(F32))
        for head in range(PAIR):
            lane = slice(head * DIM, (head + 1) * DIM)
            lifted = jnp.concatenate(
                [
                    (queries * columns[head][span, level : level + 1]).astype(BF16)
                    for level in range(5)
                ],
                axis=1,
            )
            mixed = local[span, lane] + jnp.dot(lifted, held[head], preferred_element_type=F32)
            value = mixed * gates[:, lane]
            gated[span, lane] = value
            total[span] += value * value

    @pl.when(turn == XS - 1)
    def _():
        for tile in range(length // TILE):
            part = total[tile * TILE : (tile + 1) * TILE].T
            squares[tile : tile + 1] = jnp.sum(part, axis=0, keepdims=True)


def far_part(place, local, gate, rows, far_rows, near_states, far_states):
    length, width = local.shape
    wide = PAIR * DIM

    def pair(turn, place):
        return lax.rem(place[0] + XS - turn, XS)

    def column(turn, place):
        return (0, pair(turn, place))

    return pl.pallas_call(
        far_kernel,
        grid_spec=pltpu.PrefetchScalarGridSpec(
            num_scalar_prefetch=1,
            grid=(XS,),
            in_specs=[
                pl.BlockSpec((length, wide), column),
                pl.BlockSpec((length, wide), column),
                whole(length, 2 * DIM),
                pl.BlockSpec((PAIR, 8, length), lambda turn, place: (pair(turn, place), 0, 0)),
            ]
            + [whole(4 * DIM, DIM)] * XS
            + [whole(6 * DIM, DIM)] * XS,
            out_specs=[
                pl.BlockSpec((length, wide), column),
                whole(length // TILE, TILE),
            ],
            scratch_shapes=[pltpu.VMEM((PAIR, 5 * DIM, DIM), BF16), pltpu.VMEM((length, DIM), F32)],
        ),
        out_shape=[
            jax.ShapeDtypeStruct((length, width), F32),
            jax.ShapeDtypeStruct((length // TILE, TILE), F32),
        ],
        compiler_params=pltpu.CompilerParams(vmem_limit_bytes=24 * 2**20),
        cost_estimate=pl.CostEstimate(
            flops=10 * length * width * DIM, bytes_accessed=12 * 2**20, transcendentals=2**20
        ),
        name="far_part",
    )(place, local, gate, rows, far_rows, *near_states, *far_states)


def norm_kernel(total_width, gated, s0, s1, s2, s3, gain, out):
    scale = lax.rsqrt((s0[...] + s1[...] + s2[...] + s3[...]) / total_width + 1e-05)
    tiles = scale.shape[0]
    which = lax.broadcasted_iota(jnp.int32, scale.shape, 0)
    here = pl.program_id(0)
    row = jnp.sum(jnp.where(which == here, scale, 0.0), axis=0, keepdims=True)
    column = jnp.broadcast_to(row, (TILE, TILE)).T
    for piece in range(gated.shape[1] // TILE):
        lane = slice(piece * TILE, (piece + 1) * TILE)
        out[:, lane] = (gated[:, lane] * column * gain[:, lane]).astype(BF16)


def norm(gated, squares, gain, total_width):
    length, width = gated.shape
    tiles = length // TILE
    return pl.pallas_call(
        functools.partial(norm_kernel, total_width),
        grid=(tiles,),
        in_specs=[pl.BlockSpec((TILE, width), lambda i: (i, 0))]
        + [whole(tiles, TILE)] * YS
        + [whole(1, width)],
        out_specs=pl.BlockSpec((TILE, width), lambda i: (i, 0)),
        out_shape=jax.ShapeDtypeStruct((length, width), BF16),
        cost_estimate=pl.CostEstimate(
            flops=2 * length * width, bytes_accessed=6 * 2**20, transcendentals=2**10
        ),
        name="norm",
    )(gated, *squares, gain)


def local(
    mixer_input,
    state_input,
    gate_input,
    step_raw,
    decay_rate,
    conv_inner,
    conv_state,
    level_table,
    stretch_kind,
    norm_gain,
):
    length, width = mixer_input.shape
    heads = step_raw.shape[1]
    index = lax.axis_index("seq")
    place = jnp.stack([lax.rem(index, XS), lax.div(index, XS)]).astype(jnp.int32)
    tails = jnp.concatenate([mixer_input[length - HALO :], state_input[length - HALO :]], axis=1)
    halo = lax.ppermute(tails, "seq", [(i, i + 1) for i in range(XS * ZS - 1)])
    inner, rows, running, step, *parts = prepare(
        place,
        mixer_input,
        halo,
        state_input,
        conv_inner,
        conv_state,
        step_raw.T,
        decay_rate[:, None],
    )
    kinds = jnp.repeat(stretch_kind, length // stretch_kind.shape[0])[None, :]
    by_head = jnp.transpose(level_table, (2, 1, 0))
    gap = jnp.zeros((heads, 3, by_head.shape[2]), F32)
    table = jnp.concatenate([by_head[:, :5], gap, by_head[:, 5:10], gap], axis=1)
    table = table.reshape(heads * 16, by_head.shape[2])
    arrived = [parts[0]] + [along_x(parts[k], k) for k in range(1, XS)]
    local_out, far_rows = local_part(inner, rows, running, step, table, kinds)
    row_state, *near = fold_row(place, arrived)
    near = [near[0]] + [along_x(near[k], k) for k in range(1, XS)]
    other = lax.ppermute(row_state, "seq", seq_perm(lambda z, x: (z ^ 1, x)))
    pair_state = fold_pair(place, row_state, other)
    gathered = [
        lax.ppermute(
            pair_state,
            "seq",
            seq_perm(lambda z, x, far=far: (z + far, x) if z + far < ZS else None),
        )
        for far in (2, 4, 6)
    ]
    far = fold_far(place, arrived, other, gathered)
    far = [far[0]] + [along_x(far[k], k) for k in range(1, XS)]
    gated, squares = far_part(place, local_out, gate_input, rows, far_rows, near, far)
    squares = squares + lax.ppermute(squares, "head", head_perm(lambda y, core: (y, 1 - core)))
    sums = [squares] + [
        lax.ppermute(squares, "head", head_perm(lambda y, core, k=k: ((y + k) % YS, core)))
        for k in range(1, YS)
    ]
    total_width = width * lax.axis_size("head")
    return norm(gated, sums, norm_gain[None, :], total_width)


def solution(mesh):
    return jax.shard_map(
        local,
        mesh=mesh,
        in_specs=(
            P("seq", "head"),
            P("seq", None),
            P("seq", "head"),
            P("seq", "head"),
            P("head"),
            P(None, "head"),
            P(),
            P(None, None, "head"),
            P("seq"),
            P("head"),
        ),
        out_specs=P("seq", "head"),
        check_vma=False,
    )
```

time: 387 us -> 118 us (0.30)
  matrix products: 102 us -> 0 us
  waiting for transfers between devices: 93.4 us -> 20.4 us
  blocking collectives: 55 us -> 0 us
  loops' own time: 41.3 us -> 0 us
  Pallas kernels: 0 us -> 40.7 us
  starting transfers between devices: 3.4 us -> 31.9 us
  other arithmetic: 29.1 us -> 1.71 us
  local copies, waits for them, and re-layouts: 44.9 us -> 21.6 us
  between operations: 13.6 us -> 0.23 us
    dot_general x28 -> x0, matrix products: 102 us -> none  [the longest x8 56.4 us: block_one_head(): local_out = jnp.dot(mixing, values, preferred_element_type=jnp.float32)]
    all_gather x1 -> x0, waiting for transfers between devices: 93.4 us -> none  [local(): piece = lax.all_gather(own_state[None], 'seq', axis=0, tiled=True)]
    another operation x2 -> x0, loops' own time: 41.3 us -> none  [the longest x1 20.8 us: block_output(): outputs = lax.map(block_one_head, jnp.arange(heads, dtype=jnp.int32))]
    all_gather x1 -> x0, blocking collectives: 40.8 us -> none  [local(): decays = lax.all_gather(block_decay[None, :], 'seq', axis=0, tiled=True)]
    pallas_call x0 -> x7, Pallas kernels: none -> 40.7 us  [the longest x1 11.8 us: far_part(): pl.pallas_call(far_kernel, grid_spec=pltpu.PrefetchScalarGridSpec(num_sca...]
    dynamic_slice x72 -> x0, local copies, waits for them, and re-layouts: 37.4 us -> none  [the longest x16 9.72 us: local_states(): return lax.map(local_one_head, jnp.arange(heads, dtype=jnp.int32))]
    ppermute x1 -> x18, starting transfers between devices: 3.4 us -> 31.9 us  [the longest x3 12.9 us: local(): lax.ppermute(pair_state, 'seq', seq_perm(lambda z, x, far=far: (z + far,...]
    ppermute x1 -> x18, waiting for transfers between devices: 0.01 us -> 20.4 us  [the longest x9 5.41 us: along_x(): lax.ppermute(value, 'seq', seq_perm(lambda z, x: (z, (x + step) % XS)))]
  transfers between devices with their start and end apart: 2 -> 18, of which waited for: 1 -> 8; matrix products, arithmetic and copies ran while one was open for 4% -> 4% of each run, Pallas kernels for 0% -> 12%
where the time goes in v1:
time: 118 us; the launch traced here: 117 us
  Pallas kernels  40.7 us (34%)
  starting transfers between devices  31.9 us (27%)
  local copies, waits for them, and re-layouts  21.6 us (18%)
  waiting for transfers between devices  20.4 us (17%)
  other arithmetic  1.71 us (1%)
    unnamed x68, local copies, waits for them, and re-layouts  17.1 us
    ppermute x3, starting transfers between devices, local(): lax.ppermute(pair_state, 'seq', seq_perm(lambda z, x, far=far: (z + far,...  12.9 us
    pallas_call x1, Pallas kernels, far_part(): pl.pallas_call(far_kernel, grid_spec=pltpu.PrefetchScalarGridSpec(num_sca...  11.8 us
    ppermute x9, starting transfers between devices, along_x(): lax.ppermute(value, 'seq', seq_perm(lambda z, x: (z, (x + step) % XS)))  11 us
    pallas_call x1, Pallas kernels, local_part(): pl.pallas_call(local_kernel, grid=(heads,), in_specs=[pl.BlockSpec((lengt...  9.9 us
    pallas_call x1, Pallas kernels, prepare(): pl.pallas_call(prepare_kernel, grid_spec=pltpu.PrefetchScalarGridSpec(num...  6.59 us
    pallas_call x1, Pallas kernels, norm(): pl.pallas_call(functools.partial(norm_kernel, total_width), grid=(tiles,)...  6.56 us
    ppermute x9, waiting for transfers between devices, along_x(): lax.ppermute(value, 'seq', seq_perm(lambda z, x: (z, (x + step) % XS)))  5.41 us
  transfers between devices with their start and end apart: 18, of which 8 were waited for; matrix products, arithmetic and copies ran while one was open for 4% of the time, Pallas kernels for 12%

profile of v1, /device:TPU:32, one launch (start us, length us, event | category | flops | bytes accessed | tf_op | source)
XLA Modules:
  0.0 116.6 jit_solution(15370949864640484367)
XLA Ops:
  1.5 3.4 %collective-permute-start = (bf16[16,1280]{1,0:T(8,128)(2,1)S(1)}, bf16[16,1280]{1,0:T(8,128)(2,1)S(1)}, u32[]{:S(2)}, u32[]{:S(2)}) collective-permute-start(bf16[16,1280]{1,0:T(8,128)(2,1)S(1)} %pad_maximum_fusion), channel_id=1, source_target_pairs={{0,8},{8,16},{16,24},{24,32},{32,40},{40,48},{48,56},{56,64},{64,7... | collective-permute-start | bytes 122888 | tf_op jit(solution)/shard_map/ppermute | solution.py:545
  5.7 3.8 %collective-permute-done.mixer_halo.state_halo = bf16[16,1280]{1,0:T(8,128)(2,1)S(1)} collective-permute-done((bf16[16,1280]{1,0:T(8,128)(2,1)S(1)}, bf16[16,1280]{1,0:T(8,128)(2,1)S(1)}, u32[]{:S(2)}, u32[]{:S(2)}) %collective-permute-start) | collective-permute-done | bytes 40992 | tf_op jit(solution)/shard_map/ppermute | solution.py:545
  9.5 1.6 %copy-done.10 = bf16[1024,1024]{1,0:T(8,128)(2,1)S(1)} copy-done((bf16[1024,1024]{1,0:T(8,128)(2,1)S(1)}, bf16[1024,1024]{1,0:T(8,128)(2,1)}, u32[]{:S(2)}) %copy-start.10) | copy-done | bytes 2097176
  14.2 6.6 %prepare.1 = (bf16[1024,1024]{1,0:T(8,128)(2,1)S(1)}, bf16[1024,256]{1,0:T(8,128)(2,1)S(1)}, f32[8,1024]{1,0:T(8,128)S(1)}, f32[8,1024]{1,0:T(8,128)S(1)}, f32[2...) custom-call(s32[2]{0:T(128)S(1)} %pad_add_fusion.place, ...), custom_call_target="tpu_custom_call" | custom-call | flops 268435456 | bytes 8388608 | tf_op jit(solution)/shard_map/prepare/pallas_call | solution.py:148
  24.0 2.1 %collective-permute-start.2 = (f32[264,128]{1,0:T(8,128)S(1)}, f32[264,128]{1,0:T(8,128)S(1)}, u32[]{:S(2)}, u32[]{:S(2)}) collective-permute-start(f32[264,128]{1,0:T(8,128)S(1)} %get-tuple-element.34), channel_id=1, source_target_pairs={{0,16},{8,24},{16,0},{24,8},{32,48},{40,56},{48,32},{56,40},{64,80... | collective-permute-start | bytes 405512 | tf_op jit(solution)/shard_map/ppermute | solution.py:44
  27.6 4.7 %collective-permute-done.1.p1.d1 = f32[264,128]{1,0:T(8,128)S(1)} collective-permute-done((f32[264,128]{1,0:T(8,128)S(1)}, f32[264,128]{1,0:T(8,128)S(1)}, u32[]{:S(2)}, u32[]{:S(2)}) %collective-permute-start.1) | collective-permute-done | bytes 135200 | tf_op jit(solution)/shard_map/ppermute | solution.py:44
  33.6 2.1 %fold_row.1 = (f32[264,128]{1,0:T(8,128)}, bf16[512,128]{1,0:T(8,128)(2,1)}, bf16[512,128]{1,0:T(8,128)(2,1)}, bf16[512,128]{1,0:T(8,128)(2,1)}, bf16[512,128]{1,0:T(8,128)(2,1)}) custom-call(s32[2]{0:T(128)} %copy-done.8, f32[264,128]{1,0:T(8,128)} %copy-done.2, f32[264,128]{1,0:T(8,128)} %copy-done.21, f32[264,128]{1,0:T(8,128)} %copy-done.22, ...), custom_call_target="tpu_custom_call" | custom-call | flops 1048576 | bytes 1048576 | tf_op jit(solution)/shard_map/fold_row/pallas_call | solution.py:323
  36.0 4.9 %collective-permute-done.7.other = f32[264,128]{1,0:T(8,128)S(1)} collective-permute-done((f32[264,128]{1,0:T(8,128)}, f32[264,128]{1,0:T(8,128)S(1)}, u32[]{:S(2)}, u32[]{:S(2)}) %collective-permute-start.7) | collective-permute-done | bytes 135200 | tf_op jit(solution)/shard_map/ppermute | solution.py:565
  41.6 1.7 %fold_pair.1 = f32[264,128]{1,0:T(8,128)} custom-call(s32[2]{0:T(128)} %copy-done.8, f32[264,128]{1,0:T(8,128)} %get-tuple-element.40.own, f32[264,128]{1,0:T(8,128)} %copy-done.24), custom_call_target="tpu_custom_call" | custom-call | flops 262144 | bytes 524288 | tf_op jit(solution)/shard_map/fold_pair/pallas_call | solution.py:350
  43.3 7.3 %collective-permute-start.10 = (f32[264,128]{1,0:T(8,128)}, f32[264,128]{1,0:T(8,128)S(1)}, u32[]{:S(2)}, u32[]{:S(2)}) collective-permute-start(f32[264,128]{1,0:T(8,128)} %fold_pair.1), channel_id=1, source_target_pairs={{0,192},{8,200},{16,208},{24,216},{32,224},{40,232},{48,240},{56,2... | collective-permute-start | bytes 405512 | tf_op jit(solution)/shard_map/ppermute | solution.py:568
  50.6 1.7 %collective-permute-start.9 = (f32[264,128]{1,0:T(8,128)}, f32[264,128]{1,0:T(8,128)S(1)}, u32[]{:S(2)}, u32[]{:S(2)}) collective-permute-start(f32[264,128]{1,0:T(8,128)} %fold_pair.1), channel_id=1, source_target_pairs={{0,128},{8,136},{16,144},{24,152},{32,160},{40,168},{48,176},{56,1... | collective-permute-start | bytes 405512 | tf_op jit(solution)/shard_map/ppermute | solution.py:568
  52.3 3.8 %collective-permute-start.8 = (f32[264,128]{1,0:T(8,128)}, f32[264,128]{1,0:T(8,128)S(1)}, u32[]{:S(2)}, u32[]{:S(2)}) collective-permute-start(f32[264,128]{1,0:T(8,128)} %fold_pair.1), channel_id=1, source_target_pairs={{0,64},{8,72},{16,80},{24,88},{32,96},{40,104},{48,112},{56,120},{... | collective-permute-start | bytes 405512 | tf_op jit(solution)/shard_map/ppermute | solution.py:568
  57.7 2.1 %collective-permute-start.6 = (bf16[512,128]{1,0:T(8,128)(2,1)}, bf16[512,128]{1,0:T(8,128)(2,1)}, u32[]{:S(2)}, u32[]{:S(2)}) collective-permute-start(bf16[512,128]{1,0:T(8,128)(2,1)} %get-tuple-element.39), channel_id=1, source_target_pairs={{0,24},{8,0},{16,8},{24,16},{32,56},{40,32},{48,40},{56,48},{64,88... | collective-permute-start | bytes 393224 | tf_op jit(solution)/shard_map/ppermute | solution.py:44
  61.7 2.1 %fold_far.1 = (bf16[768,128]{1,0:T(8,128)(2,1)}, bf16[768,128]{1,0:T(8,128)(2,1)}, bf16[768,128]{1,0:T(8,128)(2,1)}, bf16[768,128]{1,0:T(8,128)(2,1)}) custom-call(s32[2]{0:T(128)} %copy-done.8, f32[264,128]{1,0:T(8,128)} %copy-done.2, f32[264,128]{1,0:T(8,128)} %copy-done.21, f32[264,128]{1,0:T(8,128)} %copy-done.22, f32[264,128]{1,0:T(8,128)} %copy-done.23, ...), custom_call_target="tpu_custom_call" | custom-call | flops 1048576 | bytes 1048576 | tf_op jit(solution)/shard_map/fold_far/pallas_call | solution.py:398
  63.8 3.1 %collective-permute-start.12 = (bf16[768,128]{1,0:T(8,128)(2,1)}, bf16[768,128]{1,0:T(8,128)(2,1)S(1)}, u32[]{:S(2)}, u32[]{:S(2)}) collective-permute-start(bf16[768,128]{1,0:T(8,128)(2,1)} %get-tuple-element.43), channel_id=1, source_target_pairs={{0,16},{8,24},{16,0},{24,8},{32,48},{40,56},{48,32},{56,40},{64,80... | collective-permute-start | bytes 589832 | tf_op jit(solution)/shard_map/ppermute | solution.py:44
  68.8 1.6 %pad_maximum_fusion.1 = f32[8,16,8]{1,0,2:T(8,128)} fusion(f32[8,3,8]{1,0,2:T(8,128)S(1)} %broadcast_in_dim.13, f32[8,5,8]{1,0,2:T(8,128)} %get-tuple-element.48, f32[8,5,8]{1,0,2:T(8,128)} %get-tuple-element.47), kind=kLoop, calls=%fused_computation.1 | loop fusion | flops 3072 | bytes 7424 | tf_op jit(solution)/shard_map/concatenate | solution.py:559
  70.6 1.5 %copy.12 = f32[8,16,8]{2,1,0:T(8,128)} copy(f32[8,16,8]{1,0,2:T(8,128)} %pad_maximum_fusion.1) | data formatting | bytes 8192 | tf_op jit(solution)/shard_map/concatenate | solution.py:559
  72.9 1.6 %copy-done.16 = bf16[1024,1024]{1,0:T(8,128)(2,1)S(1)} copy-done((bf16[1024,1024]{1,0:T(8,128)(2,1)S(1)}, bf16[1024,1024]{1,0:T(8,128)(2,1)}, u32[]{:S(2)}) %copy-start.16) | copy-done | bytes 2097176
  76.0 9.9 %local_part.1 = (f32[1024,1024]{1,0:T(8,128)S(1)}, f32[8,8,1024]{2,1,0:T(8,128)S(1)}) custom-call(bf16[1024,1024]{1,0:T(8,128)(2,1)S(1)} %copy-done.16, bf16[1024,256]{1,0:T(8,128)(2,1)S(1)} %get-tuple-element.27.rows, f32[8,1024]{1,0:T(8,128)S(1)} %copy-done.18, f32[8,1024]{1,0:T(8,128)S(1)} %copy-done.20, f32[128,8]{1,0:T(8,128)S(1)} %bitcast.7, ...), custom_call_target="tpu_custom_call" | custom-call | flops 1073741824 | bytes 8388608 | tf_op jit(solution)/shard_map/local_part/pallas_call | solution.py:250
  86.0 11.8 %far_part.1 = (f32[1024,1024]{1,0:T(8,128)S(1)}, f32[8,128]{1,0:T(8,128)S(1)}) custom-call(s32[2]{0:T(128)S(1)} %copy-done.9, f32[1024,1024]{1,0:T(8,128)S(1)} %get-tuple-element.30.local, bf16[1024,1024]{1,0:T(8,128)(2,1)S(1)} %copy-done.1, bf16[1024,256]{1,0:T(8,128)(2,1)S(1)} %get-tuple-element.27.rows, f32[8,8,1024]{2,1,0:T(8,128)S(1)} %get-tuple-element.31.far_rows, ...), custom_call_target="tpu_custom_call" | custom-call | flops 1342177280 | bytes 12582912 | tf_op jit(solution)/shard_map/far_part/pallas_call | solution.py:467
  97.9 2.0 %copy-done = f32[1024,1024]{1,0:T(8,128)} copy-done((f32[1024,1024]{1,0:T(8,128)}, f32[1024,1024]{1,0:T(8,128)S(1)}, u32[]{:S(2)}) %copy-start) | copy-done | bytes 4194328
  101.0 3.0 %collective-permute-start.17 = (f32[8,128]{1,0:T(8,128)S(1)}, f32[8,128]{1,0:T(8,128)S(1)}, u32[]{:S(2)}, u32[]{:S(2)}) collective-permute-start(f32[8,128]{1,0:T(8,128)S(1)} %add.3.s0), channel_id=1, source_target_pairs={{0,6},{1,7},{2,0},{3,1},{4,2},{5,3},{6,4},{7,5},{8,14},{9,15},{10,... | collective-permute-start | bytes 12296 | tf_op jit(solution)/shard_map/ppermute | solution.py:580
  105.6 3.5 %collective-permute-done.16.s2 = f32[8,128]{1,0:T(8,128)S(1)} collective-permute-done((f32[8,128]{1,0:T(8,128)S(1)}, f32[8,128]{1,0:T(8,128)S(1)}, u32[]{:S(2)}, u32[]{:S(2)}) %collective-permute-start.16) | collective-permute-done | bytes 4128 | tf_op jit(solution)/shard_map/ppermute | solution.py:580
  110.1 6.6 %norm.1 = bf16[1024,1024]{1,0:T(8,128)(2,1)} custom-call(f32[1024,1024]{1,0:T(8,128)} %copy-done, f32[8,128]{1,0:T(8,128)} %copy-done.29, f32[8,128]{1,0:T(8,128)} %copy-done.32, f32[8,128]{1,0:T(8,128)} %copy-done.31, f32[8,128]{1,0:T(8,128)} %copy-done.30, f32[1,1024]{1,0:T(1,128)} %bitcast.10), custom_call_target="tpu_custom_call" | custom-call | flops 2097152 | bytes 6291456 | tf_op jit(solution)/shard_map/norm/pallas_call | solution.py:513
  (99 shorter events, 23.9 us)
Async XLA Ops:
  1.5 8.0 %collective-permute-start = (bf16[16,1280]{1,0:T(8,128)(2,1)S(1)}, bf16[16,1280]{1,0:T(8,128)(2,1)S(1)}, u32[]{:S(2)}, u32[]{:S(2)}) collective-permute-start(bf16[16,1280]{1,0:T(8,128)(2,1)S(1)} %pad_maximum_fusion), channel_id=1, source_target_pairs={{0,8},{8,16},{16,24},{24,32},{32,40},{40,48},{48,56},{56,64},{64,7... | collective-permute-start | bytes 122888 | tf_op jit(solution)/shard_map/ppermute | solution.py:545
  4.9 28.0 %copy-start.8 = (s32[2]{0:T(128)}, s32[2]{0:T(128)S(1)}, u32[]{:S(2)}) copy-start(s32[2]{0:T(128)S(1)} %pad_add_fusion.place) | copy-start | bytes 28
  14.2 41.9 %copy-start.28 = (f32[8,13,8]{1,2,0:T(8,128)S(1)}, f32[8,13,8]{1,2,0:T(8,128)}, u32[]{:S(2)}) copy-start(f32[8,13,8]{1,2,0:T(8,128)} %param.17) | copy-start | bytes 9988
  24.0 46.4 %copy-start.33 = (s32[16]{0:T(128)S(1)}, s32[16]{0:T(128)}, u32[]{:S(2)}) copy-start(s32[16]{0:T(128)} %param.18) | copy-start | bytes 196
  24.0 8.3 %collective-permute-start.1 = (f32[264,128]{1,0:T(8,128)S(1)}, f32[264,128]{1,0:T(8,128)S(1)}, u32[]{:S(2)}, u32[]{:S(2)}) collective-permute-start(f32[264,128]{1,0:T(8,128)S(1)} %get-tuple-element.33), channel_id=1, source_target_pairs={{0,8},{8,16},{16,24},{24,0},{32,40},{40,48},{48,56},{56,32},{64,72... | collective-permute-start | bytes 405512 | tf_op jit(solution)/shard_map/ppermute | solution.py:44
  24.0 8.3 %collective-permute-start.2 = (f32[264,128]{1,0:T(8,128)S(1)}, f32[264,128]{1,0:T(8,128)S(1)}, u32[]{:S(2)}, u32[]{:S(2)}) collective-permute-start(f32[264,128]{1,0:T(8,128)S(1)} %get-tuple-element.34), channel_id=1, source_target_pairs={{0,16},{8,24},{16,0},{24,8},{32,48},{40,56},{48,32},{56,40},{64,80... | collective-permute-start | bytes 405512 | tf_op jit(solution)/shard_map/ppermute | solution.py:44
  26.1 6.8 %collective-permute-start.3 = (f32[264,128]{1,0:T(8,128)S(1)}, f32[264,128]{1,0:T(8,128)S(1)}, u32[]{:S(2)}, u32[]{:S(2)}) collective-permute-start(f32[264,128]{1,0:T(8,128)S(1)} %get-tuple-element.35), channel_id=1, source_target_pairs={{0,24},{8,0},{16,8},{24,16},{32,56},{40,32},{48,40},{56,48},{64,88... | collective-permute-start | bytes 405512 | tf_op jit(solution)/shard_map/ppermute | solution.py:44
  35.7 5.2 %collective-permute-start.7 = (f32[264,128]{1,0:T(8,128)}, f32[264,128]{1,0:T(8,128)S(1)}, u32[]{:S(2)}, u32[]{:S(2)}) collective-permute-start(f32[264,128]{1,0:T(8,128)} %get-tuple-element.40.own), channel_id=1, source_target_pairs={{0,32},{8,40},{16,48},{24,56},{32,0},{40,8},{48,16},{56,24},{64,96... | collective-permute-start | bytes 405512 | tf_op jit(solution)/shard_map/ppermute | solution.py:565
  35.7 31.2 %collective-permute-start.4 = (bf16[512,128]{1,0:T(8,128)(2,1)}, bf16[512,128]{1,0:T(8,128)(2,1)S(1)}, u32[]{:S(2)}, u32[]{:S(2)}) collective-permute-start(bf16[512,128]{1,0:T(8,128)(2,1)} %get-tuple-element.37), channel_id=1, source_target_pairs={{0,8},{8,16},{16,24},{24,0},{32,40},{40,48},{48,56},{56,32},{64,72... | collective-permute-start | bytes 393224 | tf_op jit(solution)/shard_map/ppermute | solution.py:44
  43.3 14.4 %collective-permute-start.10 = (f32[264,128]{1,0:T(8,128)}, f32[264,128]{1,0:T(8,128)S(1)}, u32[]{:S(2)}, u32[]{:S(2)}) collective-permute-start(f32[264,128]{1,0:T(8,128)} %fold_pair.1), channel_id=1, source_target_pairs={{0,192},{8,200},{16,208},{24,216},{32,224},{40,232},{48,240},{56,2... | collective-permute-start | bytes 405512 | tf_op jit(solution)/shard_map/ppermute | solution.py:568
  50.6 9.2 %collective-permute-start.9 = (f32[264,128]{1,0:T(8,128)}, f32[264,128]{1,0:T(8,128)S(1)}, u32[]{:S(2)}, u32[]{:S(2)}) collective-permute-start(f32[264,128]{1,0:T(8,128)} %fold_pair.1), channel_id=1, source_target_pairs={{0,128},{8,136},{16,144},{24,152},{32,160},{40,168},{48,176},{56,1... | collective-permute-start | bytes 405512 | tf_op jit(solution)/shard_map/ppermute | solution.py:568
  52.3 8.7 %collective-permute-start.8 = (f32[264,128]{1,0:T(8,128)}, f32[264,128]{1,0:T(8,128)S(1)}, u32[]{:S(2)}, u32[]{:S(2)}) collective-permute-start(f32[264,128]{1,0:T(8,128)} %fold_pair.1), channel_id=1, source_target_pairs={{0,64},{8,72},{16,80},{24,88},{32,96},{40,104},{48,112},{56,120},{... | collective-permute-start | bytes 405512 | tf_op jit(solution)/shard_map/ppermute | solution.py:568
  56.9 29.1 %collective-permute-start.5 = (bf16[512,128]{1,0:T(8,128)(2,1)}, bf16[512,128]{1,0:T(8,128)(2,1)}, u32[]{:S(2)}, u32[]{:S(2)}) collective-permute-start(bf16[512,128]{1,0:T(8,128)(2,1)} %get-tuple-element.38), channel_id=1, source_target_pairs={{0,16},{8,24},{16,0},{24,8},{32,48},{40,56},{48,32},{56,40},{64,80... | collective-permute-start | bytes 393224 | tf_op jit(solution)/shard_map/ppermute | solution.py:44
  57.7 28.3 %collective-permute-start.6 = (bf16[512,128]{1,0:T(8,128)(2,1)}, bf16[512,128]{1,0:T(8,128)(2,1)}, u32[]{:S(2)}, u32[]{:S(2)}) collective-permute-start(bf16[512,128]{1,0:T(8,128)(2,1)} %get-tuple-element.39), channel_id=1, source_target_pairs={{0,24},{8,0},{16,8},{24,16},{32,56},{40,32},{48,40},{56,48},{64,88... | collective-permute-start | bytes 393224 | tf_op jit(solution)/shard_map/ppermute | solution.py:44
  63.8 22.1 %collective-permute-start.11 = (bf16[768,128]{1,0:T(8,128)(2,1)}, bf16[768,128]{1,0:T(8,128)(2,1)S(1)}, u32[]{:S(2)}, u32[]{:S(2)}) collective-permute-start(bf16[768,128]{1,0:T(8,128)(2,1)} %get-tuple-element.42), channel_id=1, source_target_pairs={{0,8},{8,16},{16,24},{24,0},{32,40},{40,48},{48,56},{56,32},{64,72... | collective-permute-start | bytes 589832 | tf_op jit(solution)/shard_map/ppermute | solution.py:44
  63.8 22.1 %collective-permute-start.12 = (bf16[768,128]{1,0:T(8,128)(2,1)}, bf16[768,128]{1,0:T(8,128)(2,1)S(1)}, u32[]{:S(2)}, u32[]{:S(2)}) collective-permute-start(bf16[768,128]{1,0:T(8,128)(2,1)} %get-tuple-element.43), channel_id=1, source_target_pairs={{0,16},{8,24},{16,0},{24,8},{32,48},{40,56},{48,32},{56,40},{64,80... | collective-permute-start | bytes 589832 | tf_op jit(solution)/shard_map/ppermute | solution.py:44
  67.6 18.3 %collective-permute-start.13 = (bf16[768,128]{1,0:T(8,128)(2,1)}, bf16[768,128]{1,0:T(8,128)(2,1)S(1)}, u32[]{:S(2)}, u32[]{:S(2)}) collective-permute-start(bf16[768,128]{1,0:T(8,128)(2,1)} %get-tuple-element.44), channel_id=1, source_target_pairs={{0,24},{8,0},{16,8},{24,16},{32,56},{40,32},{48,40},{56,48},{64,88... | collective-permute-start | bytes 589832 | tf_op jit(solution)/shard_map/ppermute | solution.py:44
  68.8 17.2 %copy-start.1 = (bf16[1024,1024]{1,0:T(8,128)(2,1)S(1)}, bf16[1024,1024]{1,0:T(8,128)(2,1)}, u32[]{:S(2)}) copy-start(bf16[1024,1024]{1,0:T(8,128)(2,1)} %gate.1) | copy-start | bytes 6291460
  68.8 17.2 %copy-start.3 = (bf16[768,128]{1,0:T(8,128)(2,1)S(1)}, bf16[768,128]{1,0:T(8,128)(2,1)}, u32[]{:S(2)}) copy-start(bf16[768,128]{1,0:T(8,128)(2,1)} %get-tuple-element.41.f0) | copy-start | bytes 589828
  68.8 17.2 %copy-start.4 = (bf16[512,128]{1,0:T(8,128)(2,1)S(1)}, bf16[512,128]{1,0:T(8,128)(2,1)}, u32[]{:S(2)}) copy-start(bf16[512,128]{1,0:T(8,128)(2,1)} %get-tuple-element.36.n0) | copy-start | bytes 393220
  99.8 1.2 %collective-permute-start.14 = (f32[8,128]{1,0:T(8,128)S(1)}, f32[8,128]{1,0:T(8,128)S(1)}, u32[]{:S(2)}, u32[]{:S(2)}) collective-permute-start(f32[8,128]{1,0:T(8,128)S(1)} %get-tuple-element.46), channel_id=1, source_target_pairs={{0,1},{1,0},{2,3},{3,2},{4,5},{5,4},{6,7},{7,6},{8,9},{9,8},{10,11... | collective-permute-start | bytes 12296 | tf_op jit(solution)/shard_map/ppermute | solution.py:578
  101.0 4.6 %collective-permute-start.17 = (f32[8,128]{1,0:T(8,128)S(1)}, f32[8,128]{1,0:T(8,128)S(1)}, u32[]{:S(2)}, u32[]{:S(2)}) collective-permute-start(f32[8,128]{1,0:T(8,128)S(1)} %add.3.s0), channel_id=1, source_target_pairs={{0,6},{1,7},{2,0},{3,1},{4,2},{5,3},{6,4},{7,5},{8,14},{9,15},{10,... | collective-permute-start | bytes 12296 | tf_op jit(solution)/shard_map/ppermute | solution.py:580
  104.0 5.1 %collective-permute-start.16 = (f32[8,128]{1,0:T(8,128)S(1)}, f32[8,128]{1,0:T(8,128)S(1)}, u32[]{:S(2)}, u32[]{:S(2)}) collective-permute-start(f32[8,128]{1,0:T(8,128)S(1)} %add.3.s0), channel_id=1, source_target_pairs={{0,4},{1,5},{2,6},{3,7},{4,0},{5,1},{6,2},{7,3},{8,12},{9,13},{10,... | collective-permute-start | bytes 12296 | tf_op jit(solution)/shard_map/ppermute | solution.py:580
  104.7 4.8 %collective-permute-start.15 = (f32[8,128]{1,0:T(8,128)S(1)}, f32[8,128]{1,0:T(8,128)S(1)}, u32[]{:S(2)}, u32[]{:S(2)}) collective-permute-start(f32[8,128]{1,0:T(8,128)S(1)} %add.3.s0), channel_id=1, source_target_pairs={{0,2},{1,3},{2,4},{3,5},{4,6},{5,7},{6,0},{7,1},{8,10},{9,11},{10,... | collective-permute-start | bytes 12296 | tf_op jit(solution)/shard_map/ppermute | solution.py:580
  (28 other events, 67.3 us)

commit v2 on v1

v2 whole, which is shorter than its diff:
```python
import functools
import jax
import jax.numpy as jnp
from jax import lax
from jax.experimental import pallas as pl
from jax.experimental.pallas import tpu as pltpu
from jax.sharding import PartitionSpec as P

F32 = jnp.float32
BF16 = jnp.bfloat16

XS = 4
ZS = 8
YS = 4
CORES = 2
PAIR = 2
DIM = 128
HALO = 16
TILE = 128
WIDE = 256
TOP = 16384.0
MESSAGE = PAIR * DIM + 8


def seq_perm(move):
    pairs = []
    for z in range(ZS):
        for x in range(XS):
            target = move(z, x)
            if target is not None:
                pairs.append((z * XS + x, target[0] * XS + target[1]))
    return pairs


def head_perm(move):
    pairs = []
    for y in range(YS):
        for core in range(CORES):
            target = move(y, core)
            pairs.append((y * CORES + core, target[0] * CORES + target[1]))
    return pairs


def along_x(value, step):
    return lax.ppermute(value, "seq", seq_perm(lambda z, x: (z, (x + step) % XS)))


def silu(value):
    return value / (1.0 + jnp.exp(-value))


VMEM = pl.BlockSpec(memory_space=pltpu.VMEM)
SMEM = pl.BlockSpec(memory_space=pltpu.SMEM)
HBM = pl.BlockSpec(memory_space=pltpu.HBM)
DMA = pltpu.SemaphoreType.DMA


def params(mebibytes):
    return pltpu.CompilerParams(vmem_limit_bytes=mebibytes * 2**20)


def in_hbm(value):
    return pltpu.with_memory_space_constraint(value, pltpu.HBM)


def block_place():
    index = lax.axis_index("seq")
    return lax.rem(index, XS), lax.div(index, XS)


def conv(block, halo, taps):
    length = block.shape[0]
    width = taps.shape[0]
    joined = jnp.concatenate([halo[HALO - 8 :].astype(F32), block.astype(F32)], axis=0)
    taps = taps.astype(F32)
    total = jnp.zeros((length, block.shape[1]), F32)
    for offset in range(width):
        shift = width - 1 - offset
        moved = joined if shift == 0 else pltpu.roll(joined, shift, axis=0)
        total = total + moved[8:] * taps[offset : offset + 1]
    return silu(total).astype(BF16)


def prepare_kernel(
    mixer,
    halo,
    state,
    taps,
    state_taps,
    step_raw,
    rate,
    inner,
    rows,
    running_out,
    step_out,
    part0,
    part1,
    part2,
    part3,
    mixer_here,
    state_here,
    taps_here,
    state_taps_here,
    raw_here,
    rate_here,
    keys_t,
    scale,
    last,
    mixer_sem,
    small_sem,
):
    x, _ = block_place()
    heads, length = step_raw.shape
    width = mixer.shape[1]
    wide = PAIR * DIM
    small = [
        pltpu.make_async_copy(source, target, small_sem.at[n])
        for n, (source, target) in enumerate(
            (
                (step_raw, raw_here),
                (rate, rate_here),
                (state, state_here),
                (state_taps, state_taps_here),
                (taps, taps_here),
            )
        )
    ]
    for copy in small:
        copy.start()
    pairs = [lax.rem(x + turn, XS) for turn in range(XS)]
    columns = [pl.ds(pl.multiple_of(pair * wide, wide), wide) for pair in pairs]
    large = [
        pltpu.make_async_copy(
            mixer.at[:, columns[turn]], mixer_here.at[turn], mixer_sem.at[turn]
        )
        for turn in range(XS)
    ]
    for copy in large:
        copy.start()

    small[0].wait()
    small[1].wait()
    raw = raw_here[...]
    step = jnp.maximum(raw, 0.0) + jnp.log1p(jnp.exp(-jnp.abs(raw)))
    spot = lax.broadcasted_iota(jnp.int32, (heads, length), 0)
    rates = jnp.zeros((heads, length), F32)
    for head in range(heads):
        rates = jnp.where(spot == head, rate_here[head], rates)
    running = -rates * step
    lane = lax.broadcasted_iota(jnp.int32, (heads, length), 1)
    shift = 1
    while shift < length:
        moved = pltpu.roll(running, shift, axis=1)
        running = running + jnp.where(lane >= shift, moved, 0.0)
        shift *= 2
    final = running[:, length - 1 :]
    running_out[...] = running
    step_out[...] = step
    scale[...] = jnp.exp(final - running) * step
    last[...] = jnp.broadcast_to(final, last.shape)
    for copy in small[2:]:
        copy.wait()
    state_rows = conv(state_here[...], halo[:, width:], state_taps_here[...])
    rows[...] = state_rows
    keys_t[...] = state_rows[:, :DIM].astype(F32).T

    spot = lax.broadcasted_iota(jnp.int32, (8, DIM), 0)
    for turn, part in enumerate((part0, part1, part2, part3)):
        large[turn].wait()
        values = conv(
            mixer_here[turn], halo[:, columns[turn]], taps_here[:, columns[turn]]
        )
        inner[:, columns[turn]] = values
        pair = pairs[turn]
        for head in range(PAIR):
            row = scale[pl.ds(pair * PAIR + head, 1), :]
            scaled_t = (keys_t[...] * row).astype(BF16)
            part[head * DIM : (head + 1) * DIM] = jnp.dot(
                scaled_t, values[:, head * DIM : (head + 1) * DIM], preferred_element_type=F32
            )
        first = last[pl.ds(pair * PAIR, 1), :]
        second = last[pl.ds(pair * PAIR + 1, 1), :]
        part[2 * DIM :] = jnp.where(spot == 0, first, jnp.where(spot == 1, second, 0.0))


def prepare(mixer, halo, state, taps, state_taps, step_raw_t, rate):
    length, width = mixer.shape
    heads = step_raw_t.shape[0]
    return pl.pallas_call(
        prepare_kernel,
        in_specs=[HBM, VMEM, HBM, HBM, HBM, HBM, HBM],
        out_specs=[VMEM] * (4 + XS),
        out_shape=[
            pltpu.VMEM((length, width), BF16),
            pltpu.VMEM((length, 2 * DIM), BF16),
            pltpu.VMEM((heads, length), F32),
            pltpu.VMEM((heads, length), F32),
        ]
        + [pltpu.VMEM((MESSAGE, DIM), F32)] * XS,
        scratch_shapes=[
            pltpu.VMEM((XS, length, PAIR * DIM), BF16),
            pltpu.VMEM((length, 2 * DIM), BF16),
            pltpu.VMEM(taps.shape, BF16),
            pltpu.VMEM(state_taps.shape, BF16),
            pltpu.VMEM((heads, length), F32),
            pltpu.SMEM((heads,), F32),
            pltpu.VMEM((DIM, length), F32),
            pltpu.VMEM((heads, length), F32),
            pltpu.VMEM((heads, DIM), F32),
            DMA((XS,)),
            DMA((5,)),
        ],
        compiler_params=params(16),
        cost_estimate=pl.CostEstimate(
            flops=2 * length * width * DIM, bytes_accessed=8 * 2**20, transcendentals=2 * length * width
        ),
        name="prepare",
    )(
        in_hbm(mixer),
        halo,
        in_hbm(state),
        in_hbm(taps),
        in_hbm(state_taps),
        in_hbm(step_raw_t),
        in_hbm(rate),
    )


def shared_kernel(rows, running_in, gate, scores, gates, lifted_base, gate_here, gate_sem):
    length, width = gate.shape
    heads = width // DIM
    tiles = length // TILE
    gate_copy = pltpu.make_async_copy(gate, gate_here, gate_sem)
    gate_copy.start()
    for i in range(tiles):
        wide = (i + 1) * TILE
        scores[i * TILE : wide, :wide] = lax.dot_general(
            rows[i * TILE : wide, DIM:],
            rows[:wide, :DIM],
            (((1,), (1,)), ((), ())),
            preferred_element_type=F32,
        )
    columns = jnp.exp(running_in[...]).T
    for i in range(tiles):
        span = slice(i * TILE, (i + 1) * TILE)
        queries = rows[span, DIM:].astype(F32)
        for head in range(heads):
            lifted_base[span, head * DIM : (head + 1) * DIM] = queries * jnp.broadcast_to(
                columns[span, head : head + 1], (TILE, DIM)
            )
    gate_copy.wait()

    def one_tile(tile, carry):
        span = pl.ds(pl.multiple_of(tile * TILE, TILE), TILE)
        gates[span, :] = silu(gate_here[span, :].astype(F32))
        return carry

    lax.fori_loop(0, tiles, one_tile, 0)


def shared_part(rows, running, gate):
    length, width = gate.shape
    return pl.pallas_call(
        shared_kernel,
        in_specs=[VMEM, VMEM, HBM],
        out_specs=[VMEM] * 3,
        out_shape=[
            pltpu.VMEM((length, length), F32),
            pltpu.VMEM((length, width), F32),
            pltpu.VMEM((length, width), F32),
        ],
        scratch_shapes=[pltpu.VMEM((length, width), BF16), DMA],
        compiler_params=params(8),
        cost_estimate=pl.CostEstimate(
            flops=length * length * DIM, bytes_accessed=4 * 2**20, transcendentals=2**21
        ),
        name="shared_part",
    )(rows, running, in_hbm(gate))


def local_kernel(
    table, kinds, inner, running_in, step_in, scores, lifted_base, n0, n1, n2, n3, out, held
):
    x, _ = block_place()
    length, width = inner.shape
    heads = width // DIM
    stretch = length // kinds.shape[0]
    each = WIDE // stretch
    for k, near in enumerate((n0, n1, n2, n3)):
        pair = lax.rem(x + XS - k, XS)
        for head in range(PAIR):
            for level in range(2):
                base = (level * PAIR + head) * DIM
                held[pair * PAIR + head, level * DIM : (level + 1) * DIM] = near[
                    base : base + DIM
                ]
    row = lax.broadcasted_iota(jnp.int32, (stretch, TILE), 0)
    column = lax.broadcasted_iota(jnp.int32, (stretch, TILE), 1)
    causal = [row + part * stretch >= column for part in range(TILE // stretch)]
    lane = lax.broadcasted_iota(jnp.int32, (1, TILE), 1)
    empty = jnp.zeros((stretch, TILE), BF16)

    def one_head(head, carry):
        lanes = pl.ds(pl.multiple_of(head * DIM, DIM), DIM)
        running = running_in[pl.ds(head, 1), :]
        step = step_in[pl.ds(head, 1), :]
        starts = [running[:, i * WIDE : i * WIDE + 1] for i in range(length // WIDE)]
        ahead = jnp.concatenate(
            [
                jnp.exp(running[:, i * WIDE : (i + 1) * WIDE] - starts[i])
                for i in range(length // WIDE)
            ],
            axis=1,
        )
        columns = jnp.broadcast_to(ahead, (8, length)).T
        for i in range(length // WIDE):
            wide = (i + 1) * WIDE
            span = slice(i * WIDE, wide)
            behind = jnp.exp(starts[i] - running[:, :wide]) * step[:, :wide]
            bands = []
            lifted = []
            for part in range(each):
                here = i * each + part
                kind = kinds[here]
                weight = [table[kind, head, level] for level in range(7)]
                band = slice(here * stretch, (here + 1) * stretch)
                ahead_column = jnp.broadcast_to(columns[band, 0:1], (stretch, TILE))
                pieces = []
                for j in range(wide // TILE):
                    first, second = 2 * j, 2 * j + 1
                    if first > here:
                        pieces.append(empty)
                        continue
                    left = weight[(here ^ first).bit_length()]
                    right = weight[(here ^ second).bit_length()]
                    if second > here or (here ^ first).bit_length() == (here ^ second).bit_length():
                        factor = left
                    else:
                        factor = jnp.where(lane < stretch, left, right)
                    tile = slice(j * TILE, (j + 1) * TILE)
                    piece = scores[band, tile] * (behind[:, tile] * factor) * ahead_column
                    if second >= here:
                        piece = jnp.where(causal[here - first], piece, 0.0)
                    pieces.append(piece.astype(BF16))
                bands.append(jnp.concatenate(pieces, axis=1))
                base = lifted_base[band, lanes]
                lifted.append(
                    jnp.concatenate(
                        [(base * weight[5 + level]).astype(BF16) for level in range(2)], axis=1
                    )
                )
            out[span, lanes] = jnp.dot(
                jnp.concatenate(bands, axis=0), inner[:wide, lanes], preferred_element_type=F32
            ) + jnp.dot(
                jnp.concatenate(lifted, axis=0), held[head], preferred_element_type=F32
            )
        return carry

    lax.fori_loop(0, heads, one_head, 0)


def local_part(table, kinds, inner, running, step, scores, lifted_base, near):
    length, width = inner.shape
    heads = width // DIM
    return pl.pallas_call(
        local_kernel,
        in_specs=[SMEM, SMEM] + [VMEM] * (5 + XS),
        out_specs=VMEM,
        out_shape=pltpu.VMEM((length, width), F32),
        scratch_shapes=[pltpu.VMEM((heads, 2 * DIM, DIM), BF16)],
        compiler_params=params(8),
        cost_estimate=pl.CostEstimate(
            flops=8 * length * length * DIM, bytes_accessed=8 * 2**20, transcendentals=2**18
        ),
        name="local_part",
    )(table, kinds, inner, running, step, scores, lifted_base, *near)


def flag(condition):
    return jnp.where(condition, 1.0, 0.0).astype(F32)


def fold_row_kernel(p0, p1, p2, p3, row_out, m0, m1, m2, m3):
    x, _ = block_place()
    parts = (p0, p1, p2, p3)
    owner = [lax.rem(x + XS - k, XS) for k in range(XS)]
    decays = [part[2 * DIM :] for part in parts]

    def from_block(block):
        return [flag(owner[k] == block) for k in range(XS)]

    def pick(values, chosen):
        return sum(value * mark for value, mark in zip(values, chosen))

    block_marks = [from_block(block) for block in range(XS)]
    later = [
        jnp.exp(sum(decays[m] * flag(owner[m] > owner[k]) for m in range(XS))) for k in range(XS)
    ]
    decay_one = jnp.exp(pick(decays, block_marks[1]))
    decay_two = jnp.exp(pick(decays, block_marks[2]))
    for head in range(PAIR):
        span = slice(head * DIM, (head + 1) * DIM)
        blocks = [part[span] for part in parts]
        row_out[span] = sum(blocks[k] * later[k][head : head + 1] for k in range(XS))
        first = pick(blocks, block_marks[0])
        third = pick(blocks, block_marks[2])
        joined = first * decay_one[head : head + 1] + pick(blocks, block_marks[1])
        for k, message in enumerate((m0, m1, m2, m3)):
            target = lax.rem(x + k, XS)
            message[span] = (
                first * flag(target == 1) + third * flag(target == 3)
            ).astype(BF16)
            message[PAIR * DIM + head * DIM : PAIR * DIM + (head + 1) * DIM] = (
                joined
                * (flag(target == 2) + flag(target == 3) * decay_two[head : head + 1])
            ).astype(BF16)
    row_out[2 * DIM :] = sum(decays)


def fold_row(parts):
    return pl.pallas_call(
        fold_row_kernel,
        in_specs=[VMEM] * XS,
        out_specs=[VMEM] * (1 + XS),
        out_shape=[pltpu.VMEM((MESSAGE, DIM), F32)] + [pltpu.VMEM((4 * DIM, DIM), BF16)] * XS,
        compiler_params=params(4),
        cost_estimate=pl.CostEstimate(flops=2**20, bytes_accessed=2**20, transcendentals=2**10),
        name="fold_row",
    )(*parts)


def fold_pair_kernel(own, other, pair_out):
    _, z = block_place()
    upper = flag(lax.rem(z, 2) == 1)
    own_decay = own[2 * DIM :]
    other_decay = other[2 * DIM :]
    own_scale = jnp.exp(other_decay * (1.0 - upper))
    other_scale = jnp.exp(own_decay * upper)
    decay = own_decay + other_decay
    coarse = jnp.floor(decay)
    middle = jnp.floor((decay - coarse) * 1024.0) / 1024.0
    rest = decay - coarse - middle
    spot = lax.broadcasted_iota(jnp.int32, (8, DIM), 0)
    tail = jnp.zeros((8, DIM), F32)
    for head in range(PAIR):
        span = slice(head * DIM, (head + 1) * DIM)
        row = slice(head, head + 1)
        state = own[span] * own_scale[row] + other[span] * other_scale[row]
        most = jnp.max(jnp.max(jnp.abs(state), axis=0, keepdims=True), axis=1, keepdims=True)
        power = jnp.ceil(jnp.log(jnp.maximum(most, 1e-30)))
        pair_out[span] = state * (jnp.exp(-power) * TOP)
        for index, value in enumerate((coarse[row], middle[row], rest[row], power)):
            tail = jnp.where(spot == 2 * index + head, value, tail)
    pair_out[2 * DIM :] = tail


def fold_pair(own, other):
    return pl.pallas_call(
        fold_pair_kernel,
        in_specs=[VMEM] * 2,
        out_specs=VMEM,
        out_shape=pltpu.VMEM((MESSAGE, DIM), F32),
        compiler_params=params(4),
        cost_estimate=pl.CostEstimate(flops=2**18, bytes_accessed=2**19, transcendentals=2**10),
        name="fold_pair",
    )(own, other)


def fold_far_kernel(d0, d1, d2, d3, other, g1, g2, g3, m0, m1, m2, m3):
    x, z = block_place()
    upper = flag(lax.rem(z, 2) == 1)
    pair = lax.div(z, 2)
    odd_pair = flag(lax.rem(pair, 2) == 1)
    third_pair = flag(pair == 2)
    last_pair = flag(pair == 3)
    decays = [part[2 * DIM :] for part in (d0, d1, d2, d3)]
    owner = [lax.rem(x + XS - k, XS) for k in range(XS)]
    tails = [part[2 * DIM :] for part in (g1, g2, g3)]
    inside = [tail[0:2] + tail[2:4] + tail[4:6] for tail in tails]
    sizes = [jnp.exp(tail[6:8]) / TOP for tail in tails]
    in_pair = other[2 * DIM : 2 * DIM + PAIR] * upper
    after = in_pair + inside[0] * last_pair
    inside_first = jnp.exp(inside[0])
    inside_last = jnp.exp(inside[1])
    for head in range(PAIR):
        span = slice(head * DIM, (head + 1) * DIM)
        row = slice(head, head + 1)
        two = other[span]
        three, second, third = (
            part[span] * size[row] for part, size in zip((g1, g2, g3), sizes)
        )
        four = (second * inside_first[row] + three) * third_pair + (
            third * inside_last[row] + second
        ) * last_pair
        for k, message in enumerate((m0, m1, m2, m3)):
            target = lax.rem(x + k, XS)
            before = sum(decays[m][row] * flag(owner[m] < target) for m in range(XS))
            factors = (
                jnp.exp(before) * upper,
                jnp.exp(before + in_pair[row]) * odd_pair,
                jnp.exp(before + after[row]),
            )
            for level, (state, factor) in enumerate(zip((two, three, four), factors)):
                base = level * PAIR * DIM + head * DIM
                message[base : base + DIM] = (state * factor).astype(BF16)


def fold_far(parts, other, gathered):
    return pl.pallas_call(
        fold_far_kernel,
        in_specs=[VMEM] * (XS + 4),
        out_specs=[VMEM] * XS,
        out_shape=[pltpu.VMEM((6 * DIM, DIM), BF16)] * XS,
        compiler_params=params(4),
        cost_estimate=pl.CostEstimate(flops=2**20, bytes_accessed=2**20, transcendentals=2**12),
        name="fold_far",
    )(*parts, other, *gathered)


def far_kernel(
    table, kinds, local, gates, lifted_base, f0, f1, f2, f3, gated, squares, held, total
):
    x, _ = block_place()
    length, width = local.shape
    heads = width // DIM
    for k, far in enumerate((f0, f1, f2, f3)):
        pair = lax.rem(x + XS - k, XS)
        for head in range(PAIR):
            for level in range(3):
                base = (level * PAIR + head) * DIM
                held[pair * PAIR + head, level * DIM : (level + 1) * DIM] = far[base : base + DIM]
    total[...] = jnp.zeros_like(total)

    stretch = length // kinds.shape[0]

    def one_head(head, carry):
        lanes = pl.ds(pl.multiple_of(head * DIM, DIM), DIM)
        for tile in range(length // WIDE):
            span = slice(tile * WIDE, (tile + 1) * WIDE)
            lifted = []
            for here in range(tile * WIDE // stretch, (tile + 1) * WIDE // stretch):
                kind = kinds[here]
                base = lifted_base[here * stretch : (here + 1) * stretch, lanes]
                lifted.append(
                    jnp.concatenate(
                        [
                            (base * table[kind, head, 7 + level]).astype(BF16)
                            for level in range(3)
                        ],
                        axis=1,
                    )
                )
            mixed = local[span, lanes] + jnp.dot(
                jnp.concatenate(lifted, axis=0), held[head], preferred_element_type=F32
            )
            value = mixed * gates[span, lanes]
            gated[span, lanes] = value
            total[span] += value * value
        return carry

    lax.fori_loop(0, heads, one_head, 0)
    for tile in range(length // TILE):
        part = total[tile * TILE : (tile + 1) * TILE].T
        squares[tile : tile + 1] = jnp.sum(part, axis=0, keepdims=True)


def far_part(table, kinds, local, gates, lifted_base, far_states):
    length, width = local.shape
    heads = width // DIM
    return pl.pallas_call(
        far_kernel,
        in_specs=[SMEM, SMEM] + [VMEM] * (3 + XS),
        out_specs=[VMEM] * 2,
        out_shape=[pltpu.VMEM((length, width), F32), pltpu.VMEM((length // TILE, TILE), F32)],
        scratch_shapes=[pltpu.VMEM((heads, 3 * DIM, DIM), BF16), pltpu.VMEM((length, DIM), F32)],
        compiler_params=params(8),
        cost_estimate=pl.CostEstimate(
            flops=6 * length * width * DIM, bytes_accessed=12 * 2**20, transcendentals=0
        ),
        name="far_part",
    )(table, kinds, local, gates, lifted_base, *far_states)


def norm_kernel(total_width, gated, s0, s1, s2, s3, gain, out, made, sems):
    scale = lax.rsqrt((s0[...] + s1[...] + s2[...] + s3[...]) / total_width + 1e-05)
    length, width = gated.shape
    copies = []
    for tile in range(length // TILE):
        span = slice(tile * TILE, (tile + 1) * TILE)
        column = jnp.broadcast_to(scale[tile : tile + 1], (TILE, TILE)).T
        for piece in range(width // TILE):
            lane = slice(piece * TILE, (piece + 1) * TILE)
            made[span, lane] = (gated[span, lane] * column * gain[:, lane]).astype(BF16)
        copies.append(pltpu.make_async_copy(made.at[span], out.at[span], sems.at[tile]))
        copies[-1].start()
    for copy in copies:
        copy.wait()


def norm(gated, squares, gain, total_width):
    length, width = gated.shape
    return pl.pallas_call(
        functools.partial(norm_kernel, total_width),
        in_specs=[VMEM] * (2 + YS),
        out_specs=HBM,
        out_shape=jax.ShapeDtypeStruct((length, width), BF16),
        scratch_shapes=[pltpu.VMEM((length, width), BF16), DMA((length // TILE,))],
        compiler_params=params(8),
        cost_estimate=pl.CostEstimate(
            flops=2 * length * width, bytes_accessed=6 * 2**20, transcendentals=2**10
        ),
        name="norm",
    )(gated, *squares, gain)


def local(
    mixer_input,
    state_input,
    gate_input,
    step_raw,
    decay_rate,
    conv_inner,
    conv_state,
    level_table,
    stretch_kind,
    norm_gain,
):
    length, width = mixer_input.shape
    tails = jnp.concatenate([mixer_input[length - HALO :], state_input[length - HALO :]], axis=1)
    halo = lax.ppermute(tails, "seq", [(i, i + 1) for i in range(XS * ZS - 1)])
    inner, rows, running, step, *parts = prepare(
        mixer_input, halo, state_input, conv_inner, conv_state, step_raw.T, decay_rate
    )
    table = jnp.transpose(level_table, (0, 2, 1))
    arrived = [parts[0]] + [along_x(parts[k], k) for k in range(1, XS)]
    shared = shared_part(rows, running, gate_input)
    arrived, shared = lax.optimization_barrier((arrived, shared))
    scores, gates, lifted_base = shared
    row_state, *near = fold_row(arrived)
    near = [near[0]] + [along_x(near[k], k) for k in range(1, XS)]
    other = lax.ppermute(row_state, "seq", seq_perm(lambda z, x: (z ^ 1, x)))
    pair_state = fold_pair(row_state, other)
    narrow = pair_state.astype(jnp.float16)
    moves = (
        lambda z, x: (z + 2, x) if z + 2 < ZS else None,
        lambda z, x: ((z ^ 1) + 4, x) if z + 4 < ZS else None,
        lambda z, x: (z + 6, x) if z + 6 < ZS else None,
    )
    gathered = [lax.ppermute(narrow, "seq", seq_perm(move)).astype(F32) for move in moves]
    far = fold_far(arrived, other, gathered)
    far = [far[0]] + [along_x(far[k], k) for k in range(1, XS)]
    local_out = local_part(
        table, stretch_kind, inner, running, step, scores, lifted_base, near
    )
    gated, squares = far_part(table, stretch_kind, local_out, gates, lifted_base, far)
    squares = squares + lax.ppermute(squares, "head", head_perm(lambda y, core: (y, 1 - core)))
    sums = [squares] + [
        lax.ppermute(squares, "head", head_perm(lambda y, core, k=k: ((y + k) % YS, core)))
        for k in range(1, YS)
    ]
    total_width = width * lax.axis_size("head")
    return norm(gated, sums, norm_gain[None, :], total_width)


def solution(mesh):
    return jax.shard_map(
        local,
        mesh=mesh,
        in_specs=(
            P("seq", "head"),
            P("seq", None),
            P("seq", "head"),
            P("seq", "head"),
            P("head"),
            P(None, "head"),
            P(),
            P(None, None, "head"),
            P("seq"),
            P("head"),
        ),
        out_specs=P("seq", "head"),
        check_vma=False,
    )
```

time: 118 us -> 80.4 us (0.68)
  local copies, waits for them, and re-layouts: 21.6 us -> 1.48 us
  Pallas kernels: 40.7 us -> 26.7 us
  waiting for transfers between devices: 20.4 us -> 18.6 us
  other arithmetic: 1.71 us -> 0.06 us
    unnamed x68 -> x6, local copies, waits for them, and re-layouts: 17.1 us -> 0.02 us
    pallas_call x7 -> x8, Pallas kernels: 40.7 us -> 26.7 us  [the longest x1 11.1 us: local_part(): pl.pallas_call(local_kernel, in_specs=[SMEM, SMEM] + [VMEM] * (5 + XS), o...]
    concatenate x1 -> x0, other arithmetic: 1.62 us -> none  [local(): jnp.concatenate([by_head[:, :5], gap, by_head[:, 5:10], gap], axis=1)]
    concatenate x1 -> x0, local copies, waits for them, and re-layouts: 1.45 us -> none  [local(): jnp.concatenate([by_head[:, :5], gap, by_head[:, 5:10], gap], axis=1)]
    ppermute x3, waiting for transfers between devices: 1.32 us -> 0.01 us  [local(): lax.ppermute(narrow, 'seq', seq_perm(move)).astype(F32)]
  transfers between devices with their start and end apart: 18 -> 18, of which waited for: 8 -> 8; matrix products, arithmetic and copies ran while one was open for 4% -> 0% of each run, Pallas kernels for 12% -> 18%
where the time goes in v2:
time: 80.4 us; the launch traced here: 79.7 us
  starting transfers between devices  32.5 us (40%)
  Pallas kernels  26.7 us (33%)
  waiting for transfers between devices  18.6 us (23%)
  local copies, waits for them, and re-layouts  1.48 us (2%)
    ppermute x3, starting transfers between devices, local(): lax.ppermute(narrow, 'seq', seq_perm(move)).astype(F32)  12.4 us
    ppermute x9, starting transfers between devices, along_x(): lax.ppermute(value, 'seq', seq_perm(lambda z, x: (z, (x + step) % XS)))  11.9 us
    pallas_call x1, Pallas kernels, local_part(): pl.pallas_call(local_kernel, in_specs=[SMEM, SMEM] + [VMEM] * (5 + XS), o...  11.1 us
    pallas_call x1, Pallas kernels, prepare(): pl.pallas_call(prepare_kernel, in_specs=[HBM, VMEM, HBM, HBM, HBM, HBM, H...  6.37 us
    ppermute x1, waiting for transfers between devices, local(): other = lax.ppermute(row_state, 'seq', seq_perm(lambda z, x: (z ^ 1, x)))  4.7 us
    ppermute x3, starting transfers between devices, local(): lax.ppermute(squares, 'head', head_perm(lambda y, core, k=k: ((y + k) % Y...  4.6 us
    ppermute x1, waiting for transfers between devices, local(): halo = lax.ppermute(tails, 'seq', [(i, i + 1) for i in range(XS * ZS - 1)])  4.6 us
    pallas_call x1, Pallas kernels, far_part(): pl.pallas_call(far_kernel, in_specs=[SMEM, SMEM] + [VMEM] * (3 + XS), out...  4.36 us
  transfers between devices with their start and end apart: 18, of which 8 were waited for; matrix products, arithmetic and copies ran while one was open for 0% of the time, Pallas kernels for 18%

profile of v2, /device:TPU:32, one launch (start us, length us, event | category | flops | bytes accessed | tf_op | source)
XLA Modules:
  0.0 79.7 jit_solution(7360653375233847715)
XLA Ops:
  0.7 0.8 slice.6
  1.5 3.4 %collective-permute-start = (bf16[16,1280]{1,0:T(8,128)(2,1)S(1)}, bf16[16,1280]{1,0:T(8,128)(2,1)S(1)}, u32[]{:S(2)}, u32[]{:S(2)}) collective-permute-start(bf16[16,1280]{1,0:T(8,128)(2,1)S(1)} %pad_maximum_fusion), channel_id=1, source_target_pairs={{0,8},{8,16},{16,24},{24,32},{32,40},{40,48},{48,56},{56,64},{64,7... | collective-permute-start | bytes 122888 | tf_op jit(solution)/shard_map/ppermute | solution.py:630
  4.9 4.6 %collective-permute-done.halo = bf16[16,1280]{1,0:T(8,128)(2,1)S(1)} collective-permute-done((bf16[16,1280]{1,0:T(8,128)(2,1)S(1)}, bf16[16,1280]{1,0:T(8,128)(2,1)S(1)}, u32[]{:S(2)}, u32[]{:S(2)}) %collective-permute-start) | collective-permute-done | bytes 40992 | tf_op jit(solution)/shard_map/ppermute | solution.py:630
  9.5 6.4 %prepare.1 = (bf16[1024,1024]{1,0:T(8,128)(2,1)S(1)}, bf16[1024,256]{1,0:T(8,128)(2,1)S(1)}, f32[8,1024]{1,0:T(8,128)S(1)}, f32[8,1024]{1,0:T(8,128)S(1)}, f32[2...) custom-call(bf16[1024,1024]{1,0:T(8,128)(2,1)} %mixer.1, ...), custom_call_target="tpu_custom_call" | custom-call | flops 268435456 | bytes 8388608 | tf_op jit(solution)/shard_map/prepare/pallas_call | solution.py:189
  15.9 2.1 %collective-permute-start.2 = (f32[264,128]{1,0:T(8,128)S(1)}, f32[264,128]{1,0:T(8,128)S(1)}, u32[]{:S(2)}, u32[]{:S(2)}) collective-permute-start(f32[264,128]{1,0:T(8,128)S(1)} %get-tuple-element.39), channel_id=1, source_target_pairs={{0,16},{8,24},{16,0},{24,8},{32,48},{40,56},{48,32},{56,40},{64,80... | collective-permute-start | bytes 405512 | tf_op jit(solution)/shard_map/ppermute | solution.py:45
  18.0 1.4 %collective-permute-start.3 = (f32[264,128]{1,0:T(8,128)S(1)}, f32[264,128]{1,0:T(8,128)S(1)}, u32[]{:S(2)}, u32[]{:S(2)}) collective-permute-start(f32[264,128]{1,0:T(8,128)S(1)} %get-tuple-element.40), channel_id=1, source_target_pairs={{0,24},{8,0},{16,8},{24,16},{32,56},{40,32},{48,40},{56,48},{64,88... | collective-permute-start | bytes 405512 | tf_op jit(solution)/shard_map/ppermute | solution.py:45
  19.5 2.8 %shared_part.1 = (f32[1024,1024]{1,0:T(8,128)S(1)}, f32[1024,1024]{1,0:T(8,128)S(1)}, f32[1024,1024]{1,0:T(8,128)S(1)}) custom-call(bf16[1024,256]{1,0:T(8,128)(2,1)S(1)} %get-tuple-element.41.rows, f32[8,1024]{1,0:T(8,128)S(1)} %get-tuple-element.35.running_in, bf16[1024,1024]{1,0:T(8,128)(2,1)} %gate.1), custom_call_target="tpu_custom_call" | custom-call | flops 134217728 | bytes 4194304 | tf_op jit(solution)/shard_map/shared_part/pallas_call | solution.py:263
  22.3 1.9 %collective-permute-done.1.p1.d1 = f32[264,128]{1,0:T(8,128)S(1)} collective-permute-done((f32[264,128]{1,0:T(8,128)S(1)}, f32[264,128]{1,0:T(8,128)S(1)}, u32[]{:S(2)}, u32[]{:S(2)}) %collective-permute-start.1) | collective-permute-done | bytes 135200 | tf_op jit(solution)/shard_map/ppermute | solution.py:45
  25.5 4.7 %collective-permute-done.7.other = f32[264,128]{1,0:T(8,128)S(1)} collective-permute-done((f32[264,128]{1,0:T(8,128)S(1)}, f32[264,128]{1,0:T(8,128)S(1)}, u32[]{:S(2)}, u32[]{:S(2)}) %collective-permute-start.7) | collective-permute-done | bytes 135200 | tf_op jit(solution)/shard_map/ppermute | solution.py:641
  30.4 7.3 %collective-permute-start.10 = (f16[264,128]{1,0:T(8,128)(2,1)S(1)}, f16[264,128]{1,0:T(8,128)(2,1)S(1)}, u32[]{:S(2)}, u32[]{:S(2)}) collective-permute-start(f16[264,128]{1,0:T(8,128)(2,1)S(1)} %convert_element_type.12), channel_id=1, source_target_pairs={{0,192},{8,200},{16,208},{24,216},{32,224},{40,232},{48,240},{56,2... | collective-permute-start | bytes 202760 | tf_op jit(solution)/shard_map/ppermute | solution.py:649
  37.7 2.3 %collective-permute-start.9 = (f16[264,128]{1,0:T(8,128)(2,1)S(1)}, f16[264,128]{1,0:T(8,128)(2,1)S(1)}, u32[]{:S(2)}, u32[]{:S(2)}) collective-permute-start(f16[264,128]{1,0:T(8,128)(2,1)S(1)} %convert_element_type.12), channel_id=1, source_target_pairs={{0,160},{8,168},{16,176},{24,184},{32,128},{40,136},{48,144},{56,1... | collective-permute-start | bytes 202760 | tf_op jit(solution)/shard_map/ppermute | solution.py:649
  40.0 2.8 %collective-permute-start.8 = (f16[264,128]{1,0:T(8,128)(2,1)S(1)}, f16[264,128]{1,0:T(8,128)(2,1)S(1)}, u32[]{:S(2)}, u32[]{:S(2)}) collective-permute-start(f16[264,128]{1,0:T(8,128)(2,1)S(1)} %convert_element_type.12), channel_id=1, source_target_pairs={{0,64},{8,72},{16,80},{24,88},{32,96},{40,104},{48,112},{56,120},{... | collective-permute-start | bytes 202760 | tf_op jit(solution)/shard_map/ppermute | solution.py:649
  42.9 0.9 %collective-permute-start.5 = (bf16[512,128]{1,0:T(8,128)(2,1)S(1)}, bf16[512,128]{1,0:T(8,128)(2,1)S(1)}, u32[]{:S(2)}, u32[]{:S(2)}) collective-permute-start(bf16[512,128]{1,0:T(8,128)(2,1)S(1)} %get-tuple-element.53), channel_id=1, source_target_pairs={{0,16},{8,24},{16,0},{24,8},{32,48},{40,56},{48,32},{56,40},{64,80... | collective-permute-start | bytes 393224 | tf_op jit(solution)/shard_map/ppermute | solution.py:45
  43.8 2.1 %collective-permute-start.6 = (bf16[512,128]{1,0:T(8,128)(2,1)S(1)}, bf16[512,128]{1,0:T(8,128)(2,1)S(1)}, u32[]{:S(2)}, u32[]{:S(2)}) collective-permute-start(bf16[512,128]{1,0:T(8,128)(2,1)S(1)} %get-tuple-element.54), channel_id=1, source_target_pairs={{0,24},{8,0},{16,8},{24,16},{32,56},{40,32},{48,40},{56,48},{64,88... | collective-permute-start | bytes 393224 | tf_op jit(solution)/shard_map/ppermute | solution.py:45
  46.4 2.4 %collective-permute-start.12 = (bf16[768,128]{1,0:T(8,128)(2,1)S(1)}, bf16[768,128]{1,0:T(8,128)(2,1)S(1)}, u32[]{:S(2)}, u32[]{:S(2)}) collective-permute-start(bf16[768,128]{1,0:T(8,128)(2,1)S(1)} %get-tuple-element.59), channel_id=1, source_target_pairs={{0,16},{8,24},{16,0},{24,8},{32,48},{40,56},{48,32},{56,40},{64,80... | collective-permute-start | bytes 589832 | tf_op jit(solution)/shard_map/ppermute | solution.py:45
  48.8 2.3 %collective-permute-start.13 = (bf16[768,128]{1,0:T(8,128)(2,1)S(1)}, bf16[768,128]{1,0:T(8,128)(2,1)S(1)}, u32[]{:S(2)}, u32[]{:S(2)}) collective-permute-start(bf16[768,128]{1,0:T(8,128)(2,1)S(1)} %get-tuple-element.60), channel_id=1, source_target_pairs={{0,24},{8,0},{16,8},{24,16},{32,56},{40,32},{48,40},{56,48},{64,88... | collective-permute-start | bytes 589832 | tf_op jit(solution)/shard_map/ppermute | solution.py:45
  51.1 1.6 %collective-permute-done.6.n3 = bf16[512,128]{1,0:T(8,128)(2,1)S(1)} collective-permute-done((bf16[512,128]{1,0:T(8,128)(2,1)S(1)}, bf16[512,128]{1,0:T(8,128)(2,1)S(1)}, u32[]{:S(2)}, u32[]{:S(2)}) %collective-permute-start.6) | collective-permute-done | bytes 131104 | tf_op jit(solution)/shard_map/ppermute | solution.py:45
  52.8 11.1 %local_part.1.local = f32[1024,1024]{1,0:T(8,128)S(1)} custom-call(f32[8,8,13]{2,1,0:T(8,128)S(1)} %bitcast.3, s32[16]{0:T(128)S(1)} %copy-done.2, bf16[1024,1024]{1,0:T(8,128)(2,1)S(1)} %get-tuple-element.34.inner, f32[8,1024]{1,0:T(8,128)S(1)} %get-tuple-element.35.running_in, f32[8,1024]{1,0:T(8,128)S(1)} %get-tuple-element.36.step_in, ...), custom_call_target="tpu_custom_call" | custom-call | flops 1073741824 | bytes 8388608 | tf_op jit(solution)/shard_map/local_part/pallas_call | solution.py:365
  63.9 4.4 %far_part.1 = (f32[1024,1024]{1,0:T(8,128)S(1)}, f32[8,128]{1,0:T(8,128)S(1)}) custom-call(f32[8,8,13]{2,1,0:T(8,128)S(1)} %bitcast.4, s32[16]{0:T(128)S(1)} %copy-done.2, f32[1024,1024]{1,0:T(8,128)S(1)} %local_part.1.local, f32[1024,1024]{1,0:T(8,128)S(1)} %get-tuple-element.55.gates, f32[1024,1024]{1,0:T(8,128)S(1)} %get-tuple-element.46.lifted_base, ...), custom_call_target="tpu_custom_call" | custom-call | flops 805306368 | bytes 12582912 | tf_op jit(solution)/shard_map/far_part/pallas_call | solution.py:570
  68.4 1.2 %collective-permute-done.14 = f32[8,128]{1,0:T(8,128)S(1)} collective-permute-done((f32[8,128]{1,0:T(8,128)S(1)}, f32[8,128]{1,0:T(8,128)S(1)}, u32[]{:S(2)}, u32[]{:S(2)}) %collective-permute-start.14) | collective-permute-done | bytes 4128 | tf_op jit(solution)/shard_map/ppermute | solution.py:656
  69.5 3.0 %collective-permute-start.17 = (f32[8,128]{1,0:T(8,128)S(1)}, f32[8,128]{1,0:T(8,128)S(1)}, u32[]{:S(2)}, u32[]{:S(2)}) collective-permute-start(f32[8,128]{1,0:T(8,128)S(1)} %add.3.s0), channel_id=1, source_target_pairs={{0,6},{1,7},{2,0},{3,1},{4,2},{5,3},{6,4},{7,5},{8,14},{9,15},{10,... | collective-permute-start | bytes 12296 | tf_op jit(solution)/shard_map/ppermute | solution.py:658
  73.2 1.0 %collective-permute-start.15 = (f32[8,128]{1,0:T(8,128)S(1)}, f32[8,128]{1,0:T(8,128)S(1)}, u32[]{:S(2)}, u32[]{:S(2)}) collective-permute-start(f32[8,128]{1,0:T(8,128)S(1)} %add.3.s0), channel_id=1, source_target_pairs={{0,2},{1,3},{2,4},{3,5},{4,6},{5,7},{6,0},{7,1},{8,10},{9,11},{10,... | collective-permute-start | bytes 12296 | tf_op jit(solution)/shard_map/ppermute | solution.py:658
  74.2 3.5 %collective-permute-done.16.s2 = f32[8,128]{1,0:T(8,128)S(1)} collective-permute-done((f32[8,128]{1,0:T(8,128)S(1)}, f32[8,128]{1,0:T(8,128)S(1)}, u32[]{:S(2)}, u32[]{:S(2)}) %collective-permute-start.16) | collective-permute-done | bytes 4128 | tf_op jit(solution)/shard_map/ppermute | solution.py:658
  78.0 1.6 %norm.1 = bf16[1024,1024]{1,0:T(8,128)(2,1)} custom-call(f32[1024,1024]{1,0:T(8,128)S(1)} %get-tuple-element.61.gated, f32[8,128]{1,0:T(8,128)S(1)} %add.3.s0, f32[8,128]{1,0:T(8,128)S(1)} %collective-permute-done.15.s1, f32[8,128]{1,0:T(8,128)S(1)} %collective-permute-done.16.s2, f32[8,128]{1,0:T(8,128)S(1)} %collective-permute-done.17.s3, ...), custom_call_target="tpu_custom_call" | custom-call | flops 2097152 | bytes 6291456 | tf_op jit(solution)/shard_map/norm/pallas_call | solution.py:602
  (34 shorter events, 4.0 us)
Async XLA Ops:
  1.5 8.0 %collective-permute-start = (bf16[16,1280]{1,0:T(8,128)(2,1)S(1)}, bf16[16,1280]{1,0:T(8,128)(2,1)S(1)}, u32[]{:S(2)}, u32[]{:S(2)}) collective-permute-start(bf16[16,1280]{1,0:T(8,128)(2,1)S(1)} %pad_maximum_fusion), channel_id=1, source_target_pairs={{0,8},{8,16},{16,24},{24,32},{32,40},{40,48},{48,56},{56,64},{64,7... | collective-permute-start | bytes 122888 | tf_op jit(solution)/shard_map/ppermute | solution.py:630
  15.8 37.0 %copy-start = (f32[8,13,8]{1,2,0:T(8,128)S(1)}, f32[8,13,8]{1,2,0:T(8,128)}, u32[]{:S(2)}) copy-start(f32[8,13,8]{1,2,0:T(8,128)} %param.17) | copy-start | bytes 9988
  15.8 36.9 %copy-start.2 = (s32[16]{0:T(128)S(1)}, s32[16]{0:T(128)}, u32[]{:S(2)}) copy-start(s32[16]{0:T(128)} %kinds.3) | copy-start | bytes 196
  15.9 8.4 %collective-permute-start.1 = (f32[264,128]{1,0:T(8,128)S(1)}, f32[264,128]{1,0:T(8,128)S(1)}, u32[]{:S(2)}, u32[]{:S(2)}) collective-permute-start(f32[264,128]{1,0:T(8,128)S(1)} %get-tuple-element.38), channel_id=1, source_target_pairs={{0,8},{8,16},{16,24},{24,0},{32,40},{40,48},{48,56},{56,32},{64,72... | collective-permute-start | bytes 405512 | tf_op jit(solution)/shard_map/ppermute | solution.py:45
  15.9 8.3 %collective-permute-start.2 = (f32[264,128]{1,0:T(8,128)S(1)}, f32[264,128]{1,0:T(8,128)S(1)}, u32[]{:S(2)}, u32[]{:S(2)}) collective-permute-start(f32[264,128]{1,0:T(8,128)S(1)} %get-tuple-element.39), channel_id=1, source_target_pairs={{0,16},{8,24},{16,0},{24,8},{32,48},{40,56},{48,32},{56,40},{64,80... | collective-permute-start | bytes 405512 | tf_op jit(solution)/shard_map/ppermute | solution.py:45
  18.0 6.8 %collective-permute-start.3 = (f32[264,128]{1,0:T(8,128)S(1)}, f32[264,128]{1,0:T(8,128)S(1)}, u32[]{:S(2)}, u32[]{:S(2)}) collective-permute-start(f32[264,128]{1,0:T(8,128)S(1)} %get-tuple-element.40), channel_id=1, source_target_pairs={{0,24},{8,0},{16,8},{24,16},{32,56},{40,32},{48,40},{56,48},{64,88... | collective-permute-start | bytes 405512 | tf_op jit(solution)/shard_map/ppermute | solution.py:45
  25.1 5.1 %collective-permute-start.7 = (f32[264,128]{1,0:T(8,128)S(1)}, f32[264,128]{1,0:T(8,128)S(1)}, u32[]{:S(2)}, u32[]{:S(2)}) collective-permute-start(f32[264,128]{1,0:T(8,128)S(1)} %get-tuple-element.56.own), channel_id=1, source_target_pairs={{0,32},{8,40},{16,48},{24,56},{32,0},{40,8},{48,16},{56,24},{64,96... | collective-permute-start | bytes 405512 | tf_op jit(solution)/shard_map/ppermute | solution.py:641
  25.2 23.6 %collective-permute-start.4 = (bf16[512,128]{1,0:T(8,128)(2,1)S(1)}, bf16[512,128]{1,0:T(8,128)(2,1)S(1)}, u32[]{:S(2)}, u32[]{:S(2)}) collective-permute-start(bf16[512,128]{1,0:T(8,128)(2,1)S(1)} %get-tuple-element.52), channel_id=1, source_target_pairs={{0,8},{8,16},{16,24},{24,0},{32,40},{40,48},{48,56},{56,32},{64,72... | collective-permute-start | bytes 393224 | tf_op jit(solution)/shard_map/ppermute | solution.py:45
  30.4 13.4 %collective-permute-start.10 = (f16[264,128]{1,0:T(8,128)(2,1)S(1)}, f16[264,128]{1,0:T(8,128)(2,1)S(1)}, u32[]{:S(2)}, u32[]{:S(2)}) collective-permute-start(f16[264,128]{1,0:T(8,128)(2,1)S(1)} %convert_element_type.12), channel_id=1, source_target_pairs={{0,192},{8,200},{16,208},{24,216},{32,224},{40,232},{48,240},{56,2... | collective-permute-start | bytes 202760 | tf_op jit(solution)/shard_map/ppermute | solution.py:649
  37.7 8.1 %collective-permute-start.9 = (f16[264,128]{1,0:T(8,128)(2,1)S(1)}, f16[264,128]{1,0:T(8,128)(2,1)S(1)}, u32[]{:S(2)}, u32[]{:S(2)}) collective-permute-start(f16[264,128]{1,0:T(8,128)(2,1)S(1)} %convert_element_type.12), channel_id=1, source_target_pairs={{0,160},{8,168},{16,176},{24,184},{32,128},{40,136},{48,144},{56,1... | collective-permute-start | bytes 202760 | tf_op jit(solution)/shard_map/ppermute | solution.py:649
  40.0 5.8 %collective-permute-start.8 = (f16[264,128]{1,0:T(8,128)(2,1)S(1)}, f16[264,128]{1,0:T(8,128)(2,1)S(1)}, u32[]{:S(2)}, u32[]{:S(2)}) collective-permute-start(f16[264,128]{1,0:T(8,128)(2,1)S(1)} %convert_element_type.12), channel_id=1, source_target_pairs={{0,64},{8,72},{16,80},{24,88},{32,96},{40,104},{48,112},{56,120},{... | collective-permute-start | bytes 202760 | tf_op jit(solution)/shard_map/ppermute | solution.py:649
  42.9 8.3 %collective-permute-start.5 = (bf16[512,128]{1,0:T(8,128)(2,1)S(1)}, bf16[512,128]{1,0:T(8,128)(2,1)S(1)}, u32[]{:S(2)}, u32[]{:S(2)}) collective-permute-start(bf16[512,128]{1,0:T(8,128)(2,1)S(1)} %get-tuple-element.53), channel_id=1, source_target_pairs={{0,16},{8,24},{16,0},{24,8},{32,48},{40,56},{48,32},{56,40},{64,80... | collective-permute-start | bytes 393224 | tf_op jit(solution)/shard_map/ppermute | solution.py:45
  43.8 9.0 %collective-permute-start.6 = (bf16[512,128]{1,0:T(8,128)(2,1)S(1)}, bf16[512,128]{1,0:T(8,128)(2,1)S(1)}, u32[]{:S(2)}, u32[]{:S(2)}) collective-permute-start(bf16[512,128]{1,0:T(8,128)(2,1)S(1)} %get-tuple-element.54), channel_id=1, source_target_pairs={{0,24},{8,0},{16,8},{24,16},{32,56},{40,32},{48,40},{56,48},{64,88... | collective-permute-start | bytes 393224 | tf_op jit(solution)/shard_map/ppermute | solution.py:45
  46.1 17.8 %collective-permute-start.11 = (bf16[768,128]{1,0:T(8,128)(2,1)S(1)}, bf16[768,128]{1,0:T(8,128)(2,1)S(1)}, u32[]{:S(2)}, u32[]{:S(2)}) collective-permute-start(bf16[768,128]{1,0:T(8,128)(2,1)S(1)} %get-tuple-element.58), channel_id=1, source_target_pairs={{0,8},{8,16},{16,24},{24,0},{32,40},{40,48},{48,56},{56,32},{64,72... | collective-permute-start | bytes 589832 | tf_op jit(solution)/shard_map/ppermute | solution.py:45
  46.4 17.4 %collective-permute-start.12 = (bf16[768,128]{1,0:T(8,128)(2,1)S(1)}, bf16[768,128]{1,0:T(8,128)(2,1)S(1)}, u32[]{:S(2)}, u32[]{:S(2)}) collective-permute-start(bf16[768,128]{1,0:T(8,128)(2,1)S(1)} %get-tuple-element.59), channel_id=1, source_target_pairs={{0,16},{8,24},{16,0},{24,8},{32,48},{40,56},{48,32},{56,40},{64,80... | collective-permute-start | bytes 589832 | tf_op jit(solution)/shard_map/ppermute | solution.py:45
  48.8 15.1 %collective-permute-start.13 = (bf16[768,128]{1,0:T(8,128)(2,1)S(1)}, bf16[768,128]{1,0:T(8,128)(2,1)S(1)}, u32[]{:S(2)}, u32[]{:S(2)}) collective-permute-start(bf16[768,128]{1,0:T(8,128)(2,1)S(1)} %get-tuple-element.60), channel_id=1, source_target_pairs={{0,24},{8,0},{16,8},{24,16},{32,56},{40,32},{48,40},{56,48},{64,88... | collective-permute-start | bytes 589832 | tf_op jit(solution)/shard_map/ppermute | solution.py:45
  63.9 14.1 %copy-start.1 = (f32[1024]{0:T(1024)S(1)}, f32[1024]{0:T(1024)}, u32[]{:S(2)}) copy-start(f32[1024]{0:T(1024)} %param.19) | copy-start | bytes 12292
  68.3 1.3 %collective-permute-start.14 = (f32[8,128]{1,0:T(8,128)S(1)}, f32[8,128]{1,0:T(8,128)S(1)}, u32[]{:S(2)}, u32[]{:S(2)}) collective-permute-start(f32[8,128]{1,0:T(8,128)S(1)} %get-tuple-element.62), channel_id=1, source_target_pairs={{0,1},{1,0},{2,3},{3,2},{4,5},{5,4},{6,7},{7,6},{8,9},{9,8},{10,11... | collective-permute-start | bytes 12296 | tf_op jit(solution)/shard_map/ppermute | solution.py:656
  69.5 4.6 %collective-permute-start.17 = (f32[8,128]{1,0:T(8,128)S(1)}, f32[8,128]{1,0:T(8,128)S(1)}, u32[]{:S(2)}, u32[]{:S(2)}) collective-permute-start(f32[8,128]{1,0:T(8,128)S(1)} %add.3.s0), channel_id=1, source_target_pairs={{0,6},{1,7},{2,0},{3,1},{4,2},{5,3},{6,4},{7,5},{8,14},{9,15},{10,... | collective-permute-start | bytes 12296 | tf_op jit(solution)/shard_map/ppermute | solution.py:658
  72.5 5.1 %collective-permute-start.16 = (f32[8,128]{1,0:T(8,128)S(1)}, f32[8,128]{1,0:T(8,128)S(1)}, u32[]{:S(2)}, u32[]{:S(2)}) collective-permute-start(f32[8,128]{1,0:T(8,128)S(1)} %add.3.s0), channel_id=1, source_target_pairs={{0,4},{1,5},{2,6},{3,7},{4,0},{5,1},{6,2},{7,3},{8,12},{9,13},{10,... | collective-permute-start | bytes 12296 | tf_op jit(solution)/shard_map/ppermute | solution.py:658
  73.2 4.8 %collective-permute-start.15 = (f32[8,128]{1,0:T(8,128)S(1)}, f32[8,128]{1,0:T(8,128)S(1)}, u32[]{:S(2)}, u32[]{:S(2)}) collective-permute-start(f32[8,128]{1,0:T(8,128)S(1)} %add.3.s0), channel_id=1, source_target_pairs={{0,2},{1,3},{2,4},{3,5},{4,6},{5,7},{6,0},{7,1},{8,10},{9,11},{10,... | collective-permute-start | bytes 12296 | tf_op jit(solution)/shard_map/ppermute | solution.py:658

commit v3 on v2

--- a/solution.py
+++ b/solution.py
@@ -45,8 +45,13 @@
     return lax.ppermute(value, "seq", seq_perm(lambda z, x: (z, (x + step) % XS)))
 
 
+def sent(message, move):
+    return lax.ppermute(message.astype(jnp.float16), "seq", seq_perm(move)).astype(F32)
+
+
 def silu(value):
-    return value / (1.0 + jnp.exp(-value))
+    half = 0.5 * value
+    return half + half * jnp.tanh(half)
 
 
 VMEM = pl.BlockSpec(memory_space=pltpu.VMEM)
@@ -81,9 +86,62 @@
     return silu(total).astype(BF16)
 
 
+def flag(condition):
+    return jnp.where(condition, 1.0, 0.0).astype(F32)
+
+
+def encode(message, states, decays):
+    spot = lax.broadcasted_iota(jnp.int32, (8, DIM), 0)
+    tail = jnp.zeros((8, DIM), F32)
+    for head in range(PAIR):
+        state, decay = states[head], decays[head]
+        coarse = jnp.floor(decay)
+        middle = jnp.floor((decay - coarse) * 1024.0) / 1024.0
+        rest = decay - coarse - middle
+        most = jnp.max(jnp.max(jnp.abs(state), axis=0, keepdims=True), axis=1, keepdims=True)
+        power = jnp.ceil(jnp.log(jnp.maximum(most, 1e-30)))
+        message[head * DIM : (head + 1) * DIM] = state * (jnp.exp(-power) * TOP)
+        for index, value in enumerate((coarse, middle, rest, power)):
+            tail = jnp.where(spot == PAIR * index + head, value, tail)
+    message[PAIR * DIM :] = tail
+
+
+def decode_decay(message):
+    tail = message[PAIR * DIM :]
+    return tail[:PAIR] + tail[PAIR : 2 * PAIR] + tail[2 * PAIR : 3 * PAIR]
+
+
+def decode_size(message):
+    return jnp.exp(message[PAIR * DIM :][3 * PAIR :]) / TOP
+
+
+def tails_kernel(mixer, state, out, sems):
+    length, width = mixer.shape
+    span = pl.ds(length - HALO, HALO)
+    copies = [
+        pltpu.make_async_copy(mixer.at[span], out.at[:, :width], sems.at[0]),
+        pltpu.make_async_copy(state.at[span], out.at[:, width:], sems.at[1]),
+    ]
+    for copy in copies:
+        copy.start()
+    for copy in copies:
+        copy.wait()
+
+
+def last_rows(mixer, state):
+    return pl.pallas_call(
+        tails_kernel,
+        in_specs=[HBM, HBM],
+        out_specs=VMEM,
+        out_shape=pltpu.VMEM((HALO, mixer.shape[1] + state.shape[1]), BF16),
+        scratch_shapes=[DMA((2,))],
+        compiler_params=params(2),
+        name="last_rows",
+    )(in_hbm(mixer), in_hbm(state))
+
+
 def prepare_kernel(
     mixer,
-    halo,
     state,
     taps,
     state_taps,
@@ -93,19 +151,20 @@
     rows,
     running_out,
     step_out,
+    first_rows,
+    first_scale,
+    last,
+    taps_here,
     part0,
     part1,
     part2,
     part3,
     mixer_here,
     state_here,
-    taps_here,
-    state_taps_here,
     raw_here,
     rate_here,
     keys_t,
     scale,
-    last,
     mixer_sem,
     small_sem,
 ):
@@ -120,8 +179,8 @@
                 (step_raw, raw_here),
                 (rate, rate_here),
                 (state, state_here),
-                (state_taps, state_taps_here),
-                (taps, taps_here),
+                (state_taps, taps_here.at[:, width:]),
+                (taps, taps_here.at[:, :width]),
             )
         )
     ]
@@ -138,8 +197,8 @@
     for copy in large:
         copy.start()
 
-    small[0].wait()
-    small[1].wait()
+    for copy in small:
+        copy.wait()
     raw = raw_here[...]
     step = jnp.maximum(raw, 0.0) + jnp.log1p(jnp.exp(-jnp.abs(raw)))
     spot = lax.broadcasted_iota(jnp.int32, (heads, length), 0)
@@ -156,57 +215,55 @@
     final = running[:, length - 1 :]
     running_out[...] = running
     step_out[...] = step
-    scale[...] = jnp.exp(final - running) * step
+    scaled = jnp.exp(final - running) * step
+    first_scale[...] = scaled[:, :DIM]
+    scale[...] = jnp.where(lane < HALO, 0.0, scaled)
     last[...] = jnp.broadcast_to(final, last.shape)
-    for copy in small[2:]:
-        copy.wait()
-    state_rows = conv(state_here[...], halo[:, width:], state_taps_here[...])
+    nothing = jnp.zeros((HALO, wide), BF16)
+    first_rows[:, width:] = state_here[:HALO]
+    state_rows = conv(state_here[...], nothing, taps_here[:, width:])
     rows[...] = state_rows
     keys_t[...] = state_rows[:, :DIM].astype(F32).T
 
-    spot = lax.broadcasted_iota(jnp.int32, (8, DIM), 0)
     for turn, part in enumerate((part0, part1, part2, part3)):
         large[turn].wait()
-        values = conv(
-            mixer_here[turn], halo[:, columns[turn]], taps_here[:, columns[turn]]
-        )
+        first_rows[:, columns[turn]] = mixer_here[turn, :HALO]
+        values = conv(mixer_here[turn], nothing, taps_here[:, columns[turn]])
         inner[:, columns[turn]] = values
-        pair = pairs[turn]
         for head in range(PAIR):
-            row = scale[pl.ds(pair * PAIR + head, 1), :]
+            row = scale[pl.ds(pairs[turn] * PAIR + head, 1), :]
             scaled_t = (keys_t[...] * row).astype(BF16)
             part[head * DIM : (head + 1) * DIM] = jnp.dot(
                 scaled_t, values[:, head * DIM : (head + 1) * DIM], preferred_element_type=F32
             )
-        first = last[pl.ds(pair * PAIR, 1), :]
-        second = last[pl.ds(pair * PAIR + 1, 1), :]
-        part[2 * DIM :] = jnp.where(spot == 0, first, jnp.where(spot == 1, second, 0.0))
-
-
-def prepare(mixer, halo, state, taps, state_taps, step_raw_t, rate):
+
+
+def prepare(mixer, state, taps, state_taps, step_raw_t, rate):
     length, width = mixer.shape
     heads = step_raw_t.shape[0]
+    every = width + 2 * DIM
     return pl.pallas_call(
         prepare_kernel,
-        in_specs=[HBM, VMEM, HBM, HBM, HBM, HBM, HBM],
-        out_specs=[VMEM] * (4 + XS),
+        in_specs=[HBM] * 6,
+        out_specs=[VMEM] * (8 + XS),
         out_shape=[
             pltpu.VMEM((length, width), BF16),
             pltpu.VMEM((length, 2 * DIM), BF16),
             pltpu.VMEM((heads, length), F32),
             pltpu.VMEM((heads, length), F32),
+            pltpu.VMEM((HALO, every), BF16),
+            pltpu.VMEM((heads, DIM), F32),
+            pltpu.VMEM((heads, DIM), F32),
+            pltpu.VMEM((taps.shape[0], every), BF16),
         ]
-        + [pltpu.VMEM((MESSAGE, DIM), F32)] * XS,
+        + [pltpu.VMEM((PAIR * DIM, DIM), F32)] * XS,
         scratch_shapes=[
             pltpu.VMEM((XS, length, PAIR * DIM), BF16),
             pltpu.VMEM((length, 2 * DIM), BF16),
-            pltpu.VMEM(taps.shape, BF16),
-            pltpu.VMEM(state_taps.shape, BF16),
             pltpu.VMEM((heads, length), F32),
             pltpu.SMEM((heads,), F32),
             pltpu.VMEM((DIM, length), F32),
             pltpu.VMEM((heads, length), F32),
-            pltpu.VMEM((heads, DIM), F32),
             DMA((XS,)),
             DMA((5,)),
         ],
@@ -217,7 +274,6 @@
         name="prepare",
     )(
         in_hbm(mixer),
-        halo,
         in_hbm(state),
         in_hbm(taps),
         in_hbm(state_taps),
@@ -226,7 +282,81 @@
     )
 
 
-def shared_kernel(rows, running_in, gate, scores, gates, lifted_base, gate_here, gate_sem):
+def finish_kernel(
+    halo,
+    first_rows,
+    first_scale,
+    last,
+    taps,
+    inner_in,
+    rows_in,
+    p0,
+    p1,
+    p2,
+    p3,
+    inner,
+    rows,
+    m0,
+    m1,
+    m2,
+    m3,
+):
+    x, _ = block_place()
+    width = inner.shape[1]
+    heads = width // DIM
+    wide = PAIR * DIM
+    made = conv(first_rows[:, width:], halo[:, width:], taps[:, width:])
+    rows[:HALO] = made
+    keys = made[:, :DIM].astype(F32)
+    columns = first_scale[...].T
+    scaled = [
+        (keys * jnp.broadcast_to(columns[:HALO, head : head + 1], (HALO, DIM))).astype(BF16)
+        for head in range(heads)
+    ]
+    added = []
+    for pair in range(XS):
+        lanes = slice(pair * wide, (pair + 1) * wide)
+        values = conv(first_rows[:, lanes], halo[:, lanes], taps[:, lanes])
+        inner[:HALO, lanes] = values
+        for head in range(PAIR):
+            added.append(
+                lax.dot_general(
+                    scaled[pair * PAIR + head],
+                    values[:, head * DIM : (head + 1) * DIM],
+                    (((0,), (0,)), ((), ())),
+                    preferred_element_type=F32,
+                )
+            )
+    for turn, (part, message) in enumerate(((p0, m0), (p1, m1), (p2, m2), (p3, m3))):
+        pair = lax.rem(x + turn, XS)
+        states = []
+        decays = []
+        for head in range(PAIR):
+            extra = sum(
+                added[other * PAIR + head] * flag(pair == other) for other in range(XS)
+            )
+            states.append(part[head * DIM : (head + 1) * DIM] + extra)
+            decays.append(last[pl.ds(pair * PAIR + head, 1), :])
+        encode(message, states, decays)
+
+
+def finish(halo, first_rows, first_scale, last, taps, inner, rows, parts):
+    return pl.pallas_call(
+        finish_kernel,
+        in_specs=[VMEM] * (7 + XS),
+        out_specs=[VMEM] * (2 + XS),
+        out_shape=[pltpu.VMEM(inner.shape, BF16), pltpu.VMEM(rows.shape, BF16)]
+        + [pltpu.VMEM((MESSAGE, DIM), F32)] * XS,
+        input_output_aliases={5: 0, 6: 1},
+        compiler_params=params(4),
+        cost_estimate=pl.CostEstimate(flops=2**22, bytes_accessed=2**20, transcendentals=2**14),
+        name="finish",
+    )(halo, first_rows, first_scale, last, taps, inner, rows, *parts)
+
+
+def shared_kernel(
+    rows, running_in, gate, scores, gates, lifted_base, ahead_out, gate_here, gate_sem
+):
     length, width = gate.shape
     heads = width // DIM
     tiles = length // TILE
@@ -240,19 +370,31 @@
             (((1,), (1,)), ((), ())),
             preferred_element_type=F32,
         )
-    columns = jnp.exp(running_in[...]).T
+    running = running_in[...]
+    columns = jnp.exp(running).T
+    ahead = jnp.concatenate(
+        [
+            jnp.exp(running[:, i * WIDE : (i + 1) * WIDE] - running[:, i * WIDE : i * WIDE + 1])
+            for i in range(length // WIDE)
+        ],
+        axis=1,
+    ).T
     for i in range(tiles):
         span = slice(i * TILE, (i + 1) * TILE)
         queries = rows[span, DIM:].astype(F32)
         for head in range(heads):
-            lifted_base[span, head * DIM : (head + 1) * DIM] = queries * jnp.broadcast_to(
+            lanes = slice(head * DIM, (head + 1) * DIM)
+            lifted_base[span, lanes] = queries * jnp.broadcast_to(
                 columns[span, head : head + 1], (TILE, DIM)
             )
+            ahead_out[span, lanes] = jnp.broadcast_to(ahead[span, head : head + 1], (TILE, DIM))
     gate_copy.wait()
 
     def one_tile(tile, carry):
         span = pl.ds(pl.multiple_of(tile * TILE, TILE), TILE)
-        gates[span, :] = silu(gate_here[span, :].astype(F32))
+        for piece in range(width // DIM):
+            lane = slice(piece * DIM, (piece + 1) * DIM)
+            gates[span, lane] = silu(gate_here[span, lane].astype(F32))
         return carry
 
     lax.fori_loop(0, tiles, one_tile, 0)
@@ -263,12 +405,8 @@
     return pl.pallas_call(
         shared_kernel,
         in_specs=[VMEM, VMEM, HBM],
-        out_specs=[VMEM] * 3,
-        out_shape=[
-            pltpu.VMEM((length, length), F32),
-            pltpu.VMEM((length, width), F32),
-            pltpu.VMEM((length, width), F32),
-        ],
+        out_specs=[VMEM] * 4,
+        out_shape=[pltpu.VMEM((length, length), F32)] + [pltpu.VMEM((length, width), F32)] * 3,
         scratch_shapes=[pltpu.VMEM((length, width), BF16), DMA],
         compiler_params=params(8),
         cost_estimate=pl.CostEstimate(
@@ -279,7 +417,20 @@
 
 
 def local_kernel(
-    table, kinds, inner, running_in, step_in, scores, lifted_base, n0, n1, n2, n3, out, held
+    table,
+    kinds,
+    inner,
+    running_in,
+    step_in,
+    scores,
+    lifted_base,
+    ahead_in,
+    n0,
+    n1,
+    n2,
+    n3,
+    out,
+    held,
 ):
     x, _ = block_place()
     length, width = inner.shape
@@ -305,14 +456,6 @@
         running = running_in[pl.ds(head, 1), :]
         step = step_in[pl.ds(head, 1), :]
         starts = [running[:, i * WIDE : i * WIDE + 1] for i in range(length // WIDE)]
-        ahead = jnp.concatenate(
-            [
-                jnp.exp(running[:, i * WIDE : (i + 1) * WIDE] - starts[i])
-                for i in range(length // WIDE)
-            ],
-            axis=1,
-        )
-        columns = jnp.broadcast_to(ahead, (8, length)).T
         for i in range(length // WIDE):
             wide = (i + 1) * WIDE
             span = slice(i * WIDE, wide)
@@ -324,7 +467,7 @@
                 kind = kinds[here]
                 weight = [table[kind, head, level] for level in range(7)]
                 band = slice(here * stretch, (here + 1) * stretch)
-                ahead_column = jnp.broadcast_to(columns[band, 0:1], (stretch, TILE))
+                ahead = ahead_in[band, lanes]
                 pieces = []
                 for j in range(wide // TILE):
                     first, second = 2 * j, 2 * j + 1
@@ -338,7 +481,7 @@
                     else:
                         factor = jnp.where(lane < stretch, left, right)
                     tile = slice(j * TILE, (j + 1) * TILE)
-                    piece = scores[band, tile] * (behind[:, tile] * factor) * ahead_column
+                    piece = scores[band, tile] * (behind[:, tile] * factor) * ahead
                     if second >= here:
                         piece = jnp.where(causal[here - first], piece, 0.0)
                     pieces.append(piece.astype(BF16))
@@ -356,15 +499,15 @@
             )
         return carry
 
-    lax.fori_loop(0, heads, one_head, 0)
-
-
-def local_part(table, kinds, inner, running, step, scores, lifted_base, near):
+    lax.fori_loop(0, heads, one_head, 0, unroll=4)
+
+
+def local_part(table, kinds, inner, running, step, scores, lifted_base, ahead, near):
     length, width = inner.shape
     heads = width // DIM
     return pl.pallas_call(
         local_kernel,
-        in_specs=[SMEM, SMEM] + [VMEM] * (5 + XS),
+        in_specs=[SMEM, SMEM] + [VMEM] * (6 + XS),
         out_specs=VMEM,
         out_shape=pltpu.VMEM((length, width), F32),
         scratch_shapes=[pltpu.VMEM((heads, 2 * DIM, DIM), BF16)],
@@ -373,48 +516,45 @@
             flops=8 * length * length * DIM, bytes_accessed=8 * 2**20, transcendentals=2**18
         ),
         name="local_part",
-    )(table, kinds, inner, running, step, scores, lifted_base, *near)
-
-
-def flag(condition):
-    return jnp.where(condition, 1.0, 0.0).astype(F32)
+    )(table, kinds, inner, running, step, scores, lifted_base, ahead, *near)
 
 
 def fold_row_kernel(p0, p1, p2, p3, row_out, m0, m1, m2, m3):
     x, _ = block_place()
     parts = (p0, p1, p2, p3)
     owner = [lax.rem(x + XS - k, XS) for k in range(XS)]
-    decays = [part[2 * DIM :] for part in parts]
-
-    def from_block(block):
-        return [flag(owner[k] == block) for k in range(XS)]
-
-    def pick(values, chosen):
-        return sum(value * mark for value, mark in zip(values, chosen))
-
-    block_marks = [from_block(block) for block in range(XS)]
+    decays = [decode_decay(part) for part in parts]
+    sizes = [decode_size(part) for part in parts]
+
+    def pick(values, block):
+        return sum(value * flag(owner[k] == block) for k, value in enumerate(values))
+
     later = [
-        jnp.exp(sum(decays[m] * flag(owner[m] > owner[k]) for m in range(XS))) for k in range(XS)
+        jnp.exp(sum(decays[m] * flag(owner[m] > owner[k]) for m in range(XS))) * sizes[k]
+        for k in range(XS)
     ]
-    decay_one = jnp.exp(pick(decays, block_marks[1]))
-    decay_two = jnp.exp(pick(decays, block_marks[2]))
+    decay_one = jnp.exp(pick(decays, 1))
+    decay_two = jnp.exp(pick(decays, 2))
+    total = sum(decays)
+    row_states = []
     for head in range(PAIR):
         span = slice(head * DIM, (head + 1) * DIM)
+        row = slice(head, head + 1)
         blocks = [part[span] for part in parts]
-        row_out[span] = sum(blocks[k] * later[k][head : head + 1] for k in range(XS))
-        first = pick(blocks, block_marks[0])
-        third = pick(blocks, block_marks[2])
-        joined = first * decay_one[head : head + 1] + pick(blocks, block_marks[1])
+        row_states.append(sum(blocks[k] * later[k][row] for k in range(XS)))
+        scaled = [blocks[k] * sizes[k][row] for k in range(XS)]
+        first = pick(scaled, 0)
+        third = pick(scaled, 2)
+        joined = first * decay_one[row] + pick(scaled, 1)
         for k, message in enumerate((m0, m1, m2, m3)):
             target = lax.rem(x + k, XS)
             message[span] = (
                 first * flag(target == 1) + third * flag(target == 3)
             ).astype(BF16)
             message[PAIR * DIM + head * DIM : PAIR * DIM + (head + 1) * DIM] = (
-                joined
-                * (flag(target == 2) + flag(target == 3) * decay_two[head : head + 1])
+                joined * (flag(target == 2) + flag(target == 3) * decay_two[row])
             ).astype(BF16)
-    row_out[2 * DIM :] = sum(decays)
+    encode(row_out, row_states, [total[head : head + 1] for head in range(PAIR)])
 
 
 def fold_row(parts):
@@ -429,92 +569,70 @@
     )(*parts)
 
 
-def fold_pair_kernel(own, other, pair_out):
+def fold_two_kernel(span_rows, own, other, out):
     _, z = block_place()
-    upper = flag(lax.rem(z, 2) == 1)
-    own_decay = own[2 * DIM :]
-    other_decay = other[2 * DIM :]
-    own_scale = jnp.exp(other_decay * (1.0 - upper))
-    other_scale = jnp.exp(own_decay * upper)
+    upper = flag(lax.rem(lax.div(z, span_rows), 2) == 1)
+    own_decay = decode_decay(own)
+    other_decay = decode_decay(other)
+    own_scale = jnp.exp(other_decay * (1.0 - upper)) * decode_size(own)
+    other_scale = jnp.exp(own_decay * upper) * decode_size(other)
     decay = own_decay + other_decay
-    coarse = jnp.floor(decay)
-    middle = jnp.floor((decay - coarse) * 1024.0) / 1024.0
-    rest = decay - coarse - middle
-    spot = lax.broadcasted_iota(jnp.int32, (8, DIM), 0)
-    tail = jnp.zeros((8, DIM), F32)
+    states = []
     for head in range(PAIR):
         span = slice(head * DIM, (head + 1) * DIM)
         row = slice(head, head + 1)
-        state = own[span] * own_scale[row] + other[span] * other_scale[row]
-        most = jnp.max(jnp.max(jnp.abs(state), axis=0, keepdims=True), axis=1, keepdims=True)
-        power = jnp.ceil(jnp.log(jnp.maximum(most, 1e-30)))
-        pair_out[span] = state * (jnp.exp(-power) * TOP)
-        for index, value in enumerate((coarse[row], middle[row], rest[row], power)):
-            tail = jnp.where(spot == 2 * index + head, value, tail)
-    pair_out[2 * DIM :] = tail
-
-
-def fold_pair(own, other):
-    return pl.pallas_call(
-        fold_pair_kernel,
+        states.append(own[span] * own_scale[row] + other[span] * other_scale[row])
+    encode(out, states, [decay[head : head + 1] for head in range(PAIR)])
+
+
+def fold_two(span_rows, own, other):
+    return pl.pallas_call(
+        functools.partial(fold_two_kernel, span_rows),
         in_specs=[VMEM] * 2,
         out_specs=VMEM,
         out_shape=pltpu.VMEM((MESSAGE, DIM), F32),
         compiler_params=params(4),
         cost_estimate=pl.CostEstimate(flops=2**18, bytes_accessed=2**19, transcendentals=2**10),
-        name="fold_pair",
+        name="fold_two",
     )(own, other)
 
 
-def fold_far_kernel(d0, d1, d2, d3, other, g1, g2, g3, m0, m1, m2, m3):
+def fold_far_kernel(d0, d1, d2, d3, row_before, pair_before, quad_before, m0, m1, m2, m3):
     x, z = block_place()
-    upper = flag(lax.rem(z, 2) == 1)
-    pair = lax.div(z, 2)
-    odd_pair = flag(lax.rem(pair, 2) == 1)
-    third_pair = flag(pair == 2)
-    last_pair = flag(pair == 3)
-    decays = [part[2 * DIM :] for part in (d0, d1, d2, d3)]
+    odd = flag(lax.rem(z, 2) == 1)
+    odd_pair = flag(lax.rem(lax.div(z, 2), 2) == 1)
+    upper = flag(z >= ZS // 2)
+    decays = [decode_decay(part) for part in (d0, d1, d2, d3)]
     owner = [lax.rem(x + XS - k, XS) for k in range(XS)]
-    tails = [part[2 * DIM :] for part in (g1, g2, g3)]
-    inside = [tail[0:2] + tail[2:4] + tail[4:6] for tail in tails]
-    sizes = [jnp.exp(tail[6:8]) / TOP for tail in tails]
-    in_pair = other[2 * DIM : 2 * DIM + PAIR] * upper
-    after = in_pair + inside[0] * last_pair
-    inside_first = jnp.exp(inside[0])
-    inside_last = jnp.exp(inside[1])
-    for head in range(PAIR):
-        span = slice(head * DIM, (head + 1) * DIM)
-        row = slice(head, head + 1)
-        two = other[span]
-        three, second, third = (
-            part[span] * size[row] for part, size in zip((g1, g2, g3), sizes)
-        )
-        four = (second * inside_first[row] + three) * third_pair + (
-            third * inside_last[row] + second
-        ) * last_pair
-        for k, message in enumerate((m0, m1, m2, m3)):
-            target = lax.rem(x + k, XS)
-            before = sum(decays[m][row] * flag(owner[m] < target) for m in range(XS))
-            factors = (
-                jnp.exp(before) * upper,
-                jnp.exp(before + in_pair[row]) * odd_pair,
-                jnp.exp(before + after[row]),
-            )
-            for level, (state, factor) in enumerate(zip((two, three, four), factors)):
-                base = level * PAIR * DIM + head * DIM
-                message[base : base + DIM] = (state * factor).astype(BF16)
-
-
-def fold_far(parts, other, gathered):
+    in_pair = decode_decay(row_before) * odd
+    in_quad = in_pair + decode_decay(pair_before) * odd_pair
+    levels = (
+        (row_before, jnp.zeros_like(in_pair), decode_size(row_before) * odd),
+        (pair_before, in_pair, decode_size(pair_before) * odd_pair),
+        (quad_before, in_quad, decode_size(quad_before) * upper),
+    )
+    for k, message in enumerate((m0, m1, m2, m3)):
+        target = lax.rem(x + k, XS)
+        before = sum(decays[m] * flag(owner[m] < target) for m in range(XS))
+        for level, (state, between, size) in enumerate(levels):
+            factor = jnp.exp(before + between) * size
+            for head in range(PAIR):
+                base = (level * PAIR + head) * DIM
+                message[base : base + DIM] = (
+                    state[head * DIM : (head + 1) * DIM] * factor[head : head + 1]
+                ).astype(BF16)
+
+
+def fold_far(parts, befores):
     return pl.pallas_call(
         fold_far_kernel,
-        in_specs=[VMEM] * (XS + 4),
+        in_specs=[VMEM] * (XS + 3),
         out_specs=[VMEM] * XS,
         out_shape=[pltpu.VMEM((6 * DIM, DIM), BF16)] * XS,
         compiler_params=params(4),
         cost_estimate=pl.CostEstimate(flops=2**20, bytes_accessed=2**20, transcendentals=2**12),
         name="fold_far",
-    )(*parts, other, *gathered)
+    )(*parts, *befores)
 
 
 def far_kernel(
@@ -558,7 +676,7 @@
             total[span] += value * value
         return carry
 
-    lax.fori_loop(0, heads, one_head, 0)
+    lax.fori_loop(0, heads, one_head, 0, unroll=4)
     for tile in range(length // TILE):
         part = total[tile * TILE : (tile + 1) * TILE].T
         squares[tile : tile + 1] = jnp.sum(part, axis=0, keepdims=True)
@@ -626,31 +744,31 @@
     norm_gain,
 ):
     length, width = mixer_input.shape
-    tails = jnp.concatenate([mixer_input[length - HALO :], state_input[length - HALO :]], axis=1)
-    halo = lax.ppermute(tails, "seq", [(i, i + 1) for i in range(XS * ZS - 1)])
-    inner, rows, running, step, *parts = prepare(
-        mixer_input, halo, state_input, conv_inner, conv_state, step_raw.T, decay_rate
+    halo = lax.ppermute(
+        last_rows(mixer_input, state_input), "seq", [(i, i + 1) for i in range(XS * ZS - 1)]
     )
+    inner, rows, running, step, first_rows, first_scale, last, taps, *parts = prepare(
+        mixer_input, state_input, conv_inner, conv_state, step_raw.T, decay_rate
+    )
+    inner, rows, *parts = finish(halo, first_rows, first_scale, last, taps, inner, rows, parts)
     table = jnp.transpose(level_table, (0, 2, 1))
-    arrived = [parts[0]] + [along_x(parts[k], k) for k in range(1, XS)]
+    arrived = [parts[0]] + [
+        sent(parts[k], lambda z, x, k=k: (z, (x + k) % XS)) for k in range(1, XS)
+    ]
     shared = shared_part(rows, running, gate_input)
     arrived, shared = lax.optimization_barrier((arrived, shared))
-    scores, gates, lifted_base = shared
+    scores, gates, lifted_base, ahead = shared
     row_state, *near = fold_row(arrived)
     near = [near[0]] + [along_x(near[k], k) for k in range(1, XS)]
-    other = lax.ppermute(row_state, "seq", seq_perm(lambda z, x: (z ^ 1, x)))
-    pair_state = fold_pair(row_state, other)
-    narrow = pair_state.astype(jnp.float16)
-    moves = (
-        lambda z, x: (z + 2, x) if z + 2 < ZS else None,
-        lambda z, x: ((z ^ 1) + 4, x) if z + 4 < ZS else None,
-        lambda z, x: (z + 6, x) if z + 6 < ZS else None,
-    )
-    gathered = [lax.ppermute(narrow, "seq", seq_perm(move)).astype(F32) for move in moves]
-    far = fold_far(arrived, other, gathered)
+    row_before = sent(row_state, lambda z, x: (z ^ 1, x))
+    pair_state = fold_two(1, row_state, row_before)
+    pair_before = sent(pair_state, lambda z, x: (z ^ 2, x))
+    quad_state = fold_two(2, pair_state, pair_before)
+    quad_before = sent(quad_state, lambda z, x: (ZS - 1 - z, x) if z < ZS // 2 else None)
+    far = fold_far(arrived, (row_before, pair_before, quad_before))
     far = [far[0]] + [along_x(far[k], k) for k in range(1, XS)]
     local_out = local_part(
-        table, stretch_kind, inner, running, step, scores, lifted_base, near
+        table, stretch_kind, inner, running, step, scores, lifted_base, ahead, near
     )
     gated, squares = far_part(table, stretch_kind, local_out, gates, lifted_base, far)
     squares = squares + lax.ppermute(squares, "head", head_perm(lambda y, core: (y, 1 - core)))

time: 80.4 us -> 70.6 us (0.88)
  waiting for transfers between devices: 18.6 us -> 10.9 us
  Pallas kernels: 26.7 us -> 24 us
  starting transfers between devices: 32.5 us -> 34.9 us
  local copies, waits for them, and re-layouts: 1.48 us -> 0.02 us
    ppermute x5 -> x7, starting transfers between devices: 15.9 us -> 20.1 us  [the longest x6 16.7 us: sent(): lax.ppermute(message.astype(jnp.float16), 'seq', seq_perm(move)).astype(F32)]
    ppermute x5 -> x7, waiting for transfers between devices: 9.31 us -> 5.21 us  [the longest x6 5.21 us: sent(): lax.ppermute(message.astype(jnp.float16), 'seq', seq_perm(move)).astype(F32)]
    pallas_call x4 -> x7, Pallas kernels: 17.7 us -> 14.7 us  [the longest x1 6.36 us: local_part(): pl.pallas_call(local_kernel, in_specs=[SMEM, SMEM] + [VMEM] * (6 + XS), o...]
    ppermute x9 -> x6, starting transfers between devices: 11.9 us -> 8.95 us  [along_x(): lax.ppermute(value, 'seq', seq_perm(lambda z, x: (z, (x + step) % XS)))]
    ppermute x9 -> x6, waiting for transfers between devices: 4.27 us -> 2.28 us  [along_x(): lax.ppermute(value, 'seq', seq_perm(lambda z, x: (z, (x + step) % XS)))]
    ppermute x3, waiting for transfers between devices: 3.86 us -> 2.26 us  [local(): lax.ppermute(squares, 'head', head_perm(lambda y, core, k=k: ((y + k) % Y...]
    slice x2 -> x0, local copies, waits for them, and re-layouts: 1.46 us -> none  [the longest x1 0.76 us: local(): mixer_input[length - HALO:]]
    ppermute x3, starting transfers between devices: 4.6 us -> 5.8 us  [local(): lax.ppermute(squares, 'head', head_perm(lambda y, core, k=k: ((y + k) % Y...]
  transfers between devices with their start and end apart: 18 -> 17, of which waited for: 8 -> 6; matrix products, arithmetic and copies ran while one was open for 0% -> 0% of each run, Pallas kernels for 18% -> 23%
where the time goes in v3:
time: 70.6 us; the launch traced here: 70.4 us
  starting transfers between devices  34.9 us (49%)
  Pallas kernels  24 us (34%)
  waiting for transfers between devices  10.9 us (15%)
    ppermute x6, starting transfers between devices, sent(): lax.ppermute(message.astype(jnp.float16), 'seq', seq_perm(move)).astype(F32)  16.7 us
    ppermute x6, starting transfers between devices, along_x(): lax.ppermute(value, 'seq', seq_perm(lambda z, x: (z, (x + step) % XS)))  8.95 us
    pallas_call x1, Pallas kernels, local_part(): pl.pallas_call(local_kernel, in_specs=[SMEM, SMEM] + [VMEM] * (6 + XS), o...  6.36 us
    pallas_call x1, Pallas kernels, prepare(): pl.pallas_call(prepare_kernel, in_specs=[HBM] * 6, out_specs=[VMEM] * (8...  6.35 us
    ppermute x3, starting transfers between devices, local(): lax.ppermute(squares, 'head', head_perm(lambda y, core, k=k: ((y + k) % Y...  5.8 us
    ppermute x6, waiting for transfers between devices, sent(): lax.ppermute(message.astype(jnp.float16), 'seq', seq_perm(move)).astype(F32)  5.21 us
    pallas_call x1, Pallas kernels, far_part(): pl.pallas_call(far_kernel, in_specs=[SMEM, SMEM] + [VMEM] * (3 + XS), out...  3.93 us
    pallas_call x1, Pallas kernels, shared_part(): pl.pallas_call(shared_kernel, in_specs=[VMEM, VMEM, HBM], out_specs=[VMEM...  3.43 us
  transfers between devices with their start and end apart: 17, of which 6 were waited for; matrix products, arithmetic and copies ran while one was open for 0% of the time, Pallas kernels for 23%

profile of v3, /device:TPU:32, one launch (start us, length us, event | category | flops | bytes accessed | tf_op | source)
XLA Modules:
  0.0 70.4 jit_solution(421547415731666576)
XLA Ops:
  0.8 3.4 %collective-permute-start = (bf16[16,1280]{1,0:T(8,128)(2,1)S(1)}, bf16[16,1280]{1,0:T(8,128)(2,1)S(1)}, u32[]{:S(2)}, u32[]{:S(2)}) collective-permute-start(bf16[16,1280]{1,0:T(8,128)(2,1)S(1)} %last_rows.1), channel_id=1, source_target_pairs={{0,8},{8,16},{16,24},{24,32},{32,40},{40,48},{48,56},{56,64},{64,7... | collective-permute-start | bytes 122888 | tf_op jit(solution)/shard_map/ppermute | solution.py:747
  4.2 6.4 %prepare.1 = (bf16[1024,1024]{1,0:T(8,128)(2,1)S(1)}, bf16[1024,256]{1,0:T(8,128)(2,1)S(1)}, f32[8,1024]{1,0:T(8,128)S(1)}, f32[8,1024]{1,0:T(8,128)S(1)}, bf16[...) custom-call(bf16[1024,1024]{1,0:T(8,128)(2,1)} %mixer.3, ...), custom_call_target="tpu_custom_call" | custom-call | flops 268435456 | bytes 8388608 | tf_op jit(solution)/shard_map/prepare/pallas_call | solution.py:245
  11.3 1.6 %collective-permute-start.1 = (f16[264,128]{1,0:T(8,128)(2,1)S(1)}, f16[264,128]{1,0:T(8,128)(2,1)S(1)}, u32[]{:S(2)}, u32[]{:S(2)}) collective-permute-start(f16[264,128]{1,0:T(8,128)(2,1)S(1)} %convert_element_type.36), channel_id=1, source_target_pairs={{0,8},{8,16},{16,24},{24,0},{32,40},{40,48},{48,56},{56,32},{64,72... | collective-permute-start | bytes 202760 | tf_op jit(solution)/shard_map/ppermute | solution.py:49
  12.9 3.2 %collective-permute-start.2 = (f16[264,128]{1,0:T(8,128)(2,1)S(1)}, f16[264,128]{1,0:T(8,128)(2,1)S(1)}, u32[]{:S(2)}, u32[]{:S(2)}) collective-permute-start(f16[264,128]{1,0:T(8,128)(2,1)S(1)} %convert_element_type.38), channel_id=1, source_target_pairs={{0,16},{8,24},{16,0},{24,8},{32,48},{40,56},{48,32},{56,40},{64,80... | collective-permute-start | bytes 202760 | tf_op jit(solution)/shard_map/ppermute | solution.py:49
  17.0 3.4 %shared_part.1 = (f32[1024,1024]{1,0:T(8,128)S(1)}, f32[1024,1024]{1,0:T(8,128)S(1)}, f32[1024,1024]{1,0:T(8,128)S(1)}, f32[1024,1024]{1,0:T(8,128)S(1)}) custom-call(bf16[1024,256]{1,0:T(8,128)(2,1)S(1)} %get-tuple-element.63.rows, f32[8,1024]{1,0:T(8,128)S(1)} %get-tuple-element.57.running_in, bf16[1024,1024]{1,0:T(8,128)(2,1)} %gate.1), custom_call_target="tpu_custom_call" | custom-call | flops 134217728 | bytes 4194304 | tf_op jit(solution)/shard_map/shared_part/pallas_call | solution.py:405
  21.1 4.2 %collective-permute-done.7 = f16[264,128]{1,0:T(8,128)(2,1)S(1)} collective-permute-done((f16[264,128]{1,0:T(8,128)(2,1)S(1)}, f16[264,128]{1,0:T(8,128)(2,1)S(1)}, u32[]{:S(2)}, u32[]{:S(2)}) %collective-permute-start.7) | collective-permute-done | bytes 67616 | tf_op jit(solution)/shard_map/ppermute | solution.py:49
  25.5 4.5 %collective-permute-start.8 = (f16[264,128]{1,0:T(8,128)(2,1)S(1)}, f16[264,128]{1,0:T(8,128)(2,1)S(1)}, u32[]{:S(2)}, u32[]{:S(2)}) collective-permute-start(f16[264,128]{1,0:T(8,128)(2,1)S(1)} %convert_element_type.44), channel_id=1, source_target_pairs={{0,64},{8,72},{16,80},{24,88},{32,96},{40,104},{48,112},{56,120},{... | collective-permute-start | bytes 202760 | tf_op jit(solution)/shard_map/ppermute | solution.py:49
  30.1 1.2 %collective-permute-start.4 = (bf16[512,128]{1,0:T(8,128)(2,1)S(1)}, bf16[512,128]{1,0:T(8,128)(2,1)S(1)}, u32[]{:S(2)}, u32[]{:S(2)}) collective-permute-start(bf16[512,128]{1,0:T(8,128)(2,1)S(1)} %get-tuple-element.76), channel_id=1, source_target_pairs={{0,8},{8,16},{16,24},{24,0},{32,40},{40,48},{48,56},{56,32},{64,72... | collective-permute-start | bytes 393224 | tf_op jit(solution)/shard_map/ppermute | solution.py:45
  31.3 1.0 %collective-permute-done.8 = f16[264,128]{1,0:T(8,128)(2,1)S(1)} collective-permute-done((f16[264,128]{1,0:T(8,128)(2,1)S(1)}, f16[264,128]{1,0:T(8,128)(2,1)S(1)}, u32[]{:S(2)}, u32[]{:S(2)}) %collective-permute-start.8) | collective-permute-done | bytes 67616 | tf_op jit(solution)/shard_map/ppermute | solution.py:49
  32.5 6.3 %collective-permute-start.9 = (f16[264,128]{1,0:T(8,128)(2,1)S(1)}, f16[264,128]{1,0:T(8,128)(2,1)S(1)}, u32[]{:S(2)}, u32[]{:S(2)}) collective-permute-start(f16[264,128]{1,0:T(8,128)(2,1)S(1)} %convert_element_type.46), channel_id=1, source_target_pairs={{0,224},{8,232},{16,240},{24,248},{32,192},{40,200},{48,208},{56,2... | collective-permute-start | bytes 202760 | tf_op jit(solution)/shard_map/ppermute | solution.py:49
  38.8 0.9 %collective-permute-start.5 = (bf16[512,128]{1,0:T(8,128)(2,1)S(1)}, bf16[512,128]{1,0:T(8,128)(2,1)S(1)}, u32[]{:S(2)}, u32[]{:S(2)}) collective-permute-start(bf16[512,128]{1,0:T(8,128)(2,1)S(1)} %get-tuple-element.77), channel_id=1, source_target_pairs={{0,16},{8,24},{16,0},{24,8},{32,48},{40,56},{48,32},{56,40},{64,80... | collective-permute-start | bytes 393224 | tf_op jit(solution)/shard_map/ppermute | solution.py:45
  39.8 2.2 %collective-permute-start.6 = (bf16[512,128]{1,0:T(8,128)(2,1)S(1)}, bf16[512,128]{1,0:T(8,128)(2,1)S(1)}, u32[]{:S(2)}, u32[]{:S(2)}) collective-permute-start(bf16[512,128]{1,0:T(8,128)(2,1)S(1)} %get-tuple-element.78), channel_id=1, source_target_pairs={{0,24},{8,0},{16,8},{24,16},{32,56},{40,32},{48,40},{56,48},{64,88... | collective-permute-start | bytes 393224 | tf_op jit(solution)/shard_map/ppermute | solution.py:45
  42.2 2.5 %collective-permute-start.11 = (bf16[768,128]{1,0:T(8,128)(2,1)S(1)}, bf16[768,128]{1,0:T(8,128)(2,1)S(1)}, u32[]{:S(2)}, u32[]{:S(2)}) collective-permute-start(bf16[768,128]{1,0:T(8,128)(2,1)S(1)} %get-tuple-element.83), channel_id=1, source_target_pairs={{0,16},{8,24},{16,0},{24,8},{32,48},{40,56},{48,32},{56,40},{64,80... | collective-permute-start | bytes 589832 | tf_op jit(solution)/shard_map/ppermute | solution.py:45
  44.7 2.0 %collective-permute-start.12 = (bf16[768,128]{1,0:T(8,128)(2,1)S(1)}, bf16[768,128]{1,0:T(8,128)(2,1)S(1)}, u32[]{:S(2)}, u32[]{:S(2)}) collective-permute-start(bf16[768,128]{1,0:T(8,128)(2,1)S(1)} %get-tuple-element.84), channel_id=1, source_target_pairs={{0,24},{8,0},{16,8},{24,16},{32,56},{40,32},{48,40},{56,48},{64,88... | collective-permute-start | bytes 589832 | tf_op jit(solution)/shard_map/ppermute | solution.py:45
  46.7 2.3 %collective-permute-done.6.n3 = bf16[512,128]{1,0:T(8,128)(2,1)S(1)} collective-permute-done((bf16[512,128]{1,0:T(8,128)(2,1)S(1)}, bf16[512,128]{1,0:T(8,128)(2,1)S(1)}, u32[]{:S(2)}, u32[]{:S(2)}) %collective-permute-start.6) | collective-permute-done | bytes 131104 | tf_op jit(solution)/shard_map/ppermute | solution.py:45
  49.0 6.4 %local_part.1.local = f32[1024,1024]{1,0:T(8,128)S(1)} custom-call(f32[8,8,13]{2,1,0:T(8,128)S(1)} %bitcast.3, s32[16]{0:T(128)S(1)} %copy-done.2, bf16[1024,1024]{1,0:T(8,128)(2,1)S(1)} %get-tuple-element.56.inner, f32[8,1024]{1,0:T(8,128)S(1)} %get-tuple-element.57.running_in, f32[8,1024]{1,0:T(8,128)S(1)} %get-tuple-element.58.step_in, ...), custom_call_target="tpu_custom_call" | custom-call | flops 1073741824 | bytes 8388608 | tf_op jit(solution)/shard_map/local_part/pallas_call | solution.py:508
  55.4 3.9 %far_part.1 = (f32[1024,1024]{1,0:T(8,128)S(1)}, f32[8,128]{1,0:T(8,128)S(1)}) custom-call(f32[8,8,13]{2,1,0:T(8,128)S(1)} %bitcast.4, s32[16]{0:T(128)S(1)} %copy-done.2, f32[1024,1024]{1,0:T(8,128)S(1)} %local_part.1.local, f32[1024,1024]{1,0:T(8,128)S(1)} %get-tuple-element.79.gates, f32[1024,1024]{1,0:T(8,128)S(1)} %get-tuple-element.69.lifted_base, ...), custom_call_target="tpu_custom_call" | custom-call | flops 805306368 | bytes 12582912 | tf_op jit(solution)/shard_map/far_part/pallas_call | solution.py:688
  59.5 1.2 %collective-permute-done.13 = f32[8,128]{1,0:T(8,128)S(1)} collective-permute-done((f32[8,128]{1,0:T(8,128)S(1)}, f32[8,128]{1,0:T(8,128)S(1)}, u32[]{:S(2)}, u32[]{:S(2)}) %collective-permute-start.13) | collective-permute-done | bytes 4128 | tf_op jit(solution)/shard_map/ppermute | solution.py:774
  60.6 1.6 %collective-permute-start.14 = (f32[8,128]{1,0:T(8,128)S(1)}, f32[8,128]{1,0:T(8,128)S(1)}, u32[]{:S(2)}, u32[]{:S(2)}) collective-permute-start(f32[8,128]{1,0:T(8,128)S(1)} %add.3.s0), channel_id=1, source_target_pairs={{0,2},{1,3},{2,4},{3,5},{4,6},{5,7},{6,0},{7,1},{8,10},{9,11},{10,... | collective-permute-start | bytes 12296 | tf_op jit(solution)/shard_map/ppermute | solution.py:776
  62.2 2.9 %collective-permute-start.15 = (f32[8,128]{1,0:T(8,128)S(1)}, f32[8,128]{1,0:T(8,128)S(1)}, u32[]{:S(2)}, u32[]{:S(2)}) collective-permute-start(f32[8,128]{1,0:T(8,128)S(1)} %add.3.s0), channel_id=1, source_target_pairs={{0,4},{1,5},{2,6},{3,7},{4,0},{5,1},{6,2},{7,3},{8,12},{9,13},{10,... | collective-permute-start | bytes 12296 | tf_op jit(solution)/shard_map/ppermute | solution.py:776
  65.1 1.3 %collective-permute-start.16 = (f32[8,128]{1,0:T(8,128)S(1)}, f32[8,128]{1,0:T(8,128)S(1)}, u32[]{:S(2)}, u32[]{:S(2)}) collective-permute-start(f32[8,128]{1,0:T(8,128)S(1)} %add.3.s0), channel_id=1, source_target_pairs={{0,6},{1,7},{2,0},{3,1},{4,2},{5,3},{6,4},{7,5},{8,14},{9,15},{10,... | collective-permute-start | bytes 12296 | tf_op jit(solution)/shard_map/ppermute | solution.py:776
  66.4 0.9 %collective-permute-done.15.s2 = f32[8,128]{1,0:T(8,128)S(1)} collective-permute-done((f32[8,128]{1,0:T(8,128)S(1)}, f32[8,128]{1,0:T(8,128)S(1)}, u32[]{:S(2)}, u32[]{:S(2)}) %collective-permute-start.15) | collective-permute-done | bytes 4128 | tf_op jit(solution)/shard_map/ppermute | solution.py:776
  67.3 1.4 %collective-permute-done.16.s3 = f32[8,128]{1,0:T(8,128)S(1)} collective-permute-done((f32[8,128]{1,0:T(8,128)S(1)}, f32[8,128]{1,0:T(8,128)S(1)}, u32[]{:S(2)}, u32[]{:S(2)}) %collective-permute-start.16) | collective-permute-done | bytes 4128 | tf_op jit(solution)/shard_map/ppermute | solution.py:776
  68.7 1.6 %norm.1 = bf16[1024,1024]{1,0:T(8,128)(2,1)} custom-call(f32[1024,1024]{1,0:T(8,128)S(1)} %get-tuple-element.85.gated, f32[8,128]{1,0:T(8,128)S(1)} %add.3.s0, f32[8,128]{1,0:T(8,128)S(1)} %collective-permute-done.14.s1, f32[8,128]{1,0:T(8,128)S(1)} %collective-permute-done.15.s2, f32[8,128]{1,0:T(8,128)S(1)} %collective-permute-done.16.s3, ...), custom_call_target="tpu_custom_call" | custom-call | flops 2097152 | bytes 6291456 | tf_op jit(solution)/shard_map/norm/pallas_call | solution.py:720
  (40 shorter events, 3.8 us)
Async XLA Ops:
  0.8 9.8 %collective-permute-start = (bf16[16,1280]{1,0:T(8,128)(2,1)S(1)}, bf16[16,1280]{1,0:T(8,128)(2,1)S(1)}, u32[]{:S(2)}, u32[]{:S(2)}) collective-permute-start(bf16[16,1280]{1,0:T(8,128)(2,1)S(1)} %last_rows.1), channel_id=1, source_target_pairs={{0,8},{8,16},{16,24},{24,32},{32,40},{40,48},{48,56},{56,64},{64,7... | collective-permute-start | bytes 122888 | tf_op jit(solution)/shard_map/ppermute | solution.py:747
  11.3 9.1 %collective-permute-start.1 = (f16[264,128]{1,0:T(8,128)(2,1)S(1)}, f16[264,128]{1,0:T(8,128)(2,1)S(1)}, u32[]{:S(2)}, u32[]{:S(2)}) collective-permute-start(f16[264,128]{1,0:T(8,128)(2,1)S(1)} %convert_element_type.36), channel_id=1, source_target_pairs={{0,8},{8,16},{16,24},{24,0},{32,40},{40,48},{48,56},{56,32},{64,72... | collective-permute-start | bytes 202760 | tf_op jit(solution)/shard_map/ppermute | solution.py:49
  12.9 36.1 %copy-start = (f32[8,13,8]{1,2,0:T(8,128)S(1)}, f32[8,13,8]{1,2,0:T(8,128)}, u32[]{:S(2)}) copy-start(f32[8,13,8]{1,2,0:T(8,128)} %param.17) | copy-start | bytes 9988
  12.9 36.1 %copy-start.2 = (s32[16]{0:T(128)S(1)}, s32[16]{0:T(128)}, u32[]{:S(2)}) copy-start(s32[16]{0:T(128)} %kinds.3) | copy-start | bytes 196
  12.9 7.5 %collective-permute-start.2 = (f16[264,128]{1,0:T(8,128)(2,1)S(1)}, f16[264,128]{1,0:T(8,128)(2,1)S(1)}, u32[]{:S(2)}, u32[]{:S(2)}) collective-permute-start(f16[264,128]{1,0:T(8,128)(2,1)S(1)} %convert_element_type.38), channel_id=1, source_target_pairs={{0,16},{8,24},{16,0},{24,8},{32,48},{40,56},{48,32},{56,40},{64,80... | collective-permute-start | bytes 202760 | tf_op jit(solution)/shard_map/ppermute | solution.py:49
  16.1 4.4 %collective-permute-start.3 = (f16[264,128]{1,0:T(8,128)(2,1)S(1)}, f16[264,128]{1,0:T(8,128)(2,1)S(1)}, u32[]{:S(2)}, u32[]{:S(2)}) collective-permute-start(f16[264,128]{1,0:T(8,128)(2,1)S(1)} %convert_element_type.40), channel_id=1, source_target_pairs={{0,24},{8,0},{16,8},{24,16},{32,56},{40,32},{48,40},{56,48},{64,88... | collective-permute-start | bytes 202760 | tf_op jit(solution)/shard_map/ppermute | solution.py:49
  20.9 4.4 %collective-permute-start.7 = (f16[264,128]{1,0:T(8,128)(2,1)S(1)}, f16[264,128]{1,0:T(8,128)(2,1)S(1)}, u32[]{:S(2)}, u32[]{:S(2)}) collective-permute-start(f16[264,128]{1,0:T(8,128)(2,1)S(1)} %convert_element_type.42), channel_id=1, source_target_pairs={{0,32},{8,40},{16,48},{24,56},{32,0},{40,8},{48,16},{56,24},{64,96... | collective-permute-start | bytes 202760 | tf_op jit(solution)/shard_map/ppermute | solution.py:49
  25.5 6.8 %collective-permute-start.8 = (f16[264,128]{1,0:T(8,128)(2,1)S(1)}, f16[264,128]{1,0:T(8,128)(2,1)S(1)}, u32[]{:S(2)}, u32[]{:S(2)}) collective-permute-start(f16[264,128]{1,0:T(8,128)(2,1)S(1)} %convert_element_type.44), channel_id=1, source_target_pairs={{0,64},{8,72},{16,80},{24,88},{32,96},{40,104},{48,112},{56,120},{... | collective-permute-start | bytes 202760 | tf_op jit(solution)/shard_map/ppermute | solution.py:49
  30.1 14.7 %collective-permute-start.4 = (bf16[512,128]{1,0:T(8,128)(2,1)S(1)}, bf16[512,128]{1,0:T(8,128)(2,1)S(1)}, u32[]{:S(2)}, u32[]{:S(2)}) collective-permute-start(bf16[512,128]{1,0:T(8,128)(2,1)S(1)} %get-tuple-element.76), channel_id=1, source_target_pairs={{0,8},{8,16},{16,24},{24,0},{32,40},{40,48},{48,56},{56,32},{64,72... | collective-permute-start | bytes 393224 | tf_op jit(solution)/shard_map/ppermute | solution.py:45
  32.5 9.4 %collective-permute-start.9 = (f16[264,128]{1,0:T(8,128)(2,1)S(1)}, f16[264,128]{1,0:T(8,128)(2,1)S(1)}, u32[]{:S(2)}, u32[]{:S(2)}) collective-permute-start(f16[264,128]{1,0:T(8,128)(2,1)S(1)} %convert_element_type.46), channel_id=1, source_target_pairs={{0,224},{8,232},{16,240},{24,248},{32,192},{40,200},{48,208},{56,2... | collective-permute-start | bytes 202760 | tf_op jit(solution)/shard_map/ppermute | solution.py:49
  38.8 7.9 %collective-permute-start.5 = (bf16[512,128]{1,0:T(8,128)(2,1)S(1)}, bf16[512,128]{1,0:T(8,128)(2,1)S(1)}, u32[]{:S(2)}, u32[]{:S(2)}) collective-permute-start(bf16[512,128]{1,0:T(8,128)(2,1)S(1)} %get-tuple-element.77), channel_id=1, source_target_pairs={{0,16},{8,24},{16,0},{24,8},{32,48},{40,56},{48,32},{56,40},{64,80... | collective-permute-start | bytes 393224 | tf_op jit(solution)/shard_map/ppermute | solution.py:45
  39.8 9.2 %collective-permute-start.6 = (bf16[512,128]{1,0:T(8,128)(2,1)S(1)}, bf16[512,128]{1,0:T(8,128)(2,1)S(1)}, u32[]{:S(2)}, u32[]{:S(2)}) collective-permute-start(bf16[512,128]{1,0:T(8,128)(2,1)S(1)} %get-tuple-element.78), channel_id=1, source_target_pairs={{0,24},{8,0},{16,8},{24,16},{32,56},{40,32},{48,40},{56,48},{64,88... | collective-permute-start | bytes 393224 | tf_op jit(solution)/shard_map/ppermute | solution.py:45
  42.1 13.3 %collective-permute-start.10 = (bf16[768,128]{1,0:T(8,128)(2,1)S(1)}, bf16[768,128]{1,0:T(8,128)(2,1)S(1)}, u32[]{:S(2)}, u32[]{:S(2)}) collective-permute-start(bf16[768,128]{1,0:T(8,128)(2,1)S(1)} %get-tuple-element.82), channel_id=1, source_target_pairs={{0,8},{8,16},{16,24},{24,0},{32,40},{40,48},{48,56},{56,32},{64,72... | collective-permute-start | bytes 589832 | tf_op jit(solution)/shard_map/ppermute | solution.py:45
  42.2 13.2 %collective-permute-start.11 = (bf16[768,128]{1,0:T(8,128)(2,1)S(1)}, bf16[768,128]{1,0:T(8,128)(2,1)S(1)}, u32[]{:S(2)}, u32[]{:S(2)}) collective-permute-start(bf16[768,128]{1,0:T(8,128)(2,1)S(1)} %get-tuple-element.83), channel_id=1, source_target_pairs={{0,16},{8,24},{16,0},{24,8},{32,48},{40,56},{48,32},{56,40},{64,80... | collective-permute-start | bytes 589832 | tf_op jit(solution)/shard_map/ppermute | solution.py:45
  44.7 10.7 %collective-permute-start.12 = (bf16[768,128]{1,0:T(8,128)(2,1)S(1)}, bf16[768,128]{1,0:T(8,128)(2,1)S(1)}, u32[]{:S(2)}, u32[]{:S(2)}) collective-permute-start(bf16[768,128]{1,0:T(8,128)(2,1)S(1)} %get-tuple-element.84), channel_id=1, source_target_pairs={{0,24},{8,0},{16,8},{24,16},{32,56},{40,32},{48,40},{56,48},{64,88... | collective-permute-start | bytes 589832 | tf_op jit(solution)/shard_map/ppermute | solution.py:45
  55.4 13.3 %copy-start.1 = (f32[1024]{0:T(1024)S(1)}, f32[1024]{0:T(1024)}, u32[]{:S(2)}) copy-start(f32[1024]{0:T(1024)} %param.19) | copy-start | bytes 12292
  59.4 1.3 %collective-permute-start.13 = (f32[8,128]{1,0:T(8,128)S(1)}, f32[8,128]{1,0:T(8,128)S(1)}, u32[]{:S(2)}, u32[]{:S(2)}) collective-permute-start(f32[8,128]{1,0:T(8,128)S(1)} %get-tuple-element.86), channel_id=1, source_target_pairs={{0,1},{1,0},{2,3},{3,2},{4,5},{5,4},{6,7},{7,6},{8,9},{9,8},{10,11... | collective-permute-start | bytes 12296 | tf_op jit(solution)/shard_map/ppermute | solution.py:774
  60.6 5.8 %collective-permute-start.14 = (f32[8,128]{1,0:T(8,128)S(1)}, f32[8,128]{1,0:T(8,128)S(1)}, u32[]{:S(2)}, u32[]{:S(2)}) collective-permute-start(f32[8,128]{1,0:T(8,128)S(1)} %add.3.s0), channel_id=1, source_target_pairs={{0,2},{1,3},{2,4},{3,5},{4,6},{5,7},{6,0},{7,1},{8,10},{9,11},{10,... | collective-permute-start | bytes 12296 | tf_op jit(solution)/shard_map/ppermute | solution.py:776
  62.2 5.1 %collective-permute-start.15 = (f32[8,128]{1,0:T(8,128)S(1)}, f32[8,128]{1,0:T(8,128)S(1)}, u32[]{:S(2)}, u32[]{:S(2)}) collective-permute-start(f32[8,128]{1,0:T(8,128)S(1)} %add.3.s0), channel_id=1, source_target_pairs={{0,4},{1,5},{2,6},{3,7},{4,0},{5,1},{6,2},{7,3},{8,12},{9,13},{10,... | collective-permute-start | bytes 12296 | tf_op jit(solution)/shard_map/ppermute | solution.py:776
  65.1 3.6 %collective-permute-start.16 = (f32[8,128]{1,0:T(8,128)S(1)}, f32[8,128]{1,0:T(8,128)S(1)}, u32[]{:S(2)}, u32[]{:S(2)}) collective-permute-start(f32[8,128]{1,0:T(8,128)S(1)} %add.3.s0), channel_id=1, source_target_pairs={{0,6},{1,7},{2,0},{3,1},{4,2},{5,3},{6,4},{7,5},{8,14},{9,15},{10,... | collective-permute-start | bytes 12296 | tf_op jit(solution)/shard_map/ppermute | solution.py:776

commit v4 on v3

--- a/solution.py
+++ b/solution.py
@@ -18,6 +18,8 @@
 HALO = 16
 TILE = 128
 WIDE = 256
+NEAR = 3
+FAR = 2
 TOP = 16384.0
 MESSAGE = PAIR * DIM + 8
 
@@ -64,6 +66,14 @@
     return pltpu.CompilerParams(vmem_limit_bytes=mebibytes * 2**20)
 
 
+def cost(microseconds):
+    return pl.CostEstimate(
+        flops=int(microseconds * 1.15e9),
+        bytes_accessed=int(microseconds * 3.6e6),
+        transcendentals=0,
+    )
+
+
 def in_hbm(value):
     return pltpu.with_memory_space_constraint(value, pltpu.HBM)
 
@@ -73,17 +83,25 @@
     return lax.rem(index, XS), lax.div(index, XS)
 
 
-def conv(block, halo, taps):
-    length = block.shape[0]
-    width = taps.shape[0]
-    joined = jnp.concatenate([halo[HALO - 8 :].astype(F32), block.astype(F32)], axis=0)
+def conv(block, halo, taps, pad):
+    length, width = block.shape
+    count = taps.shape[0]
     taps = taps.astype(F32)
-    total = jnp.zeros((length, block.shape[1]), F32)
-    for offset in range(width):
-        shift = width - 1 - offset
-        moved = joined if shift == 0 else pltpu.roll(joined, shift, axis=0)
-        total = total + moved[8:] * taps[offset : offset + 1]
-    return silu(total).astype(BF16)
+    columns = []
+    for lane in range(width // DIM):
+        lanes = slice(lane * DIM, (lane + 1) * DIM)
+        pad[lane, :8] = halo[HALO - 8 :, lanes].astype(F32)
+        pad[lane, 8 : 8 + length] = block[:, lanes].astype(F32)
+        made = []
+        for base in range(0, length, TILE):
+            size = min(TILE, length)
+            total = jnp.zeros((size, DIM), F32)
+            for offset in range(count):
+                first = base + 9 - count + offset
+                total = total + pad[lane, first : first + size] * taps[offset : offset + 1, lanes]
+            made.append(silu(total).astype(BF16))
+        columns.append(jnp.concatenate(made, axis=0))
+    return jnp.concatenate(columns, axis=1)
 
 
 def flag(condition):
@@ -165,6 +183,7 @@
     rate_here,
     keys_t,
     scale,
+    pad,
     mixer_sem,
     small_sem,
 ):
@@ -221,14 +240,14 @@
     last[...] = jnp.broadcast_to(final, last.shape)
     nothing = jnp.zeros((HALO, wide), BF16)
     first_rows[:, width:] = state_here[:HALO]
-    state_rows = conv(state_here[...], nothing, taps_here[:, width:])
+    state_rows = conv(state_here[...], nothing, taps_here[:, width:], pad)
     rows[...] = state_rows
     keys_t[...] = state_rows[:, :DIM].astype(F32).T
 
     for turn, part in enumerate((part0, part1, part2, part3)):
         large[turn].wait()
         first_rows[:, columns[turn]] = mixer_here[turn, :HALO]
-        values = conv(mixer_here[turn], nothing, taps_here[:, columns[turn]])
+        values = conv(mixer_here[turn], nothing, taps_here[:, columns[turn]], pad)
         inner[:, columns[turn]] = values
         for head in range(PAIR):
             row = scale[pl.ds(pairs[turn] * PAIR + head, 1), :]
@@ -264,13 +283,12 @@
             pltpu.SMEM((heads,), F32),
             pltpu.VMEM((DIM, length), F32),
             pltpu.VMEM((heads, length), F32),
+            pltpu.VMEM((PAIR, length + 8, DIM), F32),
             DMA((XS,)),
             DMA((5,)),
         ],
         compiler_params=params(16),
-        cost_estimate=pl.CostEstimate(
-            flops=2 * length * width * DIM, bytes_accessed=8 * 2**20, transcendentals=2 * length * width
-        ),
+        cost_estimate=cost(5.7),
         name="prepare",
     )(
         in_hbm(mixer),
@@ -300,12 +318,13 @@
     m1,
     m2,
     m3,
+    pad,
 ):
     x, _ = block_place()
     width = inner.shape[1]
     heads = width // DIM
     wide = PAIR * DIM
-    made = conv(first_rows[:, width:], halo[:, width:], taps[:, width:])
+    made = conv(first_rows[:, width:], halo[:, width:], taps[:, width:], pad)
     rows[:HALO] = made
     keys = made[:, :DIM].astype(F32)
     columns = first_scale[...].T
@@ -316,7 +335,7 @@
     added = []
     for pair in range(XS):
         lanes = slice(pair * wide, (pair + 1) * wide)
-        values = conv(first_rows[:, lanes], halo[:, lanes], taps[:, lanes])
+        values = conv(first_rows[:, lanes], halo[:, lanes], taps[:, lanes], pad)
         inner[:HALO, lanes] = values
         for head in range(PAIR):
             added.append(
@@ -347,9 +366,10 @@
         out_specs=[VMEM] * (2 + XS),
         out_shape=[pltpu.VMEM(inner.shape, BF16), pltpu.VMEM(rows.shape, BF16)]
         + [pltpu.VMEM((MESSAGE, DIM), F32)] * XS,
+        scratch_shapes=[pltpu.VMEM((PAIR, HALO + 8, DIM), F32)],
         input_output_aliases={5: 0, 6: 1},
         compiler_params=params(4),
-        cost_estimate=pl.CostEstimate(flops=2**22, bytes_accessed=2**20, transcendentals=2**14),
+        cost_estimate=cost(0.75),
         name="finish",
     )(halo, first_rows, first_scale, last, taps, inner, rows, *parts)
 
@@ -409,164 +429,243 @@
         out_shape=[pltpu.VMEM((length, length), F32)] + [pltpu.VMEM((length, width), F32)] * 3,
         scratch_shapes=[pltpu.VMEM((length, width), BF16), DMA],
         compiler_params=params(8),
-        cost_estimate=pl.CostEstimate(
-            flops=length * length * DIM, bytes_accessed=4 * 2**20, transcendentals=2**21
-        ),
+        cost_estimate=cost(3.4),
         name="shared_part",
     )(rows, running, in_hbm(gate))
 
 
+def mix_head(head, table, kinds, inner, running_in, step_in, scores, ahead_in, emit):
+    length = inner.shape[0]
+    stretch = length // kinds.shape[0]
+    each = WIDE // stretch
+    row = lax.broadcasted_iota(jnp.int32, (stretch, TILE), 0)
+    column = lax.broadcasted_iota(jnp.int32, (stretch, TILE), 1)
+    causal = [row + part * stretch >= column for part in range(TILE // stretch)]
+    lane = lax.broadcasted_iota(jnp.int32, (1, TILE), 1)
+    empty = jnp.zeros((stretch, TILE), BF16)
+    lanes = pl.ds(pl.multiple_of(head * DIM, DIM), DIM)
+    running = running_in[pl.ds(head, 1), :]
+    step = step_in[pl.ds(head, 1), :]
+    for i in range(length // WIDE):
+        wide = (i + 1) * WIDE
+        start = running[:, i * WIDE : i * WIDE + 1]
+        behind = jnp.exp(start - running[:, :wide]) * step[:, :wide]
+        bands = []
+        for part in range(each):
+            here = i * each + part
+            kind = kinds[here]
+            weight = [table[kind, head, level] for level in range(5)]
+            band = slice(here * stretch, (here + 1) * stretch)
+            ahead = ahead_in[band, lanes]
+            pieces = []
+            for j in range(wide // TILE):
+                first, second = 2 * j, 2 * j + 1
+                if first > here:
+                    pieces.append(empty)
+                    continue
+                left = weight[(here ^ first).bit_length()]
+                right = weight[(here ^ second).bit_length()]
+                if second > here or (here ^ first).bit_length() == (here ^ second).bit_length():
+                    factor = left
+                else:
+                    factor = jnp.where(lane < stretch, left, right)
+                tile = slice(j * TILE, (j + 1) * TILE)
+                piece = scores[band, tile] * (behind[:, tile] * factor) * ahead
+                if second >= here:
+                    piece = jnp.where(causal[here - first], piece, 0.0)
+                pieces.append(piece.astype(BF16))
+            bands.append(jnp.concatenate(pieces, axis=1))
+        emit(
+            i,
+            jnp.dot(
+                jnp.concatenate(bands, axis=0), inner[:wide, lanes], preferred_element_type=F32
+            ),
+        )
+
+
+def lift(table, kinds, lifted_base, head, tile, levels, held):
+    length = lifted_base.shape[0]
+    stretch = length // kinds.shape[0]
+    lanes = pl.ds(pl.multiple_of(head * DIM, DIM), DIM)
+    bands = []
+    for here in range(tile * WIDE // stretch, (tile + 1) * WIDE // stretch):
+        kind = kinds[here]
+        base = lifted_base[here * stretch : (here + 1) * stretch, lanes]
+        bands.append(
+            jnp.concatenate(
+                [(base * table[kind, head, level]).astype(BF16) for level in levels], axis=1
+            )
+        )
+    return jnp.dot(jnp.concatenate(bands, axis=0), held[head], preferred_element_type=F32)
+
+
+def mix_kernel(first, table, kinds, inner, running_in, step_in, scores, ahead_in, out):
+    def one_head(offset, carry):
+        lanes = pl.ds(pl.multiple_of(offset * DIM, DIM), DIM)
+
+        def emit(i, value):
+            out[i * WIDE : (i + 1) * WIDE, lanes] = value
+
+        mix_head(
+            first + offset, table, kinds, inner, running_in, step_in, scores, ahead_in, emit
+        )
+        return carry
+
+    lax.fori_loop(0, PAIR, one_head, 0)
+
+
+def mix_part(first, table, kinds, inner, running, step, scores, ahead):
+    length, width = inner.shape
+    return pl.pallas_call(
+        functools.partial(mix_kernel, first),
+        in_specs=[SMEM, SMEM] + [VMEM] * 5,
+        out_specs=VMEM,
+        out_shape=pltpu.VMEM((length, PAIR * DIM), F32),
+        compiler_params=params(8),
+        cost_estimate=cost(2.4),
+        name="mix_part",
+    )(table, kinds, inner, running, step, scores, ahead)
+
+
 def local_kernel(
+    done,
     table,
     kinds,
     inner,
     running_in,
     step_in,
     scores,
+    ahead_in,
     lifted_base,
-    ahead_in,
-    n0,
-    n1,
-    n2,
-    n3,
-    out,
-    held,
+    *rest,
 ):
+    mixed = rest[:done]
+    nears = rest[done : done + XS]
+    out, held = rest[done + XS :]
     x, _ = block_place()
     length, width = inner.shape
     heads = width // DIM
-    stretch = length // kinds.shape[0]
-    each = WIDE // stretch
-    for k, near in enumerate((n0, n1, n2, n3)):
+    for k, near in enumerate(nears):
         pair = lax.rem(x + XS - k, XS)
         for head in range(PAIR):
-            for level in range(2):
+            for level in range(NEAR):
                 base = (level * PAIR + head) * DIM
                 held[pair * PAIR + head, level * DIM : (level + 1) * DIM] = near[
                     base : base + DIM
                 ]
-    row = lax.broadcasted_iota(jnp.int32, (stretch, TILE), 0)
-    column = lax.broadcasted_iota(jnp.int32, (stretch, TILE), 1)
-    causal = [row + part * stretch >= column for part in range(TILE // stretch)]
-    lane = lax.broadcasted_iota(jnp.int32, (1, TILE), 1)
-    empty = jnp.zeros((stretch, TILE), BF16)
+    levels = range(5, 5 + NEAR)
+    for group, value in enumerate(mixed):
+        for offset in range(PAIR):
+            head = group * PAIR + offset
+            for tile in range(length // WIDE):
+                span = slice(tile * WIDE, (tile + 1) * WIDE)
+                out[span, head * DIM : (head + 1) * DIM] = value[
+                    span, offset * DIM : (offset + 1) * DIM
+                ] + lift(table, kinds, lifted_base, head, tile, levels, held)
 
     def one_head(head, carry):
         lanes = pl.ds(pl.multiple_of(head * DIM, DIM), DIM)
-        running = running_in[pl.ds(head, 1), :]
-        step = step_in[pl.ds(head, 1), :]
-        starts = [running[:, i * WIDE : i * WIDE + 1] for i in range(length // WIDE)]
-        for i in range(length // WIDE):
-            wide = (i + 1) * WIDE
-            span = slice(i * WIDE, wide)
-            behind = jnp.exp(starts[i] - running[:, :wide]) * step[:, :wide]
-            bands = []
-            lifted = []
-            for part in range(each):
-                here = i * each + part
-                kind = kinds[here]
-                weight = [table[kind, head, level] for level in range(7)]
-                band = slice(here * stretch, (here + 1) * stretch)
-                ahead = ahead_in[band, lanes]
-                pieces = []
-                for j in range(wide // TILE):
-                    first, second = 2 * j, 2 * j + 1
-                    if first > here:
-                        pieces.append(empty)
-                        continue
-                    left = weight[(here ^ first).bit_length()]
-                    right = weight[(here ^ second).bit_length()]
-                    if second > here or (here ^ first).bit_length() == (here ^ second).bit_length():
-                        factor = left
-                    else:
-                        factor = jnp.where(lane < stretch, left, right)
-                    tile = slice(j * TILE, (j + 1) * TILE)
-                    piece = scores[band, tile] * (behind[:, tile] * factor) * ahead
-                    if second >= here:
-                        piece = jnp.where(causal[here - first], piece, 0.0)
-                    pieces.append(piece.astype(BF16))
-                bands.append(jnp.concatenate(pieces, axis=1))
-                base = lifted_base[band, lanes]
-                lifted.append(
-                    jnp.concatenate(
-                        [(base * weight[5 + level]).astype(BF16) for level in range(2)], axis=1
-                    )
-                )
-            out[span, lanes] = jnp.dot(
-                jnp.concatenate(bands, axis=0), inner[:wide, lanes], preferred_element_type=F32
-            ) + jnp.dot(
-                jnp.concatenate(lifted, axis=0), held[head], preferred_element_type=F32
+
+        def emit(i, value):
+            out[i * WIDE : (i + 1) * WIDE, lanes] = value + lift(
+                table, kinds, lifted_base, head, i, levels, held
             )
+
+        mix_head(head, table, kinds, inner, running_in, step_in, scores, ahead_in, emit)
         return carry
 
-    lax.fori_loop(0, heads, one_head, 0, unroll=4)
-
-
-def local_part(table, kinds, inner, running, step, scores, lifted_base, ahead, near):
+    lax.fori_loop(len(mixed) * PAIR, heads, one_head, 0, unroll=2)
+
+
+def local_part(table, kinds, inner, running, step, scores, ahead, lifted_base, mixed, near):
     length, width = inner.shape
     heads = width // DIM
     return pl.pallas_call(
-        local_kernel,
-        in_specs=[SMEM, SMEM] + [VMEM] * (6 + XS),
+        functools.partial(local_kernel, len(mixed)),
+        in_specs=[SMEM, SMEM] + [VMEM] * (6 + len(mixed) + XS),
         out_specs=VMEM,
         out_shape=pltpu.VMEM((length, width), F32),
-        scratch_shapes=[pltpu.VMEM((heads, 2 * DIM, DIM), BF16)],
+        scratch_shapes=[pltpu.VMEM((heads, NEAR * DIM, DIM), BF16)],
         compiler_params=params(8),
-        cost_estimate=pl.CostEstimate(
-            flops=8 * length * length * DIM, bytes_accessed=8 * 2**20, transcendentals=2**18
-        ),
+        cost_estimate=cost(3.8),
         name="local_part",
-    )(table, kinds, inner, running, step, scores, lifted_base, ahead, *near)
-
-
-def fold_row_kernel(p0, p1, p2, p3, row_out, m0, m1, m2, m3):
+    )(table, kinds, inner, running, step, scores, ahead, lifted_base, *mixed, *near)
+
+
+def fold_row_kernel(p0, p1, p2, p3, row_out):
     x, _ = block_place()
     parts = (p0, p1, p2, p3)
     owner = [lax.rem(x + XS - k, XS) for k in range(XS)]
     decays = [decode_decay(part) for part in parts]
+    later = [
+        jnp.exp(sum(decays[m] * flag(owner[m] > owner[k]) for m in range(XS)))
+        * decode_size(parts[k])
+        for k in range(XS)
+    ]
+    total = sum(decays)
+    states = []
+    for head in range(PAIR):
+        span = slice(head * DIM, (head + 1) * DIM)
+        states.append(sum(parts[k][span] * later[k][head : head + 1] for k in range(XS)))
+    encode(row_out, states, [total[head : head + 1] for head in range(PAIR)])
+
+
+def fold_row(parts):
+    return pl.pallas_call(
+        fold_row_kernel,
+        in_specs=[VMEM] * XS,
+        out_specs=VMEM,
+        out_shape=pltpu.VMEM((MESSAGE, DIM), F32),
+        compiler_params=params(4),
+        cost_estimate=cost(0.25),
+        name="fold_row",
+    )(*parts)
+
+
+def fold_near_kernel(p0, p1, p2, p3, row_before, m0, m1, m2, m3):
+    x, z = block_place()
+    parts = (p0, p1, p2, p3)
+    owner = [lax.rem(x + XS - k, XS) for k in range(XS)]
+    decays = [decode_decay(part) for part in parts]
     sizes = [decode_size(part) for part in parts]
+    odd_size = decode_size(row_before) * flag(lax.rem(z, 2) == 1)
 
     def pick(values, block):
         return sum(value * flag(owner[k] == block) for k, value in enumerate(values))
 
-    later = [
-        jnp.exp(sum(decays[m] * flag(owner[m] > owner[k]) for m in range(XS))) * sizes[k]
-        for k in range(XS)
-    ]
     decay_one = jnp.exp(pick(decays, 1))
     decay_two = jnp.exp(pick(decays, 2))
-    total = sum(decays)
-    row_states = []
     for head in range(PAIR):
         span = slice(head * DIM, (head + 1) * DIM)
         row = slice(head, head + 1)
-        blocks = [part[span] for part in parts]
-        row_states.append(sum(blocks[k] * later[k][row] for k in range(XS)))
-        scaled = [blocks[k] * sizes[k][row] for k in range(XS)]
+        scaled = [parts[k][span] * sizes[k][row] for k in range(XS)]
         first = pick(scaled, 0)
         third = pick(scaled, 2)
         joined = first * decay_one[row] + pick(scaled, 1)
+        above = row_before[span]
         for k, message in enumerate((m0, m1, m2, m3)):
             target = lax.rem(x + k, XS)
-            message[span] = (
-                first * flag(target == 1) + third * flag(target == 3)
-            ).astype(BF16)
-            message[PAIR * DIM + head * DIM : PAIR * DIM + (head + 1) * DIM] = (
-                joined * (flag(target == 2) + flag(target == 3) * decay_two[row])
-            ).astype(BF16)
-    encode(row_out, row_states, [total[head : head + 1] for head in range(PAIR)])
-
-
-def fold_row(parts):
-    return pl.pallas_call(
-        fold_row_kernel,
-        in_specs=[VMEM] * XS,
-        out_specs=[VMEM] * (1 + XS),
-        out_shape=[pltpu.VMEM((MESSAGE, DIM), F32)] + [pltpu.VMEM((4 * DIM, DIM), BF16)] * XS,
+            before = sum(decays[m][row] * flag(owner[m] < target) for m in range(XS))
+            levels = (
+                first * flag(target == 1) + third * flag(target == 3),
+                joined * (flag(target == 2) + flag(target == 3) * decay_two[row]),
+                above * (jnp.exp(before) * odd_size[row]),
+            )
+            for level, value in enumerate(levels):
+                base = (level * PAIR + head) * DIM
+                message[base : base + DIM] = value.astype(BF16)
+
+
+def fold_near(parts, row_before):
+    return pl.pallas_call(
+        fold_near_kernel,
+        in_specs=[VMEM] * (XS + 1),
+        out_specs=[VMEM] * XS,
+        out_shape=[pltpu.VMEM((NEAR * PAIR * DIM, DIM), BF16)] * XS,
         compiler_params=params(4),
-        cost_estimate=pl.CostEstimate(flops=2**20, bytes_accessed=2**20, transcendentals=2**10),
-        name="fold_row",
-    )(*parts)
+        cost_estimate=cost(0.3),
+        name="fold_near",
+    )(*parts, row_before)
 
 
 def fold_two_kernel(span_rows, own, other, out):
@@ -592,7 +691,7 @@
         out_specs=VMEM,
         out_shape=pltpu.VMEM((MESSAGE, DIM), F32),
         compiler_params=params(4),
-        cost_estimate=pl.CostEstimate(flops=2**18, bytes_accessed=2**19, transcendentals=2**10),
+        cost_estimate=cost(0.2),
         name="fold_two",
     )(own, other)
 
@@ -607,7 +706,6 @@
     in_pair = decode_decay(row_before) * odd
     in_quad = in_pair + decode_decay(pair_before) * odd_pair
     levels = (
-        (row_before, jnp.zeros_like(in_pair), decode_size(row_before) * odd),
         (pair_before, in_pair, decode_size(pair_before) * odd_pair),
         (quad_before, in_quad, decode_size(quad_before) * upper),
     )
@@ -628,9 +726,9 @@
         fold_far_kernel,
         in_specs=[VMEM] * (XS + 3),
         out_specs=[VMEM] * XS,
-        out_shape=[pltpu.VMEM((6 * DIM, DIM), BF16)] * XS,
+        out_shape=[pltpu.VMEM((FAR * PAIR * DIM, DIM), BF16)] * XS,
         compiler_params=params(4),
-        cost_estimate=pl.CostEstimate(flops=2**20, bytes_accessed=2**20, transcendentals=2**12),
+        cost_estimate=cost(0.25),
         name="fold_far",
     )(*parts, *befores)
 
@@ -644,32 +742,19 @@
     for k, far in enumerate((f0, f1, f2, f3)):
         pair = lax.rem(x + XS - k, XS)
         for head in range(PAIR):
-            for level in range(3):
+            for level in range(FAR):
                 base = (level * PAIR + head) * DIM
                 held[pair * PAIR + head, level * DIM : (level + 1) * DIM] = far[base : base + DIM]
     total[...] = jnp.zeros_like(total)
 
-    stretch = length // kinds.shape[0]
+    levels = range(5 + NEAR, 5 + NEAR + FAR)
 
     def one_head(head, carry):
         lanes = pl.ds(pl.multiple_of(head * DIM, DIM), DIM)
         for tile in range(length // WIDE):
             span = slice(tile * WIDE, (tile + 1) * WIDE)
-            lifted = []
-            for here in range(tile * WIDE // stretch, (tile + 1) * WIDE // stretch):
-                kind = kinds[here]
-                base = lifted_base[here * stretch : (here + 1) * stretch, lanes]
-                lifted.append(
-                    jnp.concatenate(
-                        [
-                            (base * table[kind, head, 7 + level]).astype(BF16)
-                            for level in range(3)
-                        ],
-                        axis=1,
-                    )
-                )
-            mixed = local[span, lanes] + jnp.dot(
-                jnp.concatenate(lifted, axis=0), held[head], preferred_element_type=F32
+            mixed = local[span, lanes] + lift(
+                table, kinds, lifted_base, head, tile, levels, held
             )
             value = mixed * gates[span, lanes]
             gated[span, lanes] = value
@@ -690,11 +775,9 @@
         in_specs=[SMEM, SMEM] + [VMEM] * (3 + XS),
         out_specs=[VMEM] * 2,
         out_shape=[pltpu.VMEM((length, width), F32), pltpu.VMEM((length // TILE, TILE), F32)],
-        scratch_shapes=[pltpu.VMEM((heads, 3 * DIM, DIM), BF16), pltpu.VMEM((length, DIM), F32)],
+        scratch_shapes=[pltpu.VMEM((heads, FAR * DIM, DIM), BF16), pltpu.VMEM((length, DIM), F32)],
         compiler_params=params(8),
-        cost_estimate=pl.CostEstimate(
-            flops=6 * length * width * DIM, bytes_accessed=12 * 2**20, transcendentals=0
-        ),
+        cost_estimate=cost(3.5),
         name="far_part",
     )(table, kinds, local, gates, lifted_base, *far_states)
 
@@ -724,9 +807,7 @@
         out_shape=jax.ShapeDtypeStruct((length, width), BF16),
         scratch_shapes=[pltpu.VMEM((length, width), BF16), DMA((length // TILE,))],
         compiler_params=params(8),
-        cost_estimate=pl.CostEstimate(
-            flops=2 * length * width, bytes_accessed=6 * 2**20, transcendentals=2**10
-        ),
+        cost_estimate=cost(1.6),
         name="norm",
     )(gated, *squares, gain)
 
@@ -758,17 +839,42 @@
     shared = shared_part(rows, running, gate_input)
     arrived, shared = lax.optimization_barrier((arrived, shared))
     scores, gates, lifted_base, ahead = shared
-    row_state, *near = fold_row(arrived)
+    mix = functools.partial(
+        mix_part,
+        table=table,
+        kinds=stretch_kind,
+        inner=inner,
+        running=running,
+        step=step,
+        scores=scores,
+        ahead=ahead,
+    )
+    row_state = fold_row(arrived)
+    row_before = sent(row_state, lambda z, x: (z ^ 1, x))
+    row_before, mixed_first = lax.optimization_barrier((row_before, mix(0)))
+    pair_state = fold_two(1, row_state, row_before)
+    near = fold_near(arrived, row_before)
+    pair_before = sent(pair_state, lambda z, x: (z ^ 2, x))
     near = [near[0]] + [along_x(near[k], k) for k in range(1, XS)]
-    row_before = sent(row_state, lambda z, x: (z ^ 1, x))
-    pair_state = fold_two(1, row_state, row_before)
-    pair_before = sent(pair_state, lambda z, x: (z ^ 2, x))
     quad_state = fold_two(2, pair_state, pair_before)
+    quad_state, step_late = lax.optimization_barrier((quad_state, step))
     quad_before = sent(quad_state, lambda z, x: (ZS - 1 - z, x) if z < ZS // 2 else None)
+    quad_before, mixed_second, mixed_third = lax.optimization_barrier(
+        (quad_before, mix(PAIR, step=step_late), mix(2 * PAIR, step=step_late))
+    )
     far = fold_far(arrived, (row_before, pair_before, quad_before))
     far = [far[0]] + [along_x(far[k], k) for k in range(1, XS)]
     local_out = local_part(
-        table, stretch_kind, inner, running, step, scores, lifted_base, ahead, near
+        table,
+        stretch_kind,
+        inner,
+        running,
+        step,
+        scores,
+        ahead,
+        lifted_base,
+        (mixed_first, mixed_second, mixed_third),
+        near,
     )
     gated, squares = far_part(table, stretch_kind, local_out, gates, lifted_base, far)
     squares = squares + lax.ppermute(squares, "head", head_perm(lambda y, core: (y, 1 - core)))

time: 70.6 us -> 67.3 us (0.953)
  starting transfers between devices: 34.9 us -> 30.2 us
  Pallas kernels: 24 us -> 27.5 us
  waiting for transfers between devices: 10.9 us -> 8.83 us
    pallas_call x2 -> x6, Pallas kernels: 6.77 us -> 11.4 us  [the longest x3 7.19 us: mix_part(): pl.pallas_call(functools.partial(mix_kernel, first), in_specs=[SMEM, SMEM...]
    ppermute x6, starting transfers between devices: 16.7 us -> 12.6 us  [sent(): lax.ppermute(message.astype(jnp.float16), 'seq', seq_perm(move)).astype(F32)]
    ppermute x6, waiting for transfers between devices: 2.28 us -> 0.02 us  [along_x(): lax.ppermute(value, 'seq', seq_perm(lambda z, x: (z, (x + step) % XS)))]
    ppermute x3, waiting for transfers between devices: 2.26 us -> 3.86 us  [local(): lax.ppermute(squares, 'head', head_perm(lambda y, core, k=k: ((y + k) % Y...]
    ppermute x6, waiting for transfers between devices: 5.21 us -> 3.8 us  [sent(): lax.ppermute(message.astype(jnp.float16), 'seq', seq_perm(move)).astype(F32)]
    ppermute x3, starting transfers between devices: 5.8 us -> 4.6 us  [local(): lax.ppermute(squares, 'head', head_perm(lambda y, core, k=k: ((y + k) % Y...]
  transfers between devices with their start and end apart: 17 -> 17, of which waited for: 6 -> 6; matrix products, arithmetic and copies ran while one was open for 0% -> 0% of each run, Pallas kernels for 23% -> 31%
where the time goes in v4:
time: 67.3 us; the launch traced here: 67.1 us
  starting transfers between devices  30.2 us (45%)
  Pallas kernels  27.5 us (41%)
  waiting for transfers between devices  8.83 us (13%)
    ppermute x6, starting transfers between devices, sent(): lax.ppermute(message.astype(jnp.float16), 'seq', seq_perm(move)).astype(F32)  12.6 us
    ppermute x6, starting transfers between devices, along_x(): lax.ppermute(value, 'seq', seq_perm(lambda z, x: (z, (x + step) % XS)))  9.52 us
    pallas_call x3, Pallas kernels, mix_part(): pl.pallas_call(functools.partial(mix_kernel, first), in_specs=[SMEM, SMEM...  7.19 us
    pallas_call x1, Pallas kernels, prepare(): pl.pallas_call(prepare_kernel, in_specs=[HBM] * 6, out_specs=[VMEM] * (8...  5.65 us
    ppermute x3, starting transfers between devices, local(): lax.ppermute(squares, 'head', head_perm(lambda y, core, k=k: ((y + k) % Y...  4.6 us
    ppermute x3, waiting for transfers between devices, local(): lax.ppermute(squares, 'head', head_perm(lambda y, core, k=k: ((y + k) % Y...  3.86 us
    ppermute x6, waiting for transfers between devices, sent(): lax.ppermute(message.astype(jnp.float16), 'seq', seq_perm(move)).astype(F32)  3.8 us
    pallas_call x1, Pallas kernels, local_part(): pl.pallas_call(functools.partial(local_kernel, len(mixed)), in_specs=[SME...  3.79 us
  transfers between devices with their start and end apart: 17, of which 6 were waited for; matrix products, arithmetic and copies ran while one was open for 0% of the time, Pallas kernels for 31%

profile of v4, /device:TPU:32, one launch (start us, length us, event | category | flops | bytes accessed | tf_op | source)
XLA Modules:
  0.0 67.1 jit_solution(3020456959644653129)
XLA Ops:
  0.8 3.4 %collective-permute-start = (bf16[16,1280]{1,0:T(8,128)(2,1)S(1)}, bf16[16,1280]{1,0:T(8,128)(2,1)S(1)}, u32[]{:S(2)}, u32[]{:S(2)}) collective-permute-start(bf16[16,1280]{1,0:T(8,128)(2,1)S(1)} %last_rows.1), channel_id=1, source_target_pairs={{0,8},{8,16},{16,24},{24,32},{32,40},{40,48},{48,56},{56,64},{64,7... | collective-permute-start | bytes 122888 | tf_op jit(solution)/shard_map/ppermute | solution.py:828
  4.2 5.7 %prepare.1 = (bf16[1024,1024]{1,0:T(8,128)(2,1)S(1)}, bf16[1024,256]{1,0:T(8,128)(2,1)S(1)}, f32[8,1024]{1,0:T(8,128)S(1)}, f32[8,1024]{1,0:T(8,128)S(1)}, bf16[...) custom-call(bf16[1024,1024]{1,0:T(8,128)(2,1)} %mixer.3, ...), custom_call_target="tpu_custom_call" | custom-call | flops 6554999808 | bytes 20520000 | tf_op jit(solution)/shard_map/prepare/pallas_call | solution.py:264
  10.7 3.2 %collective-permute-start.3 = (f16[264,128]{1,0:T(8,128)(2,1)S(1)}, f16[264,128]{1,0:T(8,128)(2,1)S(1)}, u32[]{:S(2)}, u32[]{:S(2)}) collective-permute-start(f16[264,128]{1,0:T(8,128)(2,1)S(1)} %convert_element_type.40), channel_id=1, source_target_pairs={{0,24},{8,0},{16,8},{24,16},{32,56},{40,32},{48,40},{56,48},{64,88... | collective-permute-start | bytes 202760 | tf_op jit(solution)/shard_map/ppermute | solution.py:51
  14.9 3.4 %shared_part.1 = (f32[1024,1024]{1,0:T(8,128)S(1)}, f32[1024,1024]{1,0:T(8,128)S(1)}, f32[1024,1024]{1,0:T(8,128)S(1)}, f32[1024,1024]{1,0:T(8,128)S(1)}) custom-call(bf16[1024,256]{1,0:T(8,128)(2,1)S(1)} %get-tuple-element.69.rows, f32[8,1024]{1,0:T(8,128)S(1)} %get-tuple-element.63.running_in, bf16[1024,1024]{1,0:T(8,128)(2,1)} %gate.1), custom_call_target="tpu_custom_call" | custom-call | flops 3910000128 | bytes 12240000 | tf_op jit(solution)/shard_map/shared_part/pallas_call | solution.py:425
  18.3 1.4 %collective-permute-done.2 = f16[264,128]{1,0:T(8,128)(2,1)S(1)} collective-permute-done((f16[264,128]{1,0:T(8,128)(2,1)S(1)}, f16[264,128]{1,0:T(8,128)(2,1)S(1)}, u32[]{:S(2)}, u32[]{:S(2)}) %collective-permute-start.2) | collective-permute-done | bytes 67616 | tf_op jit(solution)/shard_map/ppermute | solution.py:51
  20.8 2.4 %mix_part.3.rest_0_ = f32[1024,256]{1,0:T(8,128)S(1)} custom-call(f32[8,8,13]{2,1,0:T(8,128)S(1)} %bitcast.3, s32[16]{0:T(128)S(1)} %copy-done.1, bf16[1024,1024]{1,0:T(8,128)(2,1)S(1)} %get-tuple-element.62.inner, f32[8,1024]{1,0:T(8,128)S(1)} %get-tuple-element.63.running_in, f32[8,1024]{1,0:T(8,128)S(1)} %get-tuple-element.84.step_in, ...), custom_call_target="tpu_custom_call" | custom-call | flops 2760000000 | bytes 8640000 | tf_op jit(solution)/shard_map/mix_part/pallas_call | solution.py:519
  23.2 1.8 %collective-permute-done.4 = f16[264,128]{1,0:T(8,128)(2,1)S(1)} collective-permute-done((f16[264,128]{1,0:T(8,128)(2,1)S(1)}, f16[264,128]{1,0:T(8,128)(2,1)S(1)}, u32[]{:S(2)}, u32[]{:S(2)}) %collective-permute-start.4) | collective-permute-done | bytes 67616 | tf_op jit(solution)/shard_map/ppermute | solution.py:51
  25.2 4.3 %collective-permute-start.5 = (f16[264,128]{1,0:T(8,128)(2,1)S(1)}, f16[264,128]{1,0:T(8,128)(2,1)S(1)}, u32[]{:S(2)}, u32[]{:S(2)}) collective-permute-start(f16[264,128]{1,0:T(8,128)(2,1)S(1)} %convert_element_type.44), channel_id=1, source_target_pairs={{0,64},{8,72},{16,80},{24,88},{32,96},{40,104},{48,112},{56,120},{... | collective-permute-start | bytes 202760 | tf_op jit(solution)/shard_map/ppermute | solution.py:51
  29.7 0.8 %collective-permute-start.7 = (bf16[768,128]{1,0:T(8,128)(2,1)S(1)}, bf16[768,128]{1,0:T(8,128)(2,1)S(1)}, u32[]{:S(2)}, u32[]{:S(2)}) collective-permute-start(bf16[768,128]{1,0:T(8,128)(2,1)S(1)} %get-tuple-element.88), channel_id=1, source_target_pairs={{0,8},{8,16},{16,24},{24,0},{32,40},{40,48},{48,56},{56,32},{64,72... | collective-permute-start | bytes 589832 | tf_op jit(solution)/shard_map/ppermute | solution.py:47
  30.5 1.6 %collective-permute-start.8 = (bf16[768,128]{1,0:T(8,128)(2,1)S(1)}, bf16[768,128]{1,0:T(8,128)(2,1)S(1)}, u32[]{:S(2)}, u32[]{:S(2)}) collective-permute-start(bf16[768,128]{1,0:T(8,128)(2,1)S(1)} %get-tuple-element.89), channel_id=1, source_target_pairs={{0,16},{8,24},{16,0},{24,8},{32,48},{40,56},{48,32},{56,40},{64,80... | collective-permute-start | bytes 589832 | tf_op jit(solution)/shard_map/ppermute | solution.py:47
  32.1 1.9 %collective-permute-start.9 = (bf16[768,128]{1,0:T(8,128)(2,1)S(1)}, bf16[768,128]{1,0:T(8,128)(2,1)S(1)}, u32[]{:S(2)}, u32[]{:S(2)}) collective-permute-start(bf16[768,128]{1,0:T(8,128)(2,1)S(1)} %get-tuple-element.90), channel_id=1, source_target_pairs={{0,24},{8,0},{16,8},{24,16},{32,56},{40,32},{48,40},{56,48},{64,88... | collective-permute-start | bytes 589832 | tf_op jit(solution)/shard_map/ppermute | solution.py:47
  34.2 3.9 %collective-permute-start.6 = (f16[264,128]{1,0:T(8,128)(2,1)S(1)}, f16[264,128]{1,0:T(8,128)(2,1)S(1)}, u32[]{:S(2)}, u32[]{:S(2)}) collective-permute-start(f16[264,128]{1,0:T(8,128)(2,1)S(1)} %convert_element_type.46), channel_id=1, source_target_pairs={{0,224},{8,232},{16,240},{24,248},{32,192},{40,200},{48,208},{56,2... | collective-permute-start | bytes 202760 | tf_op jit(solution)/shard_map/ppermute | solution.py:51
  38.1 2.4 %mix_part.5.rest_2_ = f32[1024,256]{1,0:T(8,128)S(1)} custom-call(f32[8,8,13]{2,1,0:T(8,128)S(1)} %bitcast.4, s32[16]{0:T(128)S(1)} %copy-done.1, bf16[1024,1024]{1,0:T(8,128)(2,1)S(1)} %get-tuple-element.62.inner, f32[8,1024]{1,0:T(8,128)S(1)} %get-tuple-element.63.running_in, f32[8,1024]{1,0:T(8,128)S(1)} %get-tuple-element.84.step_in, ...), custom_call_target="tpu_custom_call" | custom-call | flops 2760000000 | bytes 8640000 | tf_op jit(solution)/shard_map/mix_part/pallas_call | solution.py:519
  40.5 2.4 %mix_part.4.rest_1_ = f32[1024,256]{1,0:T(8,128)S(1)} custom-call(f32[8,8,13]{2,1,0:T(8,128)S(1)} %bitcast.5, s32[16]{0:T(128)S(1)} %copy-done.1, bf16[1024,1024]{1,0:T(8,128)(2,1)S(1)} %get-tuple-element.62.inner, f32[8,1024]{1,0:T(8,128)S(1)} %get-tuple-element.63.running_in, f32[8,1024]{1,0:T(8,128)S(1)} %get-tuple-element.84.step_in, ...), custom_call_target="tpu_custom_call" | custom-call | flops 2760000000 | bytes 8640000 | tf_op jit(solution)/shard_map/mix_part/pallas_call | solution.py:519
  43.1 1.2 %collective-permute-start.10 = (bf16[512,128]{1,0:T(8,128)(2,1)S(1)}, bf16[512,128]{1,0:T(8,128)(2,1)S(1)}, u32[]{:S(2)}, u32[]{:S(2)}) collective-permute-start(bf16[512,128]{1,0:T(8,128)(2,1)S(1)} %get-tuple-element.94), channel_id=1, source_target_pairs={{0,8},{8,16},{16,24},{24,0},{32,40},{40,48},{48,56},{56,32},{64,72... | collective-permute-start | bytes 393224 | tf_op jit(solution)/shard_map/ppermute | solution.py:47
  44.2 1.5 %collective-permute-start.11 = (bf16[512,128]{1,0:T(8,128)(2,1)S(1)}, bf16[512,128]{1,0:T(8,128)(2,1)S(1)}, u32[]{:S(2)}, u32[]{:S(2)}) collective-permute-start(bf16[512,128]{1,0:T(8,128)(2,1)S(1)} %get-tuple-element.95), channel_id=1, source_target_pairs={{0,16},{8,24},{16,0},{24,8},{32,48},{40,56},{48,32},{56,40},{64,80... | collective-permute-start | bytes 393224 | tf_op jit(solution)/shard_map/ppermute | solution.py:47
  45.8 2.5 %collective-permute-start.12 = (bf16[512,128]{1,0:T(8,128)(2,1)S(1)}, bf16[512,128]{1,0:T(8,128)(2,1)S(1)}, u32[]{:S(2)}, u32[]{:S(2)}) collective-permute-start(bf16[512,128]{1,0:T(8,128)(2,1)S(1)} %get-tuple-element.96), channel_id=1, source_target_pairs={{0,24},{8,0},{16,8},{24,16},{32,56},{40,32},{48,40},{56,48},{64,88... | collective-permute-start | bytes 393224 | tf_op jit(solution)/shard_map/ppermute | solution.py:47
  48.3 3.8 %local_part.1.local = f32[1024,1024]{1,0:T(8,128)S(1)} custom-call(f32[8,8,13]{2,1,0:T(8,128)S(1)} %bitcast.6, s32[16]{0:T(128)S(1)} %copy-done.1, bf16[1024,1024]{1,0:T(8,128)(2,1)S(1)} %get-tuple-element.62.inner, f32[8,1024]{1,0:T(8,128)S(1)} %get-tuple-element.63.running_in, f32[8,1024]{1,0:T(8,128)S(1)} %get-tuple-element.84.step_in, ...), custom_call_target="tpu_custom_call" | custom-call | flops 4369999872 | bytes 13680000 | tf_op jit(solution)/shard_map/local_part/pallas_call | solution.py:583
  52.1 3.5 %far_part.1 = (f32[1024,1024]{1,0:T(8,128)S(1)}, f32[8,128]{1,0:T(8,128)S(1)}) custom-call(f32[8,8,13]{2,1,0:T(8,128)S(1)} %bitcast.7, s32[16]{0:T(128)S(1)} %copy-done.1, f32[1024,1024]{1,0:T(8,128)S(1)} %local_part.1.local, f32[1024,1024]{1,0:T(8,128)S(1)} %get-tuple-element.91.gates, f32[1024,1024]{1,0:T(8,128)S(1)} %get-tuple-element.76.lifted_base, ...), custom_call_target="tpu_custom_call" | custom-call | flops 4024999936 | bytes 12600000 | tf_op jit(solution)/shard_map/far_part/pallas_call | solution.py:773
  55.8 1.2 %collective-permute-done.13 = f32[8,128]{1,0:T(8,128)S(1)} collective-permute-done((f32[8,128]{1,0:T(8,128)S(1)}, f32[8,128]{1,0:T(8,128)S(1)}, u32[]{:S(2)}, u32[]{:S(2)}) %collective-permute-start.13) | collective-permute-done | bytes 4128 | tf_op jit(solution)/shard_map/ppermute | solution.py:880
  56.9 3.0 %collective-permute-start.16 = (f32[8,128]{1,0:T(8,128)S(1)}, f32[8,128]{1,0:T(8,128)S(1)}, u32[]{:S(2)}, u32[]{:S(2)}) collective-permute-start(f32[8,128]{1,0:T(8,128)S(1)} %add.3.s0), channel_id=1, source_target_pairs={{0,6},{1,7},{2,0},{3,1},{4,2},{5,3},{6,4},{7,5},{8,14},{9,15},{10,... | collective-permute-start | bytes 12296 | tf_op jit(solution)/shard_map/ppermute | solution.py:882
  60.6 1.0 %collective-permute-start.14 = (f32[8,128]{1,0:T(8,128)S(1)}, f32[8,128]{1,0:T(8,128)S(1)}, u32[]{:S(2)}, u32[]{:S(2)}) collective-permute-start(f32[8,128]{1,0:T(8,128)S(1)} %add.3.s0), channel_id=1, source_target_pairs={{0,2},{1,3},{2,4},{3,5},{4,6},{5,7},{6,0},{7,1},{8,10},{9,11},{10,... | collective-permute-start | bytes 12296 | tf_op jit(solution)/shard_map/ppermute | solution.py:882
  61.5 3.5 %collective-permute-done.15.s2 = f32[8,128]{1,0:T(8,128)S(1)} collective-permute-done((f32[8,128]{1,0:T(8,128)S(1)}, f32[8,128]{1,0:T(8,128)S(1)}, u32[]{:S(2)}, u32[]{:S(2)}) %collective-permute-start.15) | collective-permute-done | bytes 4128 | tf_op jit(solution)/shard_map/ppermute | solution.py:882
  65.4 1.6 %norm.1 = bf16[1024,1024]{1,0:T(8,128)(2,1)} custom-call(f32[1024,1024]{1,0:T(8,128)S(1)} %get-tuple-element.97.gated, f32[8,128]{1,0:T(8,128)S(1)} %add.3.s0, f32[8,128]{1,0:T(8,128)S(1)} %collective-permute-done.14.s1, f32[8,128]{1,0:T(8,128)S(1)} %collective-permute-done.15.s2, f32[8,128]{1,0:T(8,128)S(1)} %collective-permute-done.16.s3, ...), custom_call_target="tpu_custom_call" | custom-call | flops 1840000000 | bytes 5760000 | tf_op jit(solution)/shard_map/norm/pallas_call | solution.py:803
  (44 shorter events, 5.5 us)
Async XLA Ops:
  0.8 9.1 %collective-permute-start = (bf16[16,1280]{1,0:T(8,128)(2,1)S(1)}, bf16[16,1280]{1,0:T(8,128)(2,1)S(1)}, u32[]{:S(2)}, u32[]{:S(2)}) collective-permute-start(bf16[16,1280]{1,0:T(8,128)(2,1)S(1)} %last_rows.1), channel_id=1, source_target_pairs={{0,8},{8,16},{16,24},{24,32},{32,40},{40,48},{48,56},{56,64},{64,7... | collective-permute-start | bytes 122888 | tf_op jit(solution)/shard_map/ppermute | solution.py:828
  10.7 7.7 %collective-permute-start.3 = (f16[264,128]{1,0:T(8,128)(2,1)S(1)}, f16[264,128]{1,0:T(8,128)(2,1)S(1)}, u32[]{:S(2)}, u32[]{:S(2)}) collective-permute-start(f16[264,128]{1,0:T(8,128)(2,1)S(1)} %convert_element_type.40), channel_id=1, source_target_pairs={{0,24},{8,0},{16,8},{24,16},{32,56},{40,32},{48,40},{56,48},{64,88... | collective-permute-start | bytes 202760 | tf_op jit(solution)/shard_map/ppermute | solution.py:51
  13.8 5.9 %collective-permute-start.2 = (f16[264,128]{1,0:T(8,128)(2,1)S(1)}, f16[264,128]{1,0:T(8,128)(2,1)S(1)}, u32[]{:S(2)}, u32[]{:S(2)}) collective-permute-start(f16[264,128]{1,0:T(8,128)(2,1)S(1)} %convert_element_type.38), channel_id=1, source_target_pairs={{0,16},{8,24},{16,0},{24,8},{32,48},{40,56},{48,32},{56,40},{64,80... | collective-permute-start | bytes 202760 | tf_op jit(solution)/shard_map/ppermute | solution.py:51
  14.3 6.1 %collective-permute-start.1 = (f16[264,128]{1,0:T(8,128)(2,1)S(1)}, f16[264,128]{1,0:T(8,128)(2,1)S(1)}, u32[]{:S(2)}, u32[]{:S(2)}) collective-permute-start(f16[264,128]{1,0:T(8,128)(2,1)S(1)} %convert_element_type.36), channel_id=1, source_target_pairs={{0,8},{8,16},{16,24},{24,0},{32,40},{40,48},{48,56},{56,32},{64,72... | collective-permute-start | bytes 202760 | tf_op jit(solution)/shard_map/ppermute | solution.py:51
  14.9 5.9 %copy-start = (f32[8,13,8]{1,2,0:T(8,128)S(1)}, f32[8,13,8]{1,2,0:T(8,128)}, u32[]{:S(2)}) copy-start(f32[8,13,8]{1,2,0:T(8,128)} %param.17) | copy-start | bytes 9988
  14.9 5.9 %copy-start.1 = (s32[16]{0:T(128)S(1)}, s32[16]{0:T(128)}, u32[]{:S(2)}) copy-start(s32[16]{0:T(128)} %kinds.9) | copy-start | bytes 196
  20.6 4.4 %collective-permute-start.4 = (f16[264,128]{1,0:T(8,128)(2,1)S(1)}, f16[264,128]{1,0:T(8,128)(2,1)S(1)}, u32[]{:S(2)}, u32[]{:S(2)}) collective-permute-start(f16[264,128]{1,0:T(8,128)(2,1)S(1)} %convert_element_type.42), channel_id=1, source_target_pairs={{0,32},{8,40},{16,48},{24,56},{32,0},{40,8},{48,16},{56,24},{64,96... | collective-permute-start | bytes 202760 | tf_op jit(solution)/shard_map/ppermute | solution.py:51
  25.2 8.9 %collective-permute-start.5 = (f16[264,128]{1,0:T(8,128)(2,1)S(1)}, f16[264,128]{1,0:T(8,128)(2,1)S(1)}, u32[]{:S(2)}, u32[]{:S(2)}) collective-permute-start(f16[264,128]{1,0:T(8,128)(2,1)S(1)} %convert_element_type.44), channel_id=1, source_target_pairs={{0,64},{8,72},{16,80},{24,88},{32,96},{40,104},{48,112},{56,120},{... | collective-permute-start | bytes 202760 | tf_op jit(solution)/shard_map/ppermute | solution.py:51
  29.7 16.1 %collective-permute-start.7 = (bf16[768,128]{1,0:T(8,128)(2,1)S(1)}, bf16[768,128]{1,0:T(8,128)(2,1)S(1)}, u32[]{:S(2)}, u32[]{:S(2)}) collective-permute-start(bf16[768,128]{1,0:T(8,128)(2,1)S(1)} %get-tuple-element.88), channel_id=1, source_target_pairs={{0,8},{8,16},{16,24},{24,0},{32,40},{40,48},{48,56},{56,32},{64,72... | collective-permute-start | bytes 589832 | tf_op jit(solution)/shard_map/ppermute | solution.py:47
  30.5 17.8 %collective-permute-start.8 = (bf16[768,128]{1,0:T(8,128)(2,1)S(1)}, bf16[768,128]{1,0:T(8,128)(2,1)S(1)}, u32[]{:S(2)}, u32[]{:S(2)}) collective-permute-start(bf16[768,128]{1,0:T(8,128)(2,1)S(1)} %get-tuple-element.89), channel_id=1, source_target_pairs={{0,16},{8,24},{16,0},{24,8},{32,48},{40,56},{48,32},{56,40},{64,80... | collective-permute-start | bytes 589832 | tf_op jit(solution)/shard_map/ppermute | solution.py:47
  32.1 16.2 %collective-permute-start.9 = (bf16[768,128]{1,0:T(8,128)(2,1)S(1)}, bf16[768,128]{1,0:T(8,128)(2,1)S(1)}, u32[]{:S(2)}, u32[]{:S(2)}) collective-permute-start(bf16[768,128]{1,0:T(8,128)(2,1)S(1)} %get-tuple-element.90), channel_id=1, source_target_pairs={{0,24},{8,0},{16,8},{24,16},{32,56},{40,32},{48,40},{56,48},{64,88... | collective-permute-start | bytes 589832 | tf_op jit(solution)/shard_map/ppermute | solution.py:47
  34.2 8.7 %collective-permute-start.6 = (f16[264,128]{1,0:T(8,128)(2,1)S(1)}, f16[264,128]{1,0:T(8,128)(2,1)S(1)}, u32[]{:S(2)}, u32[]{:S(2)}) collective-permute-start(f16[264,128]{1,0:T(8,128)(2,1)S(1)} %convert_element_type.46), channel_id=1, source_target_pairs={{0,224},{8,232},{16,240},{24,248},{32,192},{40,200},{48,208},{56,2... | collective-permute-start | bytes 202760 | tf_op jit(solution)/shard_map/ppermute | solution.py:51
  43.1 9.0 %collective-permute-start.10 = (bf16[512,128]{1,0:T(8,128)(2,1)S(1)}, bf16[512,128]{1,0:T(8,128)(2,1)S(1)}, u32[]{:S(2)}, u32[]{:S(2)}) collective-permute-start(bf16[512,128]{1,0:T(8,128)(2,1)S(1)} %get-tuple-element.94), channel_id=1, source_target_pairs={{0,8},{8,16},{16,24},{24,0},{32,40},{40,48},{48,56},{56,32},{64,72... | collective-permute-start | bytes 393224 | tf_op jit(solution)/shard_map/ppermute | solution.py:47
  44.2 7.9 %collective-permute-start.11 = (bf16[512,128]{1,0:T(8,128)(2,1)S(1)}, bf16[512,128]{1,0:T(8,128)(2,1)S(1)}, u32[]{:S(2)}, u32[]{:S(2)}) collective-permute-start(bf16[512,128]{1,0:T(8,128)(2,1)S(1)} %get-tuple-element.95), channel_id=1, source_target_pairs={{0,16},{8,24},{16,0},{24,8},{32,48},{40,56},{48,32},{56,40},{64,80... | collective-permute-start | bytes 393224 | tf_op jit(solution)/shard_map/ppermute | solution.py:47
  45.8 6.4 %collective-permute-start.12 = (bf16[512,128]{1,0:T(8,128)(2,1)S(1)}, bf16[512,128]{1,0:T(8,128)(2,1)S(1)}, u32[]{:S(2)}, u32[]{:S(2)}) collective-permute-start(bf16[512,128]{1,0:T(8,128)(2,1)S(1)} %get-tuple-element.96), channel_id=1, source_target_pairs={{0,24},{8,0},{16,8},{24,16},{32,56},{40,32},{48,40},{56,48},{64,88... | collective-permute-start | bytes 393224 | tf_op jit(solution)/shard_map/ppermute | solution.py:47
  52.1 13.3 %copy-start.2 = (f32[1024]{0:T(1024)S(1)}, f32[1024]{0:T(1024)}, u32[]{:S(2)}) copy-start(f32[1024]{0:T(1024)} %param.19) | copy-start | bytes 12292
  55.7 1.3 %collective-permute-start.13 = (f32[8,128]{1,0:T(8,128)S(1)}, f32[8,128]{1,0:T(8,128)S(1)}, u32[]{:S(2)}, u32[]{:S(2)}) collective-permute-start(f32[8,128]{1,0:T(8,128)S(1)} %get-tuple-element.98), channel_id=1, source_target_pairs={{0,1},{1,0},{2,3},{3,2},{4,5},{5,4},{6,7},{7,6},{8,9},{9,8},{10,11... | collective-permute-start | bytes 12296 | tf_op jit(solution)/shard_map/ppermute | solution.py:880
  56.9 4.6 %collective-permute-start.16 = (f32[8,128]{1,0:T(8,128)S(1)}, f32[8,128]{1,0:T(8,128)S(1)}, u32[]{:S(2)}, u32[]{:S(2)}) collective-permute-start(f32[8,128]{1,0:T(8,128)S(1)} %add.3.s0), channel_id=1, source_target_pairs={{0,6},{1,7},{2,0},{3,1},{4,2},{5,3},{6,4},{7,5},{8,14},{9,15},{10,... | collective-permute-start | bytes 12296 | tf_op jit(solution)/shard_map/ppermute | solution.py:882
  59.9 5.1 %collective-permute-start.15 = (f32[8,128]{1,0:T(8,128)S(1)}, f32[8,128]{1,0:T(8,128)S(1)}, u32[]{:S(2)}, u32[]{:S(2)}) collective-permute-start(f32[8,128]{1,0:T(8,128)S(1)} %add.3.s0), channel_id=1, source_target_pairs={{0,4},{1,5},{2,6},{3,7},{4,0},{5,1},{6,2},{7,3},{8,12},{9,13},{10,... | collective-permute-start | bytes 12296 | tf_op jit(solution)/shard_map/ppermute | solution.py:882
  60.6 4.8 %collective-permute-start.14 = (f32[8,128]{1,0:T(8,128)S(1)}, f32[8,128]{1,0:T(8,128)S(1)}, u32[]{:S(2)}, u32[]{:S(2)}) collective-permute-start(f32[8,128]{1,0:T(8,128)S(1)} %add.3.s0), channel_id=1, source_target_pairs={{0,2},{1,3},{2,4},{3,5},{4,6},{5,7},{6,0},{7,1},{8,10},{9,11},{10,... | collective-permute-start | bytes 12296 | tf_op jit(solution)/shard_map/ppermute | solution.py:882

commit v5 on v4

--- a/solution.py
+++ b/solution.py
@@ -51,9 +51,12 @@
     return lax.ppermute(message.astype(jnp.float16), "seq", seq_perm(move)).astype(F32)
 
 
+def silu_of_twice(half):
+    return half + half * jnp.tanh(half)
+
+
 def silu(value):
-    half = 0.5 * value
-    return half + half * jnp.tanh(half)
+    return silu_of_twice(0.5 * value)
 
 
 VMEM = pl.BlockSpec(memory_space=pltpu.VMEM)
@@ -86,7 +89,7 @@
 def conv(block, halo, taps, pad):
     length, width = block.shape
     count = taps.shape[0]
-    taps = taps.astype(F32)
+    taps = 0.5 * taps.astype(F32)
     columns = []
     for lane in range(width // DIM):
         lanes = slice(lane * DIM, (lane + 1) * DIM)
@@ -99,7 +102,7 @@
             for offset in range(count):
                 first = base + 9 - count + offset
                 total = total + pad[lane, first : first + size] * taps[offset : offset + 1, lanes]
-            made.append(silu(total).astype(BF16))
+            made.append(silu_of_twice(total).astype(BF16))
         columns.append(jnp.concatenate(made, axis=0))
     return jnp.concatenate(columns, axis=1)
 
@@ -483,7 +486,7 @@
         )
 
 
-def lift(table, kinds, lifted_base, head, tile, levels, held):
+def lift(table, kinds, lifted_base, head, tile, levels, held, WIDE=WIDE):
     length = lifted_base.shape[0]
     stretch = length // kinds.shape[0]
     lanes = pl.ds(pl.multiple_of(head * DIM, DIM), DIM)
@@ -499,7 +502,7 @@
     return jnp.dot(jnp.concatenate(bands, axis=0), held[head], preferred_element_type=F32)
 
 
-def mix_kernel(first, table, kinds, inner, running_in, step_in, scores, ahead_in, out):
+def mix_kernel(first, count, table, kinds, inner, running_in, step_in, scores, ahead_in, out):
     def one_head(offset, carry):
         lanes = pl.ds(pl.multiple_of(offset * DIM, DIM), DIM)
 
@@ -511,18 +514,18 @@
         )
         return carry
 
-    lax.fori_loop(0, PAIR, one_head, 0)
-
-
-def mix_part(first, table, kinds, inner, running, step, scores, ahead):
+    lax.fori_loop(0, count, one_head, 0, unroll=True)
+
+
+def mix_part(first, count, table, kinds, inner, running, step, scores, ahead):
     length, width = inner.shape
     return pl.pallas_call(
-        functools.partial(mix_kernel, first),
+        functools.partial(mix_kernel, first, count),
         in_specs=[SMEM, SMEM] + [VMEM] * 5,
         out_specs=VMEM,
-        out_shape=pltpu.VMEM((length, PAIR * DIM), F32),
+        out_shape=pltpu.VMEM((length, count * DIM), F32),
         compiler_params=params(8),
-        cost_estimate=cost(2.4),
+        cost_estimate=cost(0.75 * count + 0.5),
         name="mix_part",
     )(table, kinds, inner, running, step, scores, ahead)
 
@@ -554,14 +557,15 @@
                     base : base + DIM
                 ]
     levels = range(5, 5 + NEAR)
-    for group, value in enumerate(mixed):
-        for offset in range(PAIR):
-            head = group * PAIR + offset
+    head = 0
+    for value in mixed:
+        for offset in range(value.shape[1] // DIM):
             for tile in range(length // WIDE):
                 span = slice(tile * WIDE, (tile + 1) * WIDE)
                 out[span, head * DIM : (head + 1) * DIM] = value[
                     span, offset * DIM : (offset + 1) * DIM
                 ] + lift(table, kinds, lifted_base, head, tile, levels, held)
+            head += 1
 
     def one_head(head, carry):
         lanes = pl.ds(pl.multiple_of(head * DIM, DIM), DIM)
@@ -574,7 +578,7 @@
         mix_head(head, table, kinds, inner, running_in, step_in, scores, ahead_in, emit)
         return carry
 
-    lax.fori_loop(len(mixed) * PAIR, heads, one_head, 0, unroll=2)
+    lax.fori_loop(head, heads, one_head, 0, unroll=2)
 
 
 def local_part(table, kinds, inner, running, step, scores, ahead, lifted_base, mixed, near):
@@ -745,23 +749,21 @@
             for level in range(FAR):
                 base = (level * PAIR + head) * DIM
                 held[pair * PAIR + head, level * DIM : (level + 1) * DIM] = far[base : base + DIM]
-    total[...] = jnp.zeros_like(total)
-
     levels = range(5 + NEAR, 5 + NEAR + FAR)
-
-    def one_head(head, carry):
-        lanes = pl.ds(pl.multiple_of(head * DIM, DIM), DIM)
-        for tile in range(length // WIDE):
-            span = slice(tile * WIDE, (tile + 1) * WIDE)
-            mixed = local[span, lanes] + lift(
-                table, kinds, lifted_base, head, tile, levels, held
+    for pair in range(heads // 2):
+        values = []
+        for head in (2 * pair, 2 * pair + 1):
+            lanes = slice(head * DIM, (head + 1) * DIM)
+            mixed = local[:, lanes] + lift(
+                table, kinds, lifted_base, head, 0, levels, held, length
             )
-            value = mixed * gates[span, lanes]
-            gated[span, lanes] = value
-            total[span] += value * value
-        return carry
-
-    lax.fori_loop(0, heads, one_head, 0, unroll=4)
+            value = mixed * gates[:, lanes]
+            gated[:, lanes] = value
+            values.append(value * value)
+        if pair == 0:
+            total[...] = values[0] + values[1]
+        else:
+            total[...] += values[0] + values[1]
     for tile in range(length // TILE):
         part = total[tile * TILE : (tile + 1) * TILE].T
         squares[tile : tile + 1] = jnp.sum(part, axis=0, keepdims=True)
@@ -851,7 +853,7 @@
     )
     row_state = fold_row(arrived)
     row_before = sent(row_state, lambda z, x: (z ^ 1, x))
-    row_before, mixed_first = lax.optimization_barrier((row_before, mix(0)))
+    row_before, mixed_first = lax.optimization_barrier((row_before, mix(0, PAIR)))
     pair_state = fold_two(1, row_state, row_before)
     near = fold_near(arrived, row_before)
     pair_before = sent(pair_state, lambda z, x: (z ^ 2, x))
@@ -859,8 +861,8 @@
     quad_state = fold_two(2, pair_state, pair_before)
     quad_state, step_late = lax.optimization_barrier((quad_state, step))
     quad_before = sent(quad_state, lambda z, x: (ZS - 1 - z, x) if z < ZS // 2 else None)
-    quad_before, mixed_second, mixed_third = lax.optimization_barrier(
-        (quad_before, mix(PAIR, step=step_late), mix(2 * PAIR, step=step_late))
+    quad_before, mixed_second = lax.optimization_barrier(
+        (quad_before, mix(PAIR, 2 * PAIR, step=step_late))
     )
     far = fold_far(arrived, (row_before, pair_before, quad_before))
     far = [far[0]] + [along_x(far[k], k) for k in range(1, XS)]
@@ -873,7 +875,7 @@
         scores,
         ahead,
         lifted_base,
-        (mixed_first, mixed_second, mixed_third),
+        (mixed_first, mixed_second),
         near,
     )
     gated, squares = far_part(table, stretch_kind, local_out, gates, lifted_base, far)

time: 67.3 us -> 64.3 us (0.955)
  Pallas kernels: 27.5 us -> 24.3 us
    pallas_call x3 -> x2, Pallas kernels: 7.19 us -> 5.12 us  [mix_part(): pl.pallas_call(functools.partial(mix_kernel, first, count), in_specs=[SME...]
    pallas_call x1, Pallas kernels: 3.51 us -> 2.62 us  [far_part(): pl.pallas_call(far_kernel, in_specs=[SMEM, SMEM] + [VMEM] * (3 + XS), out...]
  transfers between devices with their start and end apart: 17 -> 17, of which waited for: 6 -> 6; matrix products, arithmetic and copies ran while one was open for 0% -> 0% of each run, Pallas kernels for 31% -> 29%
where the time goes in v5:
time: 64.3 us; the launch traced here: 64.1 us
  starting transfers between devices  30.2 us (47%)
  Pallas kernels  24.3 us (38%)
  waiting for transfers between devices  9 us (14%)
    ppermute x6, starting transfers between devices, sent(): lax.ppermute(message.astype(jnp.float16), 'seq', seq_perm(move)).astype(F32)  12.6 us
    ppermute x6, starting transfers between devices, along_x(): lax.ppermute(value, 'seq', seq_perm(lambda z, x: (z, (x + step) % XS)))  9.53 us
    pallas_call x1, Pallas kernels, prepare(): pl.pallas_call(prepare_kernel, in_specs=[HBM] * 6, out_specs=[VMEM] * (8...  5.44 us
    pallas_call x2, Pallas kernels, mix_part(): pl.pallas_call(functools.partial(mix_kernel, first, count), in_specs=[SME...  5.12 us
    ppermute x3, starting transfers between devices, local(): lax.ppermute(squares, 'head', head_perm(lambda y, core, k=k: ((y + k) % Y...  4.61 us
    ppermute x6, waiting for transfers between devices, sent(): lax.ppermute(message.astype(jnp.float16), 'seq', seq_perm(move)).astype(F32)  3.97 us
    ppermute x3, waiting for transfers between devices, local(): lax.ppermute(squares, 'head', head_perm(lambda y, core, k=k: ((y + k) % Y...  3.85 us
    pallas_call x1, Pallas kernels, local_part(): pl.pallas_call(functools.partial(local_kernel, len(mixed)), in_specs=[SME...  3.8 us
  transfers between devices with their start and end apart: 17, of which 6 were waited for; matrix products, arithmetic and copies ran while one was open for 0% of the time, Pallas kernels for 29%

profile of v5, /device:TPU:32, one launch (start us, length us, event | category | flops | bytes accessed | tf_op | source)
XLA Modules:
  0.0 64.1 jit_solution(8067207432080349881)
XLA Ops:
  0.0 0.8 %last_rows.1 = bf16[16,1280]{1,0:T(8,128)(2,1)S(1)} custom-call(bf16[1024,1024]{1,0:T(8,128)(2,1)} %mixer.3, bf16[1024,256]{1,0:T(8,128)(2,1)} %state.3), custom_call_target="tpu_custom_call" | custom-call | tf_op jit(solution)/shard_map/last_rows/pallas_call | solution.py:153
  0.8 3.4 %collective-permute-start = (bf16[16,1280]{1,0:T(8,128)(2,1)S(1)}, bf16[16,1280]{1,0:T(8,128)(2,1)S(1)}, u32[]{:S(2)}, u32[]{:S(2)}) collective-permute-start(bf16[16,1280]{1,0:T(8,128)(2,1)S(1)} %last_rows.1), channel_id=1, source_target_pairs={{0,8},{8,16},{16,24},{24,32},{32,40},{40,48},{48,56},{56,64},{64,7... | collective-permute-start | bytes 122888 | tf_op jit(solution)/shard_map/ppermute | solution.py:830
  4.2 5.4 %prepare.1 = (bf16[1024,1024]{1,0:T(8,128)(2,1)S(1)}, bf16[1024,256]{1,0:T(8,128)(2,1)S(1)}, f32[8,1024]{1,0:T(8,128)S(1)}, f32[8,1024]{1,0:T(8,128)S(1)}, bf16[...) custom-call(bf16[1024,1024]{1,0:T(8,128)(2,1)} %mixer.3, ...), custom_call_target="tpu_custom_call" | custom-call | flops 6554999808 | bytes 20520000 | tf_op jit(solution)/shard_map/prepare/pallas_call | solution.py:267
  10.4 3.2 %collective-permute-start.3 = (f16[264,128]{1,0:T(8,128)(2,1)S(1)}, f16[264,128]{1,0:T(8,128)(2,1)S(1)}, u32[]{:S(2)}, u32[]{:S(2)}) collective-permute-start(f16[264,128]{1,0:T(8,128)(2,1)S(1)} %convert_element_type.40), channel_id=1, source_target_pairs={{0,24},{8,0},{16,8},{24,16},{32,56},{40,32},{48,40},{56,48},{64,88... | collective-permute-start | bytes 202760 | tf_op jit(solution)/shard_map/ppermute | solution.py:51
  14.7 3.4 %shared_part.1 = (f32[1024,1024]{1,0:T(8,128)S(1)}, f32[1024,1024]{1,0:T(8,128)S(1)}, f32[1024,1024]{1,0:T(8,128)S(1)}, f32[1024,1024]{1,0:T(8,128)S(1)}) custom-call(bf16[1024,256]{1,0:T(8,128)(2,1)S(1)} %get-tuple-element.68.rows, f32[8,1024]{1,0:T(8,128)S(1)} %get-tuple-element.62.running_in, bf16[1024,1024]{1,0:T(8,128)(2,1)} %gate.1), custom_call_target="tpu_custom_call" | custom-call | flops 3910000128 | bytes 12240000 | tf_op jit(solution)/shard_map/shared_part/pallas_call | solution.py:428
  18.1 1.3 %collective-permute-done.2 = f16[264,128]{1,0:T(8,128)(2,1)S(1)} collective-permute-done((f16[264,128]{1,0:T(8,128)(2,1)S(1)}, f16[264,128]{1,0:T(8,128)(2,1)S(1)}, u32[]{:S(2)}, u32[]{:S(2)}) %collective-permute-start.2) | collective-permute-done | bytes 67616 | tf_op jit(solution)/shard_map/ppermute | solution.py:51
  20.6 2.2 %mix_part.2.rest_0_ = f32[1024,256]{1,0:T(8,128)S(1)} custom-call(f32[8,8,13]{2,1,0:T(8,128)S(1)} %bitcast.3, s32[16]{0:T(128)S(1)} %copy-done.1, bf16[1024,1024]{1,0:T(8,128)(2,1)S(1)} %get-tuple-element.61.inner, f32[8,1024]{1,0:T(8,128)S(1)} %get-tuple-element.62.running_in, f32[8,1024]{1,0:T(8,128)S(1)} %get-tuple-element.83.step_in, ...), custom_call_target="tpu_custom_call" | custom-call | flops 2300000000 | bytes 7200000 | tf_op jit(solution)/shard_map/mix_part/pallas_call | solution.py:522
  22.8 2.0 %collective-permute-done.4 = f16[264,128]{1,0:T(8,128)(2,1)S(1)} collective-permute-done((f16[264,128]{1,0:T(8,128)(2,1)S(1)}, f16[264,128]{1,0:T(8,128)(2,1)S(1)}, u32[]{:S(2)}, u32[]{:S(2)}) %collective-permute-start.4) | collective-permute-done | bytes 67616 | tf_op jit(solution)/shard_map/ppermute | solution.py:51
  24.9 4.3 %collective-permute-start.5 = (f16[264,128]{1,0:T(8,128)(2,1)S(1)}, f16[264,128]{1,0:T(8,128)(2,1)S(1)}, u32[]{:S(2)}, u32[]{:S(2)}) collective-permute-start(f16[264,128]{1,0:T(8,128)(2,1)S(1)} %convert_element_type.44), channel_id=1, source_target_pairs={{0,64},{8,72},{16,80},{24,88},{32,96},{40,104},{48,112},{56,120},{... | collective-permute-start | bytes 202760 | tf_op jit(solution)/shard_map/ppermute | solution.py:51
  29.5 0.8 %collective-permute-start.7 = (bf16[768,128]{1,0:T(8,128)(2,1)S(1)}, bf16[768,128]{1,0:T(8,128)(2,1)S(1)}, u32[]{:S(2)}, u32[]{:S(2)}) collective-permute-start(bf16[768,128]{1,0:T(8,128)(2,1)S(1)} %get-tuple-element.86), channel_id=1, source_target_pairs={{0,8},{8,16},{16,24},{24,0},{32,40},{40,48},{48,56},{56,32},{64,72... | collective-permute-start | bytes 589832 | tf_op jit(solution)/shard_map/ppermute | solution.py:47
  30.3 1.6 %collective-permute-start.8 = (bf16[768,128]{1,0:T(8,128)(2,1)S(1)}, bf16[768,128]{1,0:T(8,128)(2,1)S(1)}, u32[]{:S(2)}, u32[]{:S(2)}) collective-permute-start(bf16[768,128]{1,0:T(8,128)(2,1)S(1)} %get-tuple-element.87), channel_id=1, source_target_pairs={{0,16},{8,24},{16,0},{24,8},{32,48},{40,56},{48,32},{56,40},{64,80... | collective-permute-start | bytes 589832 | tf_op jit(solution)/shard_map/ppermute | solution.py:47
  31.9 1.9 %collective-permute-start.9 = (bf16[768,128]{1,0:T(8,128)(2,1)S(1)}, bf16[768,128]{1,0:T(8,128)(2,1)S(1)}, u32[]{:S(2)}, u32[]{:S(2)}) collective-permute-start(bf16[768,128]{1,0:T(8,128)(2,1)S(1)} %get-tuple-element.88), channel_id=1, source_target_pairs={{0,24},{8,0},{16,8},{24,16},{32,56},{40,32},{48,40},{56,48},{64,88... | collective-permute-start | bytes 589832 | tf_op jit(solution)/shard_map/ppermute | solution.py:47
  34.0 3.9 %collective-permute-start.6 = (f16[264,128]{1,0:T(8,128)(2,1)S(1)}, f16[264,128]{1,0:T(8,128)(2,1)S(1)}, u32[]{:S(2)}, u32[]{:S(2)}) collective-permute-start(f16[264,128]{1,0:T(8,128)(2,1)S(1)} %convert_element_type.46), channel_id=1, source_target_pairs={{0,224},{8,232},{16,240},{24,248},{32,192},{40,200},{48,208},{56,2... | collective-permute-start | bytes 202760 | tf_op jit(solution)/shard_map/ppermute | solution.py:51
  37.9 2.9 %mix_part.3.rest_1_ = f32[1024,512]{1,0:T(8,128)S(1)} custom-call(f32[8,8,13]{2,1,0:T(8,128)S(1)} %bitcast.4, s32[16]{0:T(128)S(1)} %copy-done.1, bf16[1024,1024]{1,0:T(8,128)(2,1)S(1)} %get-tuple-element.61.inner, f32[8,1024]{1,0:T(8,128)S(1)} %get-tuple-element.62.running_in, f32[8,1024]{1,0:T(8,128)S(1)} %get-tuple-element.83.step_in, ...), custom_call_target="tpu_custom_call" | custom-call | flops 4024999936 | bytes 12600000 | tf_op jit(solution)/shard_map/mix_part/pallas_call | solution.py:522
  41.0 1.2 %collective-permute-start.10 = (bf16[512,128]{1,0:T(8,128)(2,1)S(1)}, bf16[512,128]{1,0:T(8,128)(2,1)S(1)}, u32[]{:S(2)}, u32[]{:S(2)}) collective-permute-start(bf16[512,128]{1,0:T(8,128)(2,1)S(1)} %get-tuple-element.92), channel_id=1, source_target_pairs={{0,8},{8,16},{16,24},{24,0},{32,40},{40,48},{48,56},{56,32},{64,72... | collective-permute-start | bytes 393224 | tf_op jit(solution)/shard_map/ppermute | solution.py:47
  42.1 1.5 %collective-permute-start.11 = (bf16[512,128]{1,0:T(8,128)(2,1)S(1)}, bf16[512,128]{1,0:T(8,128)(2,1)S(1)}, u32[]{:S(2)}, u32[]{:S(2)}) collective-permute-start(bf16[512,128]{1,0:T(8,128)(2,1)S(1)} %get-tuple-element.93), channel_id=1, source_target_pairs={{0,16},{8,24},{16,0},{24,8},{32,48},{40,56},{48,32},{56,40},{64,80... | collective-permute-start | bytes 393224 | tf_op jit(solution)/shard_map/ppermute | solution.py:47
  43.7 2.5 %collective-permute-start.12 = (bf16[512,128]{1,0:T(8,128)(2,1)S(1)}, bf16[512,128]{1,0:T(8,128)(2,1)S(1)}, u32[]{:S(2)}, u32[]{:S(2)}) collective-permute-start(bf16[512,128]{1,0:T(8,128)(2,1)S(1)} %get-tuple-element.94), channel_id=1, source_target_pairs={{0,24},{8,0},{16,8},{24,16},{32,56},{40,32},{48,40},{56,48},{64,88... | collective-permute-start | bytes 393224 | tf_op jit(solution)/shard_map/ppermute | solution.py:47
  46.2 3.8 %local_part.1.local = f32[1024,1024]{1,0:T(8,128)S(1)} custom-call(f32[8,8,13]{2,1,0:T(8,128)S(1)} %bitcast.5, s32[16]{0:T(128)S(1)} %copy-done.1, bf16[1024,1024]{1,0:T(8,128)(2,1)S(1)} %get-tuple-element.61.inner, f32[8,1024]{1,0:T(8,128)S(1)} %get-tuple-element.62.running_in, f32[8,1024]{1,0:T(8,128)S(1)} %get-tuple-element.83.step_in, ...), custom_call_target="tpu_custom_call" | custom-call | flops 4369999872 | bytes 13680000 | tf_op jit(solution)/shard_map/local_part/pallas_call | solution.py:587
  50.0 2.6 %far_part.1 = (f32[1024,1024]{1,0:T(8,128)S(1)}, f32[8,128]{1,0:T(8,128)S(1)}) custom-call(f32[8,8,13]{2,1,0:T(8,128)S(1)} %bitcast.6, s32[16]{0:T(128)S(1)} %copy-done.1, f32[1024,1024]{1,0:T(8,128)S(1)} %local_part.1.local, f32[1024,1024]{1,0:T(8,128)S(1)} %get-tuple-element.89.gates, f32[1024,1024]{1,0:T(8,128)S(1)} %get-tuple-element.75.lifted_base, ...), custom_call_target="tpu_custom_call" | custom-call | flops 4024999936 | bytes 12600000 | tf_op jit(solution)/shard_map/far_part/pallas_call | solution.py:775
  52.8 1.2 %collective-permute-done.13 = f32[8,128]{1,0:T(8,128)S(1)} collective-permute-done((f32[8,128]{1,0:T(8,128)S(1)}, f32[8,128]{1,0:T(8,128)S(1)}, u32[]{:S(2)}, u32[]{:S(2)}) %collective-permute-start.13) | collective-permute-done | bytes 4128 | tf_op jit(solution)/shard_map/ppermute | solution.py:882
  53.9 3.0 %collective-permute-start.16 = (f32[8,128]{1,0:T(8,128)S(1)}, f32[8,128]{1,0:T(8,128)S(1)}, u32[]{:S(2)}, u32[]{:S(2)}) collective-permute-start(f32[8,128]{1,0:T(8,128)S(1)} %add.3.s0), channel_id=1, source_target_pairs={{0,6},{1,7},{2,0},{3,1},{4,2},{5,3},{6,4},{7,5},{8,14},{9,15},{10,... | collective-permute-start | bytes 12296 | tf_op jit(solution)/shard_map/ppermute | solution.py:884
  57.6 1.0 %collective-permute-start.14 = (f32[8,128]{1,0:T(8,128)S(1)}, f32[8,128]{1,0:T(8,128)S(1)}, u32[]{:S(2)}, u32[]{:S(2)}) collective-permute-start(f32[8,128]{1,0:T(8,128)S(1)} %add.3.s0), channel_id=1, source_target_pairs={{0,2},{1,3},{2,4},{3,5},{4,6},{5,7},{6,0},{7,1},{8,10},{9,11},{10,... | collective-permute-start | bytes 12296 | tf_op jit(solution)/shard_map/ppermute | solution.py:884
  58.5 3.5 %collective-permute-done.15.s2 = f32[8,128]{1,0:T(8,128)S(1)} collective-permute-done((f32[8,128]{1,0:T(8,128)S(1)}, f32[8,128]{1,0:T(8,128)S(1)}, u32[]{:S(2)}, u32[]{:S(2)}) %collective-permute-start.15) | collective-permute-done | bytes 4128 | tf_op jit(solution)/shard_map/ppermute | solution.py:884
  62.4 1.6 %norm.1 = bf16[1024,1024]{1,0:T(8,128)(2,1)} custom-call(f32[1024,1024]{1,0:T(8,128)S(1)} %get-tuple-element.95.gated, f32[8,128]{1,0:T(8,128)S(1)} %add.3.s0, f32[8,128]{1,0:T(8,128)S(1)} %collective-permute-done.14.s1, f32[8,128]{1,0:T(8,128)S(1)} %collective-permute-done.15.s2, f32[8,128]{1,0:T(8,128)S(1)} %collective-permute-done.16.s3, ...), custom_call_target="tpu_custom_call" | custom-call | flops 1840000000 | bytes 5760000 | tf_op jit(solution)/shard_map/norm/pallas_call | solution.py:805
  (43 shorter events, 4.7 us)
Async XLA Ops:
  0.8 8.9 %collective-permute-start = (bf16[16,1280]{1,0:T(8,128)(2,1)S(1)}, bf16[16,1280]{1,0:T(8,128)(2,1)S(1)}, u32[]{:S(2)}, u32[]{:S(2)}) collective-permute-start(bf16[16,1280]{1,0:T(8,128)(2,1)S(1)} %last_rows.1), channel_id=1, source_target_pairs={{0,8},{8,16},{16,24},{24,32},{32,40},{40,48},{48,56},{56,64},{64,7... | collective-permute-start | bytes 122888 | tf_op jit(solution)/shard_map/ppermute | solution.py:830
  10.4 7.7 %collective-permute-start.3 = (f16[264,128]{1,0:T(8,128)(2,1)S(1)}, f16[264,128]{1,0:T(8,128)(2,1)S(1)}, u32[]{:S(2)}, u32[]{:S(2)}) collective-permute-start(f16[264,128]{1,0:T(8,128)(2,1)S(1)} %convert_element_type.40), channel_id=1, source_target_pairs={{0,24},{8,0},{16,8},{24,16},{32,56},{40,32},{48,40},{56,48},{64,88... | collective-permute-start | bytes 202760 | tf_op jit(solution)/shard_map/ppermute | solution.py:51
  13.6 5.9 %collective-permute-start.2 = (f16[264,128]{1,0:T(8,128)(2,1)S(1)}, f16[264,128]{1,0:T(8,128)(2,1)S(1)}, u32[]{:S(2)}, u32[]{:S(2)}) collective-permute-start(f16[264,128]{1,0:T(8,128)(2,1)S(1)} %convert_element_type.38), channel_id=1, source_target_pairs={{0,16},{8,24},{16,0},{24,8},{32,48},{40,56},{48,32},{56,40},{64,80... | collective-permute-start | bytes 202760 | tf_op jit(solution)/shard_map/ppermute | solution.py:51
  14.1 6.1 %collective-permute-start.1 = (f16[264,128]{1,0:T(8,128)(2,1)S(1)}, f16[264,128]{1,0:T(8,128)(2,1)S(1)}, u32[]{:S(2)}, u32[]{:S(2)}) collective-permute-start(f16[264,128]{1,0:T(8,128)(2,1)S(1)} %convert_element_type.36), channel_id=1, source_target_pairs={{0,8},{8,16},{16,24},{24,0},{32,40},{40,48},{48,56},{56,32},{64,72... | collective-permute-start | bytes 202760 | tf_op jit(solution)/shard_map/ppermute | solution.py:51
  14.7 5.9 %copy-start = (f32[8,13,8]{1,2,0:T(8,128)S(1)}, f32[8,13,8]{1,2,0:T(8,128)}, u32[]{:S(2)}) copy-start(f32[8,13,8]{1,2,0:T(8,128)} %param.17) | copy-start | bytes 9988
  14.7 5.9 %copy-start.1 = (s32[16]{0:T(128)S(1)}, s32[16]{0:T(128)}, u32[]{:S(2)}) copy-start(s32[16]{0:T(128)} %kinds.7) | copy-start | bytes 196
  20.4 4.4 %collective-permute-start.4 = (f16[264,128]{1,0:T(8,128)(2,1)S(1)}, f16[264,128]{1,0:T(8,128)(2,1)S(1)}, u32[]{:S(2)}, u32[]{:S(2)}) collective-permute-start(f16[264,128]{1,0:T(8,128)(2,1)S(1)} %convert_element_type.42), channel_id=1, source_target_pairs={{0,32},{8,40},{16,48},{24,56},{32,0},{40,8},{48,16},{56,24},{64,96... | collective-permute-start | bytes 202760 | tf_op jit(solution)/shard_map/ppermute | solution.py:51
  24.9 8.9 %collective-permute-start.5 = (f16[264,128]{1,0:T(8,128)(2,1)S(1)}, f16[264,128]{1,0:T(8,128)(2,1)S(1)}, u32[]{:S(2)}, u32[]{:S(2)}) collective-permute-start(f16[264,128]{1,0:T(8,128)(2,1)S(1)} %convert_element_type.44), channel_id=1, source_target_pairs={{0,64},{8,72},{16,80},{24,88},{32,96},{40,104},{48,112},{56,120},{... | collective-permute-start | bytes 202760 | tf_op jit(solution)/shard_map/ppermute | solution.py:51
  29.5 14.2 %collective-permute-start.7 = (bf16[768,128]{1,0:T(8,128)(2,1)S(1)}, bf16[768,128]{1,0:T(8,128)(2,1)S(1)}, u32[]{:S(2)}, u32[]{:S(2)}) collective-permute-start(bf16[768,128]{1,0:T(8,128)(2,1)S(1)} %get-tuple-element.86), channel_id=1, source_target_pairs={{0,8},{8,16},{16,24},{24,0},{32,40},{40,48},{48,56},{56,32},{64,72... | collective-permute-start | bytes 589832 | tf_op jit(solution)/shard_map/ppermute | solution.py:47
  30.3 15.9 %collective-permute-start.8 = (bf16[768,128]{1,0:T(8,128)(2,1)S(1)}, bf16[768,128]{1,0:T(8,128)(2,1)S(1)}, u32[]{:S(2)}, u32[]{:S(2)}) collective-permute-start(bf16[768,128]{1,0:T(8,128)(2,1)S(1)} %get-tuple-element.87), channel_id=1, source_target_pairs={{0,16},{8,24},{16,0},{24,8},{32,48},{40,56},{48,32},{56,40},{64,80... | collective-permute-start | bytes 589832 | tf_op jit(solution)/shard_map/ppermute | solution.py:47
  31.9 14.3 %collective-permute-start.9 = (bf16[768,128]{1,0:T(8,128)(2,1)S(1)}, bf16[768,128]{1,0:T(8,128)(2,1)S(1)}, u32[]{:S(2)}, u32[]{:S(2)}) collective-permute-start(bf16[768,128]{1,0:T(8,128)(2,1)S(1)} %get-tuple-element.88), channel_id=1, source_target_pairs={{0,24},{8,0},{16,8},{24,16},{32,56},{40,32},{48,40},{56,48},{64,88... | collective-permute-start | bytes 589832 | tf_op jit(solution)/shard_map/ppermute | solution.py:47
  34.0 6.8 %collective-permute-start.6 = (f16[264,128]{1,0:T(8,128)(2,1)S(1)}, f16[264,128]{1,0:T(8,128)(2,1)S(1)}, u32[]{:S(2)}, u32[]{:S(2)}) collective-permute-start(f16[264,128]{1,0:T(8,128)(2,1)S(1)} %convert_element_type.46), channel_id=1, source_target_pairs={{0,224},{8,232},{16,240},{24,248},{32,192},{40,200},{48,208},{56,2... | collective-permute-start | bytes 202760 | tf_op jit(solution)/shard_map/ppermute | solution.py:51
  41.0 9.1 %collective-permute-start.10 = (bf16[512,128]{1,0:T(8,128)(2,1)S(1)}, bf16[512,128]{1,0:T(8,128)(2,1)S(1)}, u32[]{:S(2)}, u32[]{:S(2)}) collective-permute-start(bf16[512,128]{1,0:T(8,128)(2,1)S(1)} %get-tuple-element.92), channel_id=1, source_target_pairs={{0,8},{8,16},{16,24},{24,0},{32,40},{40,48},{48,56},{56,32},{64,72... | collective-permute-start | bytes 393224 | tf_op jit(solution)/shard_map/ppermute | solution.py:47
  42.1 7.9 %collective-permute-start.11 = (bf16[512,128]{1,0:T(8,128)(2,1)S(1)}, bf16[512,128]{1,0:T(8,128)(2,1)S(1)}, u32[]{:S(2)}, u32[]{:S(2)}) collective-permute-start(bf16[512,128]{1,0:T(8,128)(2,1)S(1)} %get-tuple-element.93), channel_id=1, source_target_pairs={{0,16},{8,24},{16,0},{24,8},{32,48},{40,56},{48,32},{56,40},{64,80... | collective-permute-start | bytes 393224 | tf_op jit(solution)/shard_map/ppermute | solution.py:47
  43.7 6.4 %collective-permute-start.12 = (bf16[512,128]{1,0:T(8,128)(2,1)S(1)}, bf16[512,128]{1,0:T(8,128)(2,1)S(1)}, u32[]{:S(2)}, u32[]{:S(2)}) collective-permute-start(bf16[512,128]{1,0:T(8,128)(2,1)S(1)} %get-tuple-element.94), channel_id=1, source_target_pairs={{0,24},{8,0},{16,8},{24,16},{32,56},{40,32},{48,40},{56,48},{64,88... | collective-permute-start | bytes 393224 | tf_op jit(solution)/shard_map/ppermute | solution.py:47
  50.0 12.4 %copy-start.2 = (f32[1024]{0:T(1024)S(1)}, f32[1024]{0:T(1024)}, u32[]{:S(2)}) copy-start(f32[1024]{0:T(1024)} %param.19) | copy-start | bytes 12292
  52.7 1.3 %collective-permute-start.13 = (f32[8,128]{1,0:T(8,128)S(1)}, f32[8,128]{1,0:T(8,128)S(1)}, u32[]{:S(2)}, u32[]{:S(2)}) collective-permute-start(f32[8,128]{1,0:T(8,128)S(1)} %get-tuple-element.96), channel_id=1, source_target_pairs={{0,1},{1,0},{2,3},{3,2},{4,5},{5,4},{6,7},{7,6},{8,9},{9,8},{10,11... | collective-permute-start | bytes 12296 | tf_op jit(solution)/shard_map/ppermute | solution.py:882
  53.9 4.6 %collective-permute-start.16 = (f32[8,128]{1,0:T(8,128)S(1)}, f32[8,128]{1,0:T(8,128)S(1)}, u32[]{:S(2)}, u32[]{:S(2)}) collective-permute-start(f32[8,128]{1,0:T(8,128)S(1)} %add.3.s0), channel_id=1, source_target_pairs={{0,6},{1,7},{2,0},{3,1},{4,2},{5,3},{6,4},{7,5},{8,14},{9,15},{10,... | collective-permute-start | bytes 12296 | tf_op jit(solution)/shard_map/ppermute | solution.py:884
  56.9 5.1 %collective-permute-start.15 = (f32[8,128]{1,0:T(8,128)S(1)}, f32[8,128]{1,0:T(8,128)S(1)}, u32[]{:S(2)}, u32[]{:S(2)}) collective-permute-start(f32[8,128]{1,0:T(8,128)S(1)} %add.3.s0), channel_id=1, source_target_pairs={{0,4},{1,5},{2,6},{3,7},{4,0},{5,1},{6,2},{7,3},{8,12},{9,13},{10,... | collective-permute-start | bytes 12296 | tf_op jit(solution)/shard_map/ppermute | solution.py:884
  57.6 4.8 %collective-permute-start.14 = (f32[8,128]{1,0:T(8,128)S(1)}, f32[8,128]{1,0:T(8,128)S(1)}, u32[]{:S(2)}, u32[]{:S(2)}) collective-permute-start(f32[8,128]{1,0:T(8,128)S(1)} %add.3.s0), channel_id=1, source_target_pairs={{0,2},{1,3},{2,4},{3,5},{4,6},{5,7},{6,0},{7,1},{8,10},{9,11},{10,... | collective-permute-start | bytes 12296 | tf_op jit(solution)/shard_map/ppermute | solution.py:884

commit v6 on v5

--- a/solution.py
+++ b/solution.py
@@ -169,23 +169,22 @@
     step_raw,
     rate,
     inner,
-    rows,
+    keys,
     running_out,
     step_out,
+    scale,
     first_rows,
-    first_scale,
     last,
     taps_here,
-    part0,
     part1,
     part2,
     part3,
     mixer_here,
-    state_here,
+    keys_here,
     raw_here,
     rate_here,
     keys_t,
-    scale,
+    late_scale,
     pad,
     mixer_sem,
     small_sem,
@@ -194,32 +193,33 @@
     heads, length = step_raw.shape
     width = mixer.shape[1]
     wide = PAIR * DIM
+    head_span = pl.ds(0, HALO)
     small = [
         pltpu.make_async_copy(source, target, small_sem.at[n])
         for n, (source, target) in enumerate(
             (
                 (step_raw, raw_here),
                 (rate, rate_here),
-                (state, state_here),
+                (state.at[:, :DIM], keys_here),
                 (state_taps, taps_here.at[:, width:]),
                 (taps, taps_here.at[:, :width]),
+                (state.at[head_span], first_rows.at[:, width:]),
+                (mixer.at[head_span], first_rows.at[:, :width]),
             )
         )
     ]
-    for copy in small:
+    for copy in small[:5]:
         copy.start()
-    pairs = [lax.rem(x + turn, XS) for turn in range(XS)]
+    pairs = [lax.rem(x + turn, XS) for turn in range(1, XS)]
     columns = [pl.ds(pl.multiple_of(pair * wide, wide), wide) for pair in pairs]
     large = [
-        pltpu.make_async_copy(
-            mixer.at[:, columns[turn]], mixer_here.at[turn], mixer_sem.at[turn]
-        )
-        for turn in range(XS)
+        pltpu.make_async_copy(mixer.at[:, columns[turn]], mixer_here.at[turn], mixer_sem.at[turn])
+        for turn in range(XS - 1)
     ]
-    for copy in large:
+    for copy in large + small[5:]:
         copy.start()
 
-    for copy in small:
+    for copy in small[:5]:
         copy.wait()
     raw = raw_here[...]
     step = jnp.maximum(raw, 0.0) + jnp.log1p(jnp.exp(-jnp.abs(raw)))
@@ -238,60 +238,61 @@
     running_out[...] = running
     step_out[...] = step
     scaled = jnp.exp(final - running) * step
-    first_scale[...] = scaled[:, :DIM]
-    scale[...] = jnp.where(lane < HALO, 0.0, scaled)
+    scale[...] = scaled
+    late_scale[...] = jnp.where(lane < HALO, 0.0, scaled)
     last[...] = jnp.broadcast_to(final, last.shape)
     nothing = jnp.zeros((HALO, wide), BF16)
-    first_rows[:, width:] = state_here[:HALO]
-    state_rows = conv(state_here[...], nothing, taps_here[:, width:], pad)
-    rows[...] = state_rows
-    keys_t[...] = state_rows[:, :DIM].astype(F32).T
-
-    for turn, part in enumerate((part0, part1, part2, part3)):
+    made = conv(keys_here, nothing, taps_here[:, width : width + DIM], pad)
+    keys[...] = made
+    keys_t[...] = made.astype(F32).T
+
+    for turn, part in enumerate((part1, part2, part3)):
         large[turn].wait()
-        first_rows[:, columns[turn]] = mixer_here[turn, :HALO]
-        values = conv(mixer_here[turn], nothing, taps_here[:, columns[turn]], pad)
+        values = conv(mixer_here.at[turn], nothing, taps_here[:, columns[turn]], pad)
         inner[:, columns[turn]] = values
         for head in range(PAIR):
-            row = scale[pl.ds(pairs[turn] * PAIR + head, 1), :]
+            row = late_scale[pl.ds(pairs[turn] * PAIR + head, 1), :]
             scaled_t = (keys_t[...] * row).astype(BF16)
             part[head * DIM : (head + 1) * DIM] = jnp.dot(
                 scaled_t, values[:, head * DIM : (head + 1) * DIM], preferred_element_type=F32
             )
+    for copy in small[5:]:
+        copy.wait()
 
 
 def prepare(mixer, state, taps, state_taps, step_raw_t, rate):
     length, width = mixer.shape
     heads = step_raw_t.shape[0]
     every = width + 2 * DIM
+    by_token = pltpu.VMEM((heads, length), F32)
     return pl.pallas_call(
         prepare_kernel,
         in_specs=[HBM] * 6,
-        out_specs=[VMEM] * (8 + XS),
+        out_specs=[VMEM] * (7 + XS),
         out_shape=[
             pltpu.VMEM((length, width), BF16),
-            pltpu.VMEM((length, 2 * DIM), BF16),
-            pltpu.VMEM((heads, length), F32),
-            pltpu.VMEM((heads, length), F32),
+            pltpu.VMEM((length, DIM), BF16),
+            by_token,
+            by_token,
+            by_token,
             pltpu.VMEM((HALO, every), BF16),
-            pltpu.VMEM((heads, DIM), F32),
             pltpu.VMEM((heads, DIM), F32),
             pltpu.VMEM((taps.shape[0], every), BF16),
         ]
-        + [pltpu.VMEM((PAIR * DIM, DIM), F32)] * XS,
+        + [pltpu.VMEM((PAIR * DIM, DIM), F32)] * (XS - 1),
         scratch_shapes=[
-            pltpu.VMEM((XS, length, PAIR * DIM), BF16),
-            pltpu.VMEM((length, 2 * DIM), BF16),
-            pltpu.VMEM((heads, length), F32),
+            pltpu.VMEM((XS - 1, length, PAIR * DIM), BF16),
+            pltpu.VMEM((length, DIM), BF16),
+            by_token,
             pltpu.SMEM((heads,), F32),
             pltpu.VMEM((DIM, length), F32),
-            pltpu.VMEM((heads, length), F32),
+            by_token,
             pltpu.VMEM((PAIR, length + 8, DIM), F32),
-            DMA((XS,)),
-            DMA((5,)),
+            DMA((XS - 1,)),
+            DMA((7,)),
         ],
         compiler_params=params(16),
-        cost_estimate=cost(5.7),
+        cost_estimate=cost(4.5),
         name="prepare",
     )(
         in_hbm(mixer),
@@ -306,18 +307,16 @@
 def finish_kernel(
     halo,
     first_rows,
-    first_scale,
+    scale,
     last,
     taps,
     inner_in,
-    rows_in,
-    p0,
+    keys_in,
     p1,
     p2,
     p3,
     inner,
-    rows,
-    m0,
+    keys,
     m1,
     m2,
     m3,
@@ -327,18 +326,19 @@
     width = inner.shape[1]
     heads = width // DIM
     wide = PAIR * DIM
-    made = conv(first_rows[:, width:], halo[:, width:], taps[:, width:], pad)
-    rows[:HALO] = made
-    keys = made[:, :DIM].astype(F32)
-    columns = first_scale[...].T
+    states = slice(width, width + DIM)
+    made = conv(first_rows.at[:, states], halo[:, states], taps[:, states], pad)
+    keys[:HALO] = made
+    early = made.astype(F32)
+    columns = scale[:, :DIM].T
     scaled = [
-        (keys * jnp.broadcast_to(columns[:HALO, head : head + 1], (HALO, DIM))).astype(BF16)
+        (early * jnp.broadcast_to(columns[:HALO, head : head + 1], (HALO, DIM))).astype(BF16)
         for head in range(heads)
     ]
     added = []
     for pair in range(XS):
         lanes = slice(pair * wide, (pair + 1) * wide)
-        values = conv(first_rows[:, lanes], halo[:, lanes], taps[:, lanes], pad)
+        values = conv(first_rows.at[:, lanes], halo[:, lanes], taps[:, lanes], pad)
         inner[:HALO, lanes] = values
         for head in range(PAIR):
             added.append(
@@ -349,50 +349,68 @@
                     preferred_element_type=F32,
                 )
             )
-    for turn, (part, message) in enumerate(((p0, m0), (p1, m1), (p2, m2), (p3, m3))):
+    for turn, (part, message) in enumerate(((p1, m1), (p2, m2), (p3, m3)), start=1):
         pair = lax.rem(x + turn, XS)
-        states = []
+        totals = []
         decays = []
         for head in range(PAIR):
             extra = sum(
                 added[other * PAIR + head] * flag(pair == other) for other in range(XS)
             )
-            states.append(part[head * DIM : (head + 1) * DIM] + extra)
+            totals.append(part[head * DIM : (head + 1) * DIM] + extra)
             decays.append(last[pl.ds(pair * PAIR + head, 1), :])
-        encode(message, states, decays)
-
-
-def finish(halo, first_rows, first_scale, last, taps, inner, rows, parts):
+        encode(message, totals, decays)
+
+
+def finish(halo, first_rows, scale, last, taps, inner, keys, parts):
     return pl.pallas_call(
         finish_kernel,
-        in_specs=[VMEM] * (7 + XS),
-        out_specs=[VMEM] * (2 + XS),
-        out_shape=[pltpu.VMEM(inner.shape, BF16), pltpu.VMEM(rows.shape, BF16)]
-        + [pltpu.VMEM((MESSAGE, DIM), F32)] * XS,
+        in_specs=[VMEM] * (6 + XS),
+        out_specs=[VMEM] * (1 + XS),
+        out_shape=[pltpu.VMEM(inner.shape, BF16), pltpu.VMEM(keys.shape, BF16)]
+        + [pltpu.VMEM((MESSAGE, DIM), F32)] * (XS - 1),
         scratch_shapes=[pltpu.VMEM((PAIR, HALO + 8, DIM), F32)],
         input_output_aliases={5: 0, 6: 1},
         compiler_params=params(4),
         cost_estimate=cost(0.75),
         name="finish",
-    )(halo, first_rows, first_scale, last, taps, inner, rows, *parts)
+    )(halo, first_rows, scale, last, taps, inner, keys, *parts)
 
 
 def shared_kernel(
-    rows, running_in, gate, scores, gates, lifted_base, ahead_out, gate_here, gate_sem
+    mixer,
+    state,
+    halo,
+    taps,
+    scale,
+    last,
+    running_in,
+    keys,
+    inner_in,
+    inner,
+    scores,
+    lifted_base,
+    ahead_out,
+    message,
+    mixer_here,
+    state_here,
+    queries,
+    keys_t,
+    pad,
+    sems,
 ):
-    length, width = gate.shape
+    x, _ = block_place()
+    length, width = inner.shape
     heads = width // DIM
     tiles = length // TILE
-    gate_copy = pltpu.make_async_copy(gate, gate_here, gate_sem)
-    gate_copy.start()
-    for i in range(tiles):
-        wide = (i + 1) * TILE
-        scores[i * TILE : wide, :wide] = lax.dot_general(
-            rows[i * TILE : wide, DIM:],
-            rows[:wide, :DIM],
-            (((1,), (1,)), ((), ())),
-            preferred_element_type=F32,
-        )
+    wide = PAIR * DIM
+    own = pl.ds(pl.multiple_of(x * wide, wide), wide)
+    copies = [
+        pltpu.make_async_copy(state.at[:, DIM:], state_here, sems.at[0]),
+        pltpu.make_async_copy(mixer.at[:, own], mixer_here, sems.at[1]),
+    ]
+    for copy in copies:
+        copy.start()
     running = running_in[...]
     columns = jnp.exp(running).T
     ahead = jnp.concatenate(
@@ -402,39 +420,87 @@
         ],
         axis=1,
     ).T
+    keys_t[...] = keys[...].astype(F32).T
     for i in range(tiles):
         span = slice(i * TILE, (i + 1) * TILE)
-        queries = rows[span, DIM:].astype(F32)
         for head in range(heads):
-            lanes = slice(head * DIM, (head + 1) * DIM)
-            lifted_base[span, lanes] = queries * jnp.broadcast_to(
+            ahead_out[span, head * DIM : (head + 1) * DIM] = jnp.broadcast_to(
+                ahead[span, head : head + 1], (TILE, DIM)
+            )
+    for copy in copies:
+        copy.wait()
+    states = slice(width + DIM, width + 2 * DIM)
+    queries[...] = conv(state_here, halo[:, states], taps[:, states], pad)
+    values = conv(mixer_here, halo[:, own], taps[:, own], pad)
+    inner[:, own] = values
+    totals = []
+    decays = []
+    for offset in range(PAIR):
+        head = pl.ds(x * PAIR + offset, 1)
+        totals.append(
+            jnp.dot(
+                (keys_t[...] * scale[head, :]).astype(BF16),
+                values[:, offset * DIM : (offset + 1) * DIM],
+                preferred_element_type=F32,
+            )
+        )
+        decays.append(last[head, :])
+    encode(message, totals, decays)
+    for i in range(tiles):
+        span = slice(i * TILE, (i + 1) * TILE)
+        end = (i + 1) * TILE
+        scores[span, :end] = lax.dot_general(
+            queries[span],
+            keys[:end],
+            (((1,), (1,)), ((), ())),
+            preferred_element_type=F32,
+        )
+        here = queries[span].astype(F32)
+        for head in range(heads):
+            lifted_base[span, head * DIM : (head + 1) * DIM] = here * jnp.broadcast_to(
                 columns[span, head : head + 1], (TILE, DIM)
             )
-            ahead_out[span, lanes] = jnp.broadcast_to(ahead[span, head : head + 1], (TILE, DIM))
-    gate_copy.wait()
+
+
+def shared_part(mixer, state, halo, taps, scale, last, running, keys, inner):
+    length, width = inner.shape
+    return pl.pallas_call(
+        shared_kernel,
+        in_specs=[HBM, HBM] + [VMEM] * 7,
+        out_specs=[VMEM] * 5,
+        out_shape=[
+            pltpu.VMEM((length, width), BF16),
+            pltpu.VMEM((length, length), F32),
+            pltpu.VMEM((length, width), F32),
+            pltpu.VMEM((length, width), F32),
+            pltpu.VMEM((MESSAGE, DIM), F32),
+        ],
+        scratch_shapes=[
+            pltpu.VMEM((length, PAIR * DIM), BF16),
+            pltpu.VMEM((length, DIM), BF16),
+            pltpu.VMEM((length, DIM), BF16),
+            pltpu.VMEM((DIM, length), F32),
+            pltpu.VMEM((PAIR, length + 8, DIM), F32),
+            DMA((2,)),
+        ],
+        input_output_aliases={8: 0},
+        compiler_params=params(8),
+        cost_estimate=cost(3.4),
+        name="shared_part",
+    )(in_hbm(mixer), in_hbm(state), halo, taps, scale, last, running, keys, inner)
+
+
+def gates_kernel(gate, gates):
+    length, width = gate.shape
 
     def one_tile(tile, carry):
         span = pl.ds(pl.multiple_of(tile * TILE, TILE), TILE)
         for piece in range(width // DIM):
             lane = slice(piece * DIM, (piece + 1) * DIM)
-            gates[span, lane] = silu(gate_here[span, lane].astype(F32))
+            gates[span, lane] = silu(gate[span, lane].astype(F32))
         return carry
 
-    lax.fori_loop(0, tiles, one_tile, 0)
-
-
-def shared_part(rows, running, gate):
-    length, width = gate.shape
-    return pl.pallas_call(
-        shared_kernel,
-        in_specs=[VMEM, VMEM, HBM],
-        out_specs=[VMEM] * 4,
-        out_shape=[pltpu.VMEM((length, length), F32)] + [pltpu.VMEM((length, width), F32)] * 3,
-        scratch_shapes=[pltpu.VMEM((length, width), BF16), DMA],
-        compiler_params=params(8),
-        cost_estimate=cost(3.4),
-        name="shared_part",
-    )(rows, running, in_hbm(gate))
+    lax.fori_loop(0, length // TILE, one_tile, 0)
 
 
 def mix_head(head, table, kinds, inner, running_in, step_in, scores, ahead_in, emit):
@@ -530,6 +596,33 @@
     )(table, kinds, inner, running, step, scores, ahead)
 
 
+def turn_kernel(first, count, upper, *refs):
+    table, kinds, inner, running_in, step_in, scores, ahead_in, gate = refs[:8]
+    out, gates = refs[-2:]
+    _, z = block_place()
+
+    @pl.when((z >= ZS // 2) == upper)
+    def _():
+        mix_kernel(
+            first, count, table, kinds, inner, running_in, step_in, scores, ahead_in, out
+        )
+        gates_kernel(gate, gates)
+
+
+def turn_part(first, count, upper, earlier, table, kinds, inner, running, step, scores, ahead, gate):
+    length, width = inner.shape
+    return pl.pallas_call(
+        functools.partial(turn_kernel, first, count, upper),
+        in_specs=[SMEM, SMEM] + [VMEM] * (6 + len(earlier)),
+        out_specs=[VMEM] * 2,
+        out_shape=[pltpu.VMEM((length, count * DIM), F32), pltpu.VMEM(gate.shape, F32)],
+        input_output_aliases={8: 0, 9: 1} if earlier else {},
+        compiler_params=params(8),
+        cost_estimate=cost(0.6 * count + 1.2 if upper else 0.2),
+        name="turn_part",
+    )(table, kinds, inner, running, step, scores, ahead, gate, *earlier)
+
+
 def local_kernel(
     done,
     table,
@@ -830,17 +923,19 @@
     halo = lax.ppermute(
         last_rows(mixer_input, state_input), "seq", [(i, i + 1) for i in range(XS * ZS - 1)]
     )
-    inner, rows, running, step, first_rows, first_scale, last, taps, *parts = prepare(
+    inner, keys, running, step, scale, first_rows, last, taps, *parts = prepare(
         mixer_input, state_input, conv_inner, conv_state, step_raw.T, decay_rate
     )
-    inner, rows, *parts = finish(halo, first_rows, first_scale, last, taps, inner, rows, parts)
+    inner, keys, *parts = finish(halo, first_rows, scale, last, taps, inner, keys, parts)
     table = jnp.transpose(level_table, (0, 2, 1))
-    arrived = [parts[0]] + [
-        sent(parts[k], lambda z, x, k=k: (z, (x + k) % XS)) for k in range(1, XS)
-    ]
-    shared = shared_part(rows, running, gate_input)
-    arrived, shared = lax.optimization_barrier((arrived, shared))
-    scores, gates, lifted_base, ahead = shared
+    moved = {
+        k: sent(parts[k - 1], lambda z, x, k=k: (z, (x + k) % XS)) for k in (2, 1, 3)
+    }
+    arrived = [moved[k] for k in range(1, XS)]
+    inner, scores, lifted_base, ahead, own_part = shared_part(
+        mixer_input, state_input, halo, taps, scale, last, running, keys, inner
+    )
+    arrived = [own_part] + arrived
     mix = functools.partial(
         mix_part,
         table=table,
@@ -859,10 +954,25 @@
     pair_before = sent(pair_state, lambda z, x: (z ^ 2, x))
     near = [near[0]] + [along_x(near[k], k) for k in range(1, XS)]
     quad_state = fold_two(2, pair_state, pair_before)
+    turn = functools.partial(
+        turn_part,
+        PAIR,
+        2 * PAIR,
+        table=table,
+        kinds=stretch_kind,
+        inner=inner,
+        running=running,
+        scores=scores,
+        ahead=ahead,
+        gate=gate_input,
+    )
     quad_state, step_late = lax.optimization_barrier((quad_state, step))
+    quad_state, *turned = lax.optimization_barrier(
+        (quad_state, *turn(False, (), step=step_late))
+    )
     quad_before = sent(quad_state, lambda z, x: (ZS - 1 - z, x) if z < ZS // 2 else None)
-    quad_before, mixed_second = lax.optimization_barrier(
-        (quad_before, mix(PAIR, 2 * PAIR, step=step_late))
+    quad_before, mixed_second, gates = lax.optimization_barrier(
+        (quad_before, *turn(True, turned, step=step_late))
     )
     far = fold_far(arrived, (row_before, pair_before, quad_before))
     far = [far[0]] + [along_x(far[k], k) for k in range(1, XS)]
@@ -882,7 +992,7 @@
     squares = squares + lax.ppermute(squares, "head", head_perm(lambda y, core: (y, 1 - core)))
     sums = [squares] + [
         lax.ppermute(squares, "head", head_perm(lambda y, core, k=k: ((y + k) % YS, core)))
-        for k in range(1, YS)
+        for k in (2, 1, 3)
     ]
     total_width = width * lax.axis_size("head")
     return norm(gated, sums, norm_gain[None, :], total_width)

time: 64.3 us -> 63.8 us (level)
  waiting for transfers between devices: 9 us -> 6.87 us
  Pallas kernels: 24.3 us -> 25 us
  starting transfers between devices: 30.2 us -> 30.9 us
    pallas_call x3 -> x5, Pallas kernels: 9.57 us -> 13.3 us  [the longest x2 4.79 us: turn_part(): pl.pallas_call(functools.partial(turn_kernel, first, count, upper), in_sp...]
    pallas_call x2 -> x1, Pallas kernels: 5.12 us -> 2.19 us  [mix_part(): pl.pallas_call(functools.partial(mix_kernel, first, count), in_specs=[SME...]
    ppermute x3, waiting for transfers between devices: 3.85 us -> 1.58 us  [local(): lax.ppermute(squares, 'head', head_perm(lambda y, core, k=k: ((y + k) % Y...]
    ppermute x3, starting transfers between devices: 4.61 us -> 6.43 us  [local(): lax.ppermute(squares, 'head', head_perm(lambda y, core, k=k: ((y + k) % Y...]
    ppermute x6, waiting for transfers between devices: 3.97 us -> 2.77 us  [sent(): lax.ppermute(message.astype(jnp.float16), 'seq', seq_perm(move)).astype(F32)]
    ppermute x6, starting transfers between devices: 9.53 us -> 8.36 us  [along_x(): lax.ppermute(value, 'seq', seq_perm(lambda z, x: (z, (x + step) % XS)))]
    ppermute x6, waiting for transfers between devices: 0.02 us -> 0.91 us  [along_x(): lax.ppermute(value, 'seq', seq_perm(lambda z, x: (z, (x + step) % XS)))]
  transfers between devices with their start and end apart: 17 -> 17, of which waited for: 6 -> 6; matrix products, arithmetic and copies ran while one was open for 0% -> 0% of each run, Pallas kernels for 29% -> 30%
where the time goes in v6:
time: 63.8 us; the launch traced here: 63.4 us
  starting transfers between devices  30.9 us (48%)
  Pallas kernels  25 us (39%)
  waiting for transfers between devices  6.87 us (11%)
    ppermute x6, starting transfers between devices, sent(): lax.ppermute(message.astype(jnp.float16), 'seq', seq_perm(move)).astype(F32)  12.6 us
    ppermute x6, starting transfers between devices, along_x(): lax.ppermute(value, 'seq', seq_perm(lambda z, x: (z, (x + step) % XS)))  8.36 us
    ppermute x3, starting transfers between devices, local(): lax.ppermute(squares, 'head', head_perm(lambda y, core, k=k: ((y + k) % Y...  6.43 us
    pallas_call x2, Pallas kernels, turn_part(): pl.pallas_call(functools.partial(turn_kernel, first, count, upper), in_sp...  4.79 us
    pallas_call x1, Pallas kernels, prepare(): pl.pallas_call(prepare_kernel, in_specs=[HBM] * 6, out_specs=[VMEM] * (7...  4.13 us
    pallas_call x1, Pallas kernels, local_part(): pl.pallas_call(functools.partial(local_kernel, len(mixed)), in_specs=[SME...  3.81 us
    pallas_call x1, Pallas kernels, shared_part(): pl.pallas_call(shared_kernel, in_specs=[HBM, HBM] + [VMEM] * 7, out_specs...  3.71 us
    ppermute x1, starting transfers between devices, local(): lax.ppermute(last_rows(mixer_input, state_input), 'seq', [(i, i + 1) for...  3.4 us
  transfers between devices with their start and end apart: 17, of which 6 were waited for; matrix products, arithmetic and copies ran while one was open for 0% of the time, Pallas kernels for 30%

profile of v6, /device:TPU:32, one launch (start us, length us, event | category | flops | bytes accessed | tf_op | source)
XLA Modules:
  0.0 63.4 jit_solution(941236508507639027)
XLA Ops:
  0.8 3.4 %collective-permute-start = (bf16[16,1280]{1,0:T(8,128)(2,1)S(1)}, bf16[16,1280]{1,0:T(8,128)(2,1)S(1)}, u32[]{:S(2)}, u32[]{:S(2)}) collective-permute-start(bf16[16,1280]{1,0:T(8,128)(2,1)S(1)} %last_rows.1), channel_id=1, source_target_pairs={{0,8},{8,16},{16,24},{24,32},{32,40},{40,48},{48,56},{56,64},{64,7... | collective-permute-start | bytes 122888 | tf_op jit(solution)/shard_map/ppermute | solution.py:923
  4.2 4.1 %prepare.1 = (bf16[1024,1024]{1,0:T(8,128)(2,1)S(1)}, bf16[1024,128]{1,0:T(8,128)(2,1)S(1)}, f32[8,1024]{1,0:T(8,128)S(1)}, f32[8,1024]{1,0:T(8,128)S(1)}, f32[8...) custom-call(bf16[1024,1024]{1,0:T(8,128)(2,1)} %mixer.5, ...), custom_call_target="tpu_custom_call" | custom-call | flops 5175000064 | bytes 16200000 | tf_op jit(solution)/shard_map/prepare/pallas_call | solution.py:268
  9.5 1.1 %collective-permute-start.1 = (f16[264,128]{1,0:T(8,128)(2,1)S(1)}, f16[264,128]{1,0:T(8,128)(2,1)S(1)}, u32[]{:S(2)}, u32[]{:S(2)}) collective-permute-start(f16[264,128]{1,0:T(8,128)(2,1)S(1)} %convert_element_type.36), channel_id=1, source_target_pairs={{0,8},{8,16},{16,24},{24,0},{32,40},{40,48},{48,56},{56,32},{64,72... | collective-permute-start | bytes 202760 | tf_op jit(solution)/shard_map/ppermute | solution.py:51
  10.6 3.2 %collective-permute-start.2 = (f16[264,128]{1,0:T(8,128)(2,1)S(1)}, f16[264,128]{1,0:T(8,128)(2,1)S(1)}, u32[]{:S(2)}, u32[]{:S(2)}) collective-permute-start(f16[264,128]{1,0:T(8,128)(2,1)S(1)} %convert_element_type.38), channel_id=1, source_target_pairs={{0,16},{8,24},{16,0},{24,8},{32,48},{40,56},{48,32},{56,40},{64,80... | collective-permute-start | bytes 202760 | tf_op jit(solution)/shard_map/ppermute | solution.py:51
  13.8 0.9 %collective-permute-start.3 = (f16[264,128]{1,0:T(8,128)(2,1)S(1)}, f16[264,128]{1,0:T(8,128)(2,1)S(1)}, u32[]{:S(2)}, u32[]{:S(2)}) collective-permute-start(f16[264,128]{1,0:T(8,128)(2,1)S(1)} %convert_element_type.40), channel_id=1, source_target_pairs={{0,24},{8,0},{16,8},{24,16},{32,56},{40,32},{48,40},{56,48},{64,88... | collective-permute-start | bytes 202760 | tf_op jit(solution)/shard_map/ppermute | solution.py:51
  14.7 3.7 %shared_part.1 = (bf16[1024,1024]{1,0:T(8,128)(2,1)S(1)}, f32[1024,1024]{1,0:T(8,128)S(1)}, f32[1024,1024]{1,0:T(8,128)S(1)}, f32[1024,1024]{1,0:T(8,128)S(1)}, f32[264,128]{1,0:T(8,128)S(1)}) custom-call(bf16[1024,1024]{1,0:T(8,128)(2,1)} %mixer.5, bf16[1024,256]{1,0:T(8,128)(2,1)} %state.5, ...), custom_call_target="tpu_custom_call", output_to_operand_aliasing={{0}: (8, {})} | custom-call | flops 3910000128 | bytes 12240000 | tf_op jit(solution)/shard_map/shared_part/pallas_call | solution.py:467
  18.9 2.2 %mix_part.1.rest_0_ = f32[1024,256]{1,0:T(8,128)S(1)} custom-call(f32[8,8,13]{2,1,0:T(8,128)S(1)} %bitcast.3, s32[16]{0:T(128)S(1)} %copy-done.2, bf16[1024,1024]{1,0:T(8,128)(2,1)S(1)} %get-tuple-element.62.inner.refs_2_, f32[8,1024]{1,0:T(8,128)S(1)} %get-tuple-element.53.running_in.refs_3_, f32[8,1024]{1,0:T(8,128)S(1)} %get-tuple-element.74.step_in.refs_4_, ...), custom_call_target="tpu_custom_call" | custom-call | flops 2300000000 | bytes 7200000 | tf_op jit(solution)/shard_map/mix_part/pallas_call | solution.py:588
  21.1 2.0 %collective-permute-done.4 = f16[264,128]{1,0:T(8,128)(2,1)S(1)} collective-permute-done((f16[264,128]{1,0:T(8,128)(2,1)S(1)}, f16[264,128]{1,0:T(8,128)(2,1)S(1)}, u32[]{:S(2)}, u32[]{:S(2)}) %collective-permute-start.4) | collective-permute-done | bytes 67616 | tf_op jit(solution)/shard_map/ppermute | solution.py:51
  23.3 4.2 %collective-permute-start.5 = (f16[264,128]{1,0:T(8,128)(2,1)S(1)}, f16[264,128]{1,0:T(8,128)(2,1)S(1)}, u32[]{:S(2)}, u32[]{:S(2)}) collective-permute-start(f16[264,128]{1,0:T(8,128)(2,1)S(1)} %convert_element_type.44), channel_id=1, source_target_pairs={{0,64},{8,72},{16,80},{24,88},{32,96},{40,104},{48,112},{56,120},{... | collective-permute-start | bytes 202760 | tf_op jit(solution)/shard_map/ppermute | solution.py:51
  27.8 1.6 %collective-permute-start.7 = (bf16[768,128]{1,0:T(8,128)(2,1)S(1)}, bf16[768,128]{1,0:T(8,128)(2,1)S(1)}, u32[]{:S(2)}, u32[]{:S(2)}) collective-permute-start(bf16[768,128]{1,0:T(8,128)(2,1)S(1)} %get-tuple-element.84), channel_id=1, source_target_pairs={{0,8},{8,16},{16,24},{24,0},{32,40},{40,48},{48,56},{56,32},{64,72... | collective-permute-start | bytes 589832 | tf_op jit(solution)/shard_map/ppermute | solution.py:47
  29.4 1.1 %collective-permute-start.8 = (bf16[768,128]{1,0:T(8,128)(2,1)S(1)}, bf16[768,128]{1,0:T(8,128)(2,1)S(1)}, u32[]{:S(2)}, u32[]{:S(2)}) collective-permute-start(bf16[768,128]{1,0:T(8,128)(2,1)S(1)} %get-tuple-element.85), channel_id=1, source_target_pairs={{0,16},{8,24},{16,0},{24,8},{32,48},{40,56},{48,32},{56,40},{64,80... | collective-permute-start | bytes 589832 | tf_op jit(solution)/shard_map/ppermute | solution.py:47
  30.5 1.8 %collective-permute-start.9 = (bf16[768,128]{1,0:T(8,128)(2,1)S(1)}, bf16[768,128]{1,0:T(8,128)(2,1)S(1)}, u32[]{:S(2)}, u32[]{:S(2)}) collective-permute-start(bf16[768,128]{1,0:T(8,128)(2,1)S(1)} %get-tuple-element.86), channel_id=1, source_target_pairs={{0,24},{8,0},{16,8},{24,16},{32,56},{40,32},{48,40},{56,48},{64,88... | collective-permute-start | bytes 589832 | tf_op jit(solution)/shard_map/ppermute | solution.py:47
  32.5 3.7 %turn_part.2 = (f32[1024,512]{1,0:T(8,128)S(1)}, f32[1024,1024]{1,0:T(8,128)S(1)}) custom-call(f32[8,8,13]{2,1,0:T(8,128)S(1)} %bitcast.4, s32[16]{0:T(128)S(1)} %copy-done.2, bf16[1024,1024]{1,0:T(8,128)(2,1)S(1)} %get-tuple-element.62.inner.refs_2_, f32[8,1024]{1,0:T(8,128)S(1)} %get-tuple-element.53.running_in.refs_3_, ...), custom_call_target="tpu_custom_call" | custom-call | flops 230000000 | bytes 720000 | tf_op jit(solution)/shard_map/turn_part/pallas_call | solution.py:614
  36.3 3.0 %collective-permute-start.6 = (f16[264,128]{1,0:T(8,128)(2,1)S(1)}, f16[264,128]{1,0:T(8,128)(2,1)S(1)}, u32[]{:S(2)}, u32[]{:S(2)}) collective-permute-start(f16[264,128]{1,0:T(8,128)(2,1)S(1)} %convert_element_type.46), channel_id=1, source_target_pairs={{0,224},{8,232},{16,240},{24,248},{32,192},{40,200},{48,208},{56,2... | collective-permute-start | bytes 202760 | tf_op jit(solution)/shard_map/ppermute | solution.py:51
  39.3 1.1 %turn_part.3 = (f32[1024,512]{1,0:T(8,128)S(1)}, f32[1024,1024]{1,0:T(8,128)S(1)}) custom-call(f32[8,8,13]{2,1,0:T(8,128)S(1)} %bitcast.5, s32[16]{0:T(128)S(1)} %copy-done.2, bf16[1024,1024]{1,0:T(8,128)(2,1)S(1)} %get-tuple-element.62.inner.refs_2_, ...), custom_call_target="tpu_custom_call", output_to_operand_aliasing={{0}: (8, {}), {1}: (9, {})} | custom-call | flops 4140000000 | bytes 12959999 | tf_op jit(solution)/shard_map/turn_part/pallas_call | solution.py:614
  42.0 1.0 %collective-permute-start.11 = (bf16[512,128]{1,0:T(8,128)(2,1)S(1)}, bf16[512,128]{1,0:T(8,128)(2,1)S(1)}, u32[]{:S(2)}, u32[]{:S(2)}) collective-permute-start(bf16[512,128]{1,0:T(8,128)(2,1)S(1)} %get-tuple-element.91), channel_id=1, source_target_pairs={{0,16},{8,24},{16,0},{24,8},{32,48},{40,56},{48,32},{56,40},{64,80... | collective-permute-start | bytes 393224 | tf_op jit(solution)/shard_map/ppermute | solution.py:47
  43.0 2.2 %collective-permute-start.12 = (bf16[512,128]{1,0:T(8,128)(2,1)S(1)}, bf16[512,128]{1,0:T(8,128)(2,1)S(1)}, u32[]{:S(2)}, u32[]{:S(2)}) collective-permute-start(bf16[512,128]{1,0:T(8,128)(2,1)S(1)} %get-tuple-element.92), channel_id=1, source_target_pairs={{0,24},{8,0},{16,8},{24,16},{32,56},{40,32},{48,40},{56,48},{64,88... | collective-permute-start | bytes 393224 | tf_op jit(solution)/shard_map/ppermute | solution.py:47
  45.1 3.8 %local_part.1.local = f32[1024,1024]{1,0:T(8,128)S(1)} custom-call(f32[8,8,13]{2,1,0:T(8,128)S(1)} %bitcast.6, s32[16]{0:T(128)S(1)} %copy-done.2, bf16[1024,1024]{1,0:T(8,128)(2,1)S(1)} %get-tuple-element.62.inner.refs_2_, f32[8,1024]{1,0:T(8,128)S(1)} %get-tuple-element.53.running_in.refs_3_, f32[8,1024]{1,0:T(8,128)S(1)} %get-tuple-element.74.step_in.refs_4_, ...), custom_call_target="tpu_custom_call" | custom-call | flops 4369999872 | bytes 13680000 | tf_op jit(solution)/shard_map/local_part/pallas_call | solution.py:680
  49.9 2.5 %far_part.1 = (f32[1024,1024]{1,0:T(8,128)S(1)}, f32[8,128]{1,0:T(8,128)S(1)}) custom-call(f32[8,8,13]{2,1,0:T(8,128)S(1)} %bitcast.7, s32[16]{0:T(128)S(1)} %copy-done.2, f32[1024,1024]{1,0:T(8,128)S(1)} %local_part.1.local, f32[1024,1024]{1,0:T(8,128)S(1)} %get-tuple-element.87.gates, f32[1024,1024]{1,0:T(8,128)S(1)} %get-tuple-element.66.lifted_base, ...), custom_call_target="tpu_custom_call" | custom-call | flops 4024999936 | bytes 12600000 | tf_op jit(solution)/shard_map/far_part/pallas_call | solution.py:868
  52.5 1.2 %collective-permute-done.13 = f32[8,128]{1,0:T(8,128)S(1)} collective-permute-done((f32[8,128]{1,0:T(8,128)S(1)}, f32[8,128]{1,0:T(8,128)S(1)}, u32[]{:S(2)}, u32[]{:S(2)}) %collective-permute-start.13) | collective-permute-done | bytes 4128 | tf_op jit(solution)/shard_map/ppermute | solution.py:992
  53.7 3.2 %collective-permute-start.14 = (f32[8,128]{1,0:T(8,128)S(1)}, f32[8,128]{1,0:T(8,128)S(1)}, u32[]{:S(2)}, u32[]{:S(2)}) collective-permute-start(f32[8,128]{1,0:T(8,128)S(1)} %add.3.s0), channel_id=1, source_target_pairs={{0,4},{1,5},{2,6},{3,7},{4,0},{5,1},{6,2},{7,3},{8,12},{9,13},{10,... | collective-permute-start | bytes 12296 | tf_op jit(solution)/shard_map/ppermute | solution.py:994
  57.5 2.6 %collective-permute-start.16 = (f32[8,128]{1,0:T(8,128)S(1)}, f32[8,128]{1,0:T(8,128)S(1)}, u32[]{:S(2)}, u32[]{:S(2)}) collective-permute-start(f32[8,128]{1,0:T(8,128)S(1)} %add.3.s0), channel_id=1, source_target_pairs={{0,6},{1,7},{2,0},{3,1},{4,2},{5,3},{6,4},{7,5},{8,14},{9,15},{10,... | collective-permute-start | bytes 12296 | tf_op jit(solution)/shard_map/ppermute | solution.py:994
  60.1 1.6 %collective-permute-done.15.s2 = f32[8,128]{1,0:T(8,128)S(1)} collective-permute-done((f32[8,128]{1,0:T(8,128)S(1)}, f32[8,128]{1,0:T(8,128)S(1)}, u32[]{:S(2)}, u32[]{:S(2)}) %collective-permute-start.15) | collective-permute-done | bytes 4128 | tf_op jit(solution)/shard_map/ppermute | solution.py:994
  61.7 1.6 %norm.1 = bf16[1024,1024]{1,0:T(8,128)(2,1)} custom-call(f32[1024,1024]{1,0:T(8,128)S(1)} %get-tuple-element.93.gated, f32[8,128]{1,0:T(8,128)S(1)} %add.3.s0, f32[8,128]{1,0:T(8,128)S(1)} %collective-permute-done.14.s1, f32[8,128]{1,0:T(8,128)S(1)} %collective-permute-done.15.s2, f32[8,128]{1,0:T(8,128)S(1)} %collective-permute-done.16.s3, ...), custom_call_target="tpu_custom_call" | custom-call | flops 1840000000 | bytes 5760000 | tf_op jit(solution)/shard_map/norm/pallas_call | solution.py:898
  (46 shorter events, 6.2 us)
Async XLA Ops:
  0.8 8.0 %collective-permute-start = (bf16[16,1280]{1,0:T(8,128)(2,1)S(1)}, bf16[16,1280]{1,0:T(8,128)(2,1)S(1)}, u32[]{:S(2)}, u32[]{:S(2)}) collective-permute-start(bf16[16,1280]{1,0:T(8,128)(2,1)S(1)} %last_rows.1), channel_id=1, source_target_pairs={{0,8},{8,16},{16,24},{24,32},{32,40},{40,48},{48,56},{56,64},{64,7... | collective-permute-start | bytes 122888 | tf_op jit(solution)/shard_map/ppermute | solution.py:923
  9.5 8.9 %collective-permute-start.1 = (f16[264,128]{1,0:T(8,128)(2,1)S(1)}, f16[264,128]{1,0:T(8,128)(2,1)S(1)}, u32[]{:S(2)}, u32[]{:S(2)}) collective-permute-start(f16[264,128]{1,0:T(8,128)(2,1)S(1)} %convert_element_type.36), channel_id=1, source_target_pairs={{0,8},{8,16},{16,24},{24,0},{32,40},{40,48},{48,56},{56,32},{64,72... | collective-permute-start | bytes 202760 | tf_op jit(solution)/shard_map/ppermute | solution.py:51
  10.6 7.8 %collective-permute-start.2 = (f16[264,128]{1,0:T(8,128)(2,1)S(1)}, f16[264,128]{1,0:T(8,128)(2,1)S(1)}, u32[]{:S(2)}, u32[]{:S(2)}) collective-permute-start(f16[264,128]{1,0:T(8,128)(2,1)S(1)} %convert_element_type.38), channel_id=1, source_target_pairs={{0,16},{8,24},{16,0},{24,8},{32,48},{40,56},{48,32},{56,40},{64,80... | collective-permute-start | bytes 202760 | tf_op jit(solution)/shard_map/ppermute | solution.py:51
  13.8 4.7 %collective-permute-start.3 = (f16[264,128]{1,0:T(8,128)(2,1)S(1)}, f16[264,128]{1,0:T(8,128)(2,1)S(1)}, u32[]{:S(2)}, u32[]{:S(2)}) collective-permute-start(f16[264,128]{1,0:T(8,128)(2,1)S(1)} %convert_element_type.40), channel_id=1, source_target_pairs={{0,24},{8,0},{16,8},{24,16},{32,56},{40,32},{48,40},{56,48},{64,88... | collective-permute-start | bytes 202760 | tf_op jit(solution)/shard_map/ppermute | solution.py:51
  14.7 4.2 %copy-start.1 = (f32[8,13,8]{1,2,0:T(8,128)S(1)}, f32[8,13,8]{1,2,0:T(8,128)}, u32[]{:S(2)}) copy-start(f32[8,13,8]{1,2,0:T(8,128)} %param.17) | copy-start | bytes 9988
  14.7 4.2 %copy-start.2 = (s32[16]{0:T(128)S(1)}, s32[16]{0:T(128)}, u32[]{:S(2)}) copy-start(s32[16]{0:T(128)} %kinds.5) | copy-start | bytes 196
  18.7 4.4 %collective-permute-start.4 = (f16[264,128]{1,0:T(8,128)(2,1)S(1)}, f16[264,128]{1,0:T(8,128)(2,1)S(1)}, u32[]{:S(2)}, u32[]{:S(2)}) collective-permute-start(f16[264,128]{1,0:T(8,128)(2,1)S(1)} %convert_element_type.42), channel_id=1, source_target_pairs={{0,32},{8,40},{16,48},{24,56},{32,0},{40,8},{48,16},{56,24},{64,96... | collective-permute-start | bytes 202760 | tf_op jit(solution)/shard_map/ppermute | solution.py:51
  21.1 11.4 %copy-start = (bf16[1024,1024]{1,0:T(8,128)(2,1)S(1)}, bf16[1024,1024]{1,0:T(8,128)(2,1)}, u32[]{:S(2)}) copy-start(bf16[1024,1024]{1,0:T(8,128)(2,1)} %refs_7_.3) | copy-start | bytes 6291460
  23.3 9.1 %collective-permute-start.5 = (f16[264,128]{1,0:T(8,128)(2,1)S(1)}, f16[264,128]{1,0:T(8,128)(2,1)S(1)}, u32[]{:S(2)}, u32[]{:S(2)}) collective-permute-start(f16[264,128]{1,0:T(8,128)(2,1)S(1)} %convert_element_type.44), channel_id=1, source_target_pairs={{0,64},{8,72},{16,80},{24,88},{32,96},{40,104},{48,112},{56,120},{... | collective-permute-start | bytes 202760 | tf_op jit(solution)/shard_map/ppermute | solution.py:51
  27.8 15.2 %collective-permute-start.7 = (bf16[768,128]{1,0:T(8,128)(2,1)S(1)}, bf16[768,128]{1,0:T(8,128)(2,1)S(1)}, u32[]{:S(2)}, u32[]{:S(2)}) collective-permute-start(bf16[768,128]{1,0:T(8,128)(2,1)S(1)} %get-tuple-element.84), channel_id=1, source_target_pairs={{0,8},{8,16},{16,24},{24,0},{32,40},{40,48},{48,56},{56,32},{64,72... | collective-permute-start | bytes 589832 | tf_op jit(solution)/shard_map/ppermute | solution.py:47
  29.4 15.7 %collective-permute-start.8 = (bf16[768,128]{1,0:T(8,128)(2,1)S(1)}, bf16[768,128]{1,0:T(8,128)(2,1)S(1)}, u32[]{:S(2)}, u32[]{:S(2)}) collective-permute-start(bf16[768,128]{1,0:T(8,128)(2,1)S(1)} %get-tuple-element.85), channel_id=1, source_target_pairs={{0,16},{8,24},{16,0},{24,8},{32,48},{40,56},{48,32},{56,40},{64,80... | collective-permute-start | bytes 589832 | tf_op jit(solution)/shard_map/ppermute | solution.py:47
  30.5 14.6 %collective-permute-start.9 = (bf16[768,128]{1,0:T(8,128)(2,1)S(1)}, bf16[768,128]{1,0:T(8,128)(2,1)S(1)}, u32[]{:S(2)}, u32[]{:S(2)}) collective-permute-start(bf16[768,128]{1,0:T(8,128)(2,1)S(1)} %get-tuple-element.86), channel_id=1, source_target_pairs={{0,24},{8,0},{16,8},{24,16},{32,56},{40,32},{48,40},{56,48},{64,88... | collective-permute-start | bytes 589832 | tf_op jit(solution)/shard_map/ppermute | solution.py:47
  36.3 4.9 %collective-permute-start.6 = (f16[264,128]{1,0:T(8,128)(2,1)S(1)}, f16[264,128]{1,0:T(8,128)(2,1)S(1)}, u32[]{:S(2)}, u32[]{:S(2)}) collective-permute-start(f16[264,128]{1,0:T(8,128)(2,1)S(1)} %convert_element_type.46), channel_id=1, source_target_pairs={{0,224},{8,232},{16,240},{24,248},{32,192},{40,200},{48,208},{56,2... | collective-permute-start | bytes 202760 | tf_op jit(solution)/shard_map/ppermute | solution.py:51
  41.3 7.7 %collective-permute-start.10 = (bf16[512,128]{1,0:T(8,128)(2,1)S(1)}, bf16[512,128]{1,0:T(8,128)(2,1)S(1)}, u32[]{:S(2)}, u32[]{:S(2)}) collective-permute-start(bf16[512,128]{1,0:T(8,128)(2,1)S(1)} %get-tuple-element.90), channel_id=1, source_target_pairs={{0,8},{8,16},{16,24},{24,0},{32,40},{40,48},{48,56},{56,32},{64,72... | collective-permute-start | bytes 393224 | tf_op jit(solution)/shard_map/ppermute | solution.py:47
  42.0 7.0 %collective-permute-start.11 = (bf16[512,128]{1,0:T(8,128)(2,1)S(1)}, bf16[512,128]{1,0:T(8,128)(2,1)S(1)}, u32[]{:S(2)}, u32[]{:S(2)}) collective-permute-start(bf16[512,128]{1,0:T(8,128)(2,1)S(1)} %get-tuple-element.91), channel_id=1, source_target_pairs={{0,16},{8,24},{16,0},{24,8},{32,48},{40,56},{48,32},{56,40},{64,80... | collective-permute-start | bytes 393224 | tf_op jit(solution)/shard_map/ppermute | solution.py:47
  43.0 6.9 %collective-permute-start.12 = (bf16[512,128]{1,0:T(8,128)(2,1)S(1)}, bf16[512,128]{1,0:T(8,128)(2,1)S(1)}, u32[]{:S(2)}, u32[]{:S(2)}) collective-permute-start(bf16[512,128]{1,0:T(8,128)(2,1)S(1)} %get-tuple-element.92), channel_id=1, source_target_pairs={{0,24},{8,0},{16,8},{24,16},{32,56},{40,32},{48,40},{56,48},{64,88... | collective-permute-start | bytes 393224 | tf_op jit(solution)/shard_map/ppermute | solution.py:47
  49.9 11.8 %copy-start.3 = (f32[1024]{0:T(1024)S(1)}, f32[1024]{0:T(1024)}, u32[]{:S(2)}) copy-start(f32[1024]{0:T(1024)} %param.19) | copy-start | bytes 12292
  52.4 1.3 %collective-permute-start.13 = (f32[8,128]{1,0:T(8,128)S(1)}, f32[8,128]{1,0:T(8,128)S(1)}, u32[]{:S(2)}, u32[]{:S(2)}) collective-permute-start(f32[8,128]{1,0:T(8,128)S(1)} %get-tuple-element.94), channel_id=1, source_target_pairs={{0,1},{1,0},{2,3},{3,2},{4,5},{5,4},{6,7},{7,6},{8,9},{9,8},{10,11... | collective-permute-start | bytes 12296 | tf_op jit(solution)/shard_map/ppermute | solution.py:992
  53.7 6.4 %collective-permute-start.14 = (f32[8,128]{1,0:T(8,128)S(1)}, f32[8,128]{1,0:T(8,128)S(1)}, u32[]{:S(2)}, u32[]{:S(2)}) collective-permute-start(f32[8,128]{1,0:T(8,128)S(1)} %add.3.s0), channel_id=1, source_target_pairs={{0,4},{1,5},{2,6},{3,7},{4,0},{5,1},{6,2},{7,3},{8,12},{9,13},{10,... | collective-permute-start | bytes 12296 | tf_op jit(solution)/shard_map/ppermute | solution.py:994
  56.8 4.8 %collective-permute-start.15 = (f32[8,128]{1,0:T(8,128)S(1)}, f32[8,128]{1,0:T(8,128)S(1)}, u32[]{:S(2)}, u32[]{:S(2)}) collective-permute-start(f32[8,128]{1,0:T(8,128)S(1)} %add.3.s0), channel_id=1, source_target_pairs={{0,2},{1,3},{2,4},{3,5},{4,6},{5,7},{6,0},{7,1},{8,10},{9,11},{10,... | collective-permute-start | bytes 12296 | tf_op jit(solution)/shard_map/ppermute | solution.py:994
  57.5 4.1 %collective-permute-start.16 = (f32[8,128]{1,0:T(8,128)S(1)}, f32[8,128]{1,0:T(8,128)S(1)}, u32[]{:S(2)}, u32[]{:S(2)}) collective-permute-start(f32[8,128]{1,0:T(8,128)S(1)} %add.3.s0), channel_id=1, source_target_pairs={{0,6},{1,7},{2,0},{3,1},{4,2},{5,3},{6,4},{7,5},{8,14},{9,15},{10,... | collective-permute-start | bytes 12296 | tf_op jit(solution)/shard_map/ppermute | solution.py:994

commit v7 on v6

--- a/solution.py
+++ b/solution.py
@@ -20,6 +20,7 @@
 WIDE = 256
 NEAR = 3
 FAR = 2
+LEVELS = 5 + NEAR + FAR
 TOP = 16384.0
 MESSAGE = PAIR * DIM + 8
 
@@ -503,8 +504,13 @@
     lax.fori_loop(0, length // TILE, one_tile, 0)
 
 
+def level_weight(table, kind, head, level, heads):
+    return table[(kind * heads + head) * LEVELS + level]
+
+
 def mix_head(head, table, kinds, inner, running_in, step_in, scores, ahead_in, emit):
     length = inner.shape[0]
+    heads = inner.shape[1] // DIM
     stretch = length // kinds.shape[0]
     each = WIDE // stretch
     row = lax.broadcasted_iota(jnp.int32, (stretch, TILE), 0)
@@ -523,7 +529,7 @@
         for part in range(each):
             here = i * each + part
             kind = kinds[here]
-            weight = [table[kind, head, level] for level in range(5)]
+            weight = [level_weight(table, kind, head, level, heads) for level in range(5)]
             band = slice(here * stretch, (here + 1) * stretch)
             ahead = ahead_in[band, lanes]
             pieces = []
@@ -556,13 +562,14 @@
     length = lifted_base.shape[0]
     stretch = length // kinds.shape[0]
     lanes = pl.ds(pl.multiple_of(head * DIM, DIM), DIM)
+    heads = lifted_base.shape[1] // DIM
     bands = []
     for here in range(tile * WIDE // stretch, (tile + 1) * WIDE // stretch):
         kind = kinds[here]
         base = lifted_base[here * stretch : (here + 1) * stretch, lanes]
         bands.append(
             jnp.concatenate(
-                [(base * table[kind, head, level]).astype(BF16) for level in levels], axis=1
+                [(base * level_weight(table, kind, head, level, heads)).astype(BF16) for level in levels], axis=1
             )
         )
     return jnp.dot(jnp.concatenate(bands, axis=0), held[head], preferred_element_type=F32)
@@ -598,29 +605,51 @@
 
 def turn_kernel(first, count, upper, *refs):
     table, kinds, inner, running_in, step_in, scores, ahead_in, gate = refs[:8]
-    out, gates = refs[-2:]
+    out, gates, table_here, kinds_here, sems = refs[-5:]
     _, z = block_place()
 
     @pl.when((z >= ZS // 2) == upper)
     def _():
+        copies = [
+            pltpu.make_async_copy(table, table_here, sems.at[0]),
+            pltpu.make_async_copy(kinds, kinds_here, sems.at[1]),
+        ]
+        for copy in copies:
+            copy.start()
+        gates_kernel(gate, gates)
+        for copy in copies:
+            copy.wait()
         mix_kernel(
-            first, count, table, kinds, inner, running_in, step_in, scores, ahead_in, out
+            first,
+            count,
+            table_here,
+            kinds_here,
+            inner,
+            running_in,
+            step_in,
+            scores,
+            ahead_in,
+            out,
         )
-        gates_kernel(gate, gates)
 
 
 def turn_part(first, count, upper, earlier, table, kinds, inner, running, step, scores, ahead, gate):
     length, width = inner.shape
     return pl.pallas_call(
         functools.partial(turn_kernel, first, count, upper),
-        in_specs=[SMEM, SMEM] + [VMEM] * (6 + len(earlier)),
+        in_specs=[HBM, HBM] + [VMEM] * (6 + len(earlier)),
         out_specs=[VMEM] * 2,
         out_shape=[pltpu.VMEM((length, count * DIM), F32), pltpu.VMEM(gate.shape, F32)],
+        scratch_shapes=[
+            pltpu.SMEM(table.shape, F32),
+            pltpu.SMEM(kinds.shape, jnp.int32),
+            DMA((2,)),
+        ],
         input_output_aliases={8: 0, 9: 1} if earlier else {},
         compiler_params=params(8),
         cost_estimate=cost(0.6 * count + 1.2 if upper else 0.2),
         name="turn_part",
-    )(table, kinds, inner, running, step, scores, ahead, gate, *earlier)
+    )(in_hbm(table), in_hbm(kinds), inner, running, step, scores, ahead, gate, *earlier)
 
 
 def local_kernel(
@@ -927,7 +956,7 @@
         mixer_input, state_input, conv_inner, conv_state, step_raw.T, decay_rate
     )
     inner, keys, *parts = finish(halo, first_rows, scale, last, taps, inner, keys, parts)
-    table = jnp.transpose(level_table, (0, 2, 1))
+    table = jnp.transpose(level_table, (0, 2, 1))[:, :, :LEVELS].reshape(-1)
     moved = {
         k: sent(parts[k - 1], lambda z, x, k=k: (z, (x + k) % XS)) for k in (2, 1, 3)
     }

time: 63.8 us -> 62.3 us (0.976)
  Pallas kernels: 25 us -> 21.7 us
  waiting for transfers between devices: 6.87 us -> 8.47 us
    pallas_call x2, Pallas kernels: 4.79 us -> 2.84 us  [turn_part(): pl.pallas_call(functools.partial(turn_kernel, first, count, upper), in_sp...]
    ppermute x6, waiting for transfers between devices: 2.77 us -> 4.29 us  [sent(): lax.ppermute(message.astype(jnp.float16), 'seq', seq_perm(move)).astype(F32)]
  transfers between devices with their start and end apart: 17 -> 17, of which waited for: 6 -> 7; matrix products, arithmetic and copies ran while one was open for 0% -> 0% of each run, Pallas kernels for 30% -> 26%
where the time goes in v7:
time: 62.3 us; the launch traced here: 61.9 us
  starting transfers between devices  30.9 us (50%)
  Pallas kernels  21.7 us (35%)
  waiting for transfers between devices  8.47 us (14%)
    ppermute x6, starting transfers between devices, sent(): lax.ppermute(message.astype(jnp.float16), 'seq', seq_perm(move)).astype(F32)  12.5 us
    ppermute x6, starting transfers between devices, along_x(): lax.ppermute(value, 'seq', seq_perm(lambda z, x: (z, (x + step) % XS)))  8.52 us
    ppermute x3, starting transfers between devices, local(): lax.ppermute(squares, 'head', head_perm(lambda y, core, k=k: ((y + k) % Y...  6.43 us
    ppermute x6, waiting for transfers between devices, sent(): lax.ppermute(message.astype(jnp.float16), 'seq', seq_perm(move)).astype(F32)  4.29 us
    pallas_call x1, Pallas kernels, prepare(): pl.pallas_call(prepare_kernel, in_specs=[HBM] * 6, out_specs=[VMEM] * (7...  4.13 us
    pallas_call x1, Pallas kernels, shared_part(): pl.pallas_call(shared_kernel, in_specs=[HBM, HBM] + [VMEM] * 7, out_specs...  3.71 us
    ppermute x1, starting transfers between devices, local(): lax.ppermute(last_rows(mixer_input, state_input), 'seq', [(i, i + 1) for...  3.4 us
    pallas_call x1, Pallas kernels, local_part(): pl.pallas_call(functools.partial(local_kernel, len(mixed)), in_specs=[SME...  3.37 us
  transfers between devices with their start and end apart: 17, of which 7 were waited for; matrix products, arithmetic and copies ran while one was open for 0% of the time, Pallas kernels for 26%

profile of v7, /device:TPU:32, one launch (start us, length us, event | category | flops | bytes accessed | tf_op | source)
XLA Modules:
  0.0 61.9 jit_solution(18215185567908834477)
XLA Ops:
  0.8 3.4 %collective-permute-start = (bf16[16,1280]{1,0:T(8,128)(2,1)S(1)}, bf16[16,1280]{1,0:T(8,128)(2,1)S(1)}, u32[]{:S(2)}, u32[]{:S(2)}) collective-permute-start(bf16[16,1280]{1,0:T(8,128)(2,1)S(1)} %last_rows.1), channel_id=1, source_target_pairs={{0,8},{8,16},{16,24},{24,32},{32,40},{40,48},{48,56},{56,64},{64,7... | collective-permute-start | bytes 122888 | tf_op jit(solution)/shard_map/ppermute | solution.py:952
  4.2 4.1 %prepare.1 = (bf16[1024,1024]{1,0:T(8,128)(2,1)S(1)}, bf16[1024,128]{1,0:T(8,128)(2,1)S(1)}, f32[8,1024]{1,0:T(8,128)S(1)}, f32[8,1024]{1,0:T(8,128)S(1)}, f32[8...) custom-call(bf16[1024,1024]{1,0:T(8,128)(2,1)} %mixer.5, ...), custom_call_target="tpu_custom_call" | custom-call | flops 5175000064 | bytes 16200000 | tf_op jit(solution)/shard_map/prepare/pallas_call | solution.py:269
  9.5 1.3 %collective-permute-start.1 = (f16[264,128]{1,0:T(8,128)(2,1)S(1)}, f16[264,128]{1,0:T(8,128)(2,1)S(1)}, u32[]{:S(2)}, u32[]{:S(2)}) collective-permute-start(f16[264,128]{1,0:T(8,128)(2,1)S(1)} %convert_element_type.36), channel_id=1, source_target_pairs={{0,8},{8,16},{16,24},{24,0},{32,40},{40,48},{48,56},{56,32},{64,72... | collective-permute-start | bytes 202760 | tf_op jit(solution)/shard_map/ppermute | solution.py:52
  10.8 3.2 %collective-permute-start.2 = (f16[264,128]{1,0:T(8,128)(2,1)S(1)}, f16[264,128]{1,0:T(8,128)(2,1)S(1)}, u32[]{:S(2)}, u32[]{:S(2)}) collective-permute-start(f16[264,128]{1,0:T(8,128)(2,1)S(1)} %convert_element_type.38), channel_id=1, source_target_pairs={{0,16},{8,24},{16,0},{24,8},{32,48},{40,56},{48,32},{56,40},{64,80... | collective-permute-start | bytes 202760 | tf_op jit(solution)/shard_map/ppermute | solution.py:52
  14.0 0.9 %collective-permute-start.3 = (f16[264,128]{1,0:T(8,128)(2,1)S(1)}, f16[264,128]{1,0:T(8,128)(2,1)S(1)}, u32[]{:S(2)}, u32[]{:S(2)}) collective-permute-start(f16[264,128]{1,0:T(8,128)(2,1)S(1)} %convert_element_type.40), channel_id=1, source_target_pairs={{0,24},{8,0},{16,8},{24,16},{32,56},{40,32},{48,40},{56,48},{64,88... | collective-permute-start | bytes 202760 | tf_op jit(solution)/shard_map/ppermute | solution.py:52
  14.8 3.7 %shared_part.1 = (bf16[1024,1024]{1,0:T(8,128)(2,1)S(1)}, f32[1024,1024]{1,0:T(8,128)S(1)}, f32[1024,1024]{1,0:T(8,128)S(1)}, f32[1024,1024]{1,0:T(8,128)S(1)}, f32[264,128]{1,0:T(8,128)S(1)}) custom-call(bf16[1024,1024]{1,0:T(8,128)(2,1)} %mixer.5, bf16[1024,256]{1,0:T(8,128)(2,1)} %state.5, ...), custom_call_target="tpu_custom_call", output_to_operand_aliasing={{0}: (8, {})} | custom-call | flops 3910000128 | bytes 12240000 | tf_op jit(solution)/shard_map/shared_part/pallas_call | solution.py:468
  19.1 1.7 %mix_part.1.rest_0_ = f32[1024,256]{1,0:T(8,128)S(1)} custom-call(f32[640]{0:T(1024)S(1)} %reshape.3.table.refs_0_, s32[16]{0:T(128)S(1)} %copy-done.3, bf16[1024,1024]{1,0:T(8,128)(2,1)S(1)} %get-tuple-element.62.inner.refs_2_, f32[8,1024]{1,0:T(8,128)S(1)} %get-tuple-element.53.running_in.refs_3_, f32[8,1024]{1,0:T(8,128)S(1)} %get-tuple-element.74.step_in.refs_4_, ...), custom_call_target="tpu_custom_call" | custom-call | flops 2300000000 | bytes 7200000 | tf_op jit(solution)/shard_map/mix_part/pallas_call | solution.py:595
  20.8 2.4 %collective-permute-done.4 = f16[264,128]{1,0:T(8,128)(2,1)S(1)} collective-permute-done((f16[264,128]{1,0:T(8,128)(2,1)S(1)}, f16[264,128]{1,0:T(8,128)(2,1)S(1)}, u32[]{:S(2)}, u32[]{:S(2)}) %collective-permute-start.4) | collective-permute-done | bytes 67616 | tf_op jit(solution)/shard_map/ppermute | solution.py:52
  23.4 4.3 %collective-permute-start.5 = (f16[264,128]{1,0:T(8,128)(2,1)S(1)}, f16[264,128]{1,0:T(8,128)(2,1)S(1)}, u32[]{:S(2)}, u32[]{:S(2)}) collective-permute-start(f16[264,128]{1,0:T(8,128)(2,1)S(1)} %convert_element_type.44), channel_id=1, source_target_pairs={{0,64},{8,72},{16,80},{24,88},{32,96},{40,104},{48,112},{56,120},{... | collective-permute-start | bytes 202760 | tf_op jit(solution)/shard_map/ppermute | solution.py:52
  28.0 1.6 %collective-permute-start.7 = (bf16[768,128]{1,0:T(8,128)(2,1)S(1)}, bf16[768,128]{1,0:T(8,128)(2,1)S(1)}, u32[]{:S(2)}, u32[]{:S(2)}) collective-permute-start(bf16[768,128]{1,0:T(8,128)(2,1)S(1)} %get-tuple-element.84), channel_id=1, source_target_pairs={{0,8},{8,16},{16,24},{24,0},{32,40},{40,48},{48,56},{56,32},{64,72... | collective-permute-start | bytes 589832 | tf_op jit(solution)/shard_map/ppermute | solution.py:48
  29.6 1.1 %collective-permute-start.8 = (bf16[768,128]{1,0:T(8,128)(2,1)S(1)}, bf16[768,128]{1,0:T(8,128)(2,1)S(1)}, u32[]{:S(2)}, u32[]{:S(2)}) collective-permute-start(bf16[768,128]{1,0:T(8,128)(2,1)S(1)} %get-tuple-element.85), channel_id=1, source_target_pairs={{0,16},{8,24},{16,0},{24,8},{32,48},{40,56},{48,32},{56,40},{64,80... | collective-permute-start | bytes 589832 | tf_op jit(solution)/shard_map/ppermute | solution.py:48
  30.7 1.8 %collective-permute-start.9 = (bf16[768,128]{1,0:T(8,128)(2,1)S(1)}, bf16[768,128]{1,0:T(8,128)(2,1)S(1)}, u32[]{:S(2)}, u32[]{:S(2)}) collective-permute-start(bf16[768,128]{1,0:T(8,128)(2,1)S(1)} %get-tuple-element.86), channel_id=1, source_target_pairs={{0,24},{8,0},{16,8},{24,16},{32,56},{40,32},{48,40},{56,48},{64,88... | collective-permute-start | bytes 589832 | tf_op jit(solution)/shard_map/ppermute | solution.py:48
  32.7 2.8 %turn_part.2 = (f32[1024,512]{1,0:T(8,128)S(1)}, f32[1024,1024]{1,0:T(8,128)S(1)}) custom-call(f32[640]{0:T(1024)} %copy-done.1, s32[16]{0:T(128)} %kinds.5, bf16[1024,1024]{1,0:T(8,128)(2,1)S(1)} %get-tuple-element.62.inner.refs_2_, f32[8,1024]{1,0:T(8,128)S(1)} %get-tuple-element.53.running_in.refs_3_, f32[8,1024]{1,0:T(8,128)S(1)} %get-tuple-element.74.step_in.refs_4_, ...), custom_call_target="tpu_custom_call" | custom-call | flops 230000000 | bytes 720000 | tf_op jit(solution)/shard_map/turn_part/pallas_call | solution.py:638
  35.6 2.7 %collective-permute-start.6 = (f16[264,128]{1,0:T(8,128)(2,1)S(1)}, f16[264,128]{1,0:T(8,128)(2,1)S(1)}, u32[]{:S(2)}, u32[]{:S(2)}) collective-permute-start(f16[264,128]{1,0:T(8,128)(2,1)S(1)} %convert_element_type.46), channel_id=1, source_target_pairs={{0,224},{8,232},{16,240},{24,248},{32,192},{40,200},{48,208},{56,2... | collective-permute-start | bytes 202760 | tf_op jit(solution)/shard_map/ppermute | solution.py:52
  38.3 1.9 %collective-permute-done.6 = f16[264,128]{1,0:T(8,128)(2,1)S(1)} collective-permute-done((f16[264,128]{1,0:T(8,128)(2,1)S(1)}, f16[264,128]{1,0:T(8,128)(2,1)S(1)}, u32[]{:S(2)}, u32[]{:S(2)}) %collective-permute-start.6) | collective-permute-done | bytes 67616 | tf_op jit(solution)/shard_map/ppermute | solution.py:52
  41.0 1.2 %collective-permute-start.11 = (bf16[512,128]{1,0:T(8,128)(2,1)S(1)}, bf16[512,128]{1,0:T(8,128)(2,1)S(1)}, u32[]{:S(2)}, u32[]{:S(2)}) collective-permute-start(bf16[512,128]{1,0:T(8,128)(2,1)S(1)} %get-tuple-element.91), channel_id=1, source_target_pairs={{0,16},{8,24},{16,0},{24,8},{32,48},{40,56},{48,32},{56,40},{64,80... | collective-permute-start | bytes 393224 | tf_op jit(solution)/shard_map/ppermute | solution.py:48
  42.1 2.2 %collective-permute-start.12 = (bf16[512,128]{1,0:T(8,128)(2,1)S(1)}, bf16[512,128]{1,0:T(8,128)(2,1)S(1)}, u32[]{:S(2)}, u32[]{:S(2)}) collective-permute-start(bf16[512,128]{1,0:T(8,128)(2,1)S(1)} %get-tuple-element.92), channel_id=1, source_target_pairs={{0,24},{8,0},{16,8},{24,16},{32,56},{40,32},{48,40},{56,48},{64,88... | collective-permute-start | bytes 393224 | tf_op jit(solution)/shard_map/ppermute | solution.py:48
  44.3 3.4 %local_part.1.local = f32[1024,1024]{1,0:T(8,128)S(1)} custom-call(f32[640]{0:T(1024)S(1)} %copy-done.2, s32[16]{0:T(128)S(1)} %copy-done.4, bf16[1024,1024]{1,0:T(8,128)(2,1)S(1)} %get-tuple-element.62.inner.refs_2_, f32[8,1024]{1,0:T(8,128)S(1)} %get-tuple-element.53.running_in.refs_3_, f32[8,1024]{1,0:T(8,128)S(1)} %get-tuple-element.74.step_in.refs_4_, ...), custom_call_target="tpu_custom_call" | custom-call | flops 4369999872 | bytes 13680000 | tf_op jit(solution)/shard_map/local_part/pallas_call | solution.py:709
  48.8 2.0 %far_part.1 = (f32[1024,1024]{1,0:T(8,128)S(1)}, f32[8,128]{1,0:T(8,128)S(1)}) custom-call(f32[640]{0:T(1024)S(1)} %copy-done.2, s32[16]{0:T(128)S(1)} %copy-done.4, f32[1024,1024]{1,0:T(8,128)S(1)} %local_part.1.local, f32[1024,1024]{1,0:T(8,128)S(1)} %get-tuple-element.87.gates, f32[1024,1024]{1,0:T(8,128)S(1)} %get-tuple-element.66.lifted_base, ...), custom_call_target="tpu_custom_call" | custom-call | flops 4024999936 | bytes 12600000 | tf_op jit(solution)/shard_map/far_part/pallas_call | solution.py:897
  51.0 1.2 %collective-permute-done.13 = f32[8,128]{1,0:T(8,128)S(1)} collective-permute-done((f32[8,128]{1,0:T(8,128)S(1)}, f32[8,128]{1,0:T(8,128)S(1)}, u32[]{:S(2)}, u32[]{:S(2)}) %collective-permute-start.13) | collective-permute-done | bytes 4128 | tf_op jit(solution)/shard_map/ppermute | solution.py:1021
  52.1 3.2 %collective-permute-start.14 = (f32[8,128]{1,0:T(8,128)S(1)}, f32[8,128]{1,0:T(8,128)S(1)}, u32[]{:S(2)}, u32[]{:S(2)}) collective-permute-start(f32[8,128]{1,0:T(8,128)S(1)} %add.3.s0), channel_id=1, source_target_pairs={{0,4},{1,5},{2,6},{3,7},{4,0},{5,1},{6,2},{7,3},{8,12},{9,13},{10,... | collective-permute-start | bytes 12296 | tf_op jit(solution)/shard_map/ppermute | solution.py:1023
  56.0 2.6 %collective-permute-start.16 = (f32[8,128]{1,0:T(8,128)S(1)}, f32[8,128]{1,0:T(8,128)S(1)}, u32[]{:S(2)}, u32[]{:S(2)}) collective-permute-start(f32[8,128]{1,0:T(8,128)S(1)} %add.3.s0), channel_id=1, source_target_pairs={{0,6},{1,7},{2,0},{3,1},{4,2},{5,3},{6,4},{7,5},{8,14},{9,15},{10,... | collective-permute-start | bytes 12296 | tf_op jit(solution)/shard_map/ppermute | solution.py:1023
  58.6 1.6 %collective-permute-done.15.s2 = f32[8,128]{1,0:T(8,128)S(1)} collective-permute-done((f32[8,128]{1,0:T(8,128)S(1)}, f32[8,128]{1,0:T(8,128)S(1)}, u32[]{:S(2)}, u32[]{:S(2)}) %collective-permute-start.15) | collective-permute-done | bytes 4128 | tf_op jit(solution)/shard_map/ppermute | solution.py:1023
  60.2 1.6 %norm.1 = bf16[1024,1024]{1,0:T(8,128)(2,1)} custom-call(f32[1024,1024]{1,0:T(8,128)S(1)} %get-tuple-element.93.gated, f32[8,128]{1,0:T(8,128)S(1)} %add.3.s0, f32[8,128]{1,0:T(8,128)S(1)} %collective-permute-done.14.s1, f32[8,128]{1,0:T(8,128)S(1)} %collective-permute-done.15.s2, f32[8,128]{1,0:T(8,128)S(1)} %collective-permute-done.16.s3, ...), custom_call_target="tpu_custom_call" | custom-call | flops 1840000000 | bytes 5760000 | tf_op jit(solution)/shard_map/norm/pallas_call | solution.py:927
  (53 shorter events, 5.7 us)
Async XLA Ops:
  0.8 8.0 %collective-permute-start = (bf16[16,1280]{1,0:T(8,128)(2,1)S(1)}, bf16[16,1280]{1,0:T(8,128)(2,1)S(1)}, u32[]{:S(2)}, u32[]{:S(2)}) collective-permute-start(bf16[16,1280]{1,0:T(8,128)(2,1)S(1)} %last_rows.1), channel_id=1, source_target_pairs={{0,8},{8,16},{16,24},{24,32},{32,40},{40,48},{48,56},{56,64},{64,7... | collective-permute-start | bytes 122888 | tf_op jit(solution)/shard_map/ppermute | solution.py:952
  4.2 4.2 %copy-start.6 = (f32[8,13,8]{1,2,0:T(8,128)S(1)}, f32[8,13,8]{1,2,0:T(8,128)}, u32[]{:S(2)}) copy-start(f32[8,13,8]{1,2,0:T(8,128)} %param.17) | copy-start | bytes 9988
  8.5 10.6 %copy-start.1 = (f32[640]{0:T(1024)}, f32[640]{0:T(1024)S(1)}, u32[]{:S(2)}) copy-start(f32[640]{0:T(1024)S(1)} %reshape.3.table.refs_0_) | copy-start | bytes 7684
  9.5 9.1 %collective-permute-start.1 = (f16[264,128]{1,0:T(8,128)(2,1)S(1)}, f16[264,128]{1,0:T(8,128)(2,1)S(1)}, u32[]{:S(2)}, u32[]{:S(2)}) collective-permute-start(f16[264,128]{1,0:T(8,128)(2,1)S(1)} %convert_element_type.36), channel_id=1, source_target_pairs={{0,8},{8,16},{16,24},{24,0},{32,40},{40,48},{48,56},{56,32},{64,72... | collective-permute-start | bytes 202760 | tf_op jit(solution)/shard_map/ppermute | solution.py:52
  10.8 7.8 %collective-permute-start.2 = (f16[264,128]{1,0:T(8,128)(2,1)S(1)}, f16[264,128]{1,0:T(8,128)(2,1)S(1)}, u32[]{:S(2)}, u32[]{:S(2)}) collective-permute-start(f16[264,128]{1,0:T(8,128)(2,1)S(1)} %convert_element_type.38), channel_id=1, source_target_pairs={{0,16},{8,24},{16,0},{24,8},{32,48},{40,56},{48,32},{56,40},{64,80... | collective-permute-start | bytes 202760 | tf_op jit(solution)/shard_map/ppermute | solution.py:52
  14.0 4.7 %collective-permute-start.3 = (f16[264,128]{1,0:T(8,128)(2,1)S(1)}, f16[264,128]{1,0:T(8,128)(2,1)S(1)}, u32[]{:S(2)}, u32[]{:S(2)}) collective-permute-start(f16[264,128]{1,0:T(8,128)(2,1)S(1)} %convert_element_type.40), channel_id=1, source_target_pairs={{0,24},{8,0},{16,8},{24,16},{32,56},{40,32},{48,40},{56,48},{64,88... | collective-permute-start | bytes 202760 | tf_op jit(solution)/shard_map/ppermute | solution.py:52
  14.8 4.2 %copy-start.3 = (s32[16]{0:T(128)S(1)}, s32[16]{0:T(128)}, u32[]{:S(2)}) copy-start(s32[16]{0:T(128)} %kinds.5) | copy-start | bytes 196
  18.9 4.4 %collective-permute-start.4 = (f16[264,128]{1,0:T(8,128)(2,1)S(1)}, f16[264,128]{1,0:T(8,128)(2,1)S(1)}, u32[]{:S(2)}, u32[]{:S(2)}) collective-permute-start(f16[264,128]{1,0:T(8,128)(2,1)S(1)} %convert_element_type.42), channel_id=1, source_target_pairs={{0,32},{8,40},{16,48},{24,56},{32,0},{40,8},{48,16},{56,24},{64,96... | collective-permute-start | bytes 202760 | tf_op jit(solution)/shard_map/ppermute | solution.py:52
  20.8 11.9 %copy-start = (bf16[1024,1024]{1,0:T(8,128)(2,1)S(1)}, bf16[1024,1024]{1,0:T(8,128)(2,1)}, u32[]{:S(2)}) copy-start(bf16[1024,1024]{1,0:T(8,128)(2,1)} %refs_7_.3) | copy-start | bytes 6291460
  23.4 9.1 %collective-permute-start.5 = (f16[264,128]{1,0:T(8,128)(2,1)S(1)}, f16[264,128]{1,0:T(8,128)(2,1)S(1)}, u32[]{:S(2)}, u32[]{:S(2)}) collective-permute-start(f16[264,128]{1,0:T(8,128)(2,1)S(1)} %convert_element_type.44), channel_id=1, source_target_pairs={{0,64},{8,72},{16,80},{24,88},{32,96},{40,104},{48,112},{56,120},{... | collective-permute-start | bytes 202760 | tf_op jit(solution)/shard_map/ppermute | solution.py:52
  28.0 14.2 %collective-permute-start.7 = (bf16[768,128]{1,0:T(8,128)(2,1)S(1)}, bf16[768,128]{1,0:T(8,128)(2,1)S(1)}, u32[]{:S(2)}, u32[]{:S(2)}) collective-permute-start(bf16[768,128]{1,0:T(8,128)(2,1)S(1)} %get-tuple-element.84), channel_id=1, source_target_pairs={{0,8},{8,16},{16,24},{24,0},{32,40},{40,48},{48,56},{56,32},{64,72... | collective-permute-start | bytes 589832 | tf_op jit(solution)/shard_map/ppermute | solution.py:48
  29.6 14.7 %collective-permute-start.8 = (bf16[768,128]{1,0:T(8,128)(2,1)S(1)}, bf16[768,128]{1,0:T(8,128)(2,1)S(1)}, u32[]{:S(2)}, u32[]{:S(2)}) collective-permute-start(bf16[768,128]{1,0:T(8,128)(2,1)S(1)} %get-tuple-element.85), channel_id=1, source_target_pairs={{0,16},{8,24},{16,0},{24,8},{32,48},{40,56},{48,32},{56,40},{64,80... | collective-permute-start | bytes 589832 | tf_op jit(solution)/shard_map/ppermute | solution.py:48
  30.7 13.6 %collective-permute-start.9 = (bf16[768,128]{1,0:T(8,128)(2,1)S(1)}, bf16[768,128]{1,0:T(8,128)(2,1)S(1)}, u32[]{:S(2)}, u32[]{:S(2)}) collective-permute-start(bf16[768,128]{1,0:T(8,128)(2,1)S(1)} %get-tuple-element.86), channel_id=1, source_target_pairs={{0,24},{8,0},{16,8},{24,16},{32,56},{40,32},{48,40},{56,48},{64,88... | collective-permute-start | bytes 589832 | tf_op jit(solution)/shard_map/ppermute | solution.py:48
  35.6 8.7 %copy-start.2 = (f32[640]{0:T(1024)S(1)}, f32[640]{0:T(1024)}, u32[]{:S(2)}) copy-start(f32[640]{0:T(1024)} %copy-done.1) | copy-start | bytes 7684
  35.6 8.7 %copy-start.4 = (s32[16]{0:T(128)S(1)}, s32[16]{0:T(128)}, u32[]{:S(2)}) copy-start(s32[16]{0:T(128)} %kinds.5) | copy-start | bytes 196
  35.6 4.6 %collective-permute-start.6 = (f16[264,128]{1,0:T(8,128)(2,1)S(1)}, f16[264,128]{1,0:T(8,128)(2,1)S(1)}, u32[]{:S(2)}, u32[]{:S(2)}) collective-permute-start(f16[264,128]{1,0:T(8,128)(2,1)S(1)} %convert_element_type.46), channel_id=1, source_target_pairs={{0,224},{8,232},{16,240},{24,248},{32,192},{40,200},{48,208},{56,2... | collective-permute-start | bytes 202760 | tf_op jit(solution)/shard_map/ppermute | solution.py:52
  40.3 7.7 %collective-permute-start.10 = (bf16[512,128]{1,0:T(8,128)(2,1)S(1)}, bf16[512,128]{1,0:T(8,128)(2,1)S(1)}, u32[]{:S(2)}, u32[]{:S(2)}) collective-permute-start(bf16[512,128]{1,0:T(8,128)(2,1)S(1)} %get-tuple-element.90), channel_id=1, source_target_pairs={{0,8},{8,16},{16,24},{24,0},{32,40},{40,48},{48,56},{56,32},{64,72... | collective-permute-start | bytes 393224 | tf_op jit(solution)/shard_map/ppermute | solution.py:48
  41.0 7.0 %collective-permute-start.11 = (bf16[512,128]{1,0:T(8,128)(2,1)S(1)}, bf16[512,128]{1,0:T(8,128)(2,1)S(1)}, u32[]{:S(2)}, u32[]{:S(2)}) collective-permute-start(bf16[512,128]{1,0:T(8,128)(2,1)S(1)} %get-tuple-element.91), channel_id=1, source_target_pairs={{0,16},{8,24},{16,0},{24,8},{32,48},{40,56},{48,32},{56,40},{64,80... | collective-permute-start | bytes 393224 | tf_op jit(solution)/shard_map/ppermute | solution.py:48
  42.1 6.7 %collective-permute-start.12 = (bf16[512,128]{1,0:T(8,128)(2,1)S(1)}, bf16[512,128]{1,0:T(8,128)(2,1)S(1)}, u32[]{:S(2)}, u32[]{:S(2)}) collective-permute-start(bf16[512,128]{1,0:T(8,128)(2,1)S(1)} %get-tuple-element.92), channel_id=1, source_target_pairs={{0,24},{8,0},{16,8},{24,16},{32,56},{40,32},{48,40},{56,48},{64,88... | collective-permute-start | bytes 393224 | tf_op jit(solution)/shard_map/ppermute | solution.py:48
  48.8 11.3 %copy-start.5 = (f32[1024]{0:T(1024)S(1)}, f32[1024]{0:T(1024)}, u32[]{:S(2)}) copy-start(f32[1024]{0:T(1024)} %param.19) | copy-start | bytes 12292
  50.9 1.3 %collective-permute-start.13 = (f32[8,128]{1,0:T(8,128)S(1)}, f32[8,128]{1,0:T(8,128)S(1)}, u32[]{:S(2)}, u32[]{:S(2)}) collective-permute-start(f32[8,128]{1,0:T(8,128)S(1)} %get-tuple-element.94), channel_id=1, source_target_pairs={{0,1},{1,0},{2,3},{3,2},{4,5},{5,4},{6,7},{7,6},{8,9},{9,8},{10,11... | collective-permute-start | bytes 12296 | tf_op jit(solution)/shard_map/ppermute | solution.py:1021
  52.1 6.4 %collective-permute-start.14 = (f32[8,128]{1,0:T(8,128)S(1)}, f32[8,128]{1,0:T(8,128)S(1)}, u32[]{:S(2)}, u32[]{:S(2)}) collective-permute-start(f32[8,128]{1,0:T(8,128)S(1)} %add.3.s0), channel_id=1, source_target_pairs={{0,4},{1,5},{2,6},{3,7},{4,0},{5,1},{6,2},{7,3},{8,12},{9,13},{10,... | collective-permute-start | bytes 12296 | tf_op jit(solution)/shard_map/ppermute | solution.py:1023
  55.3 4.8 %collective-permute-start.15 = (f32[8,128]{1,0:T(8,128)S(1)}, f32[8,128]{1,0:T(8,128)S(1)}, u32[]{:S(2)}, u32[]{:S(2)}) collective-permute-start(f32[8,128]{1,0:T(8,128)S(1)} %add.3.s0), channel_id=1, source_target_pairs={{0,2},{1,3},{2,4},{3,5},{4,6},{5,7},{6,0},{7,1},{8,10},{9,11},{10,... | collective-permute-start | bytes 12296 | tf_op jit(solution)/shard_map/ppermute | solution.py:1023
  56.0 4.1 %collective-permute-start.16 = (f32[8,128]{1,0:T(8,128)S(1)}, f32[8,128]{1,0:T(8,128)S(1)}, u32[]{:S(2)}, u32[]{:S(2)}) collective-permute-start(f32[8,128]{1,0:T(8,128)S(1)} %add.3.s0), channel_id=1, source_target_pairs={{0,6},{1,7},{2,0},{3,1},{4,2},{5,3},{6,4},{7,5},{8,14},{9,15},{10,... | collective-permute-start | bytes 12296 | tf_op jit(solution)/shard_map/ppermute | solution.py:1023

commit v8 on v7

--- a/solution.py
+++ b/solution.py
@@ -558,21 +558,30 @@
         )
 
 
-def lift(table, kinds, lifted_base, head, tile, levels, held, WIDE=WIDE):
+def lift_operand(table, kinds, lifted_base, head, tile, levels, size):
     length = lifted_base.shape[0]
     stretch = length // kinds.shape[0]
     lanes = pl.ds(pl.multiple_of(head * DIM, DIM), DIM)
     heads = lifted_base.shape[1] // DIM
     bands = []
-    for here in range(tile * WIDE // stretch, (tile + 1) * WIDE // stretch):
+    for here in range(tile * size // stretch, (tile + 1) * size // stretch):
         kind = kinds[here]
         base = lifted_base[here * stretch : (here + 1) * stretch, lanes]
         bands.append(
             jnp.concatenate(
-                [(base * level_weight(table, kind, head, level, heads)).astype(BF16) for level in levels], axis=1
+                [
+                    (base * level_weight(table, kind, head, level, heads)).astype(BF16)
+                    for level in levels
+                ],
+                axis=1,
             )
         )
-    return jnp.dot(jnp.concatenate(bands, axis=0), held[head], preferred_element_type=F32)
+    return jnp.concatenate(bands, axis=0)
+
+
+def lift(table, kinds, lifted_base, head, tile, levels, held):
+    operand = lift_operand(table, kinds, lifted_base, head, tile, levels, WIDE)
+    return jnp.dot(operand, held[head], preferred_element_type=F32)
 
 
 def mix_kernel(first, count, table, kinds, inner, running_in, step_in, scores, ahead_in, out):
@@ -666,7 +675,7 @@
 ):
     mixed = rest[:done]
     nears = rest[done : done + XS]
-    out, held = rest[done + XS :]
+    out, lifted_far, held = rest[done + XS :]
     x, _ = block_place()
     length, width = inner.shape
     heads = width // DIM
@@ -701,6 +710,11 @@
         return carry
 
     lax.fori_loop(head, heads, one_head, 0, unroll=2)
+    far_levels = range(5 + NEAR, 5 + NEAR + FAR)
+    for head in range(heads):
+        lifted_far[:, head * FAR * DIM : (head + 1) * FAR * DIM] = lift_operand(
+            table, kinds, lifted_base, head, 0, far_levels, length
+        )
 
 
 def local_part(table, kinds, inner, running, step, scores, ahead, lifted_base, mixed, near):
@@ -709,8 +723,8 @@
     return pl.pallas_call(
         functools.partial(local_kernel, len(mixed)),
         in_specs=[SMEM, SMEM] + [VMEM] * (6 + len(mixed) + XS),
-        out_specs=VMEM,
-        out_shape=pltpu.VMEM((length, width), F32),
+        out_specs=[VMEM] * 2,
+        out_shape=[pltpu.VMEM((length, width), F32), pltpu.VMEM((length, FAR * width), BF16)],
         scratch_shapes=[pltpu.VMEM((heads, NEAR * DIM, DIM), BF16)],
         compiler_params=params(8),
         cost_estimate=cost(3.8),
@@ -859,9 +873,7 @@
     )(*parts, *befores)
 
 
-def far_kernel(
-    table, kinds, local, gates, lifted_base, f0, f1, f2, f3, gated, squares, held, total
-):
+def far_kernel(local, gates, lifted, f0, f1, f2, f3, gated, squares, held, total):
     x, _ = block_place()
     length, width = local.shape
     heads = width // DIM
@@ -871,13 +883,14 @@
             for level in range(FAR):
                 base = (level * PAIR + head) * DIM
                 held[pair * PAIR + head, level * DIM : (level + 1) * DIM] = far[base : base + DIM]
-    levels = range(5 + NEAR, 5 + NEAR + FAR)
     for pair in range(heads // 2):
         values = []
         for head in (2 * pair, 2 * pair + 1):
             lanes = slice(head * DIM, (head + 1) * DIM)
-            mixed = local[:, lanes] + lift(
-                table, kinds, lifted_base, head, 0, levels, held, length
+            mixed = local[:, lanes] + jnp.dot(
+                lifted[:, head * FAR * DIM : (head + 1) * FAR * DIM],
+                held[head],
+                preferred_element_type=F32,
             )
             value = mixed * gates[:, lanes]
             gated[:, lanes] = value
@@ -891,19 +904,19 @@
         squares[tile : tile + 1] = jnp.sum(part, axis=0, keepdims=True)
 
 
-def far_part(table, kinds, local, gates, lifted_base, far_states):
+def far_part(local, gates, lifted, far_states):
     length, width = local.shape
     heads = width // DIM
     return pl.pallas_call(
         far_kernel,
-        in_specs=[SMEM, SMEM] + [VMEM] * (3 + XS),
+        in_specs=[VMEM] * (3 + XS),
         out_specs=[VMEM] * 2,
         out_shape=[pltpu.VMEM((length, width), F32), pltpu.VMEM((length // TILE, TILE), F32)],
         scratch_shapes=[pltpu.VMEM((heads, FAR * DIM, DIM), BF16), pltpu.VMEM((length, DIM), F32)],
         compiler_params=params(8),
         cost_estimate=cost(3.5),
         name="far_part",
-    )(table, kinds, local, gates, lifted_base, *far_states)
+    )(local, gates, lifted, *far_states)
 
 
 def norm_kernel(total_width, gated, s0, s1, s2, s3, gain, out, made, sems):
@@ -1005,7 +1018,7 @@
     )
     far = fold_far(arrived, (row_before, pair_before, quad_before))
     far = [far[0]] + [along_x(far[k], k) for k in range(1, XS)]
-    local_out = local_part(
+    local_out, lifted = local_part(
         table,
         stretch_kind,
         inner,
@@ -1017,7 +1030,7 @@
         (mixed_first, mixed_second),
         near,
     )
-    gated, squares = far_part(table, stretch_kind, local_out, gates, lifted_base, far)
+    gated, squares = far_part(local_out, gates, lifted, far)
     squares = squares + lax.ppermute(squares, "head", head_perm(lambda y, core: (y, 1 - core)))
     sums = [squares] + [
         lax.ppermute(squares, "head", head_perm(lambda y, core, k=k: ((y + k) % YS, core)))

time: 62.3 us -> 61.9 us (level)
  starting transfers between devices: 30.9 us -> 28 us
  waiting for transfers between devices: 8.47 us -> 10.4 us
    ppermute x6, waiting for transfers between devices: 4.29 us -> 5.98 us  [sent(): lax.ppermute(message.astype(jnp.float16), 'seq', seq_perm(move)).astype(F32)]
    ppermute x6, starting transfers between devices: 12.5 us -> 10.9 us  [sent(): lax.ppermute(message.astype(jnp.float16), 'seq', seq_perm(move)).astype(F32)]
    ppermute x3, waiting for transfers between devices: 1.58 us -> 2.91 us  [local(): lax.ppermute(squares, 'head', head_perm(lambda y, core, k=k: ((y + k) % Y...]
    ppermute x3, starting transfers between devices: 6.43 us -> 5.22 us  [local(): lax.ppermute(squares, 'head', head_perm(lambda y, core, k=k: ((y + k) % Y...]
    pallas_call x1, Pallas kernels: 3.37 us -> 4.56 us  [local_part(): pl.pallas_call(functools.partial(local_kernel, len(mixed)), in_specs=[SME...]
    ppermute x6, waiting for transfers between devices: 1.17 us -> 0.06 us  [along_x(): lax.ppermute(value, 'seq', seq_perm(lambda z, x: (z, (x + step) % XS)))]
  transfers between devices with their start and end apart: 17 -> 17, of which waited for: 7 -> 9; matrix products, arithmetic and copies ran while one was open for 0% -> 0% of each run, Pallas kernels for 26% -> 29%
where the time goes in v8:
time: 61.9 us; the launch traced here: 61.5 us
  starting transfers between devices  28 us (45%)
  Pallas kernels  22.3 us (36%)
  waiting for transfers between devices  10.4 us (17%)
    ppermute x6, starting transfers between devices, sent(): lax.ppermute(message.astype(jnp.float16), 'seq', seq_perm(move)).astype(F32)  10.9 us
    ppermute x6, starting transfers between devices, along_x(): lax.ppermute(value, 'seq', seq_perm(lambda z, x: (z, (x + step) % XS)))  8.15 us
    ppermute x6, waiting for transfers between devices, sent(): lax.ppermute(message.astype(jnp.float16), 'seq', seq_perm(move)).astype(F32)  5.98 us
    ppermute x3, starting transfers between devices, local(): lax.ppermute(squares, 'head', head_perm(lambda y, core, k=k: ((y + k) % Y...  5.22 us
    pallas_call x1, Pallas kernels, local_part(): pl.pallas_call(functools.partial(local_kernel, len(mixed)), in_specs=[SME...  4.56 us
    pallas_call x1, Pallas kernels, prepare(): pl.pallas_call(prepare_kernel, in_specs=[HBM] * 6, out_specs=[VMEM] * (7...  4.13 us
    pallas_call x1, Pallas kernels, shared_part(): pl.pallas_call(shared_kernel, in_specs=[HBM, HBM] + [VMEM] * 7, out_specs...  3.72 us
    ppermute x1, starting transfers between devices, local(): lax.ppermute(last_rows(mixer_input, state_input), 'seq', [(i, i + 1) for...  3.4 us
  transfers between devices with their start and end apart: 17, of which 9 were waited for; matrix products, arithmetic and copies ran while one was open for 0% of the time, Pallas kernels for 29%

profile of v8, /device:TPU:32, one launch (start us, length us, event | category | flops | bytes accessed | tf_op | source)
XLA Modules:
  0.0 61.5 jit_solution(954317606546142098)
XLA Ops:
  0.0 0.8 %last_rows.1 = bf16[16,1280]{1,0:T(8,128)(2,1)S(1)} custom-call(bf16[1024,1024]{1,0:T(8,128)(2,1)} %mixer.5, bf16[1024,256]{1,0:T(8,128)(2,1)} %state.5), custom_call_target="tpu_custom_call" | custom-call | tf_op jit(solution)/shard_map/last_rows/pallas_call | solution.py:154
  0.8 3.4 %collective-permute-start = (bf16[16,1280]{1,0:T(8,128)(2,1)S(1)}, bf16[16,1280]{1,0:T(8,128)(2,1)S(1)}, u32[]{:S(2)}, u32[]{:S(2)}) collective-permute-start(bf16[16,1280]{1,0:T(8,128)(2,1)S(1)} %last_rows.1), channel_id=1, source_target_pairs={{0,8},{8,16},{16,24},{24,32},{32,40},{40,48},{48,56},{56,64},{64,7... | collective-permute-start | bytes 122888 | tf_op jit(solution)/shard_map/ppermute | solution.py:965
  4.2 4.1 %prepare.1 = (bf16[1024,1024]{1,0:T(8,128)(2,1)S(1)}, bf16[1024,128]{1,0:T(8,128)(2,1)S(1)}, f32[8,1024]{1,0:T(8,128)S(1)}, f32[8,1024]{1,0:T(8,128)S(1)}, f32[8...) custom-call(bf16[1024,1024]{1,0:T(8,128)(2,1)} %mixer.5, ...), custom_call_target="tpu_custom_call" | custom-call | flops 5175000064 | bytes 16200000 | tf_op jit(solution)/shard_map/prepare/pallas_call | solution.py:269
  9.5 2.9 %collective-permute-start.3 = (f16[264,128]{1,0:T(8,128)(2,1)S(1)}, f16[264,128]{1,0:T(8,128)(2,1)S(1)}, u32[]{:S(2)}, u32[]{:S(2)}) collective-permute-start(f16[264,128]{1,0:T(8,128)(2,1)S(1)} %convert_element_type.40), channel_id=1, source_target_pairs={{0,24},{8,0},{16,8},{24,16},{32,56},{40,32},{48,40},{56,48},{64,88... | collective-permute-start | bytes 202760 | tf_op jit(solution)/shard_map/ppermute | solution.py:52
  13.5 3.7 %shared_part.1 = (bf16[1024,1024]{1,0:T(8,128)(2,1)S(1)}, f32[1024,1024]{1,0:T(8,128)S(1)}, f32[1024,1024]{1,0:T(8,128)S(1)}, f32[1024,1024]{1,0:T(8,128)S(1)}, f32[264,128]{1,0:T(8,128)S(1)}) custom-call(bf16[1024,1024]{1,0:T(8,128)(2,1)} %mixer.5, bf16[1024,256]{1,0:T(8,128)(2,1)} %state.5, ...), custom_call_target="tpu_custom_call", output_to_operand_aliasing={{0}: (8, {})} | custom-call | flops 3910000128 | bytes 12240000 | tf_op jit(solution)/shard_map/shared_part/pallas_call | solution.py:468
  17.2 1.0 %collective-permute-done.2 = f16[264,128]{1,0:T(8,128)(2,1)S(1)} collective-permute-done((f16[264,128]{1,0:T(8,128)(2,1)S(1)}, f16[264,128]{1,0:T(8,128)(2,1)S(1)}, u32[]{:S(2)}, u32[]{:S(2)}) %collective-permute-start.2) | collective-permute-done | bytes 67616 | tf_op jit(solution)/shard_map/ppermute | solution.py:52
  19.4 1.7 %mix_part.1.rest_0_ = f32[1024,256]{1,0:T(8,128)S(1)} custom-call(f32[640]{0:T(1024)S(1)} %reshape.3.table.refs_0_, s32[16]{0:T(128)S(1)} %copy-done.3, bf16[1024,1024]{1,0:T(8,128)(2,1)S(1)} %get-tuple-element.64.inner.refs_2_, f32[8,1024]{1,0:T(8,128)S(1)} %get-tuple-element.55.running_in.refs_3_, f32[8,1024]{1,0:T(8,128)S(1)} %get-tuple-element.76.step_in.refs_4_, ...), custom_call_target="tpu_custom_call" | custom-call | flops 2300000000 | bytes 7200000 | tf_op jit(solution)/shard_map/mix_part/pallas_call | solution.py:604
  21.1 2.4 %collective-permute-done.4 = f16[264,128]{1,0:T(8,128)(2,1)S(1)} collective-permute-done((f16[264,128]{1,0:T(8,128)(2,1)S(1)}, f16[264,128]{1,0:T(8,128)(2,1)S(1)}, u32[]{:S(2)}, u32[]{:S(2)}) %collective-permute-start.4) | collective-permute-done | bytes 67616 | tf_op jit(solution)/shard_map/ppermute | solution.py:52
  23.7 4.3 %collective-permute-start.5 = (f16[264,128]{1,0:T(8,128)(2,1)S(1)}, f16[264,128]{1,0:T(8,128)(2,1)S(1)}, u32[]{:S(2)}, u32[]{:S(2)}) collective-permute-start(f16[264,128]{1,0:T(8,128)(2,1)S(1)} %convert_element_type.44), channel_id=1, source_target_pairs={{0,64},{8,72},{16,80},{24,88},{32,96},{40,104},{48,112},{56,120},{... | collective-permute-start | bytes 202760 | tf_op jit(solution)/shard_map/ppermute | solution.py:52
  28.3 1.2 %collective-permute-start.7 = (bf16[768,128]{1,0:T(8,128)(2,1)S(1)}, bf16[768,128]{1,0:T(8,128)(2,1)S(1)}, u32[]{:S(2)}, u32[]{:S(2)}) collective-permute-start(bf16[768,128]{1,0:T(8,128)(2,1)S(1)} %get-tuple-element.86), channel_id=1, source_target_pairs={{0,8},{8,16},{16,24},{24,0},{32,40},{40,48},{48,56},{56,32},{64,72... | collective-permute-start | bytes 589832 | tf_op jit(solution)/shard_map/ppermute | solution.py:48
  29.4 1.2 %collective-permute-start.8 = (bf16[768,128]{1,0:T(8,128)(2,1)S(1)}, bf16[768,128]{1,0:T(8,128)(2,1)S(1)}, u32[]{:S(2)}, u32[]{:S(2)}) collective-permute-start(bf16[768,128]{1,0:T(8,128)(2,1)S(1)} %get-tuple-element.87), channel_id=1, source_target_pairs={{0,16},{8,24},{16,0},{24,8},{32,48},{40,56},{48,32},{56,40},{64,80... | collective-permute-start | bytes 589832 | tf_op jit(solution)/shard_map/ppermute | solution.py:48
  30.7 1.9 %collective-permute-start.9 = (bf16[768,128]{1,0:T(8,128)(2,1)S(1)}, bf16[768,128]{1,0:T(8,128)(2,1)S(1)}, u32[]{:S(2)}, u32[]{:S(2)}) collective-permute-start(bf16[768,128]{1,0:T(8,128)(2,1)S(1)} %get-tuple-element.88), channel_id=1, source_target_pairs={{0,24},{8,0},{16,8},{24,16},{32,56},{40,32},{48,40},{56,48},{64,88... | collective-permute-start | bytes 589832 | tf_op jit(solution)/shard_map/ppermute | solution.py:48
  32.8 2.8 %turn_part.2 = (f32[1024,512]{1,0:T(8,128)S(1)}, f32[1024,1024]{1,0:T(8,128)S(1)}) custom-call(f32[640]{0:T(1024)} %copy-done.1, s32[16]{0:T(128)} %kinds.3, bf16[1024,1024]{1,0:T(8,128)(2,1)S(1)} %get-tuple-element.64.inner.refs_2_, f32[8,1024]{1,0:T(8,128)S(1)} %get-tuple-element.55.running_in.refs_3_, f32[8,1024]{1,0:T(8,128)S(1)} %get-tuple-element.76.step_in.refs_4_, ...), custom_call_target="tpu_custom_call" | custom-call | flops 230000000 | bytes 720000 | tf_op jit(solution)/shard_map/turn_part/pallas_call | solution.py:647
  35.6 2.5 %collective-permute-start.6 = (f16[264,128]{1,0:T(8,128)(2,1)S(1)}, f16[264,128]{1,0:T(8,128)(2,1)S(1)}, u32[]{:S(2)}, u32[]{:S(2)}) collective-permute-start(f16[264,128]{1,0:T(8,128)(2,1)S(1)} %convert_element_type.46), channel_id=1, source_target_pairs={{0,224},{8,232},{16,240},{24,248},{32,192},{40,200},{48,208},{56,2... | collective-permute-start | bytes 202760 | tf_op jit(solution)/shard_map/ppermute | solution.py:52
  38.2 1.9 %collective-permute-done.6 = f16[264,128]{1,0:T(8,128)(2,1)S(1)} collective-permute-done((f16[264,128]{1,0:T(8,128)(2,1)S(1)}, f16[264,128]{1,0:T(8,128)(2,1)S(1)}, u32[]{:S(2)}, u32[]{:S(2)}) %collective-permute-start.6) | collective-permute-done | bytes 67616 | tf_op jit(solution)/shard_map/ppermute | solution.py:52
  40.3 1.5 %collective-permute-start.11 = (bf16[512,128]{1,0:T(8,128)(2,1)S(1)}, bf16[512,128]{1,0:T(8,128)(2,1)S(1)}, u32[]{:S(2)}, u32[]{:S(2)}) collective-permute-start(bf16[512,128]{1,0:T(8,128)(2,1)S(1)} %get-tuple-element.95), channel_id=1, source_target_pairs={{0,16},{8,24},{16,0},{24,8},{32,48},{40,56},{48,32},{56,40},{64,80... | collective-permute-start | bytes 393224 | tf_op jit(solution)/shard_map/ppermute | solution.py:48
  41.7 2.3 %collective-permute-start.12 = (bf16[512,128]{1,0:T(8,128)(2,1)S(1)}, bf16[512,128]{1,0:T(8,128)(2,1)S(1)}, u32[]{:S(2)}, u32[]{:S(2)}) collective-permute-start(bf16[512,128]{1,0:T(8,128)(2,1)S(1)} %get-tuple-element.96), channel_id=1, source_target_pairs={{0,24},{8,0},{16,8},{24,16},{32,56},{40,32},{48,40},{56,48},{64,88... | collective-permute-start | bytes 393224 | tf_op jit(solution)/shard_map/ppermute | solution.py:48
  44.0 4.6 %local_part.1 = (f32[1024,1024]{1,0:T(8,128)S(1)}, bf16[1024,2048]{1,0:T(8,128)(2,1)S(1)}) custom-call(f32[640]{0:T(1024)S(1)} %copy-done.2, s32[16]{0:T(128)S(1)} %copy-done.4, bf16[1024,1024]{1,0:T(8,128)(2,1)S(1)} %get-tuple-element.64.inner.refs_2_, f32[8,1024]{1,0:T(8,128)S(1)} %get-tuple-element.55.running_in.refs_3_, ...), custom_call_target="tpu_custom_call" | custom-call | flops 4369999872 | bytes 13680000 | tf_op jit(solution)/shard_map/local_part/pallas_call | solution.py:723
  48.7 1.5 %far_part.1 = (f32[1024,1024]{1,0:T(8,128)S(1)}, f32[8,128]{1,0:T(8,128)S(1)}) custom-call(f32[1024,1024]{1,0:T(8,128)S(1)} %get-tuple-element.89.local, f32[1024,1024]{1,0:T(8,128)S(1)} %get-tuple-element.90.gates, bf16[1024,2048]{1,0:T(8,128)(2,1)S(1)} %get-tuple-element.91.lifted, bf16[512,128]{1,0:T(8,128)(2,1)S(1)} %get-tuple-element.93.f0, ...), custom_call_target="tpu_custom_call" | custom-call | flops 4024999936 | bytes 12600000 | tf_op jit(solution)/shard_map/far_part/pallas_call | solution.py:910
  50.5 1.2 %collective-permute-done.13 = f32[8,128]{1,0:T(8,128)S(1)} collective-permute-done((f32[8,128]{1,0:T(8,128)S(1)}, f32[8,128]{1,0:T(8,128)S(1)}, u32[]{:S(2)}, u32[]{:S(2)}) %collective-permute-start.13) | collective-permute-done | bytes 4128 | tf_op jit(solution)/shard_map/ppermute | solution.py:1034
  51.6 3.0 %collective-permute-start.16 = (f32[8,128]{1,0:T(8,128)S(1)}, f32[8,128]{1,0:T(8,128)S(1)}, u32[]{:S(2)}, u32[]{:S(2)}) collective-permute-start(f32[8,128]{1,0:T(8,128)S(1)} %add.3.s0), channel_id=1, source_target_pairs={{0,6},{1,7},{2,0},{3,1},{4,2},{5,3},{6,4},{7,5},{8,14},{9,15},{10,... | collective-permute-start | bytes 12296 | tf_op jit(solution)/shard_map/ppermute | solution.py:1036
  54.6 2.2 %collective-permute-start.14 = (f32[8,128]{1,0:T(8,128)S(1)}, f32[8,128]{1,0:T(8,128)S(1)}, u32[]{:S(2)}, u32[]{:S(2)}) collective-permute-start(f32[8,128]{1,0:T(8,128)S(1)} %add.3.s0), channel_id=1, source_target_pairs={{0,4},{1,5},{2,6},{3,7},{4,0},{5,1},{6,2},{7,3},{8,12},{9,13},{10,... | collective-permute-start | bytes 12296 | tf_op jit(solution)/shard_map/ppermute | solution.py:1036
  56.8 2.6 %collective-permute-done.15.s2 = f32[8,128]{1,0:T(8,128)S(1)} collective-permute-done((f32[8,128]{1,0:T(8,128)S(1)}, f32[8,128]{1,0:T(8,128)S(1)}, u32[]{:S(2)}, u32[]{:S(2)}) %collective-permute-start.15) | collective-permute-done | bytes 4128 | tf_op jit(solution)/shard_map/ppermute | solution.py:1036
  59.8 1.6 %norm.1 = bf16[1024,1024]{1,0:T(8,128)(2,1)} custom-call(f32[1024,1024]{1,0:T(8,128)S(1)} %get-tuple-element.97.gated, f32[8,128]{1,0:T(8,128)S(1)} %add.3.s0, f32[8,128]{1,0:T(8,128)S(1)} %collective-permute-done.14.s1, f32[8,128]{1,0:T(8,128)S(1)} %collective-permute-done.15.s2, f32[8,128]{1,0:T(8,128)S(1)} %collective-permute-done.16.s3, ...), custom_call_target="tpu_custom_call" | custom-call | flops 1840000000 | bytes 5760000 | tf_op jit(solution)/shard_map/norm/pallas_call | solution.py:940
  (53 shorter events, 4.8 us)
Async XLA Ops:
  0.8 8.0 %collective-permute-start = (bf16[16,1280]{1,0:T(8,128)(2,1)S(1)}, bf16[16,1280]{1,0:T(8,128)(2,1)S(1)}, u32[]{:S(2)}, u32[]{:S(2)}) collective-permute-start(bf16[16,1280]{1,0:T(8,128)(2,1)S(1)} %last_rows.1), channel_id=1, source_target_pairs={{0,8},{8,16},{16,24},{24,32},{32,40},{40,48},{48,56},{56,64},{64,7... | collective-permute-start | bytes 122888 | tf_op jit(solution)/shard_map/ppermute | solution.py:965
  4.2 4.2 %copy-start.6 = (f32[8,13,8]{1,2,0:T(8,128)S(1)}, f32[8,13,8]{1,2,0:T(8,128)}, u32[]{:S(2)}) copy-start(f32[8,13,8]{1,2,0:T(8,128)} %param.17) | copy-start | bytes 9988
  8.5 10.9 %copy-start.1 = (f32[640]{0:T(1024)}, f32[640]{0:T(1024)S(1)}, u32[]{:S(2)}) copy-start(f32[640]{0:T(1024)S(1)} %reshape.3.table.refs_0_) | copy-start | bytes 7684
  9.5 7.7 %collective-permute-start.3 = (f16[264,128]{1,0:T(8,128)(2,1)S(1)}, f16[264,128]{1,0:T(8,128)(2,1)S(1)}, u32[]{:S(2)}, u32[]{:S(2)}) collective-permute-start(f16[264,128]{1,0:T(8,128)(2,1)S(1)} %convert_element_type.40), channel_id=1, source_target_pairs={{0,24},{8,0},{16,8},{24,16},{32,56},{40,32},{48,40},{56,48},{64,88... | collective-permute-start | bytes 202760 | tf_op jit(solution)/shard_map/ppermute | solution.py:52
  12.4 5.9 %collective-permute-start.2 = (f16[264,128]{1,0:T(8,128)(2,1)S(1)}, f16[264,128]{1,0:T(8,128)(2,1)S(1)}, u32[]{:S(2)}, u32[]{:S(2)}) collective-permute-start(f16[264,128]{1,0:T(8,128)(2,1)S(1)} %convert_element_type.38), channel_id=1, source_target_pairs={{0,16},{8,24},{16,0},{24,8},{32,48},{40,56},{48,32},{56,40},{64,80... | collective-permute-start | bytes 202760 | tf_op jit(solution)/shard_map/ppermute | solution.py:52
  12.9 6.1 %collective-permute-start.1 = (f16[264,128]{1,0:T(8,128)(2,1)S(1)}, f16[264,128]{1,0:T(8,128)(2,1)S(1)}, u32[]{:S(2)}, u32[]{:S(2)}) collective-permute-start(f16[264,128]{1,0:T(8,128)(2,1)S(1)} %convert_element_type.36), channel_id=1, source_target_pairs={{0,8},{8,16},{16,24},{24,0},{32,40},{40,48},{48,56},{56,32},{64,72... | collective-permute-start | bytes 202760 | tf_op jit(solution)/shard_map/ppermute | solution.py:52
  13.5 5.9 %copy-start.3 = (s32[16]{0:T(128)S(1)}, s32[16]{0:T(128)}, u32[]{:S(2)}) copy-start(s32[16]{0:T(128)} %kinds.3) | copy-start | bytes 196
  19.2 4.4 %collective-permute-start.4 = (f16[264,128]{1,0:T(8,128)(2,1)S(1)}, f16[264,128]{1,0:T(8,128)(2,1)S(1)}, u32[]{:S(2)}, u32[]{:S(2)}) collective-permute-start(f16[264,128]{1,0:T(8,128)(2,1)S(1)} %convert_element_type.42), channel_id=1, source_target_pairs={{0,32},{8,40},{16,48},{24,56},{32,0},{40,8},{48,16},{56,24},{64,96... | collective-permute-start | bytes 202760 | tf_op jit(solution)/shard_map/ppermute | solution.py:52
  21.1 11.7 %copy-start = (bf16[1024,1024]{1,0:T(8,128)(2,1)S(1)}, bf16[1024,1024]{1,0:T(8,128)(2,1)}, u32[]{:S(2)}) copy-start(bf16[1024,1024]{1,0:T(8,128)(2,1)} %refs_7_.3) | copy-start | bytes 6291460
  23.7 8.9 %collective-permute-start.5 = (f16[264,128]{1,0:T(8,128)(2,1)S(1)}, f16[264,128]{1,0:T(8,128)(2,1)S(1)}, u32[]{:S(2)}, u32[]{:S(2)}) collective-permute-start(f16[264,128]{1,0:T(8,128)(2,1)S(1)} %convert_element_type.44), channel_id=1, source_target_pairs={{0,64},{8,72},{16,80},{24,88},{32,96},{40,104},{48,112},{56,120},{... | collective-permute-start | bytes 202760 | tf_op jit(solution)/shard_map/ppermute | solution.py:52
  28.3 13.4 %collective-permute-start.7 = (bf16[768,128]{1,0:T(8,128)(2,1)S(1)}, bf16[768,128]{1,0:T(8,128)(2,1)S(1)}, u32[]{:S(2)}, u32[]{:S(2)}) collective-permute-start(bf16[768,128]{1,0:T(8,128)(2,1)S(1)} %get-tuple-element.86), channel_id=1, source_target_pairs={{0,8},{8,16},{16,24},{24,0},{32,40},{40,48},{48,56},{56,32},{64,72... | collective-permute-start | bytes 589832 | tf_op jit(solution)/shard_map/ppermute | solution.py:48
  29.4 14.6 %collective-permute-start.8 = (bf16[768,128]{1,0:T(8,128)(2,1)S(1)}, bf16[768,128]{1,0:T(8,128)(2,1)S(1)}, u32[]{:S(2)}, u32[]{:S(2)}) collective-permute-start(bf16[768,128]{1,0:T(8,128)(2,1)S(1)} %get-tuple-element.87), channel_id=1, source_target_pairs={{0,16},{8,24},{16,0},{24,8},{32,48},{40,56},{48,32},{56,40},{64,80... | collective-permute-start | bytes 589832 | tf_op jit(solution)/shard_map/ppermute | solution.py:48
  30.7 13.3 %collective-permute-start.9 = (bf16[768,128]{1,0:T(8,128)(2,1)S(1)}, bf16[768,128]{1,0:T(8,128)(2,1)S(1)}, u32[]{:S(2)}, u32[]{:S(2)}) collective-permute-start(bf16[768,128]{1,0:T(8,128)(2,1)S(1)} %get-tuple-element.88), channel_id=1, source_target_pairs={{0,24},{8,0},{16,8},{24,16},{32,56},{40,32},{48,40},{56,48},{64,88... | collective-permute-start | bytes 589832 | tf_op jit(solution)/shard_map/ppermute | solution.py:48
  35.6 8.4 %copy-start.2 = (f32[640]{0:T(1024)S(1)}, f32[640]{0:T(1024)}, u32[]{:S(2)}) copy-start(f32[640]{0:T(1024)} %copy-done.1) | copy-start | bytes 7684
  35.6 8.4 %copy-start.4 = (s32[16]{0:T(128)S(1)}, s32[16]{0:T(128)}, u32[]{:S(2)}) copy-start(s32[16]{0:T(128)} %kinds.3) | copy-start | bytes 196
  35.6 4.4 %collective-permute-start.6 = (f16[264,128]{1,0:T(8,128)(2,1)S(1)}, f16[264,128]{1,0:T(8,128)(2,1)S(1)}, u32[]{:S(2)}, u32[]{:S(2)}) collective-permute-start(f16[264,128]{1,0:T(8,128)(2,1)S(1)} %convert_element_type.46), channel_id=1, source_target_pairs={{0,224},{8,232},{16,240},{24,248},{32,192},{40,200},{48,208},{56,2... | collective-permute-start | bytes 202760 | tf_op jit(solution)/shard_map/ppermute | solution.py:52
  40.2 8.4 %collective-permute-start.10 = (bf16[512,128]{1,0:T(8,128)(2,1)S(1)}, bf16[512,128]{1,0:T(8,128)(2,1)S(1)}, u32[]{:S(2)}, u32[]{:S(2)}) collective-permute-start(bf16[512,128]{1,0:T(8,128)(2,1)S(1)} %get-tuple-element.94), channel_id=1, source_target_pairs={{0,8},{8,16},{16,24},{24,0},{32,40},{40,48},{48,56},{56,32},{64,72... | collective-permute-start | bytes 393224 | tf_op jit(solution)/shard_map/ppermute | solution.py:48
  40.3 8.4 %collective-permute-start.11 = (bf16[512,128]{1,0:T(8,128)(2,1)S(1)}, bf16[512,128]{1,0:T(8,128)(2,1)S(1)}, u32[]{:S(2)}, u32[]{:S(2)}) collective-permute-start(bf16[512,128]{1,0:T(8,128)(2,1)S(1)} %get-tuple-element.95), channel_id=1, source_target_pairs={{0,16},{8,24},{16,0},{24,8},{32,48},{40,56},{48,32},{56,40},{64,80... | collective-permute-start | bytes 393224 | tf_op jit(solution)/shard_map/ppermute | solution.py:48
  41.7 7.0 %collective-permute-start.12 = (bf16[512,128]{1,0:T(8,128)(2,1)S(1)}, bf16[512,128]{1,0:T(8,128)(2,1)S(1)}, u32[]{:S(2)}, u32[]{:S(2)}) collective-permute-start(bf16[512,128]{1,0:T(8,128)(2,1)S(1)} %get-tuple-element.96), channel_id=1, source_target_pairs={{0,24},{8,0},{16,8},{24,16},{32,56},{40,32},{48,40},{56,48},{64,88... | collective-permute-start | bytes 393224 | tf_op jit(solution)/shard_map/ppermute | solution.py:48
  48.7 11.1 %copy-start.5 = (f32[1024]{0:T(1024)S(1)}, f32[1024]{0:T(1024)}, u32[]{:S(2)}) copy-start(f32[1024]{0:T(1024)} %param.19) | copy-start | bytes 12292
  50.1 1.5 %collective-permute-start.13 = (f32[8,128]{1,0:T(8,128)S(1)}, f32[8,128]{1,0:T(8,128)S(1)}, u32[]{:S(2)}, u32[]{:S(2)}) collective-permute-start(f32[8,128]{1,0:T(8,128)S(1)} %get-tuple-element.98), channel_id=1, source_target_pairs={{0,1},{1,0},{2,3},{3,2},{4,5},{5,4},{6,7},{7,6},{8,9},{9,8},{10,11... | collective-permute-start | bytes 12296 | tf_op jit(solution)/shard_map/ppermute | solution.py:1034
  51.6 5.2 %collective-permute-start.16 = (f32[8,128]{1,0:T(8,128)S(1)}, f32[8,128]{1,0:T(8,128)S(1)}, u32[]{:S(2)}, u32[]{:S(2)}) collective-permute-start(f32[8,128]{1,0:T(8,128)S(1)} %add.3.s0), channel_id=1, source_target_pairs={{0,6},{1,7},{2,0},{3,1},{4,2},{5,3},{6,4},{7,5},{8,14},{9,15},{10,... | collective-permute-start | bytes 12296 | tf_op jit(solution)/shard_map/ppermute | solution.py:1036
  54.6 4.8 %collective-permute-start.15 = (f32[8,128]{1,0:T(8,128)S(1)}, f32[8,128]{1,0:T(8,128)S(1)}, u32[]{:S(2)}, u32[]{:S(2)}) collective-permute-start(f32[8,128]{1,0:T(8,128)S(1)} %add.3.s0), channel_id=1, source_target_pairs={{0,2},{1,3},{2,4},{3,5},{4,6},{5,7},{6,0},{7,1},{8,10},{9,11},{10,... | collective-permute-start | bytes 12296 | tf_op jit(solution)/shard_map/ppermute | solution.py:1036
  54.6 5.1 %collective-permute-start.14 = (f32[8,128]{1,0:T(8,128)S(1)}, f32[8,128]{1,0:T(8,128)S(1)}, u32[]{:S(2)}, u32[]{:S(2)}) collective-permute-start(f32[8,128]{1,0:T(8,128)S(1)} %add.3.s0), channel_id=1, source_target_pairs={{0,4},{1,5},{2,6},{3,7},{4,0},{5,1},{6,2},{7,3},{8,12},{9,13},{10,... | collective-permute-start | bytes 12296 | tf_op jit(solution)/shard_map/ppermute | solution.py:1036
